TPU v7x, 32 devices: a whole 2x2x4 slice. The times are simulated.
32 devices in a mesh: row: 8 (over z, y), col: 4 (over x, core).
Axes of the slice: x: 2, y: 2, z: 4, core: 2. Of those that a mesh axis runs over, the one named last changes fastest.
Arguments:
- right_side: float32 [8192, 512], P(('row', 'col')), may hold values from -6 to 6
- earlier_panel: bfloat16 [8192, 8, 1024], P('row', None, 'col'), may hold values from -0.0625 to 0.0625
- earlier_solution: bfloat16 [8, 1024, 512], P('row', 'col'), may hold values from -6 to 6
- window_panel: bfloat16 [8192, 3, 1024], P(('row', 'col')), may hold values from -0.109375 to 0.109375
- diag_inverse: bfloat16 [3, 1024, 1024], P(None, 'col'), as said below
Outputs:
- solved: bfloat16 [3, 1024, 512], P(None, 'col')
- remaining: float32 [8192, 512], P(('row', 'col'))
Inputs may be any that keep to these rules, and one draw needn't show every extreme that they name: Each diag_inverse[k] is zero above its diagonal, and its diagonal lies between 0.5 and 2.
All inputs are finite; a program needn't handle non-finite values.
Results may differ from a plain program's by a relative error of at most 0.013.
Values may be sent and summed in bfloat16 or wider, within the bound.
No kernel may reach another device: no remote copies, remote signals or barrier semaphores. Data moves between devices by JAX's collectives and lax.ppermute only.
A program may use at most 64 MiB of HBM per device.

v0:
```python
import jax
import jax.numpy as jnp
from jax import lax
from jax.sharding import PartitionSpec as P


def spread(value, axis, source):
    kept = jnp.where(lax.axis_index(axis) == source, value, 0).astype(value.dtype)
    return lax.psum(kept, axis)


def on_device(right_side, earlier_panel, earlier_solution, window_panel, diag_inverse):
    step_count = diag_inverse.shape[0]
    row_index = lax.axis_index("row")
    partial_sum = jnp.einsum(
        "iqw,qwn->in",
        earlier_panel,
        lax.all_gather(earlier_solution, "row", axis=0, tiled=True),
        preferred_element_type=jnp.float32,
    )
    settled = right_side - lax.psum_scatter(
        partial_sum.astype(jnp.bfloat16), "col", scatter_dimension=0, tiled=True
    ).astype(jnp.float32)
    current = settled
    outputs = []
    for step_index in range(step_count):
        residual = current.astype(jnp.bfloat16)
        inverse_rows = diag_inverse[step_index]
        solution_strip = jnp.dot(
            inverse_rows,
            lax.all_gather(residual, "col", axis=0, tiled=True),
            preferred_element_type=jnp.float32,
        ).astype(jnp.bfloat16)
        step_panel = window_panel[:, step_index, :]
        own_strip = spread(solution_strip, "row", step_index)
        update = jnp.dot(
            step_panel,
            lax.all_gather(own_strip, "col", axis=0, tiled=True),
            preferred_element_type=jnp.float32,
        )
        outputs.append(own_strip)
        current = jnp.where(row_index > step_index, current - update, current)
    return (jnp.stack(outputs), current)


def solution(mesh):
    return jax.shard_map(
        on_device,
        mesh=mesh,
        in_specs=(
            P(("row", "col"), None),
            P("row", None, "col"),
            P("row", "col", None),
            P(("row", "col"), None, None),
            P(None, "col", None),
        ),
        out_specs=(P(None, "col", None), P(("row", "col"), None)),
        check_vma=False,
    )
```

profile of v0, /device:TPU:25, one launch (start us, length us, event | category | flops | bytes accessed | tf_op | source)
XLA Modules:
  0.0 434.2 jit_solution(2329556905765640344)
XLA Ops:
  7.2 0.0 all-gather.8.cloned.1.call-start
  7.2 0.7 all-gather.8.cloned.1.call-update
  7.9 0.0 copy-start
  7.9 0.0 reduce-scatter.2.cloned.1.call-start
  8.0 50.9 %all-gather.8.cloned.1.call-done = bf16[8,256,512]{2,1,0:T(8,128)(2,1)} async-done(((bf16[1,256,512]{2,1,0:T(8,128)(2,1)}), bf16[8,256,512]{2,1,0:T(8,128)(2,1)}) %all-gather.8.cloned.1.call-update) | async-done | bytes 2097168 | tf_op jit(solution)/shard_map/all_gather | solution.py:18
  58.8 6.2 %bitcast_convert_fusion = bf16[1024,512]{1,0:T(8,128)(2,1)} fusion(bf16[8,256,512]{2,1,0:T(8,128)(2,1)} %all-gather.8.cloned.1.call-done, bf16[1024,8,256]{2,1,0:T(8,128)(2,1)} %param.6), kind=kOutput, calls=%fused_computation.2 | convolution fusion | flops 2148007936 | bytes 7340032 | tf_op jit(solution)/shard_map/iqw,qwn->in/dot_general | solution.py:15
  65.1 0.0 reduce-scatter.2.cloned.1.call-update
  65.1 0.0 all-gather.10.cloned.1.call-start
  65.1 25.0 %reduce-scatter.2.cloned.1.call-done = bf16[256,512]{1,0:T(8,128)(2,1)} async-done(((bf16[1024,512]{1,0:T(8,128)(2,1)}), bf16[256,512]{1,0:T(8,128)(2,1)}) %reduce-scatter.2.cloned.1.call-update) | async-done | bytes 262160 | tf_op jit(solution)/shard_map/reduce_scatter | solution.py:21
  90.2 0.0 copy-done
  90.2 1.7 fusion.28
  91.9 0.0 copy-start.1
  91.9 0.0 copy-start.4
  91.9 0.0 all-gather.10.cloned.1.call-update
  91.9 0.0 all-reduce.4.cloned.1.call-start
  92.0 17.6 %all-gather.10.cloned.1.call-done = bf16[1024,512]{1,0:T(8,128)(2,1)} async-done(((bf16[256,512]{1,0:T(8,128)(2,1)}), bf16[1024,512]{1,0:T(8,128)(2,1)}) %all-gather.10.cloned.1.call-update) | async-done | bytes 1048592 | tf_op jit(solution)/shard_map/all_gather | solution.py:31
  109.5 2.6 fusion.15
  112.1 0.0 all-reduce.4.cloned.1.call-update
  112.1 0.0 all-gather.12.cloned.1.call-start
  112.2 68.9 %all-reduce.4.cloned.1.call-done = bf16[256,512]{0,1:T(8,128)(2,1)} async-done(((bf16[256,512]{0,1:T(8,128)(2,1)}), bf16[256,512]{0,1:T(8,128)(2,1)}) %all-reduce.4.cloned.1.call-update) | async-done | bytes 262160 | tf_op jit(solution)/shard_map/psum | solution.py:9
  181.1 0.0 all-gather.12.cloned.1.call-update
  181.1 0.0 all-gather.14.cloned.1.call-start
  181.1 20.7 %all-gather.12.cloned.1.call-done = bf16[1024,512]{0,1:T(8,128)(2,1)} async-done(((bf16[256,512]{0,1:T(8,128)(2,1)}), bf16[1024,512]{0,1:T(8,128)(2,1)}) %all-gather.12.cloned.1.call-update) | async-done | bytes 1048592 | tf_op jit(solution)/shard_map/all_gather | solution.py:38
  201.8 0.0 copy-done.1
  201.8 0.0 copy-done.4
  201.9 2.4 fusion.29
  204.3 0.0 all-gather.14.cloned.1.call-update
  204.3 0.0 all-reduce.6.cloned.1.call-start
  204.3 16.8 %all-gather.14.cloned.1.call-done = bf16[1024,512]{1,0:T(8,128)(2,1)} async-done(((bf16[256,512]{1,0:T(8,128)(2,1)}), bf16[1024,512]{1,0:T(8,128)(2,1)}) %all-gather.14.cloned.1.call-update) | async-done | bytes 1048592 | tf_op jit(solution)/shard_map/all_gather | solution.py:31
  221.2 2.6 fusion.14
  223.7 0.0 all-reduce.6.cloned.1.call-update
  223.7 0.0 all-gather.16.cloned.1.call-start
  223.8 68.6 %all-reduce.6.cloned.1.call-done = bf16[256,512]{0,1:T(8,128)(2,1)} async-done(((bf16[256,512]{0,1:T(8,128)(2,1)}), bf16[256,512]{0,1:T(8,128)(2,1)}) %all-reduce.6.cloned.1.call-update) | async-done | bytes 262160 | tf_op jit(solution)/shard_map/psum | solution.py:9
  292.4 0.0 all-gather.16.cloned.1.call-update
  292.5 0.0 all-gather.18.cloned.1.call-start
  292.5 20.9 %all-gather.16.cloned.1.call-done = bf16[1024,512]{0,1:T(8,128)(2,1)} async-done(((bf16[256,512]{0,1:T(8,128)(2,1)}), bf16[1024,512]{0,1:T(8,128)(2,1)}) %all-gather.16.cloned.1.call-update) | async-done | bytes 1048592 | tf_op jit(solution)/shard_map/all_gather | solution.py:38
  313.5 2.4 fusion.30
  315.9 0.0 copy-start.2
  315.9 0.0 copy-start.3
  315.9 0.0 all-gather.18.cloned.1.call-update
  315.9 0.0 all-reduce.8.cloned.1.call-start
  315.9 16.8 %all-gather.18.cloned.1.call-done = bf16[1024,512]{1,0:T(8,128)(2,1)} async-done(((bf16[256,512]{1,0:T(8,128)(2,1)}), bf16[1024,512]{1,0:T(8,128)(2,1)}) %all-gather.18.cloned.1.call-update) | async-done | bytes 1048592 | tf_op jit(solution)/shard_map/all_gather | solution.py:31
  332.8 2.6 fusion.13
  335.3 0.0 all-reduce.8.cloned.1.call-update
  335.3 0.0 all-gather.20.cloned.1.call-start
  335.4 68.9 %all-reduce.8.cloned.1.call-done = bf16[256,512]{0,1:T(8,128)(2,1)} async-done(((bf16[256,512]{0,1:T(8,128)(2,1)}), bf16[256,512]{0,1:T(8,128)(2,1)}) %all-reduce.8.cloned.1.call-update) | async-done | bytes 262160 | tf_op jit(solution)/shard_map/psum | solution.py:9
  404.3 0.0 all-gather.20.cloned.1.call-update
  404.3 0.0 copy-done.2
  404.3 0.0 copy-done.3
  404.3 1.0 pad_maximum_fusion
  405.4 1.2 copy.16
  406.5 18.7 %all-gather.20.cloned.1.call-done = bf16[1024,512]{0,1:T(8,128)(2,1)} async-done(((bf16[256,512]{0,1:T(8,128)(2,1)}), bf16[1024,512]{0,1:T(8,128)(2,1)}) %all-gather.20.cloned.1.call-update) | async-done | bytes 1048592 | tf_op jit(solution)/shard_map/all_gather | solution.py:38
  425.2 2.5 fusion.5
Async XLA Ops:
  7.2 51.7 %all-gather.8.cloned.1.call-start = ((), (), s32[]{:S(2)}) async-start(), calls=%async_computation.1 | async-start | bytes 2359296 | tf_op jit(solution)/shard_map/all_gather | solution.py:18
  7.9 82.3 %copy-start = (f32[256,512]{1,0:T(8,128)S(1)}, f32[256,512]{1,0:T(8,128)}, u32[]{:S(2)}) copy-start(f32[256,512]{1,0:T(8,128)} %param.5) | copy-start | bytes 1572868
  7.9 82.2 %reduce-scatter.2.cloned.1.call-start = ((), (), s32[]{:S(2)}) async-start(), calls=%async_computation.2 | async-start | bytes 1310720 | tf_op jit(solution)/shard_map/reduce_scatter | solution.py:21
  65.1 44.5 %all-gather.10.cloned.1.call-start = ((), (), s32[]{:S(2)}) async-start(), calls=%async_computation.3 | async-start | bytes 1310720 | tf_op jit(solution)/shard_map/all_gather | solution.py:31
  91.9 110.0 %copy-start.1 = (bf16[256,3,1024]{2,0,1:T(8,128)(2,1)S(1)}, bf16[256,3,1024]{2,0,1:T(8,128)(2,1)}, u32[]{:S(2)}) copy-start(bf16[256,3,1024]{2,0,1:T(8,128)(2,1)} %param.8) | copy-start | bytes 4718596
  91.9 110.0 %copy-start.4 = (bf16[256,512]{1,0:T(8,128)(2,1)S(1)}, bf16[256,512]{1,0:T(8,128)(2,1)}, u32[]{:S(2)}) copy-start(bf16[256,512]{1,0:T(8,128)(2,1)} %reduce-scatter.2.cloned.1.call-done) | copy-start | bytes 786436
  91.9 89.1 %all-reduce.4.cloned.1.call-start = ((), (), s32[]{:S(2)}) async-start(), calls=%async_computation.4 | async-start | bytes 524288 | tf_op jit(solution)/shard_map/psum | solution.py:9
  112.1 89.7 %all-gather.12.cloned.1.call-start = ((), (), s32[]{:S(2)}) async-start(), calls=%async_computation.5 | async-start | bytes 1310720 | tf_op jit(solution)/shard_map/all_gather | solution.py:38
  181.1 40.1 %all-gather.14.cloned.1.call-start = ((), (), s32[]{:S(2)}) async-start(), calls=%async_computation.6 | async-start | bytes 1310720 | tf_op jit(solution)/shard_map/all_gather | solution.py:31
  204.3 88.1 %all-reduce.6.cloned.1.call-start = ((), (), s32[]{:S(2)}) async-start(), calls=%async_computation.7 | async-start | bytes 524288 | tf_op jit(solution)/shard_map/psum | solution.py:9
  223.7 89.7 %all-gather.16.cloned.1.call-start = ((), (), s32[]{:S(2)}) async-start(), calls=%async_computation.8 | async-start | bytes 1310720 | tf_op jit(solution)/shard_map/all_gather | solution.py:38
  292.5 40.3 %all-gather.18.cloned.1.call-start = ((), (), s32[]{:S(2)}) async-start(), calls=%async_computation.9 | async-start | bytes 1310720 | tf_op jit(solution)/shard_map/all_gather | solution.py:31
  315.9 88.4 %copy-start.2 = (bf16[256,512]{0,1:T(8,128)(2,1)S(1)}, bf16[256,512]{0,1:T(8,128)(2,1)}, u32[]{:S(2)}) copy-start(bf16[256,512]{0,1:T(8,128)(2,1)} %all-reduce.4.cloned.1.call-done) | copy-start | bytes 786436
  315.9 88.4 %copy-start.3 = (bf16[256,512]{0,1:T(8,128)(2,1)S(1)}, bf16[256,512]{0,1:T(8,128)(2,1)}, u32[]{:S(2)}) copy-start(bf16[256,512]{0,1:T(8,128)(2,1)} %all-reduce.6.cloned.1.call-done) | copy-start | bytes 786436
  315.9 88.4 %all-reduce.8.cloned.1.call-start = ((), (), s32[]{:S(2)}) async-start(), calls=%async_computation.10 | async-start | bytes 524288 | tf_op jit(solution)/shard_map/psum | solution.py:9
  335.3 89.9 %all-gather.20.cloned.1.call-start = ((), (), s32[]{:S(2)}) async-start(), calls=%async_computation.11 | async-start | bytes 1310720 | tf_op jit(solution)/shard_map/all_gather | solution.py:38
Sparse Core Ops, SparseCore 0:
  10.1 48.6 all-gather.7
  65.2 24.9 reduce-scatter.1
  92.4 17.1 all-gather.9
  113.7 67.3 all-reduce.3
  182.5 19.3 all-gather.11
  204.4 16.7 all-gather.13
  225.1 67.3 all-reduce.5
  294.1 19.3 all-gather.15
  316.0 16.7 all-gather.17
  336.9 67.3 all-reduce.7
  405.8 19.3 all-gather.19
where the time goes:
time: 436 us; the launch traced here: 434 us
  waiting for transfers between devices  395 us (91%)
  matrix products  21.2 us (5%)
  between operations  13.9 us (3%)
    psum x3, waiting for transfers between devices, spread(): return lax.psum(kept, axis)  206 us
    all_gather x3, waiting for transfers between devices, on_device(): lax.all_gather(own_strip, 'col', axis=0, tiled=True)  60.4 us
    all_gather x3, waiting for transfers between devices, on_device(): lax.all_gather(residual, 'col', axis=0, tiled=True)  51.2 us
    all_gather x1, waiting for transfers between devices, on_device(): lax.all_gather(earlier_solution, 'row', axis=0, tiled=True)  50.9 us
    reduce_scatter x1, waiting for transfers between devices, on_device(): lax.psum_scatter(partial_sum.astype(jnp.bfloat16), 'col', scatter_dimensi...  25 us
  transfers between devices with their start and end apart: 11, of which 11 were waited for; matrix products, arithmetic and copies ran while one was open for 1% of the time, Pallas kernels for 0%

commit v1 on v0

v1 whole, which is shorter than its diff:
```python
import jax
import jax.numpy as jnp
from jax import lax
from jax.sharding import PartitionSpec as P

F32 = jnp.float32
BF16 = jnp.bfloat16


def flip(value, axis, size, bit):
    return lax.ppermute(value, axis, [(i, i ^ bit) for i in range(size)])


def matmul(left, right):
    return jnp.dot(left, right, preferred_element_type=F32)


def halves(value, bit):
    kept = lax.dynamic_index_in_dim(value, bit, 0, keepdims=False)
    sent = lax.dynamic_index_in_dim(value, 1 - bit, 0, keepdims=False)
    return kept, sent


def gather_ordered(value, n_col, col):
    bit = n_col // 2
    bits = []
    while bit:
        bits.append(bit)
        bit //= 2
    order = [b for b in bits if b > 1] + [1]
    parts = {0: value}
    for b in order:
        moved = {f ^ b: flip(v, "col", n_col, b) for f, v in parts.items()}
        parts.update(moved)
    stacked = jnp.stack([parts[f] for f in range(n_col)])
    index = jnp.arange(n_col) ^ col
    return stacked[index].reshape(-1, value.shape[1])


def reduce_chunks(value, n_col, col):
    bit = 1
    while bit < n_col:
        rest = value.shape[0] // 2
        paired = value.reshape((rest, 2) + value.shape[1:]).swapaxes(0, 1)
        kept, sent = halves(paired, (col // bit) % 2)
        value = kept + flip(sent.astype(BF16), "col", n_col, bit).astype(F32)
        bit *= 2
    return value[0]


def gather_lines(block, n_row, row):
    per_line = 1
    while 4 * per_line * per_line <= n_row:
        per_line *= 2
    lines = n_row // per_line
    blocks = [(block, row)]
    up, down = block, block
    for s in range(1, lines):
        up = lax.ppermute(up, "row", [(i, i + per_line) for i in range((s - 1) * per_line, n_row - per_line)])
        down = lax.ppermute(down, "row", [(i, i - per_line) for i in range(per_line, n_row - (s - 1) * per_line)])
        blocks += [(up, row - s * per_line), (down, row + s * per_line)]
    for bit in range(1, per_line):
        blocks += [(flip(v, "row", n_row, bit), source ^ bit) for v, source in blocks[: 2 * lines - 1]]
    return blocks


def on_device(shape, right_side, earlier_panel, earlier_solution, window_panel, diag_inverse):
    n_row, n_col = shape
    step_count = diag_inverse.shape[0]
    row, col = lax.axis_index("row"), lax.axis_index("col")
    strip, nrhs = right_side.shape
    rows = earlier_panel.shape[0]
    chunk = nrhs // n_col
    weights = []
    for j in range(step_count):
        own = jnp.where(row == j, diag_inverse[j], window_panel[:, j, :])
        weights.append(gather_ordered(own, n_col, col))

    total = jnp.zeros((n_col, strip, nrhs), F32)
    total = lax.dynamic_update_index_in_dim(total, -right_side, col, 0).reshape(rows, nrhs)
    if n_row > 8:
        everything = lax.all_gather(earlier_solution, "row", axis=0, tiled=True)
        total = total + jnp.einsum("iqw,qwn->in", earlier_panel, everything, preferred_element_type=F32)
    else:
        panel = earlier_panel.swapaxes(0, 1)
        for v, source in gather_lines(earlier_solution[0], n_row, row):
            part = lax.dynamic_index_in_dim(panel, jnp.clip(source, 0, n_row - 1), 0, keepdims=False)
            total = total + matmul(part, v)
    chunks = total.reshape(rows, n_col, chunk).swapaxes(0, 1)
    current = -reduce_chunks(chunks, n_col, col)

    bases = [[1, 2, 4], [3, 1, 4], [6, 2, 1]]
    solved = []
    for k in range(step_count):
        value = matmul(weights[k], current.astype(BF16)).astype(BF16)
        have = [k]
        bits = [b for b in bases[k]] + [1 << i for i in range(3, 16) if (1 << i) < n_row]
        for b in bits:
            moved = lax.ppermute(value, "row", [(i, i ^ b) for i in have])
            into = jnp.zeros((), bool)
            for i in have:
                into |= row == (i ^ b)
            value = jnp.where(into, moved, value)
            have += [i ^ b for i in have]
        solved.append(value)
        current = jnp.where(row > k, current - matmul(weights[k], value), current)
    early = lax.all_to_all(jnp.stack(solved[:-1]), "col", 1, 2, tiled=True)
    late = lax.all_to_all(jnp.stack([solved[-1], current.astype(BF16)]), "col", 1, 2, tiled=True)
    return jnp.concatenate([early, late[:1]]), late[1].astype(F32)


def solution(mesh):
    shape = (mesh.shape["row"], mesh.shape["col"])

    def step(*args):
        return on_device(shape, *args)

    return jax.shard_map(
        step,
        mesh=mesh,
        in_specs=(
            P(("row", "col"), None),
            P("row", None, "col"),
            P("row", "col", None),
            P(("row", "col"), None, None),
            P(None, "col", None),
        ),
        out_specs=(P(None, "col", None), P(("row", "col"), None)),
        check_vma=False,
    )
```

time: 436 us -> 239 us (0.55)
  waiting for transfers between devices: 395 us -> 76.3 us
  local copies, waits for them, and re-layouts: 1.18 us -> 66.3 us
  starting transfers between devices: 0.45 us -> 44.7 us
  other arithmetic: 2.76 us -> 19.2 us
  between operations: 13.9 us -> 1.4 us
  matrix products: 21.2 us -> 29.5 us
    psum x3 -> x0, waiting for transfers between devices: 206 us -> none  [spread(): return lax.psum(kept, axis)]
    all_gather x7 -> x0, waiting for transfers between devices: 162 us -> none  [the longest x3 60.4 us: on_device(): lax.all_gather(own_strip, 'col', axis=0, tiled=True)]
    ppermute x0 -> x33, waiting for transfers between devices: none -> 64.1 us  [the longest x9 37 us: on_device(): moved = lax.ppermute(value, 'row', [(i, i ^ b) for i in have])]
    another operation x0 -> x4, local copies, waits for them, and re-layouts: none -> 41.4 us
    ppermute x0 -> x33, starting transfers between devices: none -> 34.7 us  [the longest x18 15.5 us: flip(): return lax.ppermute(value, axis, [(i, i ^ bit) for i in range(size)])]
    reduce_scatter x1 -> x0, waiting for transfers between devices: 25 us -> none  [on_device(): lax.psum_scatter(partial_sum.astype(jnp.bfloat16), 'col', scatter_dimensi...]
    all_to_all x0 -> x2, waiting for transfers between devices: none -> 12.3 us  [the longest x1 6.32 us: on_device(): lax.all_to_all(jnp.stack([solved[-1], current.astype(BF16)]), 'col', 1, 2...]
    all_to_all x0 -> x2, starting transfers between devices: none -> 9.99 us  [the longest x1 5.68 us: on_device(): early = lax.all_to_all(jnp.stack(solved[:-1]), 'col', 1, 2, tiled=True)]
  transfers between devices with their start and end apart: 11 -> 35, of which waited for: 11 -> 13; matrix products, arithmetic and copies ran while one was open for 1% -> 43% of each run, Pallas kernels for 0% -> 0%
where the time goes in v1:
time: 239 us; the launch traced here: 237 us
  waiting for transfers between devices  76.3 us (32%)
  local copies, waits for them, and re-layouts  66.3 us (28%)
  starting transfers between devices  44.7 us (19%)
  matrix products  29.5 us (12%)
  other arithmetic  19.2 us (8%)
    another operation x2, local copies, waits for them, and re-layouts  38.7 us
    ppermute x9, waiting for transfers between devices, on_device(): moved = lax.ppermute(value, 'row', [(i, i ^ b) for i in have])  37 us
    dot_general x20, matrix products, matmul(): return jnp.dot(left, right, preferred_element_type=F32)  29.5 us
    ppermute x18, waiting for transfers between devices, flip(): return lax.ppermute(value, axis, [(i, i ^ bit) for i in range(size)])  25 us
    ppermute x18, starting transfers between devices, flip(): return lax.ppermute(value, axis, [(i, i ^ bit) for i in range(size)])  15.5 us
    ppermute x9, starting transfers between devices, on_device(): moved = lax.ppermute(value, 'row', [(i, i ^ b) for i in have])  9.47 us
    gather x3, local copies, waits for them, and re-layouts, gather_ordered(): return stacked[index].reshape(-1, value.shape[1])  8.23 us
    dynamic_update_slice x1, local copies, waits for them, and re-layouts, on_device(): lax.dynamic_update_index_in_dim(total, -right_side, col, 0)  7.22 us
  transfers between devices with their start and end apart: 35, of which 13 were waited for; matrix products, arithmetic and copies ran while one was open for 43% of the time, Pallas kernels for 0%

profile of v1, /device:TPU:25, one launch (start us, length us, event | category | flops | bytes accessed | tf_op | source)
XLA Modules:
  0.0 237.4 jit_solution(1914979231841998101)
XLA Ops:
  0.6 1.3 collective-permute-start.3
  1.9 4.0 %collective-permute-start.4 = (bf16[256,512]{1,0:T(8,128)(2,1)}, bf16[256,512]{1,0:T(8,128)(2,1)S(1)}, u32[]{:S(2)}, u32[]{:S(2)}) collective-permute-start(bf16[256,512]{1,0:T(8,128)(2,1)} %bitcast.154), channel_id=1, source_target_pairs={{8,0},{12,4},{16,8},{20,12},{24,16},{28,20},{9,1},{13,5},{17,9},{2... | collective-permute-start | bytes 786440 | tf_op jit(solution)/shard_map/ppermute | solution.py:60
  5.9 1.3 collective-permute-start.9
  7.3 3.1 %bitcast_select_fusion = (bf16[256,1024]{1,0:T(8,128)(2,1)}, bf16[256,1024]{1,0:T(8,128)(2,1)}, bf16[256,1024]{1,0:T(8,128)(2,1)}) fusion(pred[]{:T(512)S(6)} %eq.23, bf16[256,3,1024]{2,0,1:T(8,128)(2,1)} %param.8, bf16[3,256,1024]{2,1,0:T(8,128)(2,1)} %param.9, pred[]{:T(512)S(6)} %eq.50, pred[]{:T(512)S(6)} %eq.25), kind=kLoop, calls=%fused_computation.50 | loop fusion | flops 786432 | bytes 4718595 | tf_op jit(solution)/shard_map/jit(_where)/select_n | solution.py:76
  10.4 1.2 collective-permute-start.22
  12.6 7.2 %dynamic_update_slice.4 = f32[4,256,512]{1,0,2:T(4,128)S(1)} dynamic-update-slice(f32[4,256,512]{1,0,2:T(4,128)S(1)} %broadcast_in_dim.10, f32[1,256,512]{1,0,2:T(1,128)S(1)} %copy.74, s32[]{:T(128)S(6)} %select_n.180, s32[]{:T(128)} %constant.122.clone.1, s32[]{:T(128)} %constant.122.clone.1) | dynamic-update-slice | bytes 1048580 | tf_op jit(solution)/shard_map/jit(dynamic_update_index_in_dim)/dynamic_update_slice | solution.py:80
  19.8 1.8 copy.115
  21.6 38.6 %constant_dynamic-slice_fusion.1 = (bf16[1024,1,256]{2,1,0:T(2,128)(2,1)S(1)}, bf16[1024,1,256]{2,1,0:T(2,128)(2,1)S(1)}, bf16[1024,1,256]{2,1,0:T(2,128)(2,1)},...) fusion(bf16[1024,8,256]{2,1,0:T(8,128)(2,1)} %param.6, ...), kind=kLoop, calls=%fused_computation.79 | loop fusion | bytes 14680120 | tf_op jit(solution)/shard_map/dynamic-slice.13
  60.3 1.8 fusion.18
  62.1 1.4 collective-permute-start.5
  64.7 1.5 fusion.17
  66.6 1.5 fusion.11
  68.0 2.0 collective-permute-done.5
  70.8 1.3 collective-permute-start.7
  72.6 1.0 collective-permute-start.8
  74.1 4.3 %collective-permute-done.11 = bf16[256,512]{1,0:T(8,128)(2,1)S(1)} collective-permute-done((bf16[256,512]{1,0:T(8,128)(2,1)S(1)}, bf16[256,512]{1,0:T(8,128)(2,1)S(1)}, u32[]{:S(2)}, u32[]{:S(2)}) %collective-permute-start.11) | collective-permute-done | bytes 262176 | tf_op jit(solution)/shard_map/ppermute | solution.py:11
  79.1 1.3 collective-permute-start.12
  80.4 1.8 fusion.13
  82.5 1.8 fusion.12
  84.3 1.2 collective-permute-start.15
  85.6 1.8 fusion.7
  87.4 1.9 collective-permute-done.12
  89.3 1.9 fusion.8
  91.2 3.7 %collective-permute-done.14 = bf16[256,512]{1,0:T(8,128)(2,1)S(1)} collective-permute-done((bf16[256,512]{1,0:T(8,128)(2,1)S(1)}, bf16[256,512]{1,0:T(8,128)(2,1)S(1)}, u32[]{:S(2)}, u32[]{:S(2)}) %collective-permute-start.14) | collective-permute-done | bytes 262176 | tf_op jit(solution)/shard_map/ppermute | solution.py:11
  94.9 1.9 fusion.6
  96.7 3.7 %collective-permute-done.15 = bf16[256,512]{1,0:T(8,128)(2,1)S(1)} collective-permute-done((bf16[256,512]{1,0:T(8,128)(2,1)S(1)}, bf16[256,512]{1,0:T(8,128)(2,1)S(1)}, u32[]{:S(2)}, u32[]{:S(2)}) %collective-permute-start.15) | collective-permute-done | bytes 262176 | tf_op jit(solution)/shard_map/ppermute | solution.py:11
  100.5 6.2 %add_add_fusion = f32[1024,512]{0,1:T(8,128)S(1)} fusion(f32[1024,512]{0,1:T(8,128)} %fusion.6, f32[1024,512]{0,1:T(8,128)} %fusion.7, f32[1024,512]{0,1:T(8,128)} %fusion.8, f32[1024,512]{0,1:T(8,128)S(1)} %fusion.9, f32[1024,512]{0,1:T(8,128)S(1)} %fusion.10, f32[1024,512]{0,1:T(8,128)S(1)} %fusion.11, f32[1024,512]{0,1:T(8,128)} %fusion.12, ...), kind=kOutput, calls=%fused_computation.6 | convolution fusion | flops 275775488 | bytes 32243712 | tf_op jit(solution)/shard_map/dot_general | solution.py:15
  107.1 3.5 %collective-permute-start.16 = (bf16[2,1024,128]{2,1,0:T(8,128)(2,1)S(1)}, bf16[2,1024,128]{2,1,0:T(8,128)(2,1)S(1)}, u32[]{:S(2)}, u32[]{:S(2)}) collective-permute-start(bf16[2,1024,128]{2,1,0:T(8,128)(2,1)S(1)} %bitcast.150), channel_id=1, source_target_pairs={{0,1},{1,0},{2,3},{3,2},{4,5},{5,4},{6,7},{7,6},{8,9},{9,8},{10,11... | collective-permute-start | bytes 1572872 | tf_op jit(solution)/shard_map/ppermute | solution.py:11
  111.1 3.1 %bitcast_select_fusion.1 = (bf16[1,256,1024]{2,1,0:T(8,128)(2,1)}, bf16[1,256,1024]{2,1,0:T(8,128)(2,1)}, bf16[1,256,1024]{2,1,0:T(8,128)(2,1)}) fusion(pred[]{:T(512)S(6)} %eq.23, bf16[256,3,1024]{2,0,1:T(8,128)(2,1)} %param.8, bf16[3,256,1024]{2,1,0:T(8,128)(2,1)} %param.9, pred[]{:T(512)S(6)} %eq.50, pred[]{:T(512)S(6)} %eq.25), kind=kLoop, calls=%fused_computation.51 | loop fusion | flops 786432 | bytes 4718595 | tf_op jit(solution)/shard_map/jit(_where)/select_n | solution.py:76
  114.7 1.8 copy.89
  117.3 1.5 bitcast_add_fusion
  119.5 1.2 collective-permute-start.17
  120.8 3.6 %pad_maximum_fusion = (bf16[4,256,1024]{2,1,0:T(8,128)(2,1)}, bf16[4,256,1024]{2,1,0:T(8,128)(2,1)}) fusion(bf16[1,256,1024]{2,1,0:T(8,128)(2,1)} %bitcast.5, bf16[1,256,1024]{2,1,0:T(8,128)(2,1)} %bitcast.4, bf16[1,256,1024]{2,1,0:T(8,128)(2,1)} %bitcast.3, bf16[1,256,1024]{2,1,0:T(8,128)(2,1)S(1)} %copy-done.15, bf16[1,256,1024]{2,1,0:T(8,128)(2,1)} %bitcast.38, ...), kind=kLoop, calls=%fused_computation.3 | loop fusion | flops 6291456 | bytes 8388608 | tf_op jit(solution)/shard_map/stack | solution.py:35
  124.5 2.3 gather_fusion
  126.7 0.9 collective-permute-done.17
  129.1 1.4 collective-permute-start.19
  130.5 1.0 broadcast_select_fusion.7
  131.5 1.3 collective-permute-start.20
  132.8 3.6 %gather_fusion.1 = bf16[4,256,1024]{2,1,0:T(8,128)(2,1)} fusion(bf16[4,256,1024]{2,1,0:T(8,128)(2,1)} %get-tuple-element.27, s32[1024]{0:T(1024)S(1)} %pad_clamp_fusion), kind=kCustom, calls=%fused_computation.1 | custom fusion | bytes 4194320 | tf_op jit(solution)/shard_map/gather | solution.py:37
  136.4 18.7 %collective-permute-done.20 = bf16[1024,128]{1,0:T(8,128)(2,1)} collective-permute-done((bf16[1024,128]{1,0:T(8,128)(2,1)S(1)}, bf16[1024,128]{1,0:T(8,128)(2,1)}, u32[]{:S(2)}, u32[]{:S(2)}) %collective-permute-start.20) | collective-permute-done | bytes 262176 | tf_op jit(solution)/shard_map/ppermute | solution.py:99
  155.1 1.7 fusion.2
  158.3 1.3 collective-permute-start.28
  161.2 10.2 %collective-permute-done.28 = bf16[256,1024]{1,0:T(8,128)(2,1)S(1)} collective-permute-done((bf16[256,1024]{1,0:T(8,128)(2,1)S(1)}, bf16[256,1024]{1,0:T(8,128)(2,1)S(1)}, u32[]{:S(2)}, u32[]{:S(2)}) %collective-permute-start.28) | collective-permute-done | bytes 524320 | tf_op jit(solution)/shard_map/ppermute | solution.py:11
  171.4 1.4 collective-permute-start.29
  172.8 1.3 collective-permute-start.26
  174.4 2.6 %pad_maximum_fusion.2 = bf16[4,256,1024]{2,1,0:T(8,128)(2,1)} fusion(bf16[1,256,1024]{2,1,0:T(8,128)(2,1)} %bitcast.49, bf16[1,256,1024]{2,1,0:T(8,128)(2,1)S(1)} %bitcast.151, bf16[1,256,1024]{2,1,0:T(8,128)(2,1)S(1)} %bitcast.152, bf16[1,256,1024]{2,1,0:T(8,128)(2,1)S(1)} %copy-done.17), kind=kLoop, calls=%fused_computation.5 | loop fusion | flops 3145728 | bytes 4194304 | tf_op jit(solution)/shard_map/stack | solution.py:35
  177.0 2.3 gather_fusion.2
  179.4 7.3 %collective-permute-done.26 = bf16[1024,128]{1,0:T(8,128)(2,1)} collective-permute-done((bf16[1024,128]{1,0:T(8,128)(2,1)S(1)}, bf16[1024,128]{1,0:T(8,128)(2,1)}, u32[]{:S(2)}, u32[]{:S(2)}) %collective-permute-start.26) | collective-permute-done | bytes 262176 | tf_op jit(solution)/shard_map/ppermute | solution.py:99
  186.7 2.3 fusion.1
  190.5 1.3 collective-permute-start.31
  191.8 1.0 fusion.24
  192.8 11.0 %collective-permute-done.31 = bf16[1024,128]{1,0:T(8,128)(2,1)} collective-permute-done((bf16[1024,128]{1,0:T(8,128)(2,1)S(1)}, bf16[1024,128]{1,0:T(8,128)(2,1)}, u32[]{:S(2)}, u32[]{:S(2)}) %collective-permute-start.31) | collective-permute-done | bytes 262176 | tf_op jit(solution)/shard_map/ppermute | solution.py:99
  203.8 1.0 broadcast_select_fusion.1
  204.8 1.5 collective-permute-start.32
  206.3 1.0 fusion.25
  207.4 1.3 copy.91
  208.7 5.7 %all-to-all-start = ((bf16[2,1024,128]{2,0,1:T(2,128)(2,1)}), bf16[2,1024,128]{2,0,1:T(2,128)(2,1)}, u32[]{:S(2)}, u32[]{:S(2)}) async-start(bf16[2,1024,128]{2,0,1:T(2,128)(2,1)} %copy.91), calls=%async_computation | async-start | bytes 1048576 | tf_op jit(solution)/shard_map/all_to_all | solution.py:107
  215.2 1.3 copy.93
  216.6 5.9 %all-to-all-done = bf16[2,1024,128]{2,0,1:T(2,128)(2,1)} async-done(((bf16[2,1024,128]{2,0,1:T(2,128)(2,1)}), bf16[2,1024,128]{2,0,1:T(2,128)(2,1)}, u32[]{:S(2)}, u32[]{:S(2)}) %all-to-all-start) | async-done | bytes 524320 | tf_op jit(solution)/shard_map/all_to_all | solution.py:107
  222.5 4.3 %all-to-all-start.1 = ((bf16[2,1024,128]{2,0,1:T(2,128)(2,1)}), bf16[2,1024,128]{2,0,1:T(2,128)(2,1)S(1)}, u32[]{:S(2)}, u32[]{:S(2)}) async-start(bf16[2,1024,128]{2,0,1:T(2,128)(2,1)} %copy.93), calls=%async_computation.1 | async-start | bytes 1048576 | tf_op jit(solution)/shard_map/all_to_all | solution.py:108
  226.8 1.4 copy.92
  228.5 6.3 %all-to-all-done.1 = bf16[2,1024,128]{2,0,1:T(2,128)(2,1)S(1)} async-done(((bf16[2,1024,128]{2,0,1:T(2,128)(2,1)}), bf16[2,1024,128]{2,0,1:T(2,128)(2,1)S(1)}, u32[]{:S(2)}, u32[]{:S(2)}) %all-to-all-start.1) | async-done | bytes 524320 | tf_op jit(solution)/shard_map/all_to_all | solution.py:108
  235.4 1.0 copy.98
  236.4 0.9 pad_maximum_fusion.3
  (118 shorter events, 15.9 us)
Async XLA Ops:
  0.6 61.4 %collective-permute-start.3 = (bf16[256,512]{1,0:T(8,128)(2,1)}, bf16[256,512]{1,0:T(8,128)(2,1)}, u32[]{:S(2)}, u32[]{:S(2)}) collective-permute-start(bf16[256,512]{1,0:T(8,128)(2,1)} %bitcast.153), channel_id=1, source_target_pairs={{0,8},{4,12},{8,16},{12,20},{16,24},{20,28},{1,9},{5,13},{9,17},{1... | collective-permute-start | bytes 786440 | tf_op jit(solution)/shard_map/ppermute | solution.py:59
  1.9 61.6 %collective-permute-start.4 = (bf16[256,512]{1,0:T(8,128)(2,1)}, bf16[256,512]{1,0:T(8,128)(2,1)S(1)}, u32[]{:S(2)}, u32[]{:S(2)}) collective-permute-start(bf16[256,512]{1,0:T(8,128)(2,1)} %bitcast.154), channel_id=1, source_target_pairs={{8,0},{12,4},{16,8},{20,12},{24,16},{28,20},{9,1},{13,5},{17,9},{2... | collective-permute-start | bytes 786440 | tf_op jit(solution)/shard_map/ppermute | solution.py:60
  5.9 60.3 %collective-permute-start.9 = (bf16[256,512]{1,0:T(8,128)(2,1)}, bf16[256,512]{1,0:T(8,128)(2,1)}, u32[]{:S(2)}, u32[]{:S(2)}) collective-permute-start(bf16[256,512]{1,0:T(8,128)(2,1)} %bitcast.155), channel_id=1, source_target_pairs={{0,4},{4,0},{8,12},{12,8},{16,20},{20,16},{24,28},{28,24},{1,5},{5... | collective-permute-start | bytes 786440 | tf_op jit(solution)/shard_map/ppermute | solution.py:11
  7.2 4.6 %copy-start.21 = (f32[256,512]{1,0:T(8,128)S(1)}, f32[256,512]{1,0:T(8,128)}, u32[]{:S(2)}) copy-start(f32[256,512]{1,0:T(8,128)} %param.5) | copy-start | bytes 1572868
  10.4 103.8 %collective-permute-start.22 = (bf16[256,1024]{1,0:T(8,128)(2,1)}, bf16[256,1024]{1,0:T(8,128)(2,1)}, u32[]{:S(2)}, u32[]{:S(2)}) collective-permute-start(bf16[256,1024]{1,0:T(8,128)(2,1)} %get-tuple-element.23), channel_id=1, source_target_pairs={{0,2},{1,3},{2,0},{3,1},{4,6},{5,7},{6,4},{7,5},{8,10},{9,11},{10,... | collective-permute-start | bytes 1572872 | tf_op jit(solution)/shard_map/ppermute | solution.py:11
  11.6 102.7 %collective-permute-start.1 = (bf16[256,1024]{1,0:T(8,128)(2,1)}, bf16[256,1024]{1,0:T(8,128)(2,1)}, u32[]{:S(2)}, u32[]{:S(2)}) collective-permute-start(bf16[256,1024]{1,0:T(8,128)(2,1)} %get-tuple-element.22), channel_id=1, source_target_pairs={{0,2},{1,3},{2,0},{3,1},{4,6},{5,7},{6,4},{7,5},{8,10},{9,11},{10,... | collective-permute-start | bytes 1572872 | tf_op jit(solution)/shard_map/ppermute | solution.py:11
  21.6 38.7 %copy-start.24 = (bf16[1,256,512]{2,1,0:T(8,128)(2,1)S(1)}, bf16[1,256,512]{2,1,0:T(8,128)(2,1)}, u32[]{:S(2)}) copy-start(bf16[1,256,512]{2,1,0:T(8,128)(2,1)} %param.7) | copy-start | bytes 786436
  60.2 4.0 %copy-start.12 = (bf16[1024,1,256]{2,1,0:T(2,128)(2,1)S(1)}, bf16[1024,1,256]{2,1,0:T(2,128)(2,1)}, u32[]{:S(2)}) copy-start(bf16[1024,1,256]{2,1,0:T(2,128)(2,1)} %get-tuple-element.15) | copy-start | bytes 1572868
  62.1 2.7 %copy-start.11 = (bf16[1024,1,256]{2,1,0:T(2,128)(2,1)S(1)}, bf16[1024,1,256]{2,1,0:T(2,128)(2,1)}, u32[]{:S(2)}) copy-start(bf16[1024,1,256]{2,1,0:T(2,128)(2,1)} %get-tuple-element.16) | copy-start | bytes 1572868
  62.1 8.0 %collective-permute-start.5 = (bf16[256,512]{1,0:T(8,128)(2,1)}, bf16[256,512]{1,0:T(8,128)(2,1)S(1)}, u32[]{:S(2)}, u32[]{:S(2)}) collective-permute-start(bf16[256,512]{1,0:T(8,128)(2,1)} %collective-permute-done.3), channel_id=1, source_target_pairs={{8,16},{12,20},{16,24},{20,28},{9,17},{13,21},{17,25},{21,29},{10,... | collective-permute-start | bytes 786440 | tf_op jit(solution)/shard_map/ppermute | solution.py:59
  63.5 7.2 %collective-permute-start.6 = (bf16[256,512]{1,0:T(8,128)(2,1)S(1)}, bf16[256,512]{1,0:T(8,128)(2,1)S(1)}, u32[]{:S(2)}, u32[]{:S(2)}) collective-permute-start(bf16[256,512]{1,0:T(8,128)(2,1)S(1)} %collective-permute-done.4), channel_id=1, source_target_pairs={{8,0},{12,4},{16,8},{20,12},{9,1},{13,5},{17,9},{21,13},{10,2},{14... | collective-permute-start | bytes 786440 | tf_op jit(solution)/shard_map/ppermute | solution.py:60
  64.7 1.9 copy-start.10
  66.3 4.0 %copy-start.9 = (bf16[1024,1,256]{2,1,0:T(2,128)(2,1)S(1)}, bf16[1024,1,256]{2,1,0:T(2,128)(2,1)}, u32[]{:S(2)}) copy-start(bf16[1024,1,256]{2,1,0:T(2,128)(2,1)} %get-tuple-element.14) | copy-start | bytes 1572868
  66.3 6.3 %collective-permute-start.10 = (bf16[256,512]{1,0:T(8,128)(2,1)}, bf16[256,512]{1,0:T(8,128)(2,1)S(1)}, u32[]{:S(2)}, u32[]{:S(2)}) collective-permute-start(bf16[256,512]{1,0:T(8,128)(2,1)} %collective-permute-done.3), channel_id=1, source_target_pairs={{0,4},{4,0},{8,12},{12,8},{16,20},{20,16},{24,28},{28,24},{1,5},{5... | collective-permute-start | bytes 786440 | tf_op jit(solution)/shard_map/ppermute | solution.py:11
  68.0 4.0 %copy-start.8 = (bf16[1024,1,256]{2,1,0:T(2,128)(2,1)S(1)}, bf16[1024,1,256]{2,1,0:T(2,128)(2,1)}, u32[]{:S(2)}) copy-start(bf16[1024,1,256]{2,1,0:T(2,128)(2,1)} %get-tuple-element.13) | copy-start | bytes 1572868
  70.0 8.3 %collective-permute-start.11 = (bf16[256,512]{1,0:T(8,128)(2,1)S(1)}, bf16[256,512]{1,0:T(8,128)(2,1)S(1)}, u32[]{:S(2)}, u32[]{:S(2)}) collective-permute-start(bf16[256,512]{1,0:T(8,128)(2,1)S(1)} %collective-permute-done.4), channel_id=1, source_target_pairs={{0,4},{4,0},{8,12},{12,8},{16,20},{20,16},{24,28},{28,24},{1,5},{5... | collective-permute-start | bytes 786440 | tf_op jit(solution)/shard_map/ppermute | solution.py:11
  70.8 8.3 %collective-permute-start.7 = (bf16[256,512]{1,0:T(8,128)(2,1)S(1)}, bf16[256,512]{1,0:T(8,128)(2,1)S(1)}, u32[]{:S(2)}, u32[]{:S(2)}) collective-permute-start(bf16[256,512]{1,0:T(8,128)(2,1)S(1)} %collective-permute-done.5), channel_id=1, source_target_pairs={{16,24},{20,28},{17,25},{21,29},{18,26},{22,30},{19,27},{23,31}} | collective-permute-start | bytes 786440 | tf_op jit(solution)/shard_map/ppermute | solution.py:59
  72.6 6.0 %copy-start.7 = (bf16[1024,1,256]{2,1,0:T(2,128)(2,1)S(1)}, bf16[1024,1,256]{2,1,0:T(2,128)(2,1)}, u32[]{:S(2)}) copy-start(bf16[1024,1,256]{2,1,0:T(2,128)(2,1)} %get-tuple-element.8) | copy-start | bytes 1572868
  72.6 9.7 %collective-permute-start.8 = (bf16[256,512]{1,0:T(8,128)(2,1)S(1)}, bf16[256,512]{1,0:T(8,128)(2,1)S(1)}, u32[]{:S(2)}, u32[]{:S(2)}) collective-permute-start(bf16[256,512]{1,0:T(8,128)(2,1)S(1)} %collective-permute-done.6), channel_id=1, source_target_pairs={{8,0},{12,4},{9,1},{13,5},{10,2},{14,6},{11,3},{15,7}} | collective-permute-start | bytes 786440 | tf_op jit(solution)/shard_map/ppermute | solution.py:60
  74.1 6.3 %copy-start.6 = (bf16[1024,1,256]{2,1,0:T(2,128)(2,1)S(1)}, bf16[1024,1,256]{2,1,0:T(2,128)(2,1)}, u32[]{:S(2)}) copy-start(bf16[1024,1,256]{2,1,0:T(2,128)(2,1)} %get-tuple-element.12) | copy-start | bytes 1572868
  78.4 6.0 %collective-permute-start.13 = (bf16[256,512]{1,0:T(8,128)(2,1)S(1)}, bf16[256,512]{1,0:T(8,128)(2,1)S(1)}, u32[]{:S(2)}, u32[]{:S(2)}) collective-permute-start(bf16[256,512]{1,0:T(8,128)(2,1)S(1)} %collective-permute-done.6), channel_id=1, source_target_pairs={{0,4},{4,0},{8,12},{12,8},{16,20},{20,16},{24,28},{28,24},{1,5},{5... | collective-permute-start | bytes 786440 | tf_op jit(solution)/shard_map/ppermute | solution.py:11
  79.1 3.4 %copy-start.5 = (bf16[1024,1,256]{2,1,0:T(2,128)(2,1)S(1)}, bf16[1024,1,256]{2,1,0:T(2,128)(2,1)}, u32[]{:S(2)}) copy-start(bf16[1024,1,256]{2,1,0:T(2,128)(2,1)} %get-tuple-element.11) | copy-start | bytes 1572868
  79.1 10.2 %collective-permute-start.12 = (bf16[256,512]{1,0:T(8,128)(2,1)S(1)}, bf16[256,512]{1,0:T(8,128)(2,1)S(1)}, u32[]{:S(2)}, u32[]{:S(2)}) collective-permute-start(bf16[256,512]{1,0:T(8,128)(2,1)S(1)} %collective-permute-done.5), channel_id=1, source_target_pairs={{0,4},{4,0},{8,12},{12,8},{16,20},{20,16},{24,28},{28,24},{1,5},{5... | collective-permute-start | bytes 786440 | tf_op jit(solution)/shard_map/ppermute | solution.py:11
  82.2 3.3 %copy-start.4 = (bf16[1024,1,256]{2,1,0:T(2,128)(2,1)S(1)}, bf16[1024,1,256]{2,1,0:T(2,128)(2,1)}, u32[]{:S(2)}) copy-start(bf16[1024,1,256]{2,1,0:T(2,128)(2,1)} %get-tuple-element.6) | copy-start | bytes 1572868
  82.3 12.6 %collective-permute-start.14 = (bf16[256,512]{1,0:T(8,128)(2,1)S(1)}, bf16[256,512]{1,0:T(8,128)(2,1)S(1)}, u32[]{:S(2)}, u32[]{:S(2)}) collective-permute-start(bf16[256,512]{1,0:T(8,128)(2,1)S(1)} %collective-permute-done.7), channel_id=1, source_target_pairs={{0,4},{4,0},{8,12},{12,8},{16,20},{20,16},{24,28},{28,24},{1,5},{5... | collective-permute-start | bytes 786440 | tf_op jit(solution)/shard_map/ppermute | solution.py:11
  84.3 16.1 %collective-permute-start.15 = (bf16[256,512]{1,0:T(8,128)(2,1)S(1)}, bf16[256,512]{1,0:T(8,128)(2,1)S(1)}, u32[]{:S(2)}, u32[]{:S(2)}) collective-permute-start(bf16[256,512]{1,0:T(8,128)(2,1)S(1)} %collective-permute-done.8), channel_id=1, source_target_pairs={{0,4},{4,0},{8,12},{12,8},{16,20},{20,16},{24,28},{28,24},{1,5},{5... | collective-permute-start | bytes 786440 | tf_op jit(solution)/shard_map/ppermute | solution.py:11
  91.2 9.3 %copy-start.1 = (f32[64,8,4,256]{3,1,2,0:T(8,128)S(1)}, f32[64,8,4,256]{3,1,2,0:T(8,128)}, u32[]{:S(2)}) copy-start(f32[64,8,4,256]{3,1,2,0:T(8,128)} %copy.115) | copy-start | bytes 6291460
  107.1 9.5 %collective-permute-start.16 = (bf16[2,1024,128]{2,1,0:T(8,128)(2,1)S(1)}, bf16[2,1024,128]{2,1,0:T(8,128)(2,1)S(1)}, u32[]{:S(2)}, u32[]{:S(2)}) collective-permute-start(bf16[2,1024,128]{2,1,0:T(8,128)(2,1)S(1)} %bitcast.150), channel_id=1, source_target_pairs={{0,1},{1,0},{2,3},{3,2},{4,5},{5,4},{6,7},{7,6},{8,9},{9,8},{10,11... | collective-permute-start | bytes 1572872 | tf_op jit(solution)/shard_map/ppermute | solution.py:11
  110.6 10.2 %collective-permute-start = (bf16[256,1024]{1,0:T(8,128)(2,1)}, bf16[256,1024]{1,0:T(8,128)(2,1)}, u32[]{:S(2)}, u32[]{:S(2)}) collective-permute-start(bf16[256,1024]{1,0:T(8,128)(2,1)} %get-tuple-element.22), channel_id=1, source_target_pairs={{0,1},{1,0},{2,3},{3,2},{4,5},{5,4},{6,7},{7,6},{8,9},{9,8},{10,11... | collective-permute-start | bytes 1572872 | tf_op jit(solution)/shard_map/ppermute | solution.py:11
  110.7 10.1 %collective-permute-start.21 = (bf16[256,1024]{1,0:T(8,128)(2,1)}, bf16[256,1024]{1,0:T(8,128)(2,1)}, u32[]{:S(2)}, u32[]{:S(2)}) collective-permute-start(bf16[256,1024]{1,0:T(8,128)(2,1)} %get-tuple-element.23), channel_id=1, source_target_pairs={{0,1},{1,0},{2,3},{3,2},{4,5},{5,4},{6,7},{7,6},{8,9},{9,8},{10,11... | collective-permute-start | bytes 1572872 | tf_op jit(solution)/shard_map/ppermute | solution.py:11
  114.2 6.6 %collective-permute-start.23 = (bf16[256,1024]{1,0:T(8,128)(2,1)}, bf16[256,1024]{1,0:T(8,128)(2,1)}, u32[]{:S(2)}, u32[]{:S(2)}) collective-permute-start(bf16[256,1024]{1,0:T(8,128)(2,1)} %collective-permute-done.22), channel_id=1, source_target_pairs={{0,1},{1,0},{2,3},{3,2},{4,5},{5,4},{6,7},{7,6},{8,9},{9,8},{10,11... | collective-permute-start | bytes 1572872 | tf_op jit(solution)/shard_map/ppermute | solution.py:11
  114.2 6.5 %collective-permute-start.2 = (bf16[256,1024]{1,0:T(8,128)(2,1)}, bf16[256,1024]{1,0:T(8,128)(2,1)}, u32[]{:S(2)}, u32[]{:S(2)}) collective-permute-start(bf16[256,1024]{1,0:T(8,128)(2,1)} %collective-permute-done.1), channel_id=1, source_target_pairs={{0,1},{1,0},{2,3},{3,2},{4,5},{5,4},{6,7},{7,6},{8,9},{9,8},{10,11... | collective-permute-start | bytes 1572872 | tf_op jit(solution)/shard_map/ppermute | solution.py:11
  116.5 4.3 %copy-start.15 = (bf16[1,256,1024]{2,1,0:T(8,128)(2,1)S(1)}, bf16[1,256,1024]{2,1,0:T(8,128)(2,1)}, u32[]{:S(2)}) copy-start(bf16[1,256,1024]{2,1,0:T(8,128)(2,1)} %get-tuple-element.19) | copy-start | bytes 1572868
  116.5 4.3 %copy-start.16 = (bf16[1,256,1024]{2,1,0:T(8,128)(2,1)S(1)}, bf16[1,256,1024]{2,1,0:T(8,128)(2,1)}, u32[]{:S(2)}) copy-start(bf16[1,256,1024]{2,1,0:T(8,128)(2,1)} %get-tuple-element.20) | copy-start | bytes 1572868
  116.5 0.8 copy-start.22
  119.5 8.1 %collective-permute-start.17 = (bf16[1,1024,128]{2,1,0:T(8,128)(2,1)}, bf16[1,1024,128]{2,1,0:T(8,128)(2,1)S(1)}, u32[]{:S(2)}, u32[]{:S(2)}) collective-permute-start(bf16[1,1024,128]{2,1,0:T(8,128)(2,1)} %dynamic-slice_convert_fusion), channel_id=1, source_target_pairs={{0,2},{1,3},{2,0},{3,1},{4,6},{5,7},{6,4},{7,5},{8,10},{9,11},{10,... | collective-permute-start | bytes 786440 | tf_op jit(solution)/shard_map/ppermute | solution.py:11
  127.6 0.7 copy-start.18
  128.4 0.7 collective-permute-start.18
  129.1 1.4 copy-start.20
  129.1 1.4 collective-permute-start.19
  131.5 23.6 %collective-permute-start.20 = (bf16[1024,128]{1,0:T(8,128)(2,1)S(1)}, bf16[1024,128]{1,0:T(8,128)(2,1)}, u32[]{:S(2)}, u32[]{:S(2)}) collective-permute-start(bf16[1024,128]{1,0:T(8,128)(2,1)S(1)} %broadcast_select_fusion.7), channel_id=1, source_target_pairs={{0,16},{4,20},{8,24},{12,28},{1,17},{5,21},{9,25},{13,29},{2,18},{... | collective-permute-start | bytes 786440 | tf_op jit(solution)/shard_map/ppermute | solution.py:99
  136.4 20.4 %copy-start = (bf16[4,256,1024]{2,1,0:T(8,128)(2,1)S(1)}, bf16[4,256,1024]{2,1,0:T(8,128)(2,1)}, u32[]{:S(2)}) copy-start(bf16[4,256,1024]{2,1,0:T(8,128)(2,1)} %gather_fusion.1) | copy-start | bytes 6291460
  156.8 0.8 copy-start.2
  156.9 1.5 copy-start.23
  156.9 17.5 %copy-start.17 = (bf16[1,256,1024]{2,1,0:T(8,128)(2,1)S(1)}, bf16[1,256,1024]{2,1,0:T(8,128)(2,1)}, u32[]{:S(2)}) copy-start(bf16[1,256,1024]{2,1,0:T(8,128)(2,1)} %get-tuple-element.18) | copy-start | bytes 1572868
  157.6 2.0 collective-permute-start.24
  158.3 13.0 %collective-permute-start.28 = (bf16[256,1024]{1,0:T(8,128)(2,1)S(1)}, bf16[256,1024]{1,0:T(8,128)(2,1)S(1)}, u32[]{:S(2)}, u32[]{:S(2)}) collective-permute-start(bf16[256,1024]{1,0:T(8,128)(2,1)S(1)} %copy-done.23), channel_id=1, source_target_pairs={{0,2},{1,3},{2,0},{3,1},{4,6},{5,7},{6,4},{7,5},{8,10},{9,11},{10,... | collective-permute-start | bytes 1572872 | tf_op jit(solution)/shard_map/ppermute | solution.py:11
  159.6 13.1 %collective-permute-start.25 = (bf16[1024,128]{1,0:T(8,128)(2,1)S(1)}, bf16[1024,128]{1,0:T(8,128)(2,1)S(1)}, u32[]{:S(2)}, u32[]{:S(2)}) collective-permute-start(bf16[1024,128]{1,0:T(8,128)(2,1)S(1)} %broadcast_select_fusion.3), channel_id=1, source_target_pairs={{4,0},{8,12},{5,1},{9,13},{6,2},{10,14},{7,3},{11,15}} | collective-permute-start | bytes 786440 | tf_op jit(solution)/shard_map/ppermute | solution.py:99
  160.3 13.8 %collective-permute-start.27 = (bf16[256,1024]{1,0:T(8,128)(2,1)S(1)}, bf16[256,1024]{1,0:T(8,128)(2,1)S(1)}, u32[]{:S(2)}, u32[]{:S(2)}) collective-permute-start(bf16[256,1024]{1,0:T(8,128)(2,1)S(1)} %copy-done.23), channel_id=1, source_target_pairs={{0,1},{1,0},{2,3},{3,2},{4,5},{5,4},{6,7},{7,6},{8,9},{9,8},{10,11... | collective-permute-start | bytes 1572872 | tf_op jit(solution)/shard_map/ppermute | solution.py:11
  171.4 3.0 %collective-permute-start.29 = (bf16[256,1024]{1,0:T(8,128)(2,1)S(1)}, bf16[256,1024]{1,0:T(8,128)(2,1)}, u32[]{:S(2)}, u32[]{:S(2)}) collective-permute-start(bf16[256,1024]{1,0:T(8,128)(2,1)S(1)} %collective-permute-done.28), channel_id=1, source_target_pairs={{0,1},{1,0},{2,3},{3,2},{4,5},{5,4},{6,7},{7,6},{8,9},{9,8},{10,11... | collective-permute-start | bytes 1572872 | tf_op jit(solution)/shard_map/ppermute | solution.py:11
  172.8 4.3 %copy-start.13 = (bf16[1024,128]{1,0:T(8,128)(2,1)}, bf16[1024,128]{1,0:T(8,128)(2,1)S(1)}, u32[]{:S(2)}) copy-start(bf16[1024,128]{1,0:T(8,128)(2,1)S(1)} %broadcast_select_fusion.4) | copy-start | bytes 786436
  172.8 13.9 %collective-permute-start.26 = (bf16[1024,128]{1,0:T(8,128)(2,1)S(1)}, bf16[1024,128]{1,0:T(8,128)(2,1)}, u32[]{:S(2)}, u32[]{:S(2)}) collective-permute-start(bf16[1024,128]{1,0:T(8,128)(2,1)S(1)} %broadcast_select_fusion.4), channel_id=1, source_target_pairs={{4,20},{8,24},{0,16},{12,28},{5,21},{9,25},{1,17},{13,29},{6,22},{... | collective-permute-start | bytes 786440 | tf_op jit(solution)/shard_map/ppermute | solution.py:99
  177.0 9.6 %copy-start.3 = (f32[1024,128]{1,0:T(8,128)S(1)}, f32[1024,128]{1,0:T(8,128)}, u32[]{:S(2)}) copy-start(f32[1024,128]{1,0:T(8,128)} %copy-done.2) | copy-start | bytes 1572868
  189.0 17.3 %copy-start.14 = (bf16[1024,128]{1,0:T(8,128)(2,1)S(1)}, bf16[1024,128]{1,0:T(8,128)(2,1)}, u32[]{:S(2)}) copy-start(bf16[1024,128]{1,0:T(8,128)(2,1)} %copy-done.13) | copy-start | bytes 786436
  189.7 0.7 collective-permute-start.30
  190.4 2.3 copy-start.19
  190.5 13.3 %collective-permute-start.31 = (bf16[1024,128]{1,0:T(8,128)(2,1)S(1)}, bf16[1024,128]{1,0:T(8,128)(2,1)}, u32[]{:S(2)}, u32[]{:S(2)}) collective-permute-start(bf16[1024,128]{1,0:T(8,128)(2,1)S(1)} %broadcast_select_fusion), channel_id=1, source_target_pairs={{8,0},{16,24},{9,1},{17,25},{10,2},{18,26},{11,3},{19,27}} | collective-permute-start | bytes 786440 | tf_op jit(solution)/shard_map/ppermute | solution.py:99
  204.8 9.6 %collective-permute-start.32 = (bf16[1024,128]{1,0:T(8,128)(2,1)S(1)}, bf16[1024,128]{1,0:T(8,128)(2,1)S(1)}, u32[]{:S(2)}, u32[]{:S(2)}) collective-permute-start(bf16[1024,128]{1,0:T(8,128)(2,1)S(1)} %broadcast_select_fusion.1), channel_id=1, source_target_pairs={{8,12},{16,20},{0,4},{24,28},{9,13},{17,21},{1,5},{25,29},{10,14},... | collective-permute-start | bytes 786440 | tf_op jit(solution)/shard_map/ppermute | solution.py:99
  208.7 13.8 %all-to-all-start = ((bf16[2,1024,128]{2,0,1:T(2,128)(2,1)}), bf16[2,1024,128]{2,0,1:T(2,128)(2,1)}, u32[]{:S(2)}, u32[]{:S(2)}) async-start(bf16[2,1024,128]{2,0,1:T(2,128)(2,1)} %copy.91), calls=%async_computation | async-start | bytes 1048576 | tf_op jit(solution)/shard_map/all_to_all | solution.py:107
  222.5 12.3 %all-to-all-start.1 = ((bf16[2,1024,128]{2,0,1:T(2,128)(2,1)}), bf16[2,1024,128]{2,0,1:T(2,128)(2,1)S(1)}, u32[]{:S(2)}, u32[]{:S(2)}) async-start(bf16[2,1024,128]{2,0,1:T(2,128)(2,1)} %copy.93), calls=%async_computation.1 | async-start | bytes 1048576 | tf_op jit(solution)/shard_map/all_to_all | solution.py:108

commit v2 on v1

--- a/solution.py
+++ b/solution.py
@@ -1,6 +1,10 @@
+import functools
+
 import jax
 import jax.numpy as jnp
 from jax import lax
+from jax.experimental import pallas as pl
+from jax.experimental.pallas import tpu as pltpu
 from jax.sharding import PartitionSpec as P
 
 F32 = jnp.float32
@@ -109,11 +113,284 @@
     return jnp.concatenate([early, late[:1]]), late[1].astype(F32)
 
 
+def flat_index(*values):
+    return jnp.stack([jnp.asarray(v, jnp.int32) for v in values])
+
+
+PARAMS = pltpu.CompilerParams(vmem_limit_bytes=48 * 1024 * 1024)
+SMEM = pl.BlockSpec(memory_space=pltpu.SMEM)
+VMEM = pl.BlockSpec(memory_space=pltpu.VMEM)
+ANY = pl.BlockSpec(memory_space=pl.ANY)
+
+
+def shape_of(shape, dtype):
+    return jax.ShapeDtypeStruct(shape, dtype)
+
+
+def relayout_kernel(panel_ref, out_ref, *wide):
+    tile, blocks, _ = panel_ref.shape
+    for h, lanes in enumerate(wide):
+        span = pl.ds(128 * h, 128)
+        lanes[...] = panel_ref[:, :, span].astype(F32).reshape(tile * blocks, 128)
+        for j in range(blocks):
+            out_ref[j, :, span] = lanes[pl.ds(j, tile, stride=blocks), :].astype(BF16)
+
+
+def relayout(panel, tile=128):
+    rows, blocks, width = panel.shape
+    return pl.pallas_call(
+        relayout_kernel,
+        grid=(rows // tile,),
+        out_shape=shape_of((blocks, rows, width), BF16),
+        in_specs=[pl.BlockSpec((tile, blocks, width), lambda i: (i, 0, 0))],
+        out_specs=pl.BlockSpec((blocks, tile, width), lambda i: (0, i, 0)),
+        scratch_shapes=[pltpu.VMEM((tile * blocks, 128), F32)] * (width // 128),
+        compiler_params=PARAMS,
+    )(panel)
+
+
+def panel_copies(index_ref, panel_ref, held, sems, count):
+    return [pltpu.make_async_copy(panel_ref.at[index_ref[b]], held.at[b], sems.at[b]) for b in range(count)]
+
+
+def bulk_first_kernel(count, index_ref, panel_ref, *refs):
+    blocks, (side_ref, out_ref, held, sems) = refs[:count], refs[count:]
+    copies = panel_copies(index_ref, panel_ref, held, sems, count)
+    for copy in copies:
+        copy.start()
+    for copy in copies:
+        copy.wait()
+    strip = side_ref.shape[0]
+    col = index_ref[count]
+
+    def tile(t, carry):
+        span = pl.ds(pl.multiple_of(t * strip, strip), strip)
+        total = jnp.where(t == col, -side_ref[...], 0.0)
+        for b in range(count):
+            total = total + matmul(held[b, span, :], blocks[b][...])
+        out_ref[span, :] = total
+        return carry
+
+    lax.fori_loop(0, out_ref.shape[0] // strip, tile, 0)
+
+
+def bulk_last_kernel(count, n_col, index_ref, panel_ref, *refs):
+    blocks, (total_ref, kept_ref, sent_ref, held, scratch, sems) = refs[:count], refs[count:]
+    copies = panel_copies(index_ref, panel_ref, held, sems, count)
+    for copy in copies:
+        copy.start()
+    for copy in copies:
+        copy.wait()
+    strip = scratch.shape[0]
+    chunk = kept_ref.shape[2]
+    core = lax.rem(index_ref[count], 2)
+
+    def tile(t, carry):
+        span = pl.ds(pl.multiple_of(t * strip, strip), strip)
+        total = total_ref[span, :]
+        for b in range(count):
+            total = total + matmul(held[b, span, :], blocks[b][...])
+        scratch[...] = total
+        for h in range(n_col // 2):
+            kept_ref[h, span, :] = scratch[:, pl.ds(pl.multiple_of((2 * h + core) * chunk, chunk), chunk)]
+            sent_ref[h, span, :] = scratch[:, pl.ds(pl.multiple_of((2 * h + 1 - core) * chunk, chunk), chunk)].astype(BF16)
+        return carry
+
+    lax.fori_loop(0, total_ref.shape[0] // strip, tile, 0)
+
+
+def bulk(panel, blocks, sources, extra, col, n_col=None):
+    count = len(blocks)
+    rows, width = panel.shape[1:]
+    nrhs = blocks[0].shape[1]
+    index = flat_index(*sources, col)
+    scratch = [pltpu.VMEM((count, rows, width), BF16)]
+    if n_col is None:
+        kernel = functools.partial(bulk_first_kernel, count)
+        out_shape, out_specs = shape_of((rows, nrhs), F32), VMEM
+    else:
+        kernel = functools.partial(bulk_last_kernel, count, n_col)
+        part = (n_col // 2, rows, nrhs // n_col)
+        out_shape, out_specs = (shape_of(part, F32), shape_of(part, BF16)), (VMEM, VMEM)
+        scratch.append(pltpu.VMEM((rows // n_col, nrhs), F32))
+    return pl.pallas_call(
+        kernel,
+        out_shape=out_shape,
+        in_specs=[SMEM, ANY] + [VMEM] * (count + 1),
+        out_specs=out_specs,
+        scratch_shapes=scratch + [pltpu.SemaphoreType.DMA((count,))],
+        compiler_params=PARAMS,
+    )(index, panel, *blocks, extra)
+
+
+def reduce_kernel(bit, index_ref, kept_ref, moved_ref, keep_ref, send_ref):
+    mine = lax.rem(index_ref[0] // bit, 2)
+    for h in range(keep_ref.shape[0]):
+        keep_ref[h] = kept_ref[2 * h + mine] + moved_ref[2 * h + mine].astype(F32)
+        send_ref[h] = (kept_ref[2 * h + 1 - mine] + moved_ref[2 * h + 1 - mine].astype(F32)).astype(BF16)
+
+
+def reduce_step(bit, index, kept, moved):
+    part = (kept.shape[0] // 2,) + kept.shape[1:]
+    return pl.pallas_call(
+        functools.partial(reduce_kernel, bit),
+        out_shape=(shape_of(part, F32), shape_of(part, BF16)),
+        in_specs=[SMEM, VMEM, VMEM],
+        out_specs=(VMEM, VMEM),
+        compiler_params=PARAMS,
+    )(index, kept, moved)
+
+
+def apply_strips(col, strips, value, store):
+    width = strips[0].shape[1]
+    for f, strip in enumerate(strips):
+        span = pl.ds(pl.multiple_of((col ^ f) * width, width), width)
+        store(span, matmul(strip[0], value))
+
+
+def start_kernel(n_col, index_ref, kept_ref, moved_ref, *refs):
+    diag, (current_ref, solved_ref) = refs[:n_col], refs[n_col:]
+    current = -(kept_ref[0] + moved_ref[0].astype(F32))
+    current_ref[...] = current
+
+    def store(span, product):
+        solved_ref[span, :] = product.astype(BF16)
+
+    apply_strips(index_ref[1], diag, current.astype(BF16), store)
+
+
+def step_kernel(k, n_col, index_ref, current_ref, solved_ref, *refs):
+    update, diag, (out_ref, next_ref) = refs[:n_col], refs[n_col : 2 * n_col], refs[2 * n_col :]
+    row, col = index_ref[0], index_ref[1]
+    later = row > k - 1
+
+    def subtract(span, product):
+        out_ref[span, :] = current_ref[span, :] - jnp.where(later, product, 0.0)
+
+    apply_strips(col, update, solved_ref[...], subtract)
+
+    def store(span, product):
+        next_ref[span, :] = product.astype(BF16)
+
+    apply_strips(col, diag, out_ref[...].astype(BF16), store)
+
+
+def finish_kernel(k, n_col, index_ref, current_ref, solved_ref, *refs):
+    update, (pieces_ref, scratch) = refs[:n_col], refs[n_col:]
+    row, col = index_ref[0], index_ref[1]
+    later = row > k
+
+    def subtract(span, product):
+        scratch[span, :] = current_ref[span, :] - jnp.where(later, product, 0.0)
+
+    apply_strips(col, update, solved_ref[...], subtract)
+    width = pieces_ref.shape[2]
+    for f in range(n_col):
+        span = pl.ds(pl.multiple_of((col ^ f) * width, width), width)
+        pieces_ref[f, 0] = solved_ref[span, :]
+        pieces_ref[f, 1] = scratch[span, :].astype(BF16)
+
+
+def pieces_kernel(index_ref, *refs):
+    values, pieces_ref = refs[:-1], refs[-1]
+    width = pieces_ref.shape[2]
+    for f in range(pieces_ref.shape[0]):
+        span = pl.ds(pl.multiple_of((index_ref[1] ^ f) * width, width), width)
+        for j, value in enumerate(values):
+            pieces_ref[f, j] = value[span, :]
+
+
+def assemble_kernel(n_col, index_ref, *refs):
+    early, late, (solved_ref, remaining_ref) = refs[:n_col], refs[n_col : 2 * n_col], refs[2 * n_col :]
+    chunk = early[0].shape[2]
+    last = early[0].shape[0]
+    for f in range(n_col):
+        span = pl.ds(pl.multiple_of((index_ref[1] ^ f) * chunk, chunk), chunk)
+        for j in range(last):
+            solved_ref[j, :, span] = early[f][j]
+        solved_ref[last, :, span] = late[f][0]
+        remaining_ref[:, span] = late[f][1].astype(F32)
+
+
+def local(kernel, out_shape, operands, specs=None, scratch=()):
+    specs = specs or [SMEM] + [VMEM] * (len(operands) - 1)
+    out_specs = jax.tree.map(lambda _: VMEM, out_shape)
+    return pl.pallas_call(
+        kernel, grid=(1,), out_shape=out_shape, in_specs=specs, out_specs=out_specs, scratch_shapes=list(scratch), compiler_params=PARAMS
+    )(*operands)
+
+
+def swap_pieces(pieces, n_col):
+    return [pieces[0]] + [flip(pieces[f], "col", n_col, f) for f in range(1, n_col)]
+
+
+def fast(shape, right_side, earlier_panel, earlier_solution, window_panel, diag_inverse):
+    n_row, n_col = shape
+    step_count = diag_inverse.shape[0]
+    row, col = lax.axis_index("row"), lax.axis_index("col")
+    index = flat_index(row, col)
+    strip, nrhs = right_side.shape
+    rows = earlier_panel.shape[0]
+    chunk = nrhs // n_col
+
+    block = earlier_solution[0]
+    blocks = {0: block, 1: flip(block, "row", n_row, 1)}
+    for f in (2, 4, 6):
+        blocks[f] = flip(block, "row", n_row, f)
+    own = jnp.stack([jnp.where(row == j, diag_inverse[j], window_panel[:, j, :]) for j in range(step_count)])
+    strips = {0: own}
+    for b in [1 << i for i in range(1, 8) if (1 << i) < n_col] + [1]:
+        strips.update({f ^ b: flip(v, "col", n_col, b) for f, v in strips.items()})
+    panel = relayout(earlier_panel)
+    for f in (2, 4, 6):
+        blocks[f + 1] = flip(blocks[f], "row", n_row, 1)
+    early, late = (0, 1, 2, 3, 4), (5, 6, 7)
+    total = bulk(panel, [blocks[f] for f in early], [row ^ f for f in early], right_side, col)
+    kept, sent = bulk(panel, [blocks[f] for f in late], [row ^ f for f in late], total, col, n_col)
+    moved = flip(sent, "col", n_col, 1)
+    for b in [1 << i for i in range(1, 8) if (1 << i) < n_col]:
+        kept, sent = reduce_step(b, flat_index(col), kept, moved)
+        moved = flip(sent, "col", n_col, b)
+
+    def slots(k):
+        return [strips[f] for f in range(n_col)], [pl.BlockSpec((1,) + own.shape[1:], lambda i, k=k: (k, 0, 0))] * n_col
+
+    value_shape = (shape_of((rows, chunk), F32), shape_of((rows, chunk), BF16))
+    weights, specs = slots(0)
+    current, value = local(functools.partial(start_kernel, n_col), value_shape, [index, kept, moved] + weights, [SMEM, VMEM, VMEM] + specs)
+    solved = []
+    for k in range(step_count):
+        have = [k]
+        for b in ([1, 2, 4], [3, 1, 4], [6, 2, 1])[k]:
+            moved = lax.ppermute(value, "row", [(i, i ^ b) for i in have])
+            into = jnp.zeros((), bool)
+            for i in have:
+                into |= row == (i ^ b)
+            value = jnp.where(into, moved, value)
+            have += [i ^ b for i in have]
+        solved.append(value)
+        update, specs = slots(k)
+        if k < step_count - 1:
+            diag, more = slots(k + 1)
+            kernel = functools.partial(step_kernel, k + 1, n_col)
+            current, value = local(kernel, value_shape, [index, current, value] + update + diag, [SMEM, VMEM, VMEM] + specs + more)
+        else:
+            pieces = shape_of((n_col, 2, rows // n_col, chunk), BF16)
+            kernel = functools.partial(finish_kernel, k, n_col)
+            last = local(kernel, pieces, [index, current, value] + update, [SMEM, VMEM, VMEM] + specs, [pltpu.VMEM((rows, chunk), F32)])
+    first = local(pieces_kernel, shape_of((n_col, step_count - 1, rows // n_col, chunk), BF16), [index] + solved[:-1])
+    first, last = swap_pieces(first, n_col), swap_pieces(last, n_col)
+    outs = (shape_of((step_count, strip, nrhs), BF16), shape_of((strip, nrhs), F32))
+    return local(functools.partial(assemble_kernel, n_col), outs, [index] + first + last)
+
+
 def solution(mesh):
     shape = (mesh.shape["row"], mesh.shape["col"])
 
     def step(*args):
-        return on_device(shape, *args)
+        chunk = args[0].shape[1] // shape[1]
+        plan = fast if shape[0] == 8 and chunk % 128 == 0 else on_device
+        return plan(shape, *args)
 
     return jax.shard_map(
         step,

time: 239 us -> 197 us (0.82)
  local copies, waits for them, and re-layouts: 66.3 us -> 7.51 us
  waiting for transfers between devices: 76.3 us -> 125 us
  matrix products: 29.5 us -> 0 us
  Pallas kernels: 0 us -> 28 us
  starting transfers between devices: 44.7 us -> 28.8 us
  other arithmetic: 19.2 us -> 4.27 us
    another operation x4 -> x1, local copies, waits for them, and re-layouts: 41.4 us -> 0.08 us  [flat_index(): return jnp.stack([jnp.asarray(v, jnp.int32) for v in values])]
    ppermute x18, waiting for transfers between devices: 25 us -> 63.7 us  [flip(): return lax.ppermute(value, axis, [(i, i ^ bit) for i in range(size)])]
    dot_general x20 -> x0, matrix products: 29.5 us -> none  [matmul(): return jnp.dot(left, right, preferred_element_type=F32)]
    pallas_call x0 -> x10, Pallas kernels: none -> 28 us  [the longest x6 12.9 us: local(): pl.pallas_call(kernel, grid=(1,), out_shape=out_shape, in_specs=specs, ou...]
    ppermute x15 -> x9, waiting for transfers between devices: 39 us -> 61.6 us  [fast(): moved = lax.ppermute(value, 'row', [(i, i ^ b) for i in have])]
    all_to_all x2 -> x0, waiting for transfers between devices: 12.3 us -> none  [the longest x1 6.32 us: on_device(): lax.all_to_all(jnp.stack([solved[-1], current.astype(BF16)]), 'col', 1, 2...]
    all_to_all x2 -> x0, starting transfers between devices: 9.99 us -> none  [the longest x1 5.68 us: on_device(): early = lax.all_to_all(jnp.stack(solved[:-1]), 'col', 1, 2, tiled=True)]
    ppermute x15 -> x9, starting transfers between devices: 19.1 us -> 9.39 us  [fast(): moved = lax.ppermute(value, 'row', [(i, i ^ b) for i in have])]
  transfers between devices with their start and end apart: 35 -> 27, of which waited for: 13 -> 10; matrix products, arithmetic and copies ran while one was open for 43% -> 1% of each run, Pallas kernels for 0% -> 9%
where the time goes in v2:
time: 197 us; the launch traced here: 195 us
  waiting for transfers between devices  125 us (63%)
  starting transfers between devices  28.8 us (15%)
  Pallas kernels  28 us (14%)
  local copies, waits for them, and re-layouts  7.51 us (4%)
  other arithmetic  4.27 us (2%)
    ppermute x18, waiting for transfers between devices, flip(): return lax.ppermute(value, axis, [(i, i ^ bit) for i in range(size)])  63.7 us
    ppermute x9, waiting for transfers between devices, fast(): moved = lax.ppermute(value, 'row', [(i, i ^ b) for i in have])  61.6 us
    ppermute x18, starting transfers between devices, flip(): return lax.ppermute(value, axis, [(i, i ^ bit) for i in range(size)])  19.4 us
    pallas_call x6, Pallas kernels, local(): pl.pallas_call(kernel, grid=(1,), out_shape=out_shape, in_specs=specs, ou...  12.9 us
    ppermute x9, starting transfers between devices, fast(): moved = lax.ppermute(value, 'row', [(i, i ^ b) for i in have])  9.39 us
    pallas_call x2, Pallas kernels, bulk(): pl.pallas_call(kernel, out_shape=out_shape, in_specs=[SMEM, ANY] + [VMEM]...  9.06 us
    unnamed x24, local copies, waits for them, and re-layouts  7.36 us
    pallas_call x1, Pallas kernels, relayout(): pl.pallas_call(relayout_kernel, grid=(rows // tile,), out_shape=shape_of(...  5.84 us
  transfers between devices with their start and end apart: 27, of which 10 were waited for; matrix products, arithmetic and copies ran while one was open for 1% of the time, Pallas kernels for 9%

profile of v2, /device:TPU:25, one launch (start us, length us, event | category | flops | bytes accessed | tf_op | source)
XLA Modules:
  0.0 194.8 jit_solution(8973392293080447535)
XLA Ops:
  0.6 2.0 %bitcast_select_fusion.2 = (bf16[1,256,1024]{2,1,0:T(8,128)(2,1)S(1)}, bf16[1,256,1024]{2,1,0:T(8,128)(2,1)S(1)}, bf16[1,256,1024]{2,1,0:T(8,128)(2,1)S(1)}) fusion(bf16[256,3,1024]{2,0,1:T(8,128)(2,1)} %param.8, bf16[3,256,1024]{2,1,0:T(8,128)(2,1)} %param.9, pred[]{:T(512)S(6)} %eq.23, pred[]{:T(512)S(6)} %eq.20, pred[]{:T(512)S(6)} %eq.22), kind=kLoop, calls=%fused_computation.3 | loop fusion | flops 786432 | bytes 4718595 | tf_op jit(solution)/shard_map/jit(_where)/select_n | solution.py:340
  2.6 0.0 copy-start.8
  2.7 0.2 pad_maximum_fusion.refs_0_.refs_4_
  2.8 1.3 collective-permute-start.10
  4.1 0.2 collective-permute-start.5
  4.3 1.2 collective-permute-start.9
  5.5 32.6 %collective-permute-done.10.refs_2_.refs_6_ = bf16[3,256,1024]{2,1,0:T(8,128)(2,1)S(1)} collective-permute-done((bf16[3,256,1024]{2,1,0:T(8,128)(2,1)S(1)}, bf16[3,256,1024]{2,1,0:T(8,128)(2,1)S(1)}, u32[]{:S(2)}, u32[]{:S(2)}) %collective-permute-start.10) | collective-permute-done | bytes 1572896 | tf_op jit(solution)/shard_map/ppermute | solution.py:15
  38.2 1.5 collective-permute-start.11
  39.7 0.1 collective-permute-start
  39.8 1.2 collective-permute-start.4
  41.0 2.2 %collective-permute-start.2 = (bf16[256,512]{1,0:T(8,128)(2,1)S(1)}, bf16[256,512]{1,0:T(8,128)(2,1)S(1)}, u32[]{:S(2)}, u32[]{:S(2)}) collective-permute-start(bf16[256,512]{1,0:T(8,128)(2,1)S(1)} %bitcast.35), channel_id=1, source_target_pairs={{0,24},{4,28},{8,16},{12,20},{16,8},{20,12},{24,0},{28,4},{1,25},{... | collective-permute-start | bytes 786440 | tf_op jit(solution)/shard_map/ppermute | solution.py:15
  43.2 16.9 %collective-permute-done.refs_4_ = bf16[256,512]{1,0:T(8,128)(2,1)} collective-permute-done((bf16[256,512]{1,0:T(8,128)(2,1)S(1)}, bf16[256,512]{1,0:T(8,128)(2,1)}, u32[]{:S(2)}, u32[]{:S(2)}) %collective-permute-start) | collective-permute-done | bytes 262176 | tf_op jit(solution)/shard_map/ppermute | solution.py:15
  60.1 1.2 collective-permute-start.6
  61.4 0.7 copy-done.10
  62.1 0.2 collective-permute-start.1
  62.3 1.2 collective-permute-start.3
  63.5 5.8 %shard_map.68.panel_ref = bf16[8,1024,256]{2,1,0:T(8,128)(2,1)S(1)} custom-call(bf16[1024,8,256]{2,1,0:T(8,128)(2,1)} %panel_ref.1), custom_call_target="tpu_custom_call" | custom-call | tf_op jit(solution)/shard_map/pallas_call | solution.py:141
  69.4 1.9 copy-done.2
  71.4 0.1 stack.57.index_ref
  71.4 0.1 pad_add_fusion.1.index_ref
  71.5 1.0 copy-done.5
  72.6 0.9 copy-done.9
  73.5 0.9 copy-done.11
  74.5 4.9 %shard_map.69.refs_3_ = f32[1024,512]{1,0:T(8,128)S(1)} custom-call(s32[6]{0:T(128)S(1)} %stack.57.index_ref, bf16[8,1024,256]{2,1,0:T(8,128)(2,1)} %copy-done.2, bf16[256,512]{1,0:T(8,128)(2,1)S(1)} %bitcast.36, bf16[256,512]{1,0:T(8,128)(2,1)S(1)} %copy-done.11, bf16[256,512]{1,0:T(8,128)(2,1)} %collective-permute-done.5.refs_2_, ...), custom_call_target="tpu_custom_call" | custom-call | tf_op jit(solution)/shard_map/pallas_call | solution.py:216
  79.4 4.2 %shard_map.70 = (f32[2,1024,128]{2,1,0:T(8,128)S(1)}, bf16[2,1024,128]{2,1,0:T(8,128)(2,1)S(1)}) custom-call(s32[4]{0:T(128)S(1)} %pad_add_fusion.1.index_ref, bf16[8,1024,256]{2,1,0:T(8,128)(2,1)} %copy-done.2, bf16[256,512]{1,0:T(8,128)(2,1)} %collective-permute-done.1.refs_0_, bf16[256,512]{1,0:T(8,128)(2,1)S(1)} %collective-permute-done.2.refs_1_, ...), custom_call_target="tpu_custom_call" | custom-call | tf_op jit(solution)/shard_map/pallas_call | solution.py:216
  83.6 1.4 collective-permute-start.7
  85.0 1.5 collective-permute-done.7.moved_ref
  86.5 0.1 shard_map.71
  86.6 1.3 collective-permute-start.8
  87.9 0.1 pad_add_fusion.index_ref
  88.0 6.2 %collective-permute-done.8.moved_ref = bf16[1,1024,128]{2,1,0:T(8,128)(2,1)S(1)} collective-permute-done((bf16[1,1024,128]{2,1,0:T(8,128)(2,1)S(1)}, bf16[1,1024,128]{2,1,0:T(8,128)(2,1)S(1)}, u32[]{:S(2)}, u32[]{:S(2)}) %collective-permute-start.8) | collective-permute-done | bytes 262176 | tf_op jit(solution)/shard_map/ppermute | solution.py:15
  94.2 2.1 %shard_map.72 = (f32[1024,128]{1,0:T(8,128)S(1)}, bf16[1024,128]{1,0:T(8,128)(2,1)S(1)}) custom-call(s32[2]{0:T(128)S(1)} %pad_add_fusion.index_ref, f32[1,1024,128]{2,1,0:T(8,128)S(1)} %get-tuple-element.14.kept_ref, bf16[1,1024,128]{2,1,0:T(8,128)(2,1)S(1)} %collective-permute-done.8.moved_ref, bf16[3,256,1024]{2,1,0:T(8,128)(2,1)S(1)} %pad_maximum_fusion.refs_0_.refs_4_, ...), custom_call_target="tpu_custom_call" | custom-call | tf_op jit(solution)/shard_map/pallas_call | solution.py:318
  96.3 0.7 collective-permute-start.12
  97.0 0.7 collective-permute-start.13
  97.8 1.3 collective-permute-start.14
  99.1 23.5 %collective-permute-done.14 = bf16[1024,128]{1,0:T(8,128)(2,1)S(1)} collective-permute-done((bf16[1024,128]{1,0:T(8,128)(2,1)S(1)}, bf16[1024,128]{1,0:T(8,128)(2,1)S(1)}, u32[]{:S(2)}, u32[]{:S(2)}) %collective-permute-start.14) | collective-permute-done | bytes 262176 | tf_op jit(solution)/shard_map/ppermute | solution.py:365
  122.6 3.2 %shard_map.73 = (f32[1024,128]{1,0:T(8,128)S(1)}, bf16[1024,128]{1,0:T(8,128)(2,1)S(1)}) custom-call(s32[2]{0:T(128)S(1)} %pad_add_fusion.index_ref, f32[1024,128]{1,0:T(8,128)S(1)} %get-tuple-element.17.current_ref, bf16[1024,128]{1,0:T(8,128)(2,1)S(1)} %broadcast_select_fusion.8.solved_ref.refs_0_, ...), custom_call_target="tpu_custom_call" | custom-call | tf_op jit(solution)/shard_map/pallas_call | solution.py:318
  125.8 0.7 collective-permute-start.15
  126.6 0.7 collective-permute-start.16
  127.3 1.3 collective-permute-start.17
  128.6 26.2 %collective-permute-done.17 = bf16[1024,128]{1,0:T(8,128)(2,1)S(1)} collective-permute-done((bf16[1024,128]{1,0:T(8,128)(2,1)S(1)}, bf16[1024,128]{1,0:T(8,128)(2,1)S(1)}, u32[]{:S(2)}, u32[]{:S(2)}) %collective-permute-start.17) | collective-permute-done | bytes 262176 | tf_op jit(solution)/shard_map/ppermute | solution.py:365
  154.8 0.0 copy-start.3
  154.8 3.3 %shard_map.75 = (f32[1024,128]{1,0:T(8,128)S(1)}, bf16[1024,128]{1,0:T(8,128)(2,1)S(1)}) custom-call(s32[2]{0:T(128)S(1)} %pad_add_fusion.index_ref, f32[1024,128]{1,0:T(8,128)S(1)} %get-tuple-element.19.current_ref, bf16[1024,128]{1,0:T(8,128)(2,1)S(1)} %broadcast_select_fusion.5.refs_1_.solved_ref, ...), custom_call_target="tpu_custom_call" | custom-call | tf_op jit(solution)/shard_map/pallas_call | solution.py:318
  158.2 0.0 copy-start.6
  158.2 0.8 copy-done.6
  159.0 0.7 collective-permute-start.21
  159.7 1.3 collective-permute-start.22
  161.0 12.0 %collective-permute-done.22 = bf16[1024,128]{1,0:T(8,128)(2,1)S(1)} collective-permute-done((bf16[1024,128]{1,0:T(8,128)(2,1)S(1)}, bf16[1024,128]{1,0:T(8,128)(2,1)S(1)}, u32[]{:S(2)}, u32[]{:S(2)}) %collective-permute-start.22) | collective-permute-done | bytes 262176 | tf_op jit(solution)/shard_map/ppermute | solution.py:365
  173.0 0.7 broadcast_select_fusion.1
  173.7 2.1 %collective-permute-start.23 = (bf16[1024,128]{1,0:T(8,128)(2,1)}, bf16[1024,128]{1,0:T(8,128)(2,1)}, u32[]{:S(2)}, u32[]{:S(2)}) collective-permute-start(bf16[1024,128]{1,0:T(8,128)(2,1)} %broadcast_select_fusion.1), channel_id=1, source_target_pairs={{8,12},{16,20},{0,4},{24,28},{9,13},{17,21},{1,5},{25,29},{10,14},... | collective-permute-start | bytes 786440 | tf_op jit(solution)/shard_map/ppermute | solution.py:365
  175.9 0.9 copy-done.4
  176.8 0.6 shard_map.74
  177.4 1.7 collective-permute-start.18
  179.1 1.2 collective-permute-start.19
  180.4 0.5 collective-permute-start.20
  180.8 1.0 broadcast_select_fusion.2.solved_ref
  181.9 1.9 shard_map.76
  183.8 1.2 collective-permute-start.24
  185.0 1.2 collective-permute-start.25
  186.2 0.5 collective-permute-start.26
  186.7 0.5 collective-permute-done.20.refs_3_
  187.2 2.9 %collective-permute-done.25.refs_6_ = bf16[2,256,128]{2,1,0:T(8,128)(2,1)S(1)} collective-permute-done((bf16[2,256,128]{2,1,0:T(8,128)(2,1)S(1)}, bf16[2,256,128]{2,1,0:T(8,128)(2,1)S(1)}, u32[]{:S(2)}, u32[]{:S(2)}) %collective-permute-start.25) | collective-permute-done | bytes 131104 | tf_op jit(solution)/shard_map/ppermute | solution.py:15
  190.1 3.0 %collective-permute-done.26.refs_7_ = bf16[2,256,128]{2,1,0:T(8,128)(2,1)S(1)} collective-permute-done((bf16[2,256,128]{2,1,0:T(8,128)(2,1)S(1)}, bf16[2,256,128]{2,1,0:T(8,128)(2,1)S(1)}, u32[]{:S(2)}, u32[]{:S(2)}) %collective-permute-start.26) | collective-permute-done | bytes 131104 | tf_op jit(solution)/shard_map/ppermute | solution.py:15
  193.1 1.8 shard_map.77
  (40 shorter events, 0.4 us)
Async XLA Ops:
  2.6 1.5 copy-start.8
  2.8 35.3 %collective-permute-start.10 = (bf16[3,256,1024]{2,1,0:T(8,128)(2,1)S(1)}, bf16[3,256,1024]{2,1,0:T(8,128)(2,1)S(1)}, u32[]{:S(2)}, u32[]{:S(2)}) collective-permute-start(bf16[3,256,1024]{2,1,0:T(8,128)(2,1)S(1)} %pad_maximum_fusion.refs_0_.refs_4_), channel_id=1, source_target_pairs={{0,2},{1,3},{2,0},{3,1},{4,6},{5,7},{6,4},{7,5},{8,10},{9,11},{10,... | collective-permute-start | bytes 4718600 | tf_op jit(solution)/shard_map/ppermute | solution.py:15
  4.1 36.9 %collective-permute-start.5 = (bf16[256,512]{1,0:T(8,128)(2,1)S(1)}, bf16[256,512]{1,0:T(8,128)(2,1)}, u32[]{:S(2)}, u32[]{:S(2)}) collective-permute-start(bf16[256,512]{1,0:T(8,128)(2,1)S(1)} %bitcast.32), channel_id=1, source_target_pairs={{0,8},{4,12},{8,0},{12,4},{16,24},{20,28},{24,16},{28,20},{1,9},{5... | collective-permute-start | bytes 786440 | tf_op jit(solution)/shard_map/ppermute | solution.py:15
  4.3 89.9 %collective-permute-start.9 = (bf16[3,256,1024]{2,1,0:T(8,128)(2,1)S(1)}, bf16[3,256,1024]{2,1,0:T(8,128)(2,1)}, u32[]{:S(2)}, u32[]{:S(2)}) collective-permute-start(bf16[3,256,1024]{2,1,0:T(8,128)(2,1)S(1)} %pad_maximum_fusion.refs_0_.refs_4_), channel_id=1, source_target_pairs={{0,1},{1,0},{2,3},{3,2},{4,5},{5,4},{6,7},{7,6},{8,9},{9,8},{10,11... | collective-permute-start | bytes 4718600 | tf_op jit(solution)/shard_map/ppermute | solution.py:15
  38.2 31.2 %copy-start = (bf16[3,256,1024]{2,1,0:T(8,128)(2,1)}, bf16[3,256,1024]{2,1,0:T(8,128)(2,1)S(1)}, u32[]{:S(2)}) copy-start(bf16[3,256,1024]{2,1,0:T(8,128)(2,1)S(1)} %collective-permute-done.10.refs_2_.refs_6_) | copy-start | bytes 4718596
  38.2 56.0 %collective-permute-start.11 = (bf16[3,256,1024]{2,1,0:T(8,128)(2,1)S(1)}, bf16[3,256,1024]{2,1,0:T(8,128)(2,1)}, u32[]{:S(2)}, u32[]{:S(2)}) collective-permute-start(bf16[3,256,1024]{2,1,0:T(8,128)(2,1)S(1)} %collective-permute-done.10.refs_2_.refs_6_), channel_id=1, source_target_pairs={{0,1},{1,0},{2,3},{3,2},{4,5},{5,4},{6,7},{7,6},{8,9},{9,8},{10,11... | collective-permute-start | bytes 4718600 | tf_op jit(solution)/shard_map/ppermute | solution.py:15
  39.7 20.4 %collective-permute-start = (bf16[256,512]{1,0:T(8,128)(2,1)S(1)}, bf16[256,512]{1,0:T(8,128)(2,1)}, u32[]{:S(2)}, u32[]{:S(2)}) collective-permute-start(bf16[256,512]{1,0:T(8,128)(2,1)S(1)} %bitcast.33), channel_id=1, source_target_pairs={{0,16},{4,20},{8,24},{12,28},{16,0},{20,4},{24,8},{28,12},{1,17},{... | collective-permute-start | bytes 786440 | tf_op jit(solution)/shard_map/ppermute | solution.py:15
  39.8 21.6 %collective-permute-start.4 = (bf16[256,512]{1,0:T(8,128)(2,1)S(1)}, bf16[256,512]{1,0:T(8,128)(2,1)S(1)}, u32[]{:S(2)}, u32[]{:S(2)}) collective-permute-start(bf16[256,512]{1,0:T(8,128)(2,1)S(1)} %bitcast.34), channel_id=1, source_target_pairs={{0,4},{4,0},{8,12},{12,8},{16,20},{20,16},{24,28},{28,24},{1,5},{5... | collective-permute-start | bytes 786440 | tf_op jit(solution)/shard_map/ppermute | solution.py:15
  41.0 21.3 %collective-permute-start.2 = (bf16[256,512]{1,0:T(8,128)(2,1)S(1)}, bf16[256,512]{1,0:T(8,128)(2,1)S(1)}, u32[]{:S(2)}, u32[]{:S(2)}) collective-permute-start(bf16[256,512]{1,0:T(8,128)(2,1)S(1)} %bitcast.35), channel_id=1, source_target_pairs={{0,24},{4,28},{8,16},{12,20},{16,8},{20,12},{24,0},{28,4},{1,25},{... | collective-permute-start | bytes 786440 | tf_op jit(solution)/shard_map/ppermute | solution.py:15
  60.1 11.4 %collective-permute-start.6 = (bf16[256,512]{1,0:T(8,128)(2,1)}, bf16[256,512]{1,0:T(8,128)(2,1)}, u32[]{:S(2)}, u32[]{:S(2)}) collective-permute-start(bf16[256,512]{1,0:T(8,128)(2,1)} %collective-permute-done.5.refs_2_), channel_id=1, source_target_pairs={{0,4},{4,0},{8,12},{12,8},{16,20},{20,16},{24,28},{28,24},{1,5},{5... | collective-permute-start | bytes 786440 | tf_op jit(solution)/shard_map/ppermute | solution.py:15
  61.4 0.7 copy-start.10
  62.1 17.3 %collective-permute-start.1 = (bf16[256,512]{1,0:T(8,128)(2,1)}, bf16[256,512]{1,0:T(8,128)(2,1)}, u32[]{:S(2)}, u32[]{:S(2)}) collective-permute-start(bf16[256,512]{1,0:T(8,128)(2,1)} %collective-permute-done.refs_4_), channel_id=1, source_target_pairs={{0,4},{4,0},{8,12},{12,8},{16,20},{20,16},{24,28},{28,24},{1,5},{5... | collective-permute-start | bytes 786440 | tf_op jit(solution)/shard_map/ppermute | solution.py:15
  62.3 17.0 %collective-permute-start.3 = (bf16[256,512]{1,0:T(8,128)(2,1)S(1)}, bf16[256,512]{1,0:T(8,128)(2,1)}, u32[]{:S(2)}, u32[]{:S(2)}) collective-permute-start(bf16[256,512]{1,0:T(8,128)(2,1)S(1)} %collective-permute-done.2.refs_1_), channel_id=1, source_target_pairs={{0,4},{4,0},{8,12},{12,8},{16,20},{20,16},{24,28},{28,24},{1,5},{5... | collective-permute-start | bytes 786440 | tf_op jit(solution)/shard_map/ppermute | solution.py:15
  69.4 2.0 %copy-start.2 = (bf16[8,1024,256]{2,1,0:T(8,128)(2,1)}, bf16[8,1024,256]{2,1,0:T(8,128)(2,1)S(1)}, u32[]{:S(2)}) copy-start(bf16[8,1024,256]{2,1,0:T(8,128)(2,1)S(1)} %shard_map.68.panel_ref) | copy-start | bytes 12582916
  71.5 1.0 copy-start.5
  72.6 0.9 copy-start.9
  73.5 0.9 copy-start.11
  83.6 2.9 %collective-permute-start.7 = (bf16[2,1024,128]{2,1,0:T(8,128)(2,1)S(1)}, bf16[2,1024,128]{2,1,0:T(8,128)(2,1)S(1)}, u32[]{:S(2)}, u32[]{:S(2)}) collective-permute-start(bf16[2,1024,128]{2,1,0:T(8,128)(2,1)S(1)} %get-tuple-element.13), channel_id=1, source_target_pairs={{0,1},{1,0},{2,3},{3,2},{4,5},{5,4},{6,7},{7,6},{8,9},{9,8},{10,11... | collective-permute-start | bytes 1572872 | tf_op jit(solution)/shard_map/ppermute | solution.py:15
  86.6 7.6 %collective-permute-start.8 = (bf16[1,1024,128]{2,1,0:T(8,128)(2,1)S(1)}, bf16[1,1024,128]{2,1,0:T(8,128)(2,1)S(1)}, u32[]{:S(2)}, u32[]{:S(2)}) collective-permute-start(bf16[1,1024,128]{2,1,0:T(8,128)(2,1)S(1)} %get-tuple-element.15), channel_id=1, source_target_pairs={{0,2},{1,3},{2,0},{3,1},{4,6},{5,7},{6,4},{7,5},{8,10},{9,11},{10,... | collective-permute-start | bytes 786440 | tf_op jit(solution)/shard_map/ppermute | solution.py:15
  96.3 0.7 collective-permute-start.12
  97.0 0.7 collective-permute-start.13
  97.8 24.8 %collective-permute-start.14 = (bf16[1024,128]{1,0:T(8,128)(2,1)S(1)}, bf16[1024,128]{1,0:T(8,128)(2,1)S(1)}, u32[]{:S(2)}, u32[]{:S(2)}) collective-permute-start(bf16[1024,128]{1,0:T(8,128)(2,1)S(1)} %broadcast_select_fusion.7), channel_id=1, source_target_pairs={{0,16},{4,20},{8,24},{12,28},{1,17},{5,21},{9,25},{13,29},{2,18},{... | collective-permute-start | bytes 786440 | tf_op jit(solution)/shard_map/ppermute | solution.py:365
  125.8 0.7 collective-permute-start.15
  126.6 0.7 collective-permute-start.16
  127.3 27.5 %collective-permute-start.17 = (bf16[1024,128]{1,0:T(8,128)(2,1)S(1)}, bf16[1024,128]{1,0:T(8,128)(2,1)S(1)}, u32[]{:S(2)}, u32[]{:S(2)}) collective-permute-start(bf16[1024,128]{1,0:T(8,128)(2,1)S(1)} %broadcast_select_fusion.4), channel_id=1, source_target_pairs={{4,20},{8,24},{0,16},{12,28},{5,21},{9,25},{1,17},{13,29},{6,22},{... | collective-permute-start | bytes 786440 | tf_op jit(solution)/shard_map/ppermute | solution.py:365
  154.8 3.4 %copy-start.3 = (bf16[1024,128]{1,0:T(8,128)(2,1)}, bf16[1024,128]{1,0:T(8,128)(2,1)S(1)}, u32[]{:S(2)}) copy-start(bf16[1024,128]{1,0:T(8,128)(2,1)S(1)} %broadcast_select_fusion.5.refs_1_.solved_ref) | copy-start | bytes 786436
  158.2 0.8 copy-start.6
  159.0 0.7 collective-permute-start.21
  159.7 13.3 %collective-permute-start.22 = (bf16[1024,128]{1,0:T(8,128)(2,1)S(1)}, bf16[1024,128]{1,0:T(8,128)(2,1)S(1)}, u32[]{:S(2)}, u32[]{:S(2)}) collective-permute-start(bf16[1024,128]{1,0:T(8,128)(2,1)S(1)} %broadcast_select_fusion), channel_id=1, source_target_pairs={{8,0},{16,24},{9,1},{17,25},{10,2},{18,26},{11,3},{19,27}} | collective-permute-start | bytes 786440 | tf_op jit(solution)/shard_map/ppermute | solution.py:365
  173.7 8.1 %copy-start.1 = (bf16[3,256,1024]{2,1,0:T(8,128)(2,1)S(1)}, bf16[3,256,1024]{2,1,0:T(8,128)(2,1)}, u32[]{:S(2)}) copy-start(bf16[3,256,1024]{2,1,0:T(8,128)(2,1)} %copy-done) | copy-start | bytes 4718596
  173.7 7.1 %collective-permute-start.23 = (bf16[1024,128]{1,0:T(8,128)(2,1)}, bf16[1024,128]{1,0:T(8,128)(2,1)}, u32[]{:S(2)}, u32[]{:S(2)}) collective-permute-start(bf16[1024,128]{1,0:T(8,128)(2,1)} %broadcast_select_fusion.1), channel_id=1, source_target_pairs={{8,12},{16,20},{0,4},{24,28},{9,13},{17,21},{1,5},{25,29},{10,14},... | collective-permute-start | bytes 786440 | tf_op jit(solution)/shard_map/ppermute | solution.py:365
  175.9 0.9 copy-start.4
  176.8 5.0 %copy-start.7 = (f32[1024,128]{1,0:T(8,128)S(1)}, f32[1024,128]{1,0:T(8,128)}, u32[]{:S(2)}) copy-start(f32[1024,128]{1,0:T(8,128)} %copy-done.6) | copy-start | bytes 1572868
  177.4 8.8 %collective-permute-start.18 = (bf16[2,256,128]{2,1,0:T(8,128)(2,1)S(1)}, bf16[2,256,128]{2,1,0:T(8,128)(2,1)S(1)}, u32[]{:S(2)}, u32[]{:S(2)}) collective-permute-start(bf16[2,256,128]{2,1,0:T(8,128)(2,1)S(1)} %get-tuple-element.31), channel_id=1, source_target_pairs={{0,1},{1,0},{2,3},{3,2},{4,5},{5,4},{6,7},{7,6},{8,9},{9,8},{10,11... | collective-permute-start | bytes 393224 | tf_op jit(solution)/shard_map/ppermute | solution.py:15
  179.1 7.6 %collective-permute-start.19 = (bf16[2,256,128]{2,1,0:T(8,128)(2,1)S(1)}, bf16[2,256,128]{2,1,0:T(8,128)(2,1)S(1)}, u32[]{:S(2)}, u32[]{:S(2)}) collective-permute-start(bf16[2,256,128]{2,1,0:T(8,128)(2,1)S(1)} %get-tuple-element.30), channel_id=1, source_target_pairs={{0,2},{1,3},{2,0},{3,1},{4,6},{5,7},{6,4},{7,5},{8,10},{9,11},{10,... | collective-permute-start | bytes 393224 | tf_op jit(solution)/shard_map/ppermute | solution.py:15
  180.4 6.8 %collective-permute-start.20 = (bf16[2,256,128]{2,1,0:T(8,128)(2,1)S(1)}, bf16[2,256,128]{2,1,0:T(8,128)(2,1)S(1)}, u32[]{:S(2)}, u32[]{:S(2)}) collective-permute-start(bf16[2,256,128]{2,1,0:T(8,128)(2,1)S(1)} %get-tuple-element.29), channel_id=1, source_target_pairs={{0,3},{1,2},{2,1},{3,0},{4,7},{5,6},{6,5},{7,4},{8,11},{9,10},{10,... | collective-permute-start | bytes 393224 | tf_op jit(solution)/shard_map/ppermute | solution.py:15
  183.8 3.3 %collective-permute-start.24 = (bf16[2,256,128]{2,1,0:T(8,128)(2,1)S(1)}, bf16[2,256,128]{2,1,0:T(8,128)(2,1)S(1)}, u32[]{:S(2)}, u32[]{:S(2)}) collective-permute-start(bf16[2,256,128]{2,1,0:T(8,128)(2,1)S(1)} %get-tuple-element.27), channel_id=1, source_target_pairs={{0,1},{1,0},{2,3},{3,2},{4,5},{5,4},{6,7},{7,6},{8,9},{9,8},{10,11... | collective-permute-start | bytes 393224 | tf_op jit(solution)/shard_map/ppermute | solution.py:15
  185.0 5.1 %collective-permute-start.25 = (bf16[2,256,128]{2,1,0:T(8,128)(2,1)S(1)}, bf16[2,256,128]{2,1,0:T(8,128)(2,1)S(1)}, u32[]{:S(2)}, u32[]{:S(2)}) collective-permute-start(bf16[2,256,128]{2,1,0:T(8,128)(2,1)S(1)} %get-tuple-element.26), channel_id=1, source_target_pairs={{0,2},{1,3},{2,0},{3,1},{4,6},{5,7},{6,4},{7,5},{8,10},{9,11},{10,... | collective-permute-start | bytes 393224 | tf_op jit(solution)/shard_map/ppermute | solution.py:15
  186.2 6.8 %collective-permute-start.26 = (bf16[2,256,128]{2,1,0:T(8,128)(2,1)S(1)}, bf16[2,256,128]{2,1,0:T(8,128)(2,1)S(1)}, u32[]{:S(2)}, u32[]{:S(2)}) collective-permute-start(bf16[2,256,128]{2,1,0:T(8,128)(2,1)S(1)} %get-tuple-element.25), channel_id=1, source_target_pairs={{0,3},{1,2},{2,1},{3,0},{4,7},{5,6},{6,5},{7,4},{8,11},{9,10},{10,... | collective-permute-start | bytes 393224 | tf_op jit(solution)/shard_map/ppermute | solution.py:15

commit v3 on v2

--- a/solution.py
+++ b/solution.py
@@ -117,7 +117,7 @@
     return jnp.stack([jnp.asarray(v, jnp.int32) for v in values])
 
 
-PARAMS = pltpu.CompilerParams(vmem_limit_bytes=48 * 1024 * 1024)
+PARAMS = pltpu.CompilerParams(vmem_limit_bytes=24 * 1024 * 1024)
 SMEM = pl.BlockSpec(memory_space=pltpu.SMEM)
 VMEM = pl.BlockSpec(memory_space=pltpu.VMEM)
 ANY = pl.BlockSpec(memory_space=pl.ANY)
@@ -241,63 +241,77 @@
     )(index, kept, moved)
 
 
-def apply_strips(col, strips, value, store):
+def apply_strips(col, strips, k, value, store):
     width = strips[0].shape[1]
     for f, strip in enumerate(strips):
         span = pl.ds(pl.multiple_of((col ^ f) * width, width), width)
-        store(span, matmul(strip[0], value))
+        store(span, matmul(strip[k], value))
+
+
+def store_solved(index_ref, strips, k, current_ref, solved_ref):
+    own = index_ref[0] == k
+
+    def store(span, product):
+        solved_ref[span, :] = jnp.where(own, product, 0.0).astype(BF16)
+
+    apply_strips(index_ref[1], strips, k, current_ref[...].astype(BF16), store)
+
+
+def subtract(index_ref, strips, k, value, chosen, source_ref, target_ref):
+    def store(span, product):
+        target_ref[span, :] = source_ref[span, :] - jnp.where(chosen, product, 0.0)
+
+    apply_strips(index_ref[1], strips, k, value, store)
 
 
 def start_kernel(n_col, index_ref, kept_ref, moved_ref, *refs):
-    diag, (current_ref, solved_ref) = refs[:n_col], refs[n_col:]
-    current = -(kept_ref[0] + moved_ref[0].astype(F32))
-    current_ref[...] = current
-
-    def store(span, product):
-        solved_ref[span, :] = product.astype(BF16)
-
-    apply_strips(index_ref[1], diag, current.astype(BF16), store)
-
-
-def step_kernel(k, n_col, index_ref, current_ref, solved_ref, *refs):
-    update, diag, (out_ref, next_ref) = refs[:n_col], refs[n_col : 2 * n_col], refs[2 * n_col :]
-    row, col = index_ref[0], index_ref[1]
-    later = row > k - 1
-
-    def subtract(span, product):
-        out_ref[span, :] = current_ref[span, :] - jnp.where(later, product, 0.0)
-
-    apply_strips(col, update, solved_ref[...], subtract)
-
-    def store(span, product):
-        next_ref[span, :] = product.astype(BF16)
-
-    apply_strips(col, diag, out_ref[...].astype(BF16), store)
-
-
-def finish_kernel(k, n_col, index_ref, current_ref, solved_ref, *refs):
-    update, (pieces_ref, scratch) = refs[:n_col], refs[n_col:]
-    row, col = index_ref[0], index_ref[1]
-    later = row > k
-
-    def subtract(span, product):
-        scratch[span, :] = current_ref[span, :] - jnp.where(later, product, 0.0)
-
-    apply_strips(col, update, solved_ref[...], subtract)
+    strips, (current_ref, solved_ref) = refs[:n_col], refs[n_col:]
+    current_ref[...] = -(kept_ref[0] + moved_ref[0].astype(F32))
+    store_solved(index_ref, strips, 0, current_ref, solved_ref)
+
+
+def step_kernel(k, n_col, index_ref, current_ref, *refs):
+    strips, refs = refs[:n_col], refs[n_col:]
+    parts, (out_ref, known_ref, solved_ref) = refs[:-3], refs[-3:]
+    known_ref[...] = functools.reduce(jnp.add, [part[...] for part in parts])
+    subtract(index_ref, strips, k - 1, known_ref[...], index_ref[0] > k - 1, current_ref, out_ref)
+    store_solved(index_ref, strips, k, out_ref, solved_ref)
+
+
+def late_kernel(first, n_col, index_ref, current_ref, *refs):
+    strips, refs = refs[:n_col], refs[n_col:]
+    steps = strips[0].shape[0] - 1
+    parts, (out_ref, pieces_ref) = refs[:-2], refs[-2:]
+    each = len(parts) // steps
+    width = pieces_ref.shape[2]
+    for k in range(steps):
+        value = functools.reduce(jnp.add, [part[...] for part in parts[k * each : (k + 1) * each]])
+        subtract(index_ref, strips, k, value, index_ref[0] >= first, out_ref if k else current_ref, out_ref)
+        cut(index_ref, value, pieces_ref, k)
+
+
+def cut(index_ref, value, pieces_ref, k):
+    width = pieces_ref.shape[2]
+    col = index_ref[1]
+    for f in range(pieces_ref.shape[0]):
+        for owner in range(pieces_ref.shape[0]):
+
+            @pl.when((col ^ f) == owner)
+            def _():
+                pieces_ref[f, k] = value[owner * width : (owner + 1) * width, :]
+
+
+def finish_kernel(n_col, index_ref, current_ref, *refs):
+    strips, refs = refs[:n_col], refs[n_col:]
+    k = strips[0].shape[0] - 1
+    parts, (pieces_ref, scratch) = refs[:-2], refs[-2:]
+    value = functools.reduce(jnp.add, [part[...] for part in parts])
+    subtract(index_ref, strips, k, value, index_ref[0] > k, current_ref, scratch)
+    cut(index_ref, value, pieces_ref, 0)
     width = pieces_ref.shape[2]
     for f in range(n_col):
-        span = pl.ds(pl.multiple_of((col ^ f) * width, width), width)
-        pieces_ref[f, 0] = solved_ref[span, :]
+        span = pl.ds(pl.multiple_of((index_ref[1] ^ f) * width, width), width)
         pieces_ref[f, 1] = scratch[span, :].astype(BF16)
-
-
-def pieces_kernel(index_ref, *refs):
-    values, pieces_ref = refs[:-1], refs[-1]
-    width = pieces_ref.shape[2]
-    for f in range(pieces_ref.shape[0]):
-        span = pl.ds(pl.multiple_of((index_ref[1] ^ f) * width, width), width)
-        for j, value in enumerate(values):
-            pieces_ref[f, j] = value[span, :]
 
 
 def assemble_kernel(n_col, index_ref, *refs):
@@ -312,12 +326,24 @@
         remaining_ref[:, span] = late[f][1].astype(F32)
 
 
-def local(kernel, out_shape, operands, specs=None, scratch=()):
-    specs = specs or [SMEM] + [VMEM] * (len(operands) - 1)
+def local(kernel, out_shape, operands, scratch=()):
     out_specs = jax.tree.map(lambda _: VMEM, out_shape)
     return pl.pallas_call(
-        kernel, grid=(1,), out_shape=out_shape, in_specs=specs, out_specs=out_specs, scratch_shapes=list(scratch), compiler_params=PARAMS
+        kernel,
+        out_shape=out_shape,
+        in_specs=[SMEM] + [VMEM] * (len(operands) - 1),
+        out_specs=out_specs,
+        scratch_shapes=list(scratch),
+        compiler_params=PARAMS,
     )(*operands)
+
+
+def hop(value, *pairs):
+    return lax.ppermute(value, "row", pairs)
+
+
+def after(value, *others):
+    return lax.optimization_barrier((value,) + others)[0]
 
 
 def swap_pieces(pieces, n_col):
@@ -334,51 +360,52 @@
     chunk = nrhs // n_col
 
     block = earlier_solution[0]
-    blocks = {0: block, 1: flip(block, "row", n_row, 1)}
-    for f in (2, 4, 6):
+    blocks = {0: block}
+    for f in (6, 4, 2, 1):
         blocks[f] = flip(block, "row", n_row, f)
     own = jnp.stack([jnp.where(row == j, diag_inverse[j], window_panel[:, j, :]) for j in range(step_count)])
     strips = {0: own}
-    for b in [1 << i for i in range(1, 8) if (1 << i) < n_col] + [1]:
-        strips.update({f ^ b: flip(v, "col", n_col, b) for f, v in strips.items()})
+    strips[1] = flip(own, "col", n_col, 1)
+    strips[2] = flip(own, "col", n_col, 2)
     panel = relayout(earlier_panel)
     for f in (2, 4, 6):
         blocks[f + 1] = flip(blocks[f], "row", n_row, 1)
     early, late = (0, 1, 2, 3, 4), (5, 6, 7)
     total = bulk(panel, [blocks[f] for f in early], [row ^ f for f in early], right_side, col)
     kept, sent = bulk(panel, [blocks[f] for f in late], [row ^ f for f in late], total, col, n_col)
+    strips[3] = flip(after(strips[2], sent), "col", n_col, 1)
     moved = flip(sent, "col", n_col, 1)
-    for b in [1 << i for i in range(1, 8) if (1 << i) < n_col]:
-        kept, sent = reduce_step(b, flat_index(col), kept, moved)
-        moved = flip(sent, "col", n_col, b)
-
-    def slots(k):
-        return [strips[f] for f in range(n_col)], [pl.BlockSpec((1,) + own.shape[1:], lambda i, k=k: (k, 0, 0))] * n_col
-
-    value_shape = (shape_of((rows, chunk), F32), shape_of((rows, chunk), BF16))
-    weights, specs = slots(0)
-    current, value = local(functools.partial(start_kernel, n_col), value_shape, [index, kept, moved] + weights, [SMEM, VMEM, VMEM] + specs)
-    solved = []
-    for k in range(step_count):
-        have = [k]
-        for b in ([1, 2, 4], [3, 1, 4], [6, 2, 1])[k]:
-            moved = lax.ppermute(value, "row", [(i, i ^ b) for i in have])
-            into = jnp.zeros((), bool)
-            for i in have:
-                into |= row == (i ^ b)
-            value = jnp.where(into, moved, value)
-            have += [i ^ b for i in have]
-        solved.append(value)
-        update, specs = slots(k)
-        if k < step_count - 1:
-            diag, more = slots(k + 1)
-            kernel = functools.partial(step_kernel, k + 1, n_col)
-            current, value = local(kernel, value_shape, [index, current, value] + update + diag, [SMEM, VMEM, VMEM] + specs + more)
-        else:
-            pieces = shape_of((n_col, 2, rows // n_col, chunk), BF16)
-            kernel = functools.partial(finish_kernel, k, n_col)
-            last = local(kernel, pieces, [index, current, value] + update, [SMEM, VMEM, VMEM] + specs, [pltpu.VMEM((rows, chunk), F32)])
-    first = local(pieces_kernel, shape_of((n_col, step_count - 1, rows // n_col, chunk), BF16), [index] + solved[:-1])
+    kept, sent = reduce_step(2, flat_index(col), kept, moved)
+    moved = flip(sent, "col", n_col, 2)
+    strips = [strips[f] for f in range(n_col)]
+
+    wide, narrow = shape_of((rows, chunk), F32), shape_of((rows, chunk), BF16)
+    current, own0 = local(functools.partial(start_kernel, n_col), (wide, narrow), [index, kept, moved] + strips)
+    at1, at2 = hop(own0, (0, 1)), hop(own0, (0, 2))
+    step = functools.partial(step_kernel, 1, n_col)
+    current, known0, own1 = local(step, (wide, narrow, narrow), [index, current] + strips + [own0, at1, at2])
+    up2 = hop(own1, (1, 2))
+    up3 = hop(own1, (1, 3))
+    on0 = hop(known0, (1, 3), (2, 4))
+    step = functools.partial(step_kernel, 2, n_col)
+    current, known1, own2 = local(step, (wide, narrow, narrow), [index, current] + strips + [own1, up2])
+    z4 = hop(own2, (2, 4))
+    z6 = hop(own2, (2, 6))
+    z0 = hop(own2, (2, 0))
+    further0 = hop(on0, (3, 5), (4, 6))
+    up5 = hop(up3, (3, 5))
+    last0 = hop(further0, (5, 7))
+    up7 = hop(up5, (5, 7))
+    line1 = known1 + up3 + up5 + up7
+    across1 = hop(line1, (1, 0), (5, 4), (7, 6))
+    line2 = own2 + z0 + z4 + z6
+    across2 = hop(line2, (0, 1), (2, 3), (4, 5), (6, 7))
+
+    first = shape_of((n_col, step_count - 1, strip, chunk), BF16)
+    parts = [known0 + on0, further0 + last0] + [line1, across1]
+    current, first = local(functools.partial(late_kernel, step_count, n_col), (wide, first), [index, current] + strips + parts)
+    last = shape_of((n_col, 2, strip, chunk), BF16)
+    last = local(functools.partial(finish_kernel, n_col), last, [index, current] + strips + [line2, across2], [pltpu.VMEM((rows, chunk), F32)])
     first, last = swap_pieces(first, n_col), swap_pieces(last, n_col)
     outs = (shape_of((step_count, strip, nrhs), BF16), shape_of((strip, nrhs), F32))
     return local(functools.partial(assemble_kernel, n_col), outs, [index] + first + last)
@@ -389,7 +416,7 @@
 
     def step(*args):
         chunk = args[0].shape[1] // shape[1]
-        plan = fast if shape[0] == 8 and chunk % 128 == 0 else on_device
+        plan = fast if shape == (8, 4) and chunk % 128 == 0 and args[4].shape[0] == 3 else on_device
         return plan(shape, *args)
 
     return jax.shard_map(

time: 197 us -> 126 us (0.64)
  waiting for transfers between devices: 125 us -> 54.1 us
  starting transfers between devices: 28.8 us -> 38.9 us
  Pallas kernels: 28 us -> 19.7 us
    ppermute x9 -> x14, waiting for transfers between devices: 61.6 us -> 22.9 us  [hop(): return lax.ppermute(value, 'row', pairs)]
    ppermute x18, waiting for transfers between devices: 63.7 us -> 31.3 us  [flip(): return lax.ppermute(value, axis, [(i, i ^ bit) for i in range(size)])]
    ppermute x18, starting transfers between devices: 19.4 us -> 26.9 us  [flip(): return lax.ppermute(value, axis, [(i, i ^ bit) for i in range(size)])]
    pallas_call x1, Pallas kernels: 5.84 us -> 2.49 us  [relayout(): pl.pallas_call(relayout_kernel, grid=(rows // tile,), out_shape=shape_of(...]
    pallas_call x2, Pallas kernels: 9.06 us -> 6.5 us  [bulk(): pl.pallas_call(kernel, out_shape=out_shape, in_specs=[SMEM, ANY] + [VMEM]...]
    ppermute x9 -> x14, starting transfers between devices: 9.39 us -> 11.9 us  [hop(): return lax.ppermute(value, 'row', pairs)]
    pallas_call x6, Pallas kernels: 12.9 us -> 10.6 us  [local(): pl.pallas_call(kernel, out_shape=out_shape, in_specs=[SMEM] + [VMEM] * (l...]
    unnamed x24 -> x8, local copies, waits for them, and re-layouts: 7.36 us -> 7.38 us
  transfers between devices with their start and end apart: 27 -> 32, of which waited for: 10 -> 9; matrix products, arithmetic and copies ran while one was open for 1% -> 0% of each run, Pallas kernels for 9% -> 12%
where the time goes in v3:
time: 126 us; the launch traced here: 124 us
  waiting for transfers between devices  54.1 us (43%)
  starting transfers between devices  38.9 us (31%)
  Pallas kernels  19.7 us (16%)
  local copies, waits for them, and re-layouts  7.54 us (6%)
  other arithmetic  2.58 us (2%)
    ppermute x18, waiting for transfers between devices, flip(): return lax.ppermute(value, axis, [(i, i ^ bit) for i in range(size)])  31.3 us
    ppermute x18, starting transfers between devices, flip(): return lax.ppermute(value, axis, [(i, i ^ bit) for i in range(size)])  26.9 us
    ppermute x14, waiting for transfers between devices, hop(): return lax.ppermute(value, 'row', pairs)  22.9 us
    ppermute x14, starting transfers between devices, hop(): return lax.ppermute(value, 'row', pairs)  11.9 us
    pallas_call x6, Pallas kernels, local(): pl.pallas_call(kernel, out_shape=out_shape, in_specs=[SMEM] + [VMEM] * (l...  10.6 us
    unnamed x8, local copies, waits for them, and re-layouts  7.38 us
    pallas_call x2, Pallas kernels, bulk(): pl.pallas_call(kernel, out_shape=out_shape, in_specs=[SMEM, ANY] + [VMEM]...  6.5 us
  transfers between devices with their start and end apart: 32, of which 9 were waited for; matrix products, arithmetic and copies ran while one was open for 0% of the time, Pallas kernels for 12%

profile of v3, /device:TPU:25, one launch (start us, length us, event | category | flops | bytes accessed | tf_op | source)
XLA Modules:
  0.0 123.8 jit_solution(7688291839836775339)
XLA Ops:
  0.6 2.0 %bitcast_select_fusion.2 = (bf16[1,256,1024]{2,1,0:T(8,128)(2,1)S(1)}, bf16[1,256,1024]{2,1,0:T(8,128)(2,1)S(1)}, bf16[1,256,1024]{2,1,0:T(8,128)(2,1)S(1)}) fusion(bf16[256,3,1024]{2,0,1:T(8,128)(2,1)} %param.8, bf16[3,256,1024]{2,1,0:T(8,128)(2,1)} %param.9, pred[]{:T(512)S(6)} %eq.9, pred[]{:T(512)S(6)} %eq.11, pred[]{:T(512)S(6)} %eq.10), kind=kLoop, calls=%fused_computation.3 | loop fusion | flops 786432 | bytes 4718595 | tf_op jit(solution)/shard_map/jit(_where)/select_n | solution.py:366
  2.6 0.2 pad_maximum_fusion.refs_0_
  2.8 1.3 %collective-permute-start.10 = (bf16[3,256,1024]{2,1,0:T(8,128)(2,1)S(1)}, bf16[3,256,1024]{2,1,0:T(8,128)(2,1)S(1)}, u32[]{:S(2)}, u32[]{:S(2)}) collective-permute-start(bf16[3,256,1024]{2,1,0:T(8,128)(2,1)S(1)} %pad_maximum_fusion.refs_0_), channel_id=1, source_target_pairs={{0,2},{1,3},{2,0},{3,1},{4,6},{5,7},{6,4},{7,5},{8,10},{9,11},{10,... | collective-permute-start | bytes 4718600 | tf_op jit(solution)/shard_map/ppermute | solution.py:15
  4.1 0.2 collective-permute-start.5
  4.3 0.1 collective-permute-start
  4.3 3.3 %collective-permute-start.2 = (bf16[256,512]{1,0:T(8,128)(2,1)}, bf16[256,512]{1,0:T(8,128)(2,1)S(1)}, u32[]{:S(2)}, u32[]{:S(2)}) collective-permute-start(bf16[256,512]{1,0:T(8,128)(2,1)} %bitcast.5.refs_0_), channel_id=1, source_target_pairs={{0,24},{4,28},{8,16},{12,20},{16,8},{20,12},{24,0},{28,4},{1,25},{... | collective-permute-start | bytes 786440 | tf_op jit(solution)/shard_map/ppermute | solution.py:15
  7.6 1.2 %collective-permute-start.4 = (bf16[256,512]{1,0:T(8,128)(2,1)}, bf16[256,512]{1,0:T(8,128)(2,1)}, u32[]{:S(2)}, u32[]{:S(2)}) collective-permute-start(bf16[256,512]{1,0:T(8,128)(2,1)} %bitcast.5.refs_0_), channel_id=1, source_target_pairs={{0,4},{4,0},{8,12},{12,8},{16,20},{20,16},{24,28},{28,24},{1,5},{5... | collective-permute-start | bytes 786440 | tf_op jit(solution)/shard_map/ppermute | solution.py:15
  8.9 6.8 %collective-permute-done.5.refs_2_ = bf16[256,512]{1,0:T(8,128)(2,1)} collective-permute-done((bf16[256,512]{1,0:T(8,128)(2,1)}, bf16[256,512]{1,0:T(8,128)(2,1)}, u32[]{:S(2)}, u32[]{:S(2)}) %collective-permute-start.5) | collective-permute-done | bytes 262176 | tf_op jit(solution)/shard_map/ppermute | solution.py:15
  15.7 1.2 %collective-permute-start.6 = (bf16[256,512]{1,0:T(8,128)(2,1)}, bf16[256,512]{1,0:T(8,128)(2,1)}, u32[]{:S(2)}, u32[]{:S(2)}) collective-permute-start(bf16[256,512]{1,0:T(8,128)(2,1)} %collective-permute-done.5.refs_2_), channel_id=1, source_target_pairs={{0,4},{4,0},{8,12},{12,8},{16,20},{20,16},{24,28},{28,24},{1,5},{5... | collective-permute-start | bytes 786440 | tf_op jit(solution)/shard_map/ppermute | solution.py:15
  16.9 0.2 collective-permute-start.1
  17.1 5.1 %collective-permute-done.2.refs_1_ = bf16[256,512]{1,0:T(8,128)(2,1)S(1)} collective-permute-done((bf16[256,512]{1,0:T(8,128)(2,1)}, bf16[256,512]{1,0:T(8,128)(2,1)S(1)}, u32[]{:S(2)}, u32[]{:S(2)}) %collective-permute-start.2) | collective-permute-done | bytes 262176 | tf_op jit(solution)/shard_map/ppermute | solution.py:15
  22.2 1.2 %collective-permute-start.3 = (bf16[256,512]{1,0:T(8,128)(2,1)S(1)}, bf16[256,512]{1,0:T(8,128)(2,1)}, u32[]{:S(2)}, u32[]{:S(2)}) collective-permute-start(bf16[256,512]{1,0:T(8,128)(2,1)S(1)} %collective-permute-done.2.refs_1_), channel_id=1, source_target_pairs={{0,4},{4,0},{8,12},{12,8},{16,20},{20,16},{24,28},{28,24},{1,5},{5... | collective-permute-start | bytes 786440 | tf_op jit(solution)/shard_map/ppermute | solution.py:15
  23.5 2.2 %copy-done.2 = bf16[1024,8,256]{2,1,0:T(8,128)(2,1)S(1)} copy-done((bf16[1024,8,256]{2,1,0:T(8,128)(2,1)S(1)}, bf16[1024,8,256]{2,1,0:T(8,128)(2,1)}, u32[]{:S(2)}) %copy-start.2) | copy-done | bytes 4194328
  25.6 2.5 %shard_map.68.panel_ref = bf16[8,1024,256]{2,1,0:T(8,128)(2,1)S(1)} custom-call(bf16[1024,8,256]{2,1,0:T(8,128)(2,1)S(1)} %copy-done.2), custom_call_target="tpu_custom_call" | custom-call | tf_op jit(solution)/shard_map/pallas_call | solution.py:141
  28.2 2.0 %copy-done = bf16[8,1024,256]{2,1,0:T(8,128)(2,1)} copy-done((bf16[8,1024,256]{2,1,0:T(8,128)(2,1)}, bf16[8,1024,256]{2,1,0:T(8,128)(2,1)S(1)}, u32[]{:S(2)}) %copy-start) | copy-done | bytes 4194328
  30.1 0.1 stack.57.index_ref
  30.2 0.1 pad_add_fusion.1.index_ref
  30.3 5.8 %collective-permute-start.9 = (bf16[3,256,1024]{2,1,0:T(8,128)(2,1)S(1)}, bf16[3,256,1024]{2,1,0:T(8,128)(2,1)S(1)}, u32[]{:S(2)}, u32[]{:S(2)}) collective-permute-start(bf16[3,256,1024]{2,1,0:T(8,128)(2,1)S(1)} %pad_maximum_fusion.refs_0_), channel_id=1, source_target_pairs={{0,1},{1,0},{2,3},{3,2},{4,5},{5,4},{6,7},{7,6},{8,9},{9,8},{10,11... | collective-permute-start | bytes 4718600 | tf_op jit(solution)/shard_map/ppermute | solution.py:15
  36.1 2.2 %copy-done.1 = bf16[8,1024,256]{2,1,0:T(8,128)(2,1)S(1)} copy-done((bf16[8,1024,256]{2,1,0:T(8,128)(2,1)S(1)}, bf16[8,1024,256]{2,1,0:T(8,128)(2,1)}, u32[]{:S(2)}) %copy-start.1) | copy-done | bytes 4194328
  38.3 1.0 copy-done.3
  39.3 3.5 %shard_map.69.refs_3_ = f32[1024,512]{1,0:T(8,128)S(1)} custom-call(s32[6]{0:T(128)S(1)} %stack.57.index_ref, bf16[8,1024,256]{2,1,0:T(8,128)(2,1)S(1)} %copy-done.1, bf16[256,512]{1,0:T(8,128)(2,1)} %bitcast.5.refs_0_, bf16[256,512]{1,0:T(8,128)(2,1)} %collective-permute-done.4.refs_1_, bf16[256,512]{1,0:T(8,128)(2,1)} %collective-permute-done.5.refs_2_, ...), custom_call_target="tpu_custom_call" | custom-call | tf_op jit(solution)/shard_map/pallas_call | solution.py:216
  42.9 3.0 %shard_map.70 = (f32[2,1024,128]{2,1,0:T(8,128)S(1)}, bf16[2,1024,128]{2,1,0:T(8,128)(2,1)S(1)}) custom-call(s32[4]{0:T(128)S(1)} %pad_add_fusion.1.index_ref, bf16[8,1024,256]{2,1,0:T(8,128)(2,1)S(1)} %copy-done.1, bf16[256,512]{1,0:T(8,128)(2,1)} %collective-permute-done.1.refs_0_, bf16[256,512]{1,0:T(8,128)(2,1)S(1)} %collective-permute-done.2.refs_1_, ...), custom_call_target="tpu_custom_call" | custom-call | tf_op jit(solution)/shard_map/pallas_call | solution.py:216
  45.8 0.1 collective-permute-start.11
  45.9 0.5 collective-permute-start.7
  46.4 3.6 %collective-permute-done.7.moved_ref = bf16[2,1024,128]{2,1,0:T(8,128)(2,1)S(1)} collective-permute-done((bf16[2,1024,128]{2,1,0:T(8,128)(2,1)S(1)}, bf16[2,1024,128]{2,1,0:T(8,128)(2,1)S(1)}, u32[]{:S(2)}, u32[]{:S(2)}) %collective-permute-start.7) | collective-permute-done | bytes 524320 | tf_op jit(solution)/shard_map/ppermute | solution.py:15
  50.1 0.1 shard_map.71
  50.2 0.3 collective-permute-start.8
  50.5 0.1 pad_add_fusion.index_ref
  50.6 7.4 %collective-permute-done.8.moved_ref = bf16[1,1024,128]{2,1,0:T(8,128)(2,1)S(1)} collective-permute-done((bf16[1,1024,128]{2,1,0:T(8,128)(2,1)S(1)}, bf16[1,1024,128]{2,1,0:T(8,128)(2,1)S(1)}, u32[]{:S(2)}, u32[]{:S(2)}) %collective-permute-start.8) | collective-permute-done | bytes 262176 | tf_op jit(solution)/shard_map/ppermute | solution.py:15
  58.0 1.3 %shard_map.72 = (f32[1024,128]{1,0:T(8,128)S(1)}, bf16[1024,128]{1,0:T(8,128)(2,1)S(1)}) custom-call(s32[2]{0:T(128)S(1)} %pad_add_fusion.index_ref, f32[1,1024,128]{2,1,0:T(8,128)S(1)} %get-tuple-element.19.kept_ref, bf16[1,1024,128]{2,1,0:T(8,128)(2,1)S(1)} %collective-permute-done.8.moved_ref, bf16[3,256,1024]{2,1,0:T(8,128)(2,1)S(1)} %pad_maximum_fusion.refs_0_, ...), custom_call_target="tpu_custom_call" | custom-call | tf_op jit(solution)/shard_map/pallas_call | solution.py:331
  59.3 0.7 collective-permute-start.12
  60.0 0.7 collective-permute-start.13
  60.7 2.0 %shard_map.73 = (f32[1024,128]{1,0:T(8,128)S(1)}, bf16[1024,128]{1,0:T(8,128)(2,1)S(1)}, bf16[1024,128]{1,0:T(8,128)(2,1)S(1)}) custom-call(s32[2]{0:T(128)S(1)} %pad_add_fusion.index_ref, f32[1024,128]{1,0:T(8,128)S(1)} %get-tuple-element.22.current_ref, bf16[3,256,1024]{2,1,0:T(8,128)(2,1)S(1)} %pad_maximum_fusion.refs_0_, ...), custom_call_target="tpu_custom_call" | custom-call | tf_op jit(solution)/shard_map/pallas_call | solution.py:331
  62.7 0.7 collective-permute-start.18
  63.4 0.7 collective-permute-start.15
  64.1 0.7 collective-permute-start.19
  64.8 0.7 collective-permute-start.14
  65.5 1.3 %collective-permute-start.16 = (bf16[1024,128]{1,0:T(8,128)(2,1)S(1)}, bf16[1024,128]{1,0:T(8,128)(2,1)S(1)}, u32[]{:S(2)}, u32[]{:S(2)}) collective-permute-start(bf16[1024,128]{1,0:T(8,128)(2,1)S(1)} %collective-permute-done.15), channel_id=1, source_target_pairs={{12,20},{16,24},{13,21},{17,25},{14,22},{18,26},{15,23},{19,27}} | collective-permute-start | bytes 786440 | tf_op jit(solution)/shard_map/ppermute | solution.py:342
  66.8 0.7 collective-permute-start.20
  67.5 2.0 %shard_map.74 = (f32[1024,128]{1,0:T(8,128)S(1)}, bf16[1024,128]{1,0:T(8,128)(2,1)S(1)}, bf16[1024,128]{1,0:T(8,128)(2,1)S(1)}) custom-call(s32[2]{0:T(128)S(1)} %pad_add_fusion.index_ref, f32[1024,128]{1,0:T(8,128)S(1)} %get-tuple-element.24.current_ref, bf16[3,256,1024]{2,1,0:T(8,128)(2,1)S(1)} %pad_maximum_fusion.refs_0_, ...), custom_call_target="tpu_custom_call" | custom-call | tf_op jit(solution)/shard_map/pallas_call | solution.py:331
  69.5 1.3 %collective-permute-start.27 = (bf16[1024,128]{1,0:T(8,128)(2,1)S(1)}, bf16[1024,128]{1,0:T(8,128)(2,1)S(1)}, u32[]{:S(2)}, u32[]{:S(2)}) collective-permute-start(bf16[1024,128]{1,0:T(8,128)(2,1)S(1)} %get-tuple-element.31), channel_id=1, source_target_pairs={{8,24},{9,25},{10,26},{11,27}} | collective-permute-start | bytes 786440 | tf_op jit(solution)/shard_map/ppermute | solution.py:342
  70.8 0.7 collective-permute-start.26
  71.5 0.7 collective-permute-start.25
  72.1 14.4 %collective-permute-done.16 = bf16[1024,128]{1,0:T(8,128)(2,1)S(1)} collective-permute-done((bf16[1024,128]{1,0:T(8,128)(2,1)S(1)}, bf16[1024,128]{1,0:T(8,128)(2,1)S(1)}, u32[]{:S(2)}, u32[]{:S(2)}) %collective-permute-start.16) | collective-permute-done | bytes 262176 | tf_op jit(solution)/shard_map/ppermute | solution.py:342
  86.6 0.7 collective-permute-start.17
  87.3 0.1 add_add_fusion.1.refs_6_
  87.3 1.3 %collective-permute-start.21 = (bf16[1024,128]{1,0:T(8,128)(2,1)S(1)}, bf16[1024,128]{1,0:T(8,128)(2,1)S(1)}, u32[]{:S(2)}, u32[]{:S(2)}) collective-permute-start(bf16[1024,128]{1,0:T(8,128)(2,1)S(1)} %add_add_fusion.1.refs_6_), channel_id=1, source_target_pairs={{4,0},{20,16},{28,24},{5,1},{21,17},{29,25},{6,2},{22,18},{30,26},... | collective-permute-start | bytes 786440 | tf_op jit(solution)/shard_map/ppermute | solution.py:342
  88.6 8.4 %collective-permute-done.27 = bf16[1024,128]{1,0:T(8,128)(2,1)S(1)} collective-permute-done((bf16[1024,128]{1,0:T(8,128)(2,1)S(1)}, bf16[1024,128]{1,0:T(8,128)(2,1)S(1)}, u32[]{:S(2)}, u32[]{:S(2)}) %collective-permute-start.27) | collective-permute-done | bytes 262176 | tf_op jit(solution)/shard_map/ppermute | solution.py:342
  97.0 0.1 add_add_fusion.refs_4_
  97.1 1.3 %collective-permute-start.28 = (bf16[1024,128]{1,0:T(8,128)(2,1)S(1)}, bf16[1024,128]{1,0:T(8,128)(2,1)S(1)}, u32[]{:S(2)}, u32[]{:S(2)}) collective-permute-start(bf16[1024,128]{1,0:T(8,128)(2,1)S(1)} %add_add_fusion.refs_4_), channel_id=1, source_target_pairs={{0,4},{8,12},{16,20},{24,28},{1,5},{9,13},{17,21},{25,29},{2,6},{1... | collective-permute-start | bytes 786440 | tf_op jit(solution)/shard_map/ppermute | solution.py:342
  98.4 0.1 add.24.refs_4_
  98.5 0.1 add.25.refs_5_
  98.6 2.1 %shard_map.75 = (f32[1024,128]{1,0:T(8,128)S(1)}, bf16[4,2,256,128]{3,2,1,0:T(8,128)(2,1)S(1)}) custom-call(s32[2]{0:T(128)S(1)} %pad_add_fusion.index_ref, f32[1024,128]{1,0:T(8,128)S(1)} %get-tuple-element.26.current_ref, bf16[3,256,1024]{2,1,0:T(8,128)(2,1)S(1)} %pad_maximum_fusion.refs_0_, bf16[3,256,1024]{2,1,0:T(8,128)(2,1)S(1)} %collective-permute-done.9.refs_1_, ...), custom_call_target="tpu_custom_call" | custom-call | tf_op jit(solution)/shard_map/pallas_call | solution.py:331
  100.8 7.6 %collective-permute-start.22 = (bf16[2,256,128]{2,1,0:T(8,128)(2,1)S(1)}, bf16[2,256,128]{2,1,0:T(8,128)(2,1)S(1)}, u32[]{:S(2)}, u32[]{:S(2)}) collective-permute-start(bf16[2,256,128]{2,1,0:T(8,128)(2,1)S(1)} %get-tuple-element.41), channel_id=1, source_target_pairs={{0,1},{1,0},{2,3},{3,2},{4,5},{5,4},{6,7},{7,6},{8,9},{9,8},{10,11... | collective-permute-start | bytes 393224 | tf_op jit(solution)/shard_map/ppermute | solution.py:15
  108.3 0.3 collective-permute-start.23
  108.6 1.4 %collective-permute-start.24 = (bf16[2,256,128]{2,1,0:T(8,128)(2,1)S(1)}, bf16[2,256,128]{2,1,0:T(8,128)(2,1)S(1)}, u32[]{:S(2)}, u32[]{:S(2)}) collective-permute-start(bf16[2,256,128]{2,1,0:T(8,128)(2,1)S(1)} %get-tuple-element.39), channel_id=1, source_target_pairs={{0,3},{1,2},{2,1},{3,0},{4,7},{5,6},{6,5},{7,4},{8,11},{9,10},{10,... | collective-permute-start | bytes 393224 | tf_op jit(solution)/shard_map/ppermute | solution.py:15
  110.1 1.4 %shard_map.76 = bf16[4,2,256,128]{3,2,1,0:T(8,128)(2,1)S(1)} custom-call(s32[2]{0:T(128)S(1)} %pad_add_fusion.index_ref, f32[1024,128]{1,0:T(8,128)S(1)} %get-tuple-element.30.current_ref, bf16[3,256,1024]{2,1,0:T(8,128)(2,1)S(1)} %pad_maximum_fusion.refs_0_, bf16[3,256,1024]{2,1,0:T(8,128)(2,1)S(1)} %collective-permute-done.9.refs_1_, ...), custom_call_target="tpu_custom_call" | custom-call | tf_op jit(solution)/shard_map/pallas_call | solution.py:331
  111.5 0.2 collective-permute-start.29
  111.7 0.3 collective-permute-start.30
  112.0 1.7 %collective-permute-start.31 = (bf16[2,256,128]{2,1,0:T(8,128)(2,1)S(1)}, bf16[2,256,128]{2,1,0:T(8,128)(2,1)S(1)}, u32[]{:S(2)}, u32[]{:S(2)}) collective-permute-start(bf16[2,256,128]{2,1,0:T(8,128)(2,1)S(1)} %get-tuple-element.35), channel_id=1, source_target_pairs={{0,3},{1,2},{2,1},{3,0},{4,7},{5,6},{6,5},{7,4},{8,11},{9,10},{10,... | collective-permute-start | bytes 393224 | tf_op jit(solution)/shard_map/ppermute | solution.py:15
  113.7 3.1 %collective-permute-done.24.refs_3_ = bf16[2,256,128]{2,1,0:T(8,128)(2,1)S(1)} collective-permute-done((bf16[2,256,128]{2,1,0:T(8,128)(2,1)S(1)}, bf16[2,256,128]{2,1,0:T(8,128)(2,1)S(1)}, u32[]{:S(2)}, u32[]{:S(2)}) %collective-permute-start.24) | collective-permute-done | bytes 131104 | tf_op jit(solution)/shard_map/ppermute | solution.py:15
  116.8 2.2 %collective-permute-done.30.refs_6_ = bf16[2,256,128]{2,1,0:T(8,128)(2,1)S(1)} collective-permute-done((bf16[2,256,128]{2,1,0:T(8,128)(2,1)S(1)}, bf16[2,256,128]{2,1,0:T(8,128)(2,1)S(1)}, u32[]{:S(2)}, u32[]{:S(2)}) %collective-permute-start.30) | collective-permute-done | bytes 131104 | tf_op jit(solution)/shard_map/ppermute | solution.py:15
  119.0 3.0 %collective-permute-done.31.refs_7_ = bf16[2,256,128]{2,1,0:T(8,128)(2,1)S(1)} collective-permute-done((bf16[2,256,128]{2,1,0:T(8,128)(2,1)S(1)}, bf16[2,256,128]{2,1,0:T(8,128)(2,1)S(1)}, u32[]{:S(2)}, u32[]{:S(2)}) %collective-permute-start.31) | collective-permute-done | bytes 131104 | tf_op jit(solution)/shard_map/ppermute | solution.py:15
  122.0 1.8 %shard_map.77 = (bf16[3,256,512]{2,1,0:T(8,128)(2,1)}, f32[256,512]{1,0:T(8,128)}) custom-call(s32[2]{0:T(128)S(1)} %pad_add_fusion.index_ref, bf16[2,256,128]{2,1,0:T(8,128)(2,1)S(1)} %get-tuple-element.42.refs_0_, bf16[2,256,128]{2,1,0:T(8,128)(2,1)S(1)} %collective-permute-done.22.refs_1_, bf16[2,256,128]{2,1,0:T(8,128)(2,1)S(1)} %collective-permute-done.23.refs_2_, ...), custom_call_target="tpu_custom_call" | custom-call | tf_op jit(solution)/shard_map/pallas_call | solution.py:331
  (29 shorter events, 0.1 us)
Async XLA Ops:
  2.8 43.0 %collective-permute-start.10 = (bf16[3,256,1024]{2,1,0:T(8,128)(2,1)S(1)}, bf16[3,256,1024]{2,1,0:T(8,128)(2,1)S(1)}, u32[]{:S(2)}, u32[]{:S(2)}) collective-permute-start(bf16[3,256,1024]{2,1,0:T(8,128)(2,1)S(1)} %pad_maximum_fusion.refs_0_), channel_id=1, source_target_pairs={{0,2},{1,3},{2,0},{3,1},{4,6},{5,7},{6,4},{7,5},{8,10},{9,11},{10,... | collective-permute-start | bytes 4718600 | tf_op jit(solution)/shard_map/ppermute | solution.py:15
  4.1 11.6 %collective-permute-start.5 = (bf16[256,512]{1,0:T(8,128)(2,1)}, bf16[256,512]{1,0:T(8,128)(2,1)}, u32[]{:S(2)}, u32[]{:S(2)}) collective-permute-start(bf16[256,512]{1,0:T(8,128)(2,1)} %bitcast.5.refs_0_), channel_id=1, source_target_pairs={{0,8},{4,12},{8,0},{12,4},{16,24},{20,28},{24,16},{28,20},{1,9},{5... | collective-permute-start | bytes 786440 | tf_op jit(solution)/shard_map/ppermute | solution.py:15
  4.3 12.6 %collective-permute-start = (bf16[256,512]{1,0:T(8,128)(2,1)}, bf16[256,512]{1,0:T(8,128)(2,1)}, u32[]{:S(2)}, u32[]{:S(2)}) collective-permute-start(bf16[256,512]{1,0:T(8,128)(2,1)} %bitcast.5.refs_0_), channel_id=1, source_target_pairs={{0,16},{4,20},{8,24},{12,28},{16,0},{20,4},{24,8},{28,12},{1,17},{... | collective-permute-start | bytes 786440 | tf_op jit(solution)/shard_map/ppermute | solution.py:15
  4.3 17.9 %collective-permute-start.2 = (bf16[256,512]{1,0:T(8,128)(2,1)}, bf16[256,512]{1,0:T(8,128)(2,1)S(1)}, u32[]{:S(2)}, u32[]{:S(2)}) collective-permute-start(bf16[256,512]{1,0:T(8,128)(2,1)} %bitcast.5.refs_0_), channel_id=1, source_target_pairs={{0,24},{4,28},{8,16},{12,20},{16,8},{20,12},{24,0},{28,4},{1,25},{... | collective-permute-start | bytes 786440 | tf_op jit(solution)/shard_map/ppermute | solution.py:15
  7.6 22.6 %collective-permute-start.4 = (bf16[256,512]{1,0:T(8,128)(2,1)}, bf16[256,512]{1,0:T(8,128)(2,1)}, u32[]{:S(2)}, u32[]{:S(2)}) collective-permute-start(bf16[256,512]{1,0:T(8,128)(2,1)} %bitcast.5.refs_0_), channel_id=1, source_target_pairs={{0,4},{4,0},{8,12},{12,8},{16,20},{20,16},{24,28},{28,24},{1,5},{5... | collective-permute-start | bytes 786440 | tf_op jit(solution)/shard_map/ppermute | solution.py:15
  15.7 20.4 %collective-permute-start.6 = (bf16[256,512]{1,0:T(8,128)(2,1)}, bf16[256,512]{1,0:T(8,128)(2,1)}, u32[]{:S(2)}, u32[]{:S(2)}) collective-permute-start(bf16[256,512]{1,0:T(8,128)(2,1)} %collective-permute-done.5.refs_2_), channel_id=1, source_target_pairs={{0,4},{4,0},{8,12},{12,8},{16,20},{20,16},{24,28},{28,24},{1,5},{5... | collective-permute-start | bytes 786440 | tf_op jit(solution)/shard_map/ppermute | solution.py:15
  16.9 25.9 %collective-permute-start.1 = (bf16[256,512]{1,0:T(8,128)(2,1)}, bf16[256,512]{1,0:T(8,128)(2,1)}, u32[]{:S(2)}, u32[]{:S(2)}) collective-permute-start(bf16[256,512]{1,0:T(8,128)(2,1)} %collective-permute-done.refs_4_), channel_id=1, source_target_pairs={{0,4},{4,0},{8,12},{12,8},{16,20},{20,16},{24,28},{28,24},{1,5},{5... | collective-permute-start | bytes 786440 | tf_op jit(solution)/shard_map/ppermute | solution.py:15
  22.2 20.6 %collective-permute-start.3 = (bf16[256,512]{1,0:T(8,128)(2,1)S(1)}, bf16[256,512]{1,0:T(8,128)(2,1)}, u32[]{:S(2)}, u32[]{:S(2)}) collective-permute-start(bf16[256,512]{1,0:T(8,128)(2,1)S(1)} %collective-permute-done.2.refs_1_), channel_id=1, source_target_pairs={{0,4},{4,0},{8,12},{12,8},{16,20},{20,16},{24,28},{28,24},{1,5},{5... | collective-permute-start | bytes 786440 | tf_op jit(solution)/shard_map/ppermute | solution.py:15
  23.5 2.2 %copy-start.2 = (bf16[1024,8,256]{2,1,0:T(8,128)(2,1)S(1)}, bf16[1024,8,256]{2,1,0:T(8,128)(2,1)}, u32[]{:S(2)}) copy-start(bf16[1024,8,256]{2,1,0:T(8,128)(2,1)} %panel_ref.1) | copy-start | bytes 12582916
  28.1 2.0 %copy-start = (bf16[8,1024,256]{2,1,0:T(8,128)(2,1)}, bf16[8,1024,256]{2,1,0:T(8,128)(2,1)S(1)}, u32[]{:S(2)}) copy-start(bf16[8,1024,256]{2,1,0:T(8,128)(2,1)S(1)} %shard_map.68.panel_ref) | copy-start | bytes 12582916
  30.3 27.7 %collective-permute-start.9 = (bf16[3,256,1024]{2,1,0:T(8,128)(2,1)S(1)}, bf16[3,256,1024]{2,1,0:T(8,128)(2,1)S(1)}, u32[]{:S(2)}, u32[]{:S(2)}) collective-permute-start(bf16[3,256,1024]{2,1,0:T(8,128)(2,1)S(1)} %pad_maximum_fusion.refs_0_), channel_id=1, source_target_pairs={{0,1},{1,0},{2,3},{3,2},{4,5},{5,4},{6,7},{7,6},{8,9},{9,8},{10,11... | collective-permute-start | bytes 4718600 | tf_op jit(solution)/shard_map/ppermute | solution.py:15
  36.1 2.2 %copy-start.1 = (bf16[8,1024,256]{2,1,0:T(8,128)(2,1)S(1)}, bf16[8,1024,256]{2,1,0:T(8,128)(2,1)}, u32[]{:S(2)}) copy-start(bf16[8,1024,256]{2,1,0:T(8,128)(2,1)} %copy-done) | copy-start | bytes 12582916
  38.3 1.0 copy-start.3
  45.8 12.2 %collective-permute-start.11 = (bf16[3,256,1024]{2,1,0:T(8,128)(2,1)S(1)}, bf16[3,256,1024]{2,1,0:T(8,128)(2,1)S(1)}, u32[]{:S(2)}, u32[]{:S(2)}) collective-permute-start(bf16[3,256,1024]{2,1,0:T(8,128)(2,1)S(1)} %collective-permute-done.10.refs_2_), channel_id=1, source_target_pairs={{0,1},{1,0},{2,3},{3,2},{4,5},{5,4},{6,7},{7,6},{8,9},{9,8},{10,11... | collective-permute-start | bytes 4718600 | tf_op jit(solution)/shard_map/ppermute | solution.py:15
  45.9 4.1 %collective-permute-start.7 = (bf16[2,1024,128]{2,1,0:T(8,128)(2,1)S(1)}, bf16[2,1024,128]{2,1,0:T(8,128)(2,1)S(1)}, u32[]{:S(2)}, u32[]{:S(2)}) collective-permute-start(bf16[2,1024,128]{2,1,0:T(8,128)(2,1)S(1)} %get-tuple-element.18), channel_id=1, source_target_pairs={{0,1},{1,0},{2,3},{3,2},{4,5},{5,4},{6,7},{7,6},{8,9},{9,8},{10,11... | collective-permute-start | bytes 1572872 | tf_op jit(solution)/shard_map/ppermute | solution.py:15
  50.2 7.8 %collective-permute-start.8 = (bf16[1,1024,128]{2,1,0:T(8,128)(2,1)S(1)}, bf16[1,1024,128]{2,1,0:T(8,128)(2,1)S(1)}, u32[]{:S(2)}, u32[]{:S(2)}) collective-permute-start(bf16[1,1024,128]{2,1,0:T(8,128)(2,1)S(1)} %get-tuple-element.20), channel_id=1, source_target_pairs={{0,2},{1,3},{2,0},{3,1},{4,6},{5,7},{6,4},{7,5},{8,10},{9,11},{10,... | collective-permute-start | bytes 786440 | tf_op jit(solution)/shard_map/ppermute | solution.py:15
  59.3 1.4 %collective-permute-start.12 = (bf16[1024,128]{1,0:T(8,128)(2,1)S(1)}, bf16[1024,128]{1,0:T(8,128)(2,1)S(1)}, u32[]{:S(2)}, u32[]{:S(2)}) collective-permute-start(bf16[1024,128]{1,0:T(8,128)(2,1)S(1)} %get-tuple-element.23.refs_4_), channel_id=1, source_target_pairs={{0,4},{1,5},{2,6},{3,7}} | collective-permute-start | bytes 786440 | tf_op jit(solution)/shard_map/ppermute | solution.py:342
  60.0 0.7 collective-permute-start.13
  62.7 1.4 %collective-permute-start.18 = (bf16[1024,128]{1,0:T(8,128)(2,1)S(1)}, bf16[1024,128]{1,0:T(8,128)(2,1)S(1)}, u32[]{:S(2)}, u32[]{:S(2)}) collective-permute-start(bf16[1024,128]{1,0:T(8,128)(2,1)S(1)} %get-tuple-element.25.refs_4_), channel_id=1, source_target_pairs={{4,12},{5,13},{6,14},{7,15}} | collective-permute-start | bytes 786440 | tf_op jit(solution)/shard_map/ppermute | solution.py:342
  63.4 2.1 %collective-permute-start.15 = (bf16[1024,128]{1,0:T(8,128)(2,1)S(1)}, bf16[1024,128]{1,0:T(8,128)(2,1)S(1)}, u32[]{:S(2)}, u32[]{:S(2)}) collective-permute-start(bf16[1024,128]{1,0:T(8,128)(2,1)S(1)} %get-tuple-element.27), channel_id=1, source_target_pairs={{4,12},{8,16},{5,13},{9,17},{6,14},{10,18},{7,15},{11,19}} | collective-permute-start | bytes 786440 | tf_op jit(solution)/shard_map/ppermute | solution.py:342
  64.1 2.7 %collective-permute-start.19 = (bf16[1024,128]{1,0:T(8,128)(2,1)S(1)}, bf16[1024,128]{1,0:T(8,128)(2,1)S(1)}, u32[]{:S(2)}, u32[]{:S(2)}) collective-permute-start(bf16[1024,128]{1,0:T(8,128)(2,1)S(1)} %collective-permute-done.18), channel_id=1, source_target_pairs={{12,20},{13,21},{14,22},{15,23}} | collective-permute-start | bytes 786440 | tf_op jit(solution)/shard_map/ppermute | solution.py:342
  64.8 2.7 %collective-permute-start.14 = (bf16[1024,128]{1,0:T(8,128)(2,1)S(1)}, bf16[1024,128]{1,0:T(8,128)(2,1)S(1)}, u32[]{:S(2)}, u32[]{:S(2)}) collective-permute-start(bf16[1024,128]{1,0:T(8,128)(2,1)S(1)} %get-tuple-element.25.refs_4_), channel_id=1, source_target_pairs={{4,8},{5,9},{6,10},{7,11}} | collective-permute-start | bytes 786440 | tf_op jit(solution)/shard_map/ppermute | solution.py:342
  65.5 21.1 %collective-permute-start.16 = (bf16[1024,128]{1,0:T(8,128)(2,1)S(1)}, bf16[1024,128]{1,0:T(8,128)(2,1)S(1)}, u32[]{:S(2)}, u32[]{:S(2)}) collective-permute-start(bf16[1024,128]{1,0:T(8,128)(2,1)S(1)} %collective-permute-done.15), channel_id=1, source_target_pairs={{12,20},{16,24},{13,21},{17,25},{14,22},{18,26},{15,23},{19,27}} | collective-permute-start | bytes 786440 | tf_op jit(solution)/shard_map/ppermute | solution.py:342
  66.8 20.5 %collective-permute-start.20 = (bf16[1024,128]{1,0:T(8,128)(2,1)S(1)}, bf16[1024,128]{1,0:T(8,128)(2,1)S(1)}, u32[]{:S(2)}, u32[]{:S(2)}) collective-permute-start(bf16[1024,128]{1,0:T(8,128)(2,1)S(1)} %collective-permute-done.19), channel_id=1, source_target_pairs={{20,28},{21,29},{22,30},{23,31}} | collective-permute-start | bytes 786440 | tf_op jit(solution)/shard_map/ppermute | solution.py:342
  69.5 27.5 %collective-permute-start.27 = (bf16[1024,128]{1,0:T(8,128)(2,1)S(1)}, bf16[1024,128]{1,0:T(8,128)(2,1)S(1)}, u32[]{:S(2)}, u32[]{:S(2)}) collective-permute-start(bf16[1024,128]{1,0:T(8,128)(2,1)S(1)} %get-tuple-element.31), channel_id=1, source_target_pairs={{8,24},{9,25},{10,26},{11,27}} | collective-permute-start | bytes 786440 | tf_op jit(solution)/shard_map/ppermute | solution.py:342
  70.8 26.3 %collective-permute-start.26 = (bf16[1024,128]{1,0:T(8,128)(2,1)S(1)}, bf16[1024,128]{1,0:T(8,128)(2,1)S(1)}, u32[]{:S(2)}, u32[]{:S(2)}) collective-permute-start(bf16[1024,128]{1,0:T(8,128)(2,1)S(1)} %get-tuple-element.31), channel_id=1, source_target_pairs={{8,16},{9,17},{10,18},{11,19}} | collective-permute-start | bytes 786440 | tf_op jit(solution)/shard_map/ppermute | solution.py:342
  71.5 25.6 %collective-permute-start.25 = (bf16[1024,128]{1,0:T(8,128)(2,1)S(1)}, bf16[1024,128]{1,0:T(8,128)(2,1)S(1)}, u32[]{:S(2)}, u32[]{:S(2)}) collective-permute-start(bf16[1024,128]{1,0:T(8,128)(2,1)S(1)} %get-tuple-element.31), channel_id=1, source_target_pairs={{8,0},{9,1},{10,2},{11,3}} | collective-permute-start | bytes 786440 | tf_op jit(solution)/shard_map/ppermute | solution.py:342
  86.6 11.9 %collective-permute-start.17 = (bf16[1024,128]{1,0:T(8,128)(2,1)S(1)}, bf16[1024,128]{1,0:T(8,128)(2,1)S(1)}, u32[]{:S(2)}, u32[]{:S(2)}) collective-permute-start(bf16[1024,128]{1,0:T(8,128)(2,1)S(1)} %collective-permute-done.16), channel_id=1, source_target_pairs={{20,28},{21,29},{22,30},{23,31}} | collective-permute-start | bytes 786440 | tf_op jit(solution)/shard_map/ppermute | solution.py:342
  87.3 11.2 %collective-permute-start.21 = (bf16[1024,128]{1,0:T(8,128)(2,1)S(1)}, bf16[1024,128]{1,0:T(8,128)(2,1)S(1)}, u32[]{:S(2)}, u32[]{:S(2)}) collective-permute-start(bf16[1024,128]{1,0:T(8,128)(2,1)S(1)} %add_add_fusion.1.refs_6_), channel_id=1, source_target_pairs={{4,0},{20,16},{28,24},{5,1},{21,17},{29,25},{6,2},{22,18},{30,26},... | collective-permute-start | bytes 786440 | tf_op jit(solution)/shard_map/ppermute | solution.py:342
  97.1 13.0 %collective-permute-start.28 = (bf16[1024,128]{1,0:T(8,128)(2,1)S(1)}, bf16[1024,128]{1,0:T(8,128)(2,1)S(1)}, u32[]{:S(2)}, u32[]{:S(2)}) collective-permute-start(bf16[1024,128]{1,0:T(8,128)(2,1)S(1)} %add_add_fusion.refs_4_), channel_id=1, source_target_pairs={{0,4},{8,12},{16,20},{24,28},{1,5},{9,13},{17,21},{25,29},{2,6},{1... | collective-permute-start | bytes 786440 | tf_op jit(solution)/shard_map/ppermute | solution.py:342
  100.8 11.2 %collective-permute-start.22 = (bf16[2,256,128]{2,1,0:T(8,128)(2,1)S(1)}, bf16[2,256,128]{2,1,0:T(8,128)(2,1)S(1)}, u32[]{:S(2)}, u32[]{:S(2)}) collective-permute-start(bf16[2,256,128]{2,1,0:T(8,128)(2,1)S(1)} %get-tuple-element.41), channel_id=1, source_target_pairs={{0,1},{1,0},{2,3},{3,2},{4,5},{5,4},{6,7},{7,6},{8,9},{9,8},{10,11... | collective-permute-start | bytes 393224 | tf_op jit(solution)/shard_map/ppermute | solution.py:15
  108.3 5.4 %collective-permute-start.23 = (bf16[2,256,128]{2,1,0:T(8,128)(2,1)S(1)}, bf16[2,256,128]{2,1,0:T(8,128)(2,1)S(1)}, u32[]{:S(2)}, u32[]{:S(2)}) collective-permute-start(bf16[2,256,128]{2,1,0:T(8,128)(2,1)S(1)} %get-tuple-element.40), channel_id=1, source_target_pairs={{0,2},{1,3},{2,0},{3,1},{4,6},{5,7},{6,4},{7,5},{8,10},{9,11},{10,... | collective-permute-start | bytes 393224 | tf_op jit(solution)/shard_map/ppermute | solution.py:15
  108.6 8.2 %collective-permute-start.24 = (bf16[2,256,128]{2,1,0:T(8,128)(2,1)S(1)}, bf16[2,256,128]{2,1,0:T(8,128)(2,1)S(1)}, u32[]{:S(2)}, u32[]{:S(2)}) collective-permute-start(bf16[2,256,128]{2,1,0:T(8,128)(2,1)S(1)} %get-tuple-element.39), channel_id=1, source_target_pairs={{0,3},{1,2},{2,1},{3,0},{4,7},{5,6},{6,5},{7,4},{8,11},{9,10},{10,... | collective-permute-start | bytes 393224 | tf_op jit(solution)/shard_map/ppermute | solution.py:15
  111.5 5.4 %collective-permute-start.29 = (bf16[2,256,128]{2,1,0:T(8,128)(2,1)S(1)}, bf16[2,256,128]{2,1,0:T(8,128)(2,1)S(1)}, u32[]{:S(2)}, u32[]{:S(2)}) collective-permute-start(bf16[2,256,128]{2,1,0:T(8,128)(2,1)S(1)} %get-tuple-element.37), channel_id=1, source_target_pairs={{0,1},{1,0},{2,3},{3,2},{4,5},{5,4},{6,7},{7,6},{8,9},{9,8},{10,11... | collective-permute-start | bytes 393224 | tf_op jit(solution)/shard_map/ppermute | solution.py:15
  111.7 7.3 %collective-permute-start.30 = (bf16[2,256,128]{2,1,0:T(8,128)(2,1)S(1)}, bf16[2,256,128]{2,1,0:T(8,128)(2,1)S(1)}, u32[]{:S(2)}, u32[]{:S(2)}) collective-permute-start(bf16[2,256,128]{2,1,0:T(8,128)(2,1)S(1)} %get-tuple-element.36), channel_id=1, source_target_pairs={{0,2},{1,3},{2,0},{3,1},{4,6},{5,7},{6,4},{7,5},{8,10},{9,11},{10,... | collective-permute-start | bytes 393224 | tf_op jit(solution)/shard_map/ppermute | solution.py:15
  112.0 10.0 %collective-permute-start.31 = (bf16[2,256,128]{2,1,0:T(8,128)(2,1)S(1)}, bf16[2,256,128]{2,1,0:T(8,128)(2,1)S(1)}, u32[]{:S(2)}, u32[]{:S(2)}) collective-permute-start(bf16[2,256,128]{2,1,0:T(8,128)(2,1)S(1)} %get-tuple-element.35), channel_id=1, source_target_pairs={{0,3},{1,2},{2,1},{3,0},{4,7},{5,6},{6,5},{7,4},{8,11},{9,10},{10,... | collective-permute-start | bytes 393224 | tf_op jit(solution)/shard_map/ppermute | solution.py:15

commit v4 on v1

--- a/solution.py
+++ b/solution.py
@@ -1,6 +1,10 @@
+import functools
+
 import jax
 import jax.numpy as jnp
 from jax import lax
+from jax.experimental import pallas as pl
+from jax.experimental.pallas import tpu as pltpu
 from jax.sharding import PartitionSpec as P
 
 F32 = jnp.float32
@@ -109,11 +113,345 @@
     return jnp.concatenate([early, late[:1]]), late[1].astype(F32)
 
 
+def flat_index(*values):
+    return jnp.stack([jnp.asarray(v, jnp.int32) for v in values])
+
+
+PARAMS = pltpu.CompilerParams(vmem_limit_bytes=20 * 1024 * 1024)
+
+
+def cost(us):
+    return pl.CostEstimate(flops=0, bytes_accessed=int(us * 3.6e6), transcendentals=0)
+
+SMEM = pl.BlockSpec(memory_space=pltpu.SMEM)
+VMEM = pl.BlockSpec(memory_space=pltpu.VMEM)
+HBM = pl.BlockSpec(memory_space=pltpu.HBM)
+
+
+def shape_of(shape, dtype):
+    return jax.ShapeDtypeStruct(shape, dtype)
+
+
+def order_kernel(index_ref, panel_ref, out_ref, held, sems, *wide):
+    tiles, tile, sources, width = held.shape
+    row = index_ref[0]
+    copies = [pltpu.make_async_copy(panel_ref.at[pl.ds(t * tile, tile)], held.at[t], sems.at[t]) for t in range(tiles)]
+    for copy in copies:
+        copy.start()
+    for t, copy in enumerate(copies):
+        copy.wait()
+        for h, lanes in enumerate(wide):
+            lanes[...] = held[t, :, :, h * 128 : (h + 1) * 128].astype(F32).reshape(tile * sources, 128)
+            for j in range(sources):
+                start = (j ^ row) * width + h * 128
+                span = pl.ds(pl.multiple_of(start, 128), 128)
+                out_ref[t * tile : (t + 1) * tile, span] = lanes[pl.ds(j, tile, stride=sources), :].astype(BF16)
+
+
+def order_panel(index, panel, tiles=4):
+    rows, sources, width = panel.shape
+    tile = rows // tiles
+    return pl.pallas_call(
+        order_kernel,
+        out_shape=shape_of((rows, sources * width), BF16),
+        in_specs=[SMEM, HBM],
+        out_specs=VMEM,
+        scratch_shapes=[pltpu.VMEM((tiles, tile, sources, width), BF16), pltpu.SemaphoreType.DMA((tiles,))]
+        + [pltpu.VMEM((tile * sources, 128), F32)] * (width // 128),
+        compiler_params=PARAMS,
+        cost_estimate=cost(8),
+    )(index, panel)
+
+
+def bulk_kernel(count, index_ref, panel_ref, side_ref, *refs):
+    blocks, (total_ref, stacked) = refs[:count], refs[count:]
+    width = blocks[0].shape[0]
+    strip = side_ref.shape[0]
+    for f in range(count):
+        stacked[f * width : (f + 1) * width, :] = blocks[f][...]
+    for t in range(total_ref.shape[0] // strip):
+        span = slice(t * strip, (t + 1) * strip)
+        total_ref[span, :] = matmul(panel_ref[span, : count * width], stacked[...])
+    own = pl.ds(pl.multiple_of(index_ref[1] * strip, strip), strip)
+    total_ref[own, :] = total_ref[own, :] - side_ref[...]
+
+
+def bulk(index, panel, side, blocks):
+    count = len(blocks)
+    width, nrhs = blocks[0].shape
+    scratch = [pltpu.VMEM((count * width, nrhs), BF16)]
+    kernel = functools.partial(bulk_kernel, count)
+    return local(kernel, shape_of((panel.shape[0], nrhs), F32), [index, panel, side] + blocks, scratch, us=8)
+
+
+def split_kernel(n_col, index_ref, panel_ref, block_ref, total_ref, kept_ref, sent_ref, scratch):
+    chunk = kept_ref.shape[2]
+    strip = scratch.shape[0]
+    core = lax.rem(index_ref[1], 2)
+
+    def tile(t, carry):
+        span = pl.ds(pl.multiple_of(t * strip, strip), strip)
+        scratch[...] = total_ref[span, :] + matmul(panel_ref[span, panel_ref.shape[1] - block_ref.shape[0] :], block_ref[...])
+        for h in range(n_col // 2):
+            kept_ref[h, span, :] = scratch[:, pl.ds(pl.multiple_of((2 * h + core) * chunk, chunk), chunk)]
+            sent_ref[h, span, :] = scratch[:, pl.ds(pl.multiple_of((2 * h + 1 - core) * chunk, chunk), chunk)].astype(BF16)
+        return carry
+
+    lax.fori_loop(0, total_ref.shape[0] // strip, tile, 0)
+
+
+def reduce_kernel(bit, index_ref, kept_ref, moved_ref, keep_ref, send_ref):
+    mine = lax.rem(index_ref[0] // bit, 2)
+    for h in range(keep_ref.shape[0]):
+        keep_ref[h] = kept_ref[2 * h + mine] + moved_ref[2 * h + mine].astype(F32)
+        send_ref[h] = (kept_ref[2 * h + 1 - mine] + moved_ref[2 * h + 1 - mine].astype(F32)).astype(BF16)
+
+
+def reduce_step(bit, index, kept, moved):
+    part = (kept.shape[0] // 2,) + kept.shape[1:]
+    return pl.pallas_call(
+        functools.partial(reduce_kernel, bit),
+        out_shape=(shape_of(part, F32), shape_of(part, BF16)),
+        in_specs=[SMEM, VMEM, VMEM],
+        out_specs=(VMEM, VMEM),
+        compiler_params=PARAMS,
+        cost_estimate=cost(1),
+    )(index, kept, moved)
+
+
+def apply_strips(col, strips, value, store):
+    refs, slot = strips
+    width = refs[0].shape[1]
+    for f, strip in enumerate(refs):
+        span = pl.ds(pl.multiple_of((col ^ f) * width, width), width)
+        store(span, matmul(strip[slot], value))
+
+
+def store_solved(index_ref, strips, k, current_ref, solved_ref):
+    def store(span, product):
+        solved_ref[span, :] = product.astype(BF16)
+
+    @pl.when(index_ref[0] == k)
+    def _():
+        apply_strips(index_ref[1], strips, current_ref[...].astype(BF16), store)
+
+    @pl.when(index_ref[0] != k)
+    def _():
+        solved_ref[...] = jnp.zeros_like(solved_ref)
+
+
+def subtract(index_ref, strips, value, chosen, source_ref, target_ref):
+    def store(span, product):
+        target_ref[span, :] = source_ref[span, :] - product
+
+    @pl.when(chosen)
+    def _():
+        apply_strips(index_ref[1], strips, value, store)
+
+    @pl.when(jnp.logical_not(chosen))
+    def _():
+        target_ref[...] = source_ref[...]
+
+
+def added(parts):
+    return functools.reduce(jnp.add, [part[...] for part in parts])
+
+
+def start_kernel(n_col, index_ref, kept_ref, moved_ref, *refs):
+    strips, (current_ref, solved_ref) = refs[:n_col], refs[n_col:]
+    current_ref[...] = -(kept_ref[0] + moved_ref[0].astype(F32))
+    store_solved(index_ref, (strips, 0), 0, current_ref, solved_ref)
+
+
+def first_step_kernel(n_col, index_ref, current_ref, own_ref, value_ref, *refs):
+    strips, (out_ref, solved_ref) = refs[:n_col], refs[n_col:]
+    subtract(index_ref, (strips, 0), value_ref[...], index_ref[0] == 1, current_ref, out_ref)
+    store_solved(index_ref, (strips, 1), 1, out_ref, solved_ref)
+
+    @pl.when(index_ref[0] == 0)
+    def _():
+        solved_ref[...] = own_ref[...]
+
+
+def between_kernel(n_col, index_ref, current_ref, value_ref, *refs):
+    strips, (out_ref,) = refs[:n_col], refs[n_col:]
+    subtract(index_ref, (strips, 0), value_ref[...], index_ref[0] == 2, current_ref, out_ref)
+
+
+def copy_where(chosen, source_ref, target_ref):
+    @pl.when(chosen)
+    def _():
+        target_ref[...] = source_ref[...]
+
+
+def second_step_kernel(n_col, index_ref, current_ref, own_ref, first_ref, second_ref, *refs):
+    strips, (out_ref, solved_ref, line_ref) = refs[:n_col], refs[n_col:]
+    row = index_ref[0]
+    subtract(index_ref, (strips, 1), first_ref[...], row == 2, current_ref, out_ref)
+    store_solved(index_ref, (strips, 2), 2, out_ref, solved_ref)
+    copy_where(row == 0, own_ref, solved_ref)
+    copy_where(row == 3, second_ref, solved_ref)
+    copy_where(row != 6, first_ref, line_ref)
+    copy_where(row == 6, second_ref, line_ref)
+
+
+def line_kernel(index_ref, own1_ref, own2_ref, z6_ref, z4_ref, z0_ref, out_ref):
+    row = index_ref[0]
+    copy_where(row == 0, z0_ref, out_ref)
+    copy_where(row == 1, own1_ref, out_ref)
+    copy_where((row == 2) | (row == 3), own2_ref, out_ref)
+    copy_where((row == 4) | (row == 7), z4_ref, out_ref)
+    copy_where((row == 5) | (row == 6), z6_ref, out_ref)
+
+
+def update_either(index_ref, first, strips, value, source_ref, target_ref):
+    row = index_ref[0]
+
+    @pl.when((row > 2) & first)
+    def _():
+        subtract(index_ref, (strips, 1), value, row > 2, source_ref, target_ref)
+
+    @pl.when((row > 2) & jnp.logical_not(first))
+    def _():
+        subtract(index_ref, (strips, 2), value, row > 2, source_ref, target_ref)
+
+    @pl.when(row <= 2)
+    def _():
+        target_ref[...] = source_ref[...]
+
+
+def middle_kernel(n_col, index_ref, current_ref, own0_ref, at1_ref, at2_ref, z0_ref, line0_ref, across0_ref, line_ref, *refs):
+    strips, (out_ref, pieces_ref, known, between) = refs[:n_col], refs[n_col:]
+    row = index_ref[0]
+    for holder, part in enumerate((own0_ref, at1_ref, at2_ref, z0_ref, line0_ref, across0_ref, line0_ref, across0_ref)):
+        copy_where(row == holder, part, known)
+    subtract(index_ref, (strips, 0), known[...], row > 2, current_ref, between)
+    update_either(index_ref, lax.rem(row, 2) == 1, strips, line_ref[...], between, out_ref)
+    cut(index_ref, known, pieces_ref, 0)
+    cut(index_ref, line_ref, pieces_ref, 1)
+
+
+def finish_kernel(n_col, index_ref, current_ref, value_ref, *refs):
+    strips, (pieces_ref, scratch) = refs[:n_col], refs[n_col:]
+    update_either(index_ref, lax.rem(index_ref[0], 2) == 0, strips, value_ref[...], current_ref, scratch)
+    cut(index_ref, value_ref, pieces_ref, 0)
+    cut(index_ref, scratch, pieces_ref, 1)
+
+
+def cut(index_ref, value_ref, pieces_ref, k):
+    width = pieces_ref.shape[2]
+    for f in range(pieces_ref.shape[0]):
+        span = pl.ds(pl.multiple_of((index_ref[1] ^ f) * width, width), width)
+        pieces_ref[f, k] = value_ref[span, :].astype(BF16)
+
+
+def assemble_kernel(n_col, index_ref, *refs):
+    groups, (solved_ref, remaining_ref) = refs[: 2 * n_col], refs[2 * n_col :]
+    middle, late = groups[:n_col], groups[n_col:]
+    chunk = middle[0].shape[2]
+    odd = lax.rem(index_ref[0], 2)
+    for f in range(n_col):
+        span = pl.ds(pl.multiple_of((index_ref[1] ^ f) * chunk, chunk), chunk)
+        solved_ref[0, :, span] = middle[f][0]
+        solved_ref[2 - odd, :, span] = middle[f][1]
+        solved_ref[1 + odd, :, span] = late[f][0]
+        remaining_ref[:, span] = late[f][1].astype(F32)
+
+
+def local(kernel, out_shape, operands, scratch=(), us=1):
+    out_specs = jax.tree.map(lambda _: VMEM, out_shape)
+    return pl.pallas_call(
+        kernel,
+        out_shape=out_shape,
+        in_specs=[SMEM] + [VMEM] * (len(operands) - 1),
+        out_specs=out_specs,
+        scratch_shapes=list(scratch),
+        compiler_params=PARAMS,
+        cost_estimate=cost(us),
+    )(*operands)
+
+
+def hop(value, *pairs):
+    return lax.ppermute(value, "row", pairs)
+
+
+def gate(*values):
+    return lax.optimization_barrier(values)
+
+
+def swap_pieces(pieces, n_col):
+    return [pieces[0]] + [flip(pieces[f], "col", n_col, f) for f in range(1, n_col)]
+
+
+def fast(shape, right_side, earlier_panel, earlier_solution, window_panel, diag_inverse):
+    n_row, n_col = shape
+    step_count = diag_inverse.shape[0]
+    row, col = lax.axis_index("row"), lax.axis_index("col")
+    index = flat_index(row, col)
+    strip, nrhs = right_side.shape
+    rows = earlier_panel.shape[0]
+    chunk = nrhs // n_col
+
+    block = earlier_solution[0]
+    own = jnp.stack([jnp.where(row == j, diag_inverse[j], window_panel[:, j, :]) for j in range(step_count)])
+    over = flip(own, "col", n_col, 2)
+    b4 = flip(block, "row", n_row, 4)
+    b2 = flip(block, "row", n_row, 2)
+    b1 = flip(block, "row", n_row, 1)
+    b1, b2, again, panel = gate(b1, b2, block, earlier_panel)
+    b6 = flip(again, "row", n_row, 6)
+    b3 = flip(b2, "row", n_row, 1)
+    panel = order_panel(index, panel)
+    b3, b4, panel = gate(b3, b4, panel)
+    b5 = flip(b4, "row", n_row, 1)
+    b7 = flip(b6, "row", n_row, 1)
+    total = bulk(index, panel, right_side, [block, b1, b2, b3, b4, b5, b6])
+    total, b7 = gate(total, b7)
+    part = (n_col // 2, rows, chunk)
+    split = functools.partial(split_kernel, n_col)
+    kept, sent = local(split, (shape_of(part, F32), shape_of(part, BF16)), [index, panel, b7, total], [pltpu.VMEM((strip, nrhs), F32)])
+    moved = flip(sent, "col", n_col, 1)
+    moved, over = gate(moved, over)
+    kept, sent = reduce_step(2, flat_index(col), kept, moved)
+    moved = flip(sent, "col", n_col, 2)
+    slots = [own, flip(own, "col", n_col, 1), over, flip(over, "col", n_col, 1)]
+
+    wide, narrow = shape_of((rows, chunk), F32), shape_of((rows, chunk), BF16)
+    current, own0 = local(functools.partial(start_kernel, n_col), (wide, narrow), [index, kept, moved] + slots)
+    at1, at2 = hop(own0, (0, 1)), hop(own0, (0, 2))
+    step = functools.partial(first_step_kernel, n_col)
+    current, own1 = local(step, (wide, narrow), [index, current, own0, at1] + slots)
+    first, second = hop(own1, (1, 2), (0, 4)), hop(own1, (1, 3), (0, 6))
+    current = local(functools.partial(between_kernel, n_col), wide, [index, current, at2] + slots, us=8)
+    step = functools.partial(second_step_kernel, n_col)
+    current, own2, line0 = local(step, (wide, narrow, narrow), [index, current, own0, first, second] + slots)
+    z6 = hop(own2, (2, 6), (3, 5))
+    z4 = hop(own2, (2, 4), (3, 7))
+    z0 = hop(own2, (2, 0), (0, 3))
+    across0 = hop(line0, (4, 5), (6, 7))
+    line = local(line_kernel, narrow, [index, own1, own2, z6, z4, z0])
+    across = flip(line, "row", n_row, 1)
+    pieces = shape_of((n_col, 2, strip, chunk), BF16)
+    middle = functools.partial(middle_kernel, n_col)
+    parts = [own0, at1, at2, z0, line0, across0, line]
+    scratch = [pltpu.VMEM((rows, chunk), BF16), pltpu.VMEM((rows, chunk), F32)]
+    current, middle = local(middle, (wide, pieces), [index, current] + parts + slots, scratch, us=8)
+    middle = swap_pieces(middle, n_col)
+    across, *middle = gate(across, *middle)
+    finish = functools.partial(finish_kernel, n_col)
+    late = local(finish, pieces, [index, current, across] + slots, [pltpu.VMEM((rows, chunk), F32)])
+    late = swap_pieces(late, n_col)
+    outs = (shape_of((step_count, strip, nrhs), BF16), shape_of((strip, nrhs), F32))
+    return local(functools.partial(assemble_kernel, n_col), outs, [index] + middle + late)
+
+
 def solution(mesh):
     shape = (mesh.shape["row"], mesh.shape["col"])
 
     def step(*args):
-        return on_device(shape, *args)
+        chunk = args[0].shape[1] // shape[1]
+        plan = fast if shape == (8, 4) and chunk % 128 == 0 and args[4].shape[0] == 3 else on_device
+        return plan(shape, *args)
 
     return jax.shard_map(
         step,

time: 239 us -> 115 us (0.48)
  local copies, waits for them, and re-layouts: 66.3 us -> 2.98 us
  matrix products: 29.5 us -> 0 us
  other arithmetic: 19.2 us -> 2.25 us
  Pallas kernels: 0 us -> 16.8 us
  waiting for transfers between devices: 76.3 us -> 60.8 us
  starting transfers between devices: 44.7 us -> 31.1 us
    another operation x4 -> x0, local copies, waits for them, and re-layouts: 41.4 us -> none
    dot_general x20 -> x0, matrix products: 29.5 us -> none  [matmul(): return jnp.dot(left, right, preferred_element_type=F32)]
    pallas_call x0 -> x12, Pallas kernels: none -> 16.8 us  [the longest x10 13.6 us: local(): pl.pallas_call(kernel, out_shape=out_shape, in_specs=[SMEM] + [VMEM] * (l...]
    ppermute x15 -> x8, waiting for transfers between devices: 39 us -> 22.8 us  [hop(): return lax.ppermute(value, 'row', pairs)]
    ppermute x18 -> x19, waiting for transfers between devices: 25 us -> 38 us  [flip(): return lax.ppermute(value, axis, [(i, i ^ bit) for i in range(size)])]
    all_to_all x2 -> x0, waiting for transfers between devices: 12.3 us -> none  [the longest x1 6.32 us: on_device(): lax.all_to_all(jnp.stack([solved[-1], current.astype(BF16)]), 'col', 1, 2...]
    ppermute x15 -> x8, starting transfers between devices: 19.1 us -> 7.28 us  [hop(): return lax.ppermute(value, 'row', pairs)]
    all_to_all x2 -> x0, starting transfers between devices: 9.99 us -> none  [the longest x1 5.68 us: on_device(): early = lax.all_to_all(jnp.stack(solved[:-1]), 'col', 1, 2, tiled=True)]
  transfers between devices with their start and end apart: 35 -> 27, of which waited for: 13 -> 15; matrix products, arithmetic and copies ran while one was open for 43% -> 0% of each run, Pallas kernels for 0% -> 11%
where the time goes in v4:
time: 115 us
  waiting for transfers between devices  60.8 us (53%)
  starting transfers between devices  31.1 us (27%)
  Pallas kernels  16.8 us (15%)
  local copies, waits for them, and re-layouts  2.98 us (3%)
  other arithmetic  2.25 us (2%)
    ppermute x19, waiting for transfers between devices, flip(): return lax.ppermute(value, axis, [(i, i ^ bit) for i in range(size)])  38 us
    ppermute x19, starting transfers between devices, flip(): return lax.ppermute(value, axis, [(i, i ^ bit) for i in range(size)])  23.8 us
    ppermute x8, waiting for transfers between devices, hop(): return lax.ppermute(value, 'row', pairs)  22.8 us
    pallas_call x10, Pallas kernels, local(): pl.pallas_call(kernel, out_shape=out_shape, in_specs=[SMEM] + [VMEM] * (l...  13.6 us
    ppermute x8, starting transfers between devices, hop(): return lax.ppermute(value, 'row', pairs)  7.28 us
    pallas_call x1, Pallas kernels, order_panel(): pl.pallas_call(order_kernel, out_shape=shape_of((rows, sources * width),...  3.08 us
    unnamed x10, local copies, waits for them, and re-layouts  2.9 us
  transfers between devices with their start and end apart: 27, of which 15 were waited for; matrix products, arithmetic and copies ran while one was open for 0% of the time, Pallas kernels for 11%

profile of v4, /device:TPU:25, one launch (start us, length us, event | category | flops | bytes accessed | tf_op | source)
XLA Modules:
  0.0 114.8 jit_solution(13361101113339185302)
XLA Ops:
  0.6 2.0 %bitcast_select_fusion.2 = (bf16[1,256,1024]{2,1,0:T(8,128)(2,1)S(1)}, bf16[1,256,1024]{2,1,0:T(8,128)(2,1)S(1)}, bf16[1,256,1024]{2,1,0:T(8,128)(2,1)S(1)}) fusion(bf16[256,3,1024]{2,0,1:T(8,128)(2,1)} %param.8, bf16[3,256,1024]{2,1,0:T(8,128)(2,1)} %param.9, pred[]{:T(512)S(6)} %eq.9, pred[]{:T(512)S(6)} %eq.11, pred[]{:T(512)S(6)} %eq.10), kind=kLoop, calls=%fused_computation.3 | loop fusion | flops 786432 | bytes 4718595 | tf_op jit(solution)/shard_map/jit(_where)/select_n | solution.py:396
  2.6 0.0 copy-start.2
  2.7 0.2 pad_maximum_fusion.refs_0_
  2.8 1.3 %collective-permute-start.8 = (bf16[3,256,1024]{2,1,0:T(8,128)(2,1)S(1)}, bf16[3,256,1024]{2,1,0:T(8,128)(2,1)S(1)}, u32[]{:S(2)}, u32[]{:S(2)}) collective-permute-start(bf16[3,256,1024]{2,1,0:T(8,128)(2,1)S(1)} %pad_maximum_fusion.refs_0_), channel_id=1, source_target_pairs={{0,2},{1,3},{2,0},{3,1},{4,6},{5,7},{6,4},{7,5},{8,10},{9,11},{10,... | collective-permute-start | bytes 4718600 | tf_op jit(solution)/shard_map/ppermute | solution.py:15
  4.1 1.2 %collective-permute-start = (bf16[256,512]{1,0:T(8,128)(2,1)S(1)}, bf16[256,512]{1,0:T(8,128)(2,1)S(1)}, u32[]{:S(2)}, u32[]{:S(2)}) collective-permute-start(bf16[256,512]{1,0:T(8,128)(2,1)S(1)} %bitcast.25), channel_id=1, source_target_pairs={{0,4},{4,0},{8,12},{12,8},{16,20},{20,16},{24,28},{28,24},{1,5},{5... | collective-permute-start | bytes 786440 | tf_op jit(solution)/shard_map/ppermute | solution.py:15
  5.4 0.2 collective-permute-start.1
  5.5 0.1 collective-permute-start.3
  5.6 5.4 %collective-permute-done.refs_1_ = bf16[256,512]{1,0:T(8,128)(2,1)S(1)} collective-permute-done((bf16[256,512]{1,0:T(8,128)(2,1)S(1)}, bf16[256,512]{1,0:T(8,128)(2,1)S(1)}, u32[]{:S(2)}, u32[]{:S(2)}) %collective-permute-start) | collective-permute-done | bytes 262176 | tf_op jit(solution)/shard_map/ppermute | solution.py:15
  11.0 0.7 copy-done.3
  11.7 5.3 %collective-permute-done.1.refs_2_ = bf16[256,512]{1,0:T(8,128)(2,1)} collective-permute-done((bf16[256,512]{1,0:T(8,128)(2,1)S(1)}, bf16[256,512]{1,0:T(8,128)(2,1)}, u32[]{:S(2)}, u32[]{:S(2)}) %collective-permute-start.1) | collective-permute-done | bytes 262176 | tf_op jit(solution)/shard_map/ppermute | solution.py:15
  16.9 0.2 collective-permute-start.2
  17.2 0.3 collective-permute-start.5
  17.4 0.1 pad_add_fusion.index_ref
  17.5 2.2 %copy-done = bf16[1024,8,256]{2,1,0:T(8,128)(2,1)S(1)} copy-done((bf16[1024,8,256]{2,1,0:T(8,128)(2,1)S(1)}, bf16[1024,8,256]{2,1,0:T(8,128)(2,1)}, u32[]{:S(2)}) %copy-start) | copy-done | bytes 4194328
  19.7 3.1 %shard_map.68.panel_ref = bf16[1024,2048]{1,0:T(8,128)(2,1)S(1)} custom-call(s32[2]{0:T(128)S(1)} %pad_add_fusion.index_ref, bf16[1024,8,256]{2,1,0:T(8,128)(2,1)S(1)} %copy-done), custom_call_target="tpu_custom_call" | custom-call | bytes 28800000 | tf_op jit(solution)/shard_map/pallas_call | solution.py:154
  22.8 0.6 collective-permute-done.2.refs_3_
  23.4 0.7 collective-permute-start.4
  24.1 0.9 collective-permute-done.5.refs_6_
  25.0 1.2 %collective-permute-start.6 = (bf16[256,512]{1,0:T(8,128)(2,1)}, bf16[256,512]{1,0:T(8,128)(2,1)S(1)}, u32[]{:S(2)}, u32[]{:S(2)}) collective-permute-start(bf16[256,512]{1,0:T(8,128)(2,1)} %collective-permute-done.5.refs_6_), channel_id=1, source_target_pairs={{0,4},{4,0},{8,12},{12,8},{16,20},{20,16},{24,28},{28,24},{1,5},{5... | collective-permute-start | bytes 786440 | tf_op jit(solution)/shard_map/ppermute | solution.py:15
  26.3 2.9 %collective-permute-done.4.refs_5_ = bf16[256,512]{1,0:T(8,128)(2,1)S(1)} collective-permute-done((bf16[256,512]{1,0:T(8,128)(2,1)}, bf16[256,512]{1,0:T(8,128)(2,1)S(1)}, u32[]{:S(2)}, u32[]{:S(2)}) %collective-permute-start.4) | collective-permute-done | bytes 262176 | tf_op jit(solution)/shard_map/ppermute | solution.py:15
  29.2 3.4 %shard_map.69.total_ref = f32[1024,512]{1,0:T(8,128)S(1)} custom-call(s32[2]{0:T(128)S(1)} %pad_add_fusion.index_ref, bf16[1024,2048]{1,0:T(8,128)(2,1)S(1)} %shard_map.68.panel_ref, f32[256,512]{1,0:T(8,128)S(1)} %copy-done.1, bf16[256,512]{1,0:T(8,128)(2,1)S(1)} %bitcast.29, bf16[256,512]{1,0:T(8,128)(2,1)S(1)} %copy-done.4, ...), custom_call_target="tpu_custom_call" | custom-call | bytes 28800000 | tf_op jit(solution)/shard_map/pallas_call | solution.py:363
  32.5 2.0 %collective-permute-done.6.block_ref = bf16[256,512]{1,0:T(8,128)(2,1)S(1)} collective-permute-done((bf16[256,512]{1,0:T(8,128)(2,1)}, bf16[256,512]{1,0:T(8,128)(2,1)S(1)}, u32[]{:S(2)}, u32[]{:S(2)}) %collective-permute-start.6) | collective-permute-done | bytes 262176 | tf_op jit(solution)/shard_map/ppermute | solution.py:15
  34.5 1.7 %shard_map.70 = (f32[2,1024,128]{2,1,0:T(8,128)S(1)}, bf16[2,1024,128]{2,1,0:T(8,128)(2,1)S(1)}) custom-call(s32[2]{0:T(128)S(1)} %pad_add_fusion.index_ref, bf16[1024,2048]{1,0:T(8,128)(2,1)S(1)} %shard_map.68.panel_ref, bf16[256,512]{1,0:T(8,128)(2,1)S(1)} %collective-permute-done.6.block_ref, f32[1024,512]{1,0:T(8,128)S(1)} %shard_map.69.total_ref), custom_call_target="tpu_custom_call" | custom-call | bytes 3600000 | tf_op jit(solution)/shard_map/pallas_call | solution.py:363
  36.2 4.1 %collective-permute-start.7 = (bf16[2,1024,128]{2,1,0:T(8,128)(2,1)S(1)}, bf16[2,1024,128]{2,1,0:T(8,128)(2,1)S(1)}, u32[]{:S(2)}, u32[]{:S(2)}) collective-permute-start(bf16[2,1024,128]{2,1,0:T(8,128)(2,1)S(1)} %get-tuple-element.41), channel_id=1, source_target_pairs={{0,1},{1,0},{2,3},{3,2},{4,5},{5,4},{6,7},{7,6},{8,9},{9,8},{10,11... | collective-permute-start | bytes 1572872 | tf_op jit(solution)/shard_map/ppermute | solution.py:15
  40.4 0.1 collective-permute-start.10
  40.4 1.5 %collective-permute-done.7.moved_ref = bf16[2,1024,128]{2,1,0:T(8,128)(2,1)S(1)} collective-permute-done((bf16[2,1024,128]{2,1,0:T(8,128)(2,1)S(1)}, bf16[2,1024,128]{2,1,0:T(8,128)(2,1)S(1)}, u32[]{:S(2)}, u32[]{:S(2)}) %collective-permute-start.7) | collective-permute-done | bytes 524320 | tf_op jit(solution)/shard_map/ppermute | solution.py:15
  41.9 0.0 collective-permute-done.8.refs_2_
  41.9 0.4 collective-permute-start.11
  42.3 0.1 shard_map.71
  42.4 0.8 collective-permute-start.9
  43.2 1.0 collective-permute-done.10.refs_1_
  44.2 6.1 %collective-permute-done.9.moved_ref = bf16[1,1024,128]{2,1,0:T(8,128)(2,1)S(1)} collective-permute-done((bf16[1,1024,128]{2,1,0:T(8,128)(2,1)S(1)}, bf16[1,1024,128]{2,1,0:T(8,128)(2,1)S(1)}, u32[]{:S(2)}, u32[]{:S(2)}) %collective-permute-start.9) | collective-permute-done | bytes 262176 | tf_op jit(solution)/shard_map/ppermute | solution.py:15
  50.2 0.0 collective-permute-done.11.refs_3_
  50.2 0.6 shard_map.72
  50.8 0.7 collective-permute-start.12
  51.5 0.7 collective-permute-start.13
  52.2 0.7 shard_map.73
  52.9 0.7 collective-permute-start.14
  53.6 1.3 %collective-permute-start.15 = (bf16[1024,128]{1,0:T(8,128)(2,1)S(1)}, bf16[1024,128]{1,0:T(8,128)(2,1)S(1)}, u32[]{:S(2)}, u32[]{:S(2)}) collective-permute-start(bf16[1024,128]{1,0:T(8,128)(2,1)S(1)} %get-tuple-element.48.own1_ref), channel_id=1, source_target_pairs={{4,12},{0,24},{5,13},{1,25},{6,14},{2,26},{7,15},{3,27}} | collective-permute-start | bytes 786440 | tf_op jit(solution)/shard_map/ppermute | solution.py:375
  54.9 0.0 collective-permute-done.13.value_ref.at2_ref
  54.9 0.6 shard_map.74.current_ref
  55.5 0.0 collective-permute-done.14.first_ref
  55.5 18.4 %collective-permute-done.15.second_ref = bf16[1024,128]{1,0:T(8,128)(2,1)S(1)} collective-permute-done((bf16[1024,128]{1,0:T(8,128)(2,1)S(1)}, bf16[1024,128]{1,0:T(8,128)(2,1)S(1)}, u32[]{:S(2)}, u32[]{:S(2)}) %collective-permute-start.15) | collective-permute-done | bytes 262176 | tf_op jit(solution)/shard_map/ppermute | solution.py:375
  73.9 0.7 shard_map.75
  74.6 1.3 %collective-permute-start.16 = (bf16[1024,128]{1,0:T(8,128)(2,1)S(1)}, bf16[1024,128]{1,0:T(8,128)(2,1)S(1)}, u32[]{:S(2)}, u32[]{:S(2)}) collective-permute-start(bf16[1024,128]{1,0:T(8,128)(2,1)S(1)} %get-tuple-element.50.own2_ref), channel_id=1, source_target_pairs={{8,24},{12,20},{9,25},{13,21},{10,26},{14,22},{11,27},{15,23}} | collective-permute-start | bytes 786440 | tf_op jit(solution)/shard_map/ppermute | solution.py:375
  75.9 0.7 collective-permute-start.17
  76.6 0.7 collective-permute-start.18
  77.3 1.3 %collective-permute-start.20 = (bf16[1024,128]{1,0:T(8,128)(2,1)S(1)}, bf16[1024,128]{1,0:T(8,128)(2,1)S(1)}, u32[]{:S(2)}, u32[]{:S(2)}) collective-permute-start(bf16[1024,128]{1,0:T(8,128)(2,1)S(1)} %get-tuple-element.52.line0_ref), channel_id=1, source_target_pairs={{16,20},{24,28},{17,21},{25,29},{18,22},{26,30},{19,23},{27,31}} | collective-permute-start | bytes 786440 | tf_op jit(solution)/shard_map/ppermute | solution.py:375
  78.6 4.4 %collective-permute-done.16.z6_ref = bf16[1024,128]{1,0:T(8,128)(2,1)S(1)} collective-permute-done((bf16[1024,128]{1,0:T(8,128)(2,1)S(1)}, bf16[1024,128]{1,0:T(8,128)(2,1)S(1)}, u32[]{:S(2)}, u32[]{:S(2)}) %collective-permute-start.16) | collective-permute-done | bytes 262176 | tf_op jit(solution)/shard_map/ppermute | solution.py:375
  83.0 0.6 shard_map.76.line_ref
  83.6 5.8 %collective-permute-start.19 = (bf16[1024,128]{1,0:T(8,128)(2,1)S(1)}, bf16[1024,128]{1,0:T(8,128)(2,1)S(1)}, u32[]{:S(2)}, u32[]{:S(2)}) collective-permute-start(bf16[1024,128]{1,0:T(8,128)(2,1)S(1)} %shard_map.76.line_ref), channel_id=1, source_target_pairs={{0,4},{4,0},{8,12},{12,8},{16,20},{20,16},{24,28},{28,24},{1,5},{5... | collective-permute-start | bytes 786440 | tf_op jit(solution)/shard_map/ppermute | solution.py:15
  89.5 2.3 %shard_map.77 = (f32[1024,128]{1,0:T(8,128)S(1)}, bf16[4,2,256,128]{3,2,1,0:T(8,128)(2,1)S(1)}) custom-call(s32[2]{0:T(128)S(1)} %pad_add_fusion.index_ref, f32[1024,128]{1,0:T(8,128)S(1)} %get-tuple-element.51.current_ref, bf16[1024,128]{1,0:T(8,128)(2,1)S(1)} %get-tuple-element.47.own_ref.own0_ref, ...), custom_call_target="tpu_custom_call" | custom-call | bytes 28800000 | tf_op jit(solution)/shard_map/pallas_call | solution.py:363
  91.8 3.5 %collective-permute-start.21 = (bf16[2,256,128]{2,1,0:T(8,128)(2,1)S(1)}, bf16[2,256,128]{2,1,0:T(8,128)(2,1)S(1)}, u32[]{:S(2)}, u32[]{:S(2)}) collective-permute-start(bf16[2,256,128]{2,1,0:T(8,128)(2,1)S(1)} %get-tuple-element.69), channel_id=1, source_target_pairs={{0,1},{1,0},{2,3},{3,2},{4,5},{5,4},{6,7},{7,6},{8,9},{9,8},{10,11... | collective-permute-start | bytes 393224 | tf_op jit(solution)/shard_map/ppermute | solution.py:15
  95.3 0.7 collective-permute-start.22
  96.0 1.0 collective-permute-start.23
  97.0 3.4 %collective-permute-done.22.refs_2_ = bf16[2,256,128]{2,1,0:T(8,128)(2,1)S(1)} collective-permute-done((bf16[2,256,128]{2,1,0:T(8,128)(2,1)S(1)}, bf16[2,256,128]{2,1,0:T(8,128)(2,1)S(1)}, u32[]{:S(2)}, u32[]{:S(2)}) %collective-permute-start.22) | collective-permute-done | bytes 131104 | tf_op jit(solution)/shard_map/ppermute | solution.py:15
  100.4 3.0 %collective-permute-done.23.refs_3_ = bf16[2,256,128]{2,1,0:T(8,128)(2,1)S(1)} collective-permute-done((bf16[2,256,128]{2,1,0:T(8,128)(2,1)S(1)}, bf16[2,256,128]{2,1,0:T(8,128)(2,1)S(1)}, u32[]{:S(2)}, u32[]{:S(2)}) %collective-permute-start.23) | collective-permute-done | bytes 131104 | tf_op jit(solution)/shard_map/ppermute | solution.py:15
  103.3 1.3 %shard_map.78 = bf16[4,2,256,128]{3,2,1,0:T(8,128)(2,1)S(1)} custom-call(s32[2]{0:T(128)S(1)} %pad_add_fusion.index_ref, f32[1024,128]{1,0:T(8,128)S(1)} %get-tuple-element.58.current_ref, bf16[1024,128]{1,0:T(8,128)(2,1)S(1)} %collective-permute-done.19.value_ref, bf16[3,256,1024]{2,1,0:T(8,128)(2,1)S(1)} %pad_maximum_fusion.refs_0_, ...), custom_call_target="tpu_custom_call" | custom-call | bytes 3600000 | tf_op jit(solution)/shard_map/pallas_call | solution.py:363
  104.7 0.3 collective-permute-start.24
  105.0 0.7 collective-permute-start.25
  105.7 1.2 %collective-permute-start.26 = (bf16[2,256,128]{2,1,0:T(8,128)(2,1)S(1)}, bf16[2,256,128]{2,1,0:T(8,128)(2,1)S(1)}, u32[]{:S(2)}, u32[]{:S(2)}) collective-permute-start(bf16[2,256,128]{2,1,0:T(8,128)(2,1)S(1)} %get-tuple-element.63), channel_id=1, source_target_pairs={{0,3},{1,2},{2,1},{3,0},{4,7},{5,6},{6,5},{7,4},{8,11},{9,10},{10,... | collective-permute-start | bytes 393224 | tf_op jit(solution)/shard_map/ppermute | solution.py:15
  106.9 2.9 %collective-permute-done.25.refs_6_ = bf16[2,256,128]{2,1,0:T(8,128)(2,1)S(1)} collective-permute-done((bf16[2,256,128]{2,1,0:T(8,128)(2,1)S(1)}, bf16[2,256,128]{2,1,0:T(8,128)(2,1)S(1)}, u32[]{:S(2)}, u32[]{:S(2)}) %collective-permute-start.25) | collective-permute-done | bytes 131104 | tf_op jit(solution)/shard_map/ppermute | solution.py:15
  109.8 3.2 %collective-permute-done.26.refs_7_ = bf16[2,256,128]{2,1,0:T(8,128)(2,1)S(1)} collective-permute-done((bf16[2,256,128]{2,1,0:T(8,128)(2,1)S(1)}, bf16[2,256,128]{2,1,0:T(8,128)(2,1)S(1)}, u32[]{:S(2)}, u32[]{:S(2)}) %collective-permute-start.26) | collective-permute-done | bytes 131104 | tf_op jit(solution)/shard_map/ppermute | solution.py:15
  113.1 1.8 %shard_map.79 = (bf16[3,256,512]{2,1,0:T(8,128)(2,1)}, f32[256,512]{1,0:T(8,128)}) custom-call(s32[2]{0:T(128)S(1)} %pad_add_fusion.index_ref, bf16[2,256,128]{2,1,0:T(8,128)(2,1)S(1)} %get-tuple-element.54.refs_0_, bf16[2,256,128]{2,1,0:T(8,128)(2,1)S(1)} %collective-permute-done.21.refs_1_, bf16[2,256,128]{2,1,0:T(8,128)(2,1)S(1)} %collective-permute-done.22.refs_2_, ...), custom_call_target="tpu_custom_call" | custom-call | bytes 3600000 | tf_op jit(solution)/shard_map/pallas_call | solution.py:363
  (17 shorter events, 0.1 us)
Async XLA Ops:
  2.6 1.5 %copy-start.2 = (bf16[1,256,512]{2,1,0:T(8,128)(2,1)S(1)}, bf16[1,256,512]{2,1,0:T(8,128)(2,1)}, u32[]{:S(2)}) copy-start(bf16[1,256,512]{2,1,0:T(8,128)(2,1)} %param.7) | copy-start | bytes 786436
  2.8 39.1 %collective-permute-start.8 = (bf16[3,256,1024]{2,1,0:T(8,128)(2,1)S(1)}, bf16[3,256,1024]{2,1,0:T(8,128)(2,1)S(1)}, u32[]{:S(2)}, u32[]{:S(2)}) collective-permute-start(bf16[3,256,1024]{2,1,0:T(8,128)(2,1)S(1)} %pad_maximum_fusion.refs_0_), channel_id=1, source_target_pairs={{0,2},{1,3},{2,0},{3,1},{4,6},{5,7},{6,4},{7,5},{8,10},{9,11},{10,... | collective-permute-start | bytes 4718600 | tf_op jit(solution)/shard_map/ppermute | solution.py:15
  4.1 6.9 %collective-permute-start = (bf16[256,512]{1,0:T(8,128)(2,1)S(1)}, bf16[256,512]{1,0:T(8,128)(2,1)S(1)}, u32[]{:S(2)}, u32[]{:S(2)}) collective-permute-start(bf16[256,512]{1,0:T(8,128)(2,1)S(1)} %bitcast.25), channel_id=1, source_target_pairs={{0,4},{4,0},{8,12},{12,8},{16,20},{20,16},{24,28},{28,24},{1,5},{5... | collective-permute-start | bytes 786440 | tf_op jit(solution)/shard_map/ppermute | solution.py:15
  5.4 11.6 %collective-permute-start.1 = (bf16[256,512]{1,0:T(8,128)(2,1)S(1)}, bf16[256,512]{1,0:T(8,128)(2,1)}, u32[]{:S(2)}, u32[]{:S(2)}) collective-permute-start(bf16[256,512]{1,0:T(8,128)(2,1)S(1)} %bitcast.26), channel_id=1, source_target_pairs={{0,8},{4,12},{8,0},{12,4},{16,24},{20,28},{24,16},{28,20},{1,9},{5... | collective-permute-start | bytes 786440 | tf_op jit(solution)/shard_map/ppermute | solution.py:15
  5.5 17.3 %collective-permute-start.3 = (bf16[256,512]{1,0:T(8,128)(2,1)S(1)}, bf16[256,512]{1,0:T(8,128)(2,1)}, u32[]{:S(2)}, u32[]{:S(2)}) collective-permute-start(bf16[256,512]{1,0:T(8,128)(2,1)S(1)} %bitcast.27), channel_id=1, source_target_pairs={{0,16},{4,20},{8,24},{12,28},{16,0},{20,4},{24,8},{28,12},{1,17},{... | collective-permute-start | bytes 786440 | tf_op jit(solution)/shard_map/ppermute | solution.py:15
  11.0 0.7 copy-start.3
  16.9 6.5 %collective-permute-start.2 = (bf16[256,512]{1,0:T(8,128)(2,1)}, bf16[256,512]{1,0:T(8,128)(2,1)}, u32[]{:S(2)}, u32[]{:S(2)}) collective-permute-start(bf16[256,512]{1,0:T(8,128)(2,1)} %collective-permute-done.1.refs_2_), channel_id=1, source_target_pairs={{0,4},{4,0},{8,12},{12,8},{16,20},{20,16},{24,28},{28,24},{1,5},{5... | collective-permute-start | bytes 786440 | tf_op jit(solution)/shard_map/ppermute | solution.py:15
  17.2 7.9 %collective-permute-start.5 = (bf16[256,512]{1,0:T(8,128)(2,1)S(1)}, bf16[256,512]{1,0:T(8,128)(2,1)}, u32[]{:S(2)}, u32[]{:S(2)}) collective-permute-start(bf16[256,512]{1,0:T(8,128)(2,1)S(1)} %bitcast.28), channel_id=1, source_target_pairs={{0,24},{4,28},{8,16},{12,20},{16,8},{20,12},{24,0},{28,4},{1,25},{... | collective-permute-start | bytes 786440 | tf_op jit(solution)/shard_map/ppermute | solution.py:15
  17.5 2.2 %copy-start = (bf16[1024,8,256]{2,1,0:T(8,128)(2,1)S(1)}, bf16[1024,8,256]{2,1,0:T(8,128)(2,1)}, u32[]{:S(2)}) copy-start(bf16[1024,8,256]{2,1,0:T(8,128)(2,1)} %panel_ref) | copy-start | bytes 12582916
  19.7 9.4 %copy-start.1 = (f32[256,512]{1,0:T(8,128)S(1)}, f32[256,512]{1,0:T(8,128)}, u32[]{:S(2)}) copy-start(f32[256,512]{1,0:T(8,128)} %side_ref.1) | copy-start | bytes 1572868
  19.7 9.4 %copy-start.4 = (bf16[256,512]{1,0:T(8,128)(2,1)S(1)}, bf16[256,512]{1,0:T(8,128)(2,1)}, u32[]{:S(2)}) copy-start(bf16[256,512]{1,0:T(8,128)(2,1)} %copy-done.3) | copy-start | bytes 786436
  23.4 5.7 %collective-permute-start.4 = (bf16[256,512]{1,0:T(8,128)(2,1)}, bf16[256,512]{1,0:T(8,128)(2,1)S(1)}, u32[]{:S(2)}, u32[]{:S(2)}) collective-permute-start(bf16[256,512]{1,0:T(8,128)(2,1)} %collective-permute-done.3.refs_4_), channel_id=1, source_target_pairs={{0,4},{4,0},{8,12},{12,8},{16,20},{20,16},{24,28},{28,24},{1,5},{5... | collective-permute-start | bytes 786440 | tf_op jit(solution)/shard_map/ppermute | solution.py:15
  25.0 9.5 %collective-permute-start.6 = (bf16[256,512]{1,0:T(8,128)(2,1)}, bf16[256,512]{1,0:T(8,128)(2,1)S(1)}, u32[]{:S(2)}, u32[]{:S(2)}) collective-permute-start(bf16[256,512]{1,0:T(8,128)(2,1)} %collective-permute-done.5.refs_6_), channel_id=1, source_target_pairs={{0,4},{4,0},{8,12},{12,8},{16,20},{20,16},{24,28},{28,24},{1,5},{5... | collective-permute-start | bytes 786440 | tf_op jit(solution)/shard_map/ppermute | solution.py:15
  36.2 5.7 %collective-permute-start.7 = (bf16[2,1024,128]{2,1,0:T(8,128)(2,1)S(1)}, bf16[2,1024,128]{2,1,0:T(8,128)(2,1)S(1)}, u32[]{:S(2)}, u32[]{:S(2)}) collective-permute-start(bf16[2,1024,128]{2,1,0:T(8,128)(2,1)S(1)} %get-tuple-element.41), channel_id=1, source_target_pairs={{0,1},{1,0},{2,3},{3,2},{4,5},{5,4},{6,7},{7,6},{8,9},{9,8},{10,11... | collective-permute-start | bytes 1572872 | tf_op jit(solution)/shard_map/ppermute | solution.py:15
  40.4 3.8 %collective-permute-start.10 = (bf16[3,256,1024]{2,1,0:T(8,128)(2,1)S(1)}, bf16[3,256,1024]{2,1,0:T(8,128)(2,1)S(1)}, u32[]{:S(2)}, u32[]{:S(2)}) collective-permute-start(bf16[3,256,1024]{2,1,0:T(8,128)(2,1)S(1)} %pad_maximum_fusion.refs_0_), channel_id=1, source_target_pairs={{0,1},{1,0},{2,3},{3,2},{4,5},{5,4},{6,7},{7,6},{8,9},{9,8},{10,11... | collective-permute-start | bytes 4718600 | tf_op jit(solution)/shard_map/ppermute | solution.py:15
  41.9 8.3 %collective-permute-start.11 = (bf16[3,256,1024]{2,1,0:T(8,128)(2,1)S(1)}, bf16[3,256,1024]{2,1,0:T(8,128)(2,1)S(1)}, u32[]{:S(2)}, u32[]{:S(2)}) collective-permute-start(bf16[3,256,1024]{2,1,0:T(8,128)(2,1)S(1)} %collective-permute-done.8.refs_2_), channel_id=1, source_target_pairs={{0,1},{1,0},{2,3},{3,2},{4,5},{5,4},{6,7},{7,6},{8,9},{9,8},{10,11... | collective-permute-start | bytes 4718600 | tf_op jit(solution)/shard_map/ppermute | solution.py:15
  42.4 7.8 %collective-permute-start.9 = (bf16[1,1024,128]{2,1,0:T(8,128)(2,1)S(1)}, bf16[1,1024,128]{2,1,0:T(8,128)(2,1)S(1)}, u32[]{:S(2)}, u32[]{:S(2)}) collective-permute-start(bf16[1,1024,128]{2,1,0:T(8,128)(2,1)S(1)} %get-tuple-element.44), channel_id=1, source_target_pairs={{0,2},{1,3},{2,0},{3,1},{4,6},{5,7},{6,4},{7,5},{8,10},{9,11},{10,... | collective-permute-start | bytes 786440 | tf_op jit(solution)/shard_map/ppermute | solution.py:15
  50.8 1.4 %collective-permute-start.12 = (bf16[1024,128]{1,0:T(8,128)(2,1)S(1)}, bf16[1024,128]{1,0:T(8,128)(2,1)S(1)}, u32[]{:S(2)}, u32[]{:S(2)}) collective-permute-start(bf16[1024,128]{1,0:T(8,128)(2,1)S(1)} %get-tuple-element.47.own_ref.own0_ref), channel_id=1, source_target_pairs={{0,4},{1,5},{2,6},{3,7}} | collective-permute-start | bytes 786440 | tf_op jit(solution)/shard_map/ppermute | solution.py:375
  51.5 3.4 %collective-permute-start.13 = (bf16[1024,128]{1,0:T(8,128)(2,1)S(1)}, bf16[1024,128]{1,0:T(8,128)(2,1)S(1)}, u32[]{:S(2)}, u32[]{:S(2)}) collective-permute-start(bf16[1024,128]{1,0:T(8,128)(2,1)S(1)} %get-tuple-element.47.own_ref.own0_ref), channel_id=1, source_target_pairs={{0,8},{1,9},{2,10},{3,11}} | collective-permute-start | bytes 786440 | tf_op jit(solution)/shard_map/ppermute | solution.py:375
  52.9 2.6 %collective-permute-start.14 = (bf16[1024,128]{1,0:T(8,128)(2,1)S(1)}, bf16[1024,128]{1,0:T(8,128)(2,1)S(1)}, u32[]{:S(2)}, u32[]{:S(2)}) collective-permute-start(bf16[1024,128]{1,0:T(8,128)(2,1)S(1)} %get-tuple-element.48.own1_ref), channel_id=1, source_target_pairs={{4,8},{0,16},{5,9},{1,17},{6,10},{2,18},{7,11},{3,19}} | collective-permute-start | bytes 786440 | tf_op jit(solution)/shard_map/ppermute | solution.py:375
  53.6 20.3 %collective-permute-start.15 = (bf16[1024,128]{1,0:T(8,128)(2,1)S(1)}, bf16[1024,128]{1,0:T(8,128)(2,1)S(1)}, u32[]{:S(2)}, u32[]{:S(2)}) collective-permute-start(bf16[1024,128]{1,0:T(8,128)(2,1)S(1)} %get-tuple-element.48.own1_ref), channel_id=1, source_target_pairs={{4,12},{0,24},{5,13},{1,25},{6,14},{2,26},{7,15},{3,27}} | collective-permute-start | bytes 786440 | tf_op jit(solution)/shard_map/ppermute | solution.py:375
  74.6 8.4 %collective-permute-start.16 = (bf16[1024,128]{1,0:T(8,128)(2,1)S(1)}, bf16[1024,128]{1,0:T(8,128)(2,1)S(1)}, u32[]{:S(2)}, u32[]{:S(2)}) collective-permute-start(bf16[1024,128]{1,0:T(8,128)(2,1)S(1)} %get-tuple-element.50.own2_ref), channel_id=1, source_target_pairs={{8,24},{12,20},{9,25},{13,21},{10,26},{14,22},{11,27},{15,23}} | collective-permute-start | bytes 786440 | tf_op jit(solution)/shard_map/ppermute | solution.py:375
  75.9 7.1 %collective-permute-start.17 = (bf16[1024,128]{1,0:T(8,128)(2,1)S(1)}, bf16[1024,128]{1,0:T(8,128)(2,1)S(1)}, u32[]{:S(2)}, u32[]{:S(2)}) collective-permute-start(bf16[1024,128]{1,0:T(8,128)(2,1)S(1)} %get-tuple-element.50.own2_ref), channel_id=1, source_target_pairs={{8,16},{12,28},{9,17},{13,29},{10,18},{14,30},{11,19},{15,31}} | collective-permute-start | bytes 786440 | tf_op jit(solution)/shard_map/ppermute | solution.py:375
  76.6 6.4 %collective-permute-start.18 = (bf16[1024,128]{1,0:T(8,128)(2,1)S(1)}, bf16[1024,128]{1,0:T(8,128)(2,1)S(1)}, u32[]{:S(2)}, u32[]{:S(2)}) collective-permute-start(bf16[1024,128]{1,0:T(8,128)(2,1)S(1)} %get-tuple-element.50.own2_ref), channel_id=1, source_target_pairs={{8,0},{0,12},{9,1},{1,13},{10,2},{2,14},{11,3},{3,15}} | collective-permute-start | bytes 786440 | tf_op jit(solution)/shard_map/ppermute | solution.py:375
  77.3 12.2 %collective-permute-start.20 = (bf16[1024,128]{1,0:T(8,128)(2,1)S(1)}, bf16[1024,128]{1,0:T(8,128)(2,1)S(1)}, u32[]{:S(2)}, u32[]{:S(2)}) collective-permute-start(bf16[1024,128]{1,0:T(8,128)(2,1)S(1)} %get-tuple-element.52.line0_ref), channel_id=1, source_target_pairs={{16,20},{24,28},{17,21},{25,29},{18,22},{26,30},{19,23},{27,31}} | collective-permute-start | bytes 786440 | tf_op jit(solution)/shard_map/ppermute | solution.py:375
  83.6 19.7 %collective-permute-start.19 = (bf16[1024,128]{1,0:T(8,128)(2,1)S(1)}, bf16[1024,128]{1,0:T(8,128)(2,1)S(1)}, u32[]{:S(2)}, u32[]{:S(2)}) collective-permute-start(bf16[1024,128]{1,0:T(8,128)(2,1)S(1)} %shard_map.76.line_ref), channel_id=1, source_target_pairs={{0,4},{4,0},{8,12},{12,8},{16,20},{20,16},{24,28},{28,24},{1,5},{5... | collective-permute-start | bytes 786440 | tf_op jit(solution)/shard_map/ppermute | solution.py:15
  91.8 5.2 %collective-permute-start.21 = (bf16[2,256,128]{2,1,0:T(8,128)(2,1)S(1)}, bf16[2,256,128]{2,1,0:T(8,128)(2,1)S(1)}, u32[]{:S(2)}, u32[]{:S(2)}) collective-permute-start(bf16[2,256,128]{2,1,0:T(8,128)(2,1)S(1)} %get-tuple-element.69), channel_id=1, source_target_pairs={{0,1},{1,0},{2,3},{3,2},{4,5},{5,4},{6,7},{7,6},{8,9},{9,8},{10,11... | collective-permute-start | bytes 393224 | tf_op jit(solution)/shard_map/ppermute | solution.py:15
  95.3 5.1 %collective-permute-start.22 = (bf16[2,256,128]{2,1,0:T(8,128)(2,1)S(1)}, bf16[2,256,128]{2,1,0:T(8,128)(2,1)S(1)}, u32[]{:S(2)}, u32[]{:S(2)}) collective-permute-start(bf16[2,256,128]{2,1,0:T(8,128)(2,1)S(1)} %get-tuple-element.68), channel_id=1, source_target_pairs={{0,2},{1,3},{2,0},{3,1},{4,6},{5,7},{6,4},{7,5},{8,10},{9,11},{10,... | collective-permute-start | bytes 393224 | tf_op jit(solution)/shard_map/ppermute | solution.py:15
  96.0 7.3 %collective-permute-start.23 = (bf16[2,256,128]{2,1,0:T(8,128)(2,1)S(1)}, bf16[2,256,128]{2,1,0:T(8,128)(2,1)S(1)}, u32[]{:S(2)}, u32[]{:S(2)}) collective-permute-start(bf16[2,256,128]{2,1,0:T(8,128)(2,1)S(1)} %get-tuple-element.67), channel_id=1, source_target_pairs={{0,3},{1,2},{2,1},{3,0},{4,7},{5,6},{6,5},{7,4},{8,11},{9,10},{10,... | collective-permute-start | bytes 393224 | tf_op jit(solution)/shard_map/ppermute | solution.py:15
  104.7 2.2 %collective-permute-start.24 = (bf16[2,256,128]{2,1,0:T(8,128)(2,1)S(1)}, bf16[2,256,128]{2,1,0:T(8,128)(2,1)S(1)}, u32[]{:S(2)}, u32[]{:S(2)}) collective-permute-start(bf16[2,256,128]{2,1,0:T(8,128)(2,1)S(1)} %get-tuple-element.65), channel_id=1, source_target_pairs={{0,1},{1,0},{2,3},{3,2},{4,5},{5,4},{6,7},{7,6},{8,9},{9,8},{10,11... | collective-permute-start | bytes 393224 | tf_op jit(solution)/shard_map/ppermute | solution.py:15
  105.0 4.8 %collective-permute-start.25 = (bf16[2,256,128]{2,1,0:T(8,128)(2,1)S(1)}, bf16[2,256,128]{2,1,0:T(8,128)(2,1)S(1)}, u32[]{:S(2)}, u32[]{:S(2)}) collective-permute-start(bf16[2,256,128]{2,1,0:T(8,128)(2,1)S(1)} %get-tuple-element.64), channel_id=1, source_target_pairs={{0,2},{1,3},{2,0},{3,1},{4,6},{5,7},{6,4},{7,5},{8,10},{9,11},{10,... | collective-permute-start | bytes 393224 | tf_op jit(solution)/shard_map/ppermute | solution.py:15
  105.7 7.3 %collective-permute-start.26 = (bf16[2,256,128]{2,1,0:T(8,128)(2,1)S(1)}, bf16[2,256,128]{2,1,0:T(8,128)(2,1)S(1)}, u32[]{:S(2)}, u32[]{:S(2)}) collective-permute-start(bf16[2,256,128]{2,1,0:T(8,128)(2,1)S(1)} %get-tuple-element.63), channel_id=1, source_target_pairs={{0,3},{1,2},{2,1},{3,0},{4,7},{5,6},{6,5},{7,4},{8,11},{9,10},{10,... | collective-permute-start | bytes 393224 | tf_op jit(solution)/shard_map/ppermute | solution.py:15

commit v5 on v4

--- a/solution.py
+++ b/solution.py
@@ -200,23 +200,12 @@
     lax.fori_loop(0, total_ref.shape[0] // strip, tile, 0)
 
 
-def reduce_kernel(bit, index_ref, kept_ref, moved_ref, keep_ref, send_ref):
-    mine = lax.rem(index_ref[0] // bit, 2)
-    for h in range(keep_ref.shape[0]):
-        keep_ref[h] = kept_ref[2 * h + mine] + moved_ref[2 * h + mine].astype(F32)
-        send_ref[h] = (kept_ref[2 * h + 1 - mine] + moved_ref[2 * h + 1 - mine].astype(F32)).astype(BF16)
-
-
-def reduce_step(bit, index, kept, moved):
-    part = (kept.shape[0] // 2,) + kept.shape[1:]
-    return pl.pallas_call(
-        functools.partial(reduce_kernel, bit),
-        out_shape=(shape_of(part, F32), shape_of(part, BF16)),
-        in_specs=[SMEM, VMEM, VMEM],
-        out_specs=(VMEM, VMEM),
-        compiler_params=PARAMS,
-        cost_estimate=cost(1),
-    )(index, kept, moved)
+def reduce_kernel(bit, index_ref, kept_ref, moved_ref, keep_ref, also_ref, send_ref):
+    mine = lax.rem(index_ref[1] // bit, 2)
+    keep = kept_ref[mine] + moved_ref[mine].astype(F32)
+    keep_ref[...] = keep
+    also_ref[...] = keep.astype(BF16)
+    send_ref[...] = (kept_ref[1 - mine] + moved_ref[1 - mine].astype(F32)).astype(BF16)
 
 
 def apply_strips(col, strips, value, store):
@@ -257,42 +246,97 @@
     return functools.reduce(jnp.add, [part[...] for part in parts])
 
 
-def start_kernel(n_col, index_ref, kept_ref, moved_ref, *refs):
-    strips, (current_ref, solved_ref) = refs[:n_col], refs[n_col:]
-    current_ref[...] = -(kept_ref[0] + moved_ref[0].astype(F32))
-    store_solved(index_ref, (strips, 0), 0, current_ref, solved_ref)
-
-
-def first_step_kernel(n_col, index_ref, current_ref, own_ref, value_ref, *refs):
-    strips, (out_ref, solved_ref) = refs[:n_col], refs[n_col:]
-    subtract(index_ref, (strips, 0), value_ref[...], index_ref[0] == 1, current_ref, out_ref)
-    store_solved(index_ref, (strips, 1), 1, out_ref, solved_ref)
-
-    @pl.when(index_ref[0] == 0)
-    def _():
-        solved_ref[...] = own_ref[...]
-
-
-def between_kernel(n_col, index_ref, current_ref, value_ref, *refs):
-    strips, (out_ref,) = refs[:n_col], refs[n_col:]
-    subtract(index_ref, (strips, 0), value_ref[...], index_ref[0] == 2, current_ref, out_ref)
-
-
 def copy_where(chosen, source_ref, target_ref):
     @pl.when(chosen)
     def _():
         target_ref[...] = source_ref[...]
 
 
-def second_step_kernel(n_col, index_ref, current_ref, own_ref, first_ref, second_ref, *refs):
-    strips, (out_ref, solved_ref, line_ref) = refs[:n_col], refs[n_col:]
-    row = index_ref[0]
-    subtract(index_ref, (strips, 1), first_ref[...], row == 2, current_ref, out_ref)
-    store_solved(index_ref, (strips, 2), 2, out_ref, solved_ref)
+def product_kernel(n_col, index_ref, *refs):
+    strips, (out_ref, right, last) = refs[:n_col], refs[n_col:]
+    row, col = index_ref[0], index_ref[1]
+    width = strips[0].shape[1]
+    spans = [pl.ds(pl.multiple_of((col ^ f) * width, width), width) for f in range(n_col)]
+
+    @pl.when(row == 1)
+    def _():
+        for span, strip in zip(spans, strips):
+            right[span, :] = strip[0]
+            last[span, :] = strip[2]
+        for span, strip in zip(spans, strips):
+            part = matmul(strip[1], right[...]).astype(BF16)
+            out_ref[span, :] = matmul(part, last[...]).astype(BF16)
+
+    @pl.when(row == 2)
+    def _():
+        for span, strip in zip(spans, strips):
+            right[span, :] = strip[1]
+        for span, strip in zip(spans, strips):
+            out_ref[span, :] = matmul(strip[2], right[...]).astype(BF16)
+
+    @pl.when((row < 1) | (row > 2))
+    def _():
+        out_ref[...] = jnp.zeros_like(out_ref)
+
+
+def start_kernel(n_col, index_ref, kept_ref, moved_ref, *refs):
+    strips, (current_ref, solved_ref, ahead_ref) = refs[:n_col], refs[n_col:]
+    current_ref[...] = -(kept_ref[...] + moved_ref[...].astype(F32))
+    store_solved(index_ref, (strips, 0), 0, current_ref, solved_ref)
+
+    def store(span, product):
+        ahead_ref[span, :] = product
+
+    @pl.when(index_ref[0] == 1)
+    def _():
+        apply_strips(index_ref[1], (strips, 1), current_ref[...].astype(BF16), store)
+
+
+def first_step_kernel(index_ref, own_ref, ahead_ref, product_ref, at1a_ref, at1b_ref, solved_ref):
+    row = index_ref[0]
+
+    @pl.when(row == 1)
+    def _():
+        rows0 = -(at1a_ref[...].astype(F32) + at1b_ref[...].astype(F32))
+        solved_ref[...] = (ahead_ref[...] - matmul(product_ref[...], rows0.astype(BF16))).astype(BF16)
+
+    copy_where(row == 0, own_ref, solved_ref)
+
+    @pl.when(row > 1)
+    def _():
+        solved_ref[...] = jnp.zeros_like(solved_ref)
+
+
+def between_kernel(n_col, index_ref, current_ref, value_ref, *refs):
+    strips, (out_ref, ahead_ref) = refs[:n_col], refs[n_col:]
+    row = index_ref[0]
+    subtract(index_ref, (strips, 0), value_ref[...], row == 2, current_ref, out_ref)
+
+    def store(span, product):
+        ahead_ref[span, :] = product
+
+    @pl.when(row == 2)
+    def _():
+        apply_strips(index_ref[1], (strips, 2), out_ref[...].astype(BF16), store)
+
+
+def second_step_kernel(index_ref, own_ref, ahead_ref, product_ref, first_ref, second_ref, solved_ref, line_ref):
+    row = index_ref[0]
+
+    @pl.when(row == 2)
+    def _():
+        solved_ref[...] = (ahead_ref[...] - matmul(product_ref[...], first_ref[...])).astype(BF16)
+
     copy_where(row == 0, own_ref, solved_ref)
     copy_where(row == 3, second_ref, solved_ref)
-    copy_where(row != 6, first_ref, line_ref)
-    copy_where(row == 6, second_ref, line_ref)
+
+    @pl.when((row == 1) | (row > 3))
+    def _():
+        solved_ref[...] = jnp.zeros_like(solved_ref)
+
+    copy_where(row == 0, own_ref, line_ref)
+    copy_where(row == 4, second_ref, line_ref)
+    copy_where((row != 0) & (row != 4), first_ref, line_ref)
 
 
 def line_kernel(index_ref, own1_ref, own2_ref, z6_ref, z4_ref, z0_ref, out_ref):
@@ -320,13 +364,18 @@
         target_ref[...] = source_ref[...]
 
 
-def middle_kernel(n_col, index_ref, current_ref, own0_ref, at1_ref, at2_ref, z0_ref, line0_ref, across0_ref, line_ref, *refs):
+def middle_kernel(n_col, index_ref, current_ref, own0_ref, at2_ref, z0_ref, line0_ref, across0_ref, first_ref, line_ref, *refs):
     strips, (out_ref, pieces_ref, known, between) = refs[:n_col], refs[n_col:]
     row = index_ref[0]
-    for holder, part in enumerate((own0_ref, at1_ref, at2_ref, z0_ref, line0_ref, across0_ref, line0_ref, across0_ref)):
+    for holder, part in enumerate((own0_ref, across0_ref, at2_ref, z0_ref, line0_ref, across0_ref, line0_ref, across0_ref)):
         copy_where(row == holder, part, known)
-    subtract(index_ref, (strips, 0), known[...], row > 2, current_ref, between)
+    subtract(index_ref, (strips, 0), known[...], (row == 1) | (row > 2), current_ref, between)
     update_either(index_ref, lax.rem(row, 2) == 1, strips, line_ref[...], between, out_ref)
+
+    @pl.when(row == 2)
+    def _():
+        subtract(index_ref, (strips, 1), first_ref[...], row == 2, between, out_ref)
+
     cut(index_ref, known, pieces_ref, 0)
     cut(index_ref, line_ref, pieces_ref, 1)
 
@@ -393,16 +442,16 @@
     chunk = nrhs // n_col
 
     block = earlier_solution[0]
-    own = jnp.stack([jnp.where(row == j, diag_inverse[j], window_panel[:, j, :]) for j in range(step_count)])
+    own = [jnp.where(row == j, diag_inverse[j], window_panel[:, j, :]) for j in range(step_count)]
+    own = jnp.stack(own[:2] + [jnp.where(row == 1, diag_inverse[0], own[2])])
     over = flip(own, "col", n_col, 2)
     b4 = flip(block, "row", n_row, 4)
     b2 = flip(block, "row", n_row, 2)
     b1 = flip(block, "row", n_row, 1)
-    b1, b2, again, panel = gate(b1, b2, block, earlier_panel)
+    panel = order_panel(index, earlier_panel)
+    b1, b2, again, panel = gate(b1, b2, block, panel)
     b6 = flip(again, "row", n_row, 6)
     b3 = flip(b2, "row", n_row, 1)
-    panel = order_panel(index, panel)
-    b3, b4, panel = gate(b3, b4, panel)
     b5 = flip(b4, "row", n_row, 1)
     b7 = flip(b6, "row", n_row, 1)
     total = bulk(index, panel, right_side, [block, b1, b2, b3, b4, b5, b6])
@@ -412,28 +461,33 @@
     kept, sent = local(split, (shape_of(part, F32), shape_of(part, BF16)), [index, panel, b7, total], [pltpu.VMEM((strip, nrhs), F32)])
     moved = flip(sent, "col", n_col, 1)
     moved, over = gate(moved, over)
-    kept, sent = reduce_step(2, flat_index(col), kept, moved)
+    slots = [own, flip(own, "col", n_col, 1), over, flip(over, "col", n_col, 1)]
+    wide, narrow = shape_of((rows, chunk), F32), shape_of((rows, chunk), BF16)
+    kept, also, sent = local(functools.partial(reduce_kernel, 2), (wide, narrow, narrow), [index, kept, moved])
+    at1a = hop(also, (0, 1))
+    at1b = lax.ppermute(sent, ("row", "col"), [(c, n_col + (c ^ 2)) for c in range(n_col)])
     moved = flip(sent, "col", n_col, 2)
-    slots = [own, flip(own, "col", n_col, 1), over, flip(over, "col", n_col, 1)]
-
-    wide, narrow = shape_of((rows, chunk), F32), shape_of((rows, chunk), BF16)
-    current, own0 = local(functools.partial(start_kernel, n_col), (wide, narrow), [index, kept, moved] + slots)
-    at1, at2 = hop(own0, (0, 1)), hop(own0, (0, 2))
-    step = functools.partial(first_step_kernel, n_col)
-    current, own1 = local(step, (wide, narrow), [index, current, own0, at1] + slots)
-    first, second = hop(own1, (1, 2), (0, 4)), hop(own1, (1, 3), (0, 6))
-    current = local(functools.partial(between_kernel, n_col), wide, [index, current, at2] + slots, us=8)
-    step = functools.partial(second_step_kernel, n_col)
-    current, own2, line0 = local(step, (wide, narrow, narrow), [index, current, own0, first, second] + slots)
+    scratch = [pltpu.VMEM((rows, rows), BF16)] * 2
+    product = local(functools.partial(product_kernel, n_col), shape_of((rows, rows), BF16), [index] + slots, scratch, us=8)
+
+    kept, product = gate(kept, product)
+    start = functools.partial(start_kernel, n_col)
+    current, own0, ahead = local(start, (wide, narrow, wide), [index, kept, moved] + slots)
+    at2 = hop(own0, (0, 2))
+    own1 = local(first_step_kernel, narrow, [index, own0, ahead, product, at1a, at1b])
+    first, second = hop(own1, (1, 2), (0, 6)), hop(own1, (1, 3), (0, 4))
+    between = functools.partial(between_kernel, n_col)
+    current, ahead = local(between, (wide, wide), [index, current, at2] + slots, us=8)
+    own2, line0 = local(second_step_kernel, (narrow, narrow), [index, own0, ahead, product, first, second])
     z6 = hop(own2, (2, 6), (3, 5))
     z4 = hop(own2, (2, 4), (3, 7))
     z0 = hop(own2, (2, 0), (0, 3))
-    across0 = hop(line0, (4, 5), (6, 7))
+    across0 = hop(line0, (0, 1), (4, 5), (6, 7))
     line = local(line_kernel, narrow, [index, own1, own2, z6, z4, z0])
     across = flip(line, "row", n_row, 1)
     pieces = shape_of((n_col, 2, strip, chunk), BF16)
     middle = functools.partial(middle_kernel, n_col)
-    parts = [own0, at1, at2, z0, line0, across0, line]
+    parts = [own0, at2, z0, line0, across0, first, line]
     scratch = [pltpu.VMEM((rows, chunk), BF16), pltpu.VMEM((rows, chunk), F32)]
     current, middle = local(middle, (wide, pieces), [index, current] + parts + slots, scratch, us=8)
     middle = swap_pieces(middle, n_col)

time: 115 us -> 112 us (0.974)
  waiting for transfers between devices: 60.8 us -> 51.4 us
  starting transfers between devices: 31.1 us -> 37.4 us
    ppermute x19, starting transfers between devices: 23.8 us -> 29.4 us  [flip(): return lax.ppermute(value, axis, [(i, i ^ bit) for i in range(size)])]
    ppermute x8, waiting for transfers between devices: 22.8 us -> 17.7 us  [hop(): return lax.ppermute(value, 'row', pairs)]
    ppermute x19, waiting for transfers between devices: 38 us -> 33.8 us  [flip(): return lax.ppermute(value, axis, [(i, i ^ bit) for i in range(size)])]
    pallas_call x10 -> x12, Pallas kernels: 13.6 us -> 14.8 us  [local(): pl.pallas_call(kernel, out_shape=out_shape, in_specs=[SMEM] + [VMEM] * (l...]
    unnamed x10 -> x6, local copies, waits for them, and re-layouts: 2.9 us -> 2.2 us
  transfers between devices with their start and end apart: 27 -> 28, of which waited for: 15 -> 14; matrix products, arithmetic and copies ran while one was open for 0% -> 0% of each run, Pallas kernels for 11% -> 13%
where the time goes in v5:
time: 112 us
  waiting for transfers between devices  51.4 us (46%)
  starting transfers between devices  37.4 us (33%)
  Pallas kernels  17.9 us (16%)
  local copies, waits for them, and re-layouts  2.27 us (2%)
  other arithmetic  2.25 us (2%)
    ppermute x19, waiting for transfers between devices, flip(): return lax.ppermute(value, axis, [(i, i ^ bit) for i in range(size)])  33.8 us
    ppermute x19, starting transfers between devices, flip(): return lax.ppermute(value, axis, [(i, i ^ bit) for i in range(size)])  29.4 us
    ppermute x8, waiting for transfers between devices, hop(): return lax.ppermute(value, 'row', pairs)  17.7 us
    pallas_call x12, Pallas kernels, local(): pl.pallas_call(kernel, out_shape=out_shape, in_specs=[SMEM] + [VMEM] * (l...  14.8 us
    ppermute x8, starting transfers between devices, hop(): return lax.ppermute(value, 'row', pairs)  7.26 us
    pallas_call x1, Pallas kernels, order_panel(): pl.pallas_call(order_kernel, out_shape=shape_of((rows, sources * width),...  3.08 us
  transfers between devices with their start and end apart: 28, of which 14 were waited for; matrix products, arithmetic and copies ran while one was open for 0% of the time, Pallas kernels for 13%

profile of v5, /device:TPU:25, one launch (start us, length us, event | category | flops | bytes accessed | tf_op | source)
XLA Modules:
  0.0 112.1 jit_solution(6179513933476405229)
XLA Ops:
  0.6 2.0 %bitcast_select_fusion.2 = (bf16[1,256,1024]{2,1,0:T(8,128)(2,1)S(1)}, bf16[1,256,1024]{2,1,0:T(8,128)(2,1)S(1)}, bf16[1,256,1024]{2,1,0:T(8,128)(2,1)S(1)}) fusion(bf16[256,3,1024]{2,0,1:T(8,128)(2,1)} %param.8, pred[]{:T(512)S(6)} %eq.10, bf16[3,256,1024]{2,1,0:T(8,128)(2,1)} %param.9, pred[]{:T(512)S(6)} %eq.12, pred[]{:T(512)S(6)} %eq.11), kind=kLoop, calls=%fused_computation.4 | loop fusion | flops 1048576 | bytes 4718595 | tf_op jit(solution)/shard_map/jit(_where)/select_n | solution.py:445
  2.6 0.0 copy-start.2
  2.7 0.2 pad_maximum_fusion.refs_0_
  2.8 1.3 %collective-permute-start.8 = (bf16[3,256,1024]{2,1,0:T(8,128)(2,1)S(1)}, bf16[3,256,1024]{2,1,0:T(8,128)(2,1)S(1)}, u32[]{:S(2)}, u32[]{:S(2)}) collective-permute-start(bf16[3,256,1024]{2,1,0:T(8,128)(2,1)S(1)} %pad_maximum_fusion.refs_0_), channel_id=1, source_target_pairs={{0,2},{1,3},{2,0},{3,1},{4,6},{5,7},{6,4},{7,5},{8,10},{9,11},{10,... | collective-permute-start | bytes 4718600 | tf_op jit(solution)/shard_map/ppermute | solution.py:15
  4.1 1.2 %collective-permute-start = (bf16[256,512]{1,0:T(8,128)(2,1)S(1)}, bf16[256,512]{1,0:T(8,128)(2,1)}, u32[]{:S(2)}, u32[]{:S(2)}) collective-permute-start(bf16[256,512]{1,0:T(8,128)(2,1)S(1)} %bitcast.27), channel_id=1, source_target_pairs={{0,4},{4,0},{8,12},{12,8},{16,20},{20,16},{24,28},{28,24},{1,5},{5... | collective-permute-start | bytes 786440 | tf_op jit(solution)/shard_map/ppermute | solution.py:15
  5.4 0.2 collective-permute-start.1
  5.5 0.1 collective-permute-start.3
  5.6 0.1 pad_add_fusion.index_ref
  5.7 2.2 %copy-done = bf16[1024,8,256]{2,1,0:T(8,128)(2,1)S(1)} copy-done((bf16[1024,8,256]{2,1,0:T(8,128)(2,1)S(1)}, bf16[1024,8,256]{2,1,0:T(8,128)(2,1)}, u32[]{:S(2)}) %copy-start) | copy-done | bytes 4194328
  7.8 3.1 %shard_map.68.panel_ref = bf16[1024,2048]{1,0:T(8,128)(2,1)S(1)} custom-call(s32[2]{0:T(128)S(1)} %pad_add_fusion.index_ref, bf16[1024,8,256]{2,1,0:T(8,128)(2,1)S(1)} %copy-done), custom_call_target="tpu_custom_call" | custom-call | bytes 28800000 | tf_op jit(solution)/shard_map/pallas_call | solution.py:154
  10.9 0.1 collective-permute-done.refs_1_
  11.1 5.9 %collective-permute-done.1.refs_2_ = bf16[256,512]{1,0:T(8,128)(2,1)} collective-permute-done((bf16[256,512]{1,0:T(8,128)(2,1)S(1)}, bf16[256,512]{1,0:T(8,128)(2,1)}, u32[]{:S(2)}, u32[]{:S(2)}) %collective-permute-start.1) | collective-permute-done | bytes 262176 | tf_op jit(solution)/shard_map/ppermute | solution.py:15
  16.9 0.3 collective-permute-start.5
  17.2 0.2 collective-permute-start.2
  17.4 0.0 collective-permute-done.3.refs_4_
  17.4 1.2 %collective-permute-start.4 = (bf16[256,512]{1,0:T(8,128)(2,1)}, bf16[256,512]{1,0:T(8,128)(2,1)S(1)}, u32[]{:S(2)}, u32[]{:S(2)}) collective-permute-start(bf16[256,512]{1,0:T(8,128)(2,1)} %collective-permute-done.3.refs_4_), channel_id=1, source_target_pairs={{0,4},{4,0},{8,12},{12,8},{16,20},{20,16},{24,28},{28,24},{1,5},{5... | collective-permute-start | bytes 786440 | tf_op jit(solution)/shard_map/ppermute | solution.py:15
  18.7 6.3 %collective-permute-done.5.refs_6_ = bf16[256,512]{1,0:T(8,128)(2,1)S(1)} collective-permute-done((bf16[256,512]{1,0:T(8,128)(2,1)S(1)}, bf16[256,512]{1,0:T(8,128)(2,1)S(1)}, u32[]{:S(2)}, u32[]{:S(2)}) %collective-permute-start.5) | collective-permute-done | bytes 262176 | tf_op jit(solution)/shard_map/ppermute | solution.py:15
  25.0 0.2 collective-permute-start.6
  25.2 2.9 %collective-permute-done.4.refs_5_ = bf16[256,512]{1,0:T(8,128)(2,1)S(1)} collective-permute-done((bf16[256,512]{1,0:T(8,128)(2,1)}, bf16[256,512]{1,0:T(8,128)(2,1)S(1)}, u32[]{:S(2)}, u32[]{:S(2)}) %collective-permute-start.4) | collective-permute-done | bytes 262176 | tf_op jit(solution)/shard_map/ppermute | solution.py:15
  28.1 3.3 %shard_map.69.total_ref = f32[1024,512]{1,0:T(8,128)S(1)} custom-call(s32[2]{0:T(128)S(1)} %pad_add_fusion.index_ref, bf16[1024,2048]{1,0:T(8,128)(2,1)S(1)} %shard_map.68.panel_ref, f32[256,512]{1,0:T(8,128)S(1)} %copy-done.1, bf16[256,512]{1,0:T(8,128)(2,1)S(1)} %bitcast.31, bf16[256,512]{1,0:T(8,128)(2,1)} %collective-permute-done.refs_1_, ...), custom_call_target="tpu_custom_call" | custom-call | bytes 28800000 | tf_op jit(solution)/shard_map/pallas_call | solution.py:412
  31.4 0.2 collective-permute-done.6.block_ref
  31.6 1.7 %shard_map.70 = (f32[2,1024,128]{2,1,0:T(8,128)S(1)}, bf16[2,1024,128]{2,1,0:T(8,128)(2,1)S(1)}) custom-call(s32[2]{0:T(128)S(1)} %pad_add_fusion.index_ref, bf16[1024,2048]{1,0:T(8,128)(2,1)S(1)} %shard_map.68.panel_ref, bf16[256,512]{1,0:T(8,128)(2,1)S(1)} %collective-permute-done.6.block_ref, f32[1024,512]{1,0:T(8,128)S(1)} %shard_map.69.total_ref), custom_call_target="tpu_custom_call" | custom-call | bytes 3600000 | tf_op jit(solution)/shard_map/pallas_call | solution.py:412
  33.3 6.4 %collective-permute-start.7 = (bf16[2,1024,128]{2,1,0:T(8,128)(2,1)S(1)}, bf16[2,1024,128]{2,1,0:T(8,128)(2,1)S(1)}, u32[]{:S(2)}, u32[]{:S(2)}) collective-permute-start(bf16[2,1024,128]{2,1,0:T(8,128)(2,1)S(1)} %get-tuple-element.38), channel_id=1, source_target_pairs={{0,1},{1,0},{2,3},{3,2},{4,5},{5,4},{6,7},{7,6},{8,9},{9,8},{10,11... | collective-permute-start | bytes 1572872 | tf_op jit(solution)/shard_map/ppermute | solution.py:15
  39.7 0.1 collective-permute-start.9
  39.8 1.5 %collective-permute-done.7.moved_ref = bf16[2,1024,128]{2,1,0:T(8,128)(2,1)S(1)} collective-permute-done((bf16[2,1024,128]{2,1,0:T(8,128)(2,1)S(1)}, bf16[2,1024,128]{2,1,0:T(8,128)(2,1)S(1)}, u32[]{:S(2)}, u32[]{:S(2)}) %collective-permute-start.7) | collective-permute-done | bytes 524320 | tf_op jit(solution)/shard_map/ppermute | solution.py:15
  41.2 0.0 collective-permute-done.8.refs_2_
  41.2 0.4 collective-permute-start.10
  41.6 0.7 shard_map.71
  42.3 1.3 %collective-permute-start.11 = (bf16[1024,128]{1,0:T(8,128)(2,1)S(1)}, bf16[1024,128]{1,0:T(8,128)(2,1)S(1)}, u32[]{:S(2)}, u32[]{:S(2)}) collective-permute-start(bf16[1024,128]{1,0:T(8,128)(2,1)S(1)} %get-tuple-element.43), channel_id=1, source_target_pairs={{0,2},{1,3},{2,0},{3,1},{4,6},{5,7},{6,4},{7,5},{8,10},{9,11},{10,... | collective-permute-start | bytes 786440 | tf_op jit(solution)/shard_map/ppermute | solution.py:15
  43.6 0.7 collective-permute-start.12
  44.2 0.7 collective-permute-start.13
  44.9 0.8 collective-permute-done.10.refs_3_
  45.7 0.7 shard_map.72.product_ref
  46.4 3.7 %collective-permute-done.11.moved_ref = bf16[1024,128]{1,0:T(8,128)(2,1)S(1)} collective-permute-done((bf16[1024,128]{1,0:T(8,128)(2,1)S(1)}, bf16[1024,128]{1,0:T(8,128)(2,1)S(1)}, u32[]{:S(2)}, u32[]{:S(2)}) %collective-permute-start.11) | collective-permute-done | bytes 262176 | tf_op jit(solution)/shard_map/ppermute | solution.py:15
  50.1 0.8 shard_map.73
  50.9 0.7 collective-permute-start.14
  51.6 0.6 shard_map.74.own1_ref
  52.2 1.3 %collective-permute-start.15 = (bf16[1024,128]{1,0:T(8,128)(2,1)S(1)}, bf16[1024,128]{1,0:T(8,128)(2,1)S(1)}, u32[]{:S(2)}, u32[]{:S(2)}) collective-permute-start(bf16[1024,128]{1,0:T(8,128)(2,1)S(1)} %shard_map.74.own1_ref), channel_id=1, source_target_pairs={{4,8},{0,24},{5,9},{1,25},{6,10},{2,26},{7,11},{3,27}} | collective-permute-start | bytes 786440 | tf_op jit(solution)/shard_map/ppermute | solution.py:424
  53.5 0.7 collective-permute-start.16
  54.2 0.0 collective-permute-done.14.value_ref.at2_ref
  54.2 0.6 shard_map.75
  54.8 12.7 %collective-permute-done.15.first_ref = bf16[1024,128]{1,0:T(8,128)(2,1)S(1)} collective-permute-done((bf16[1024,128]{1,0:T(8,128)(2,1)S(1)}, bf16[1024,128]{1,0:T(8,128)(2,1)S(1)}, u32[]{:S(2)}, u32[]{:S(2)}) %collective-permute-start.15) | collective-permute-done | bytes 262176 | tf_op jit(solution)/shard_map/ppermute | solution.py:424
  67.5 0.6 shard_map.76
  68.1 1.3 %collective-permute-start.17 = (bf16[1024,128]{1,0:T(8,128)(2,1)S(1)}, bf16[1024,128]{1,0:T(8,128)(2,1)S(1)}, u32[]{:S(2)}, u32[]{:S(2)}) collective-permute-start(bf16[1024,128]{1,0:T(8,128)(2,1)S(1)} %get-tuple-element.50.own2_ref), channel_id=1, source_target_pairs={{8,24},{12,20},{9,25},{13,21},{10,26},{14,22},{11,27},{15,23}} | collective-permute-start | bytes 786440 | tf_op jit(solution)/shard_map/ppermute | solution.py:424
  69.4 0.7 collective-permute-start.18
  70.1 0.7 collective-permute-start.19
  70.8 1.3 %collective-permute-start.21 = (bf16[1024,128]{1,0:T(8,128)(2,1)S(1)}, bf16[1024,128]{1,0:T(8,128)(2,1)S(1)}, u32[]{:S(2)}, u32[]{:S(2)}) collective-permute-start(bf16[1024,128]{1,0:T(8,128)(2,1)S(1)} %get-tuple-element.52.line0_ref), channel_id=1, source_target_pairs={{0,4},{16,20},{24,28},{1,5},{17,21},{25,29},{2,6},{18,22},{26,30},... | collective-permute-start | bytes 786440 | tf_op jit(solution)/shard_map/ppermute | solution.py:424
  72.1 5.0 %collective-permute-done.17.z6_ref = bf16[1024,128]{1,0:T(8,128)(2,1)S(1)} collective-permute-done((bf16[1024,128]{1,0:T(8,128)(2,1)S(1)}, bf16[1024,128]{1,0:T(8,128)(2,1)S(1)}, u32[]{:S(2)}, u32[]{:S(2)}) %collective-permute-start.17) | collective-permute-done | bytes 262176 | tf_op jit(solution)/shard_map/ppermute | solution.py:424
  77.1 0.0 collective-permute-done.18.z4_ref
  77.1 0.6 shard_map.77.line_ref
  77.7 9.8 %collective-permute-start.20 = (bf16[1024,128]{1,0:T(8,128)(2,1)S(1)}, bf16[1024,128]{1,0:T(8,128)(2,1)S(1)}, u32[]{:S(2)}, u32[]{:S(2)}) collective-permute-start(bf16[1024,128]{1,0:T(8,128)(2,1)S(1)} %shard_map.77.line_ref), channel_id=1, source_target_pairs={{0,4},{4,0},{8,12},{12,8},{16,20},{20,16},{24,28},{28,24},{1,5},{5... | collective-permute-start | bytes 786440 | tf_op jit(solution)/shard_map/ppermute | solution.py:15
  87.5 2.1 %shard_map.78 = (f32[1024,128]{1,0:T(8,128)S(1)}, bf16[4,2,256,128]{3,2,1,0:T(8,128)(2,1)S(1)}) custom-call(s32[2]{0:T(128)S(1)} %pad_add_fusion.index_ref, f32[1024,128]{1,0:T(8,128)S(1)} %get-tuple-element.51.current_ref, bf16[1024,128]{1,0:T(8,128)(2,1)S(1)} %get-tuple-element.44.own_ref.own0_ref, ...), custom_call_target="tpu_custom_call" | custom-call | bytes 28800000 | tf_op jit(solution)/shard_map/pallas_call | solution.py:412
  89.6 2.9 %collective-permute-start.22 = (bf16[2,256,128]{2,1,0:T(8,128)(2,1)S(1)}, bf16[2,256,128]{2,1,0:T(8,128)(2,1)S(1)}, u32[]{:S(2)}, u32[]{:S(2)}) collective-permute-start(bf16[2,256,128]{2,1,0:T(8,128)(2,1)S(1)} %get-tuple-element.69), channel_id=1, source_target_pairs={{0,1},{1,0},{2,3},{3,2},{4,5},{5,4},{6,7},{7,6},{8,9},{9,8},{10,11... | collective-permute-start | bytes 393224 | tf_op jit(solution)/shard_map/ppermute | solution.py:15
  92.5 0.8 collective-permute-start.23
  93.3 0.9 collective-permute-start.24
  94.2 3.4 %collective-permute-done.23.refs_2_ = bf16[2,256,128]{2,1,0:T(8,128)(2,1)S(1)} collective-permute-done((bf16[2,256,128]{2,1,0:T(8,128)(2,1)S(1)}, bf16[2,256,128]{2,1,0:T(8,128)(2,1)S(1)}, u32[]{:S(2)}, u32[]{:S(2)}) %collective-permute-start.23) | collective-permute-done | bytes 131104 | tf_op jit(solution)/shard_map/ppermute | solution.py:15
  97.6 3.0 %collective-permute-done.24.refs_3_ = bf16[2,256,128]{2,1,0:T(8,128)(2,1)S(1)} collective-permute-done((bf16[2,256,128]{2,1,0:T(8,128)(2,1)S(1)}, bf16[2,256,128]{2,1,0:T(8,128)(2,1)S(1)}, u32[]{:S(2)}, u32[]{:S(2)}) %collective-permute-start.24) | collective-permute-done | bytes 131104 | tf_op jit(solution)/shard_map/ppermute | solution.py:15
  100.6 1.3 %shard_map.79 = bf16[4,2,256,128]{3,2,1,0:T(8,128)(2,1)S(1)} custom-call(s32[2]{0:T(128)S(1)} %pad_add_fusion.index_ref, f32[1024,128]{1,0:T(8,128)S(1)} %get-tuple-element.58.current_ref, bf16[1024,128]{1,0:T(8,128)(2,1)S(1)} %collective-permute-done.20.value_ref, bf16[3,256,1024]{2,1,0:T(8,128)(2,1)S(1)} %pad_maximum_fusion.refs_0_, ...), custom_call_target="tpu_custom_call" | custom-call | bytes 3600000 | tf_op jit(solution)/shard_map/pallas_call | solution.py:412
  102.0 0.3 collective-permute-start.25
  102.3 0.8 collective-permute-start.26
  103.0 1.1 %collective-permute-start.27 = (bf16[2,256,128]{2,1,0:T(8,128)(2,1)S(1)}, bf16[2,256,128]{2,1,0:T(8,128)(2,1)S(1)}, u32[]{:S(2)}, u32[]{:S(2)}) collective-permute-start(bf16[2,256,128]{2,1,0:T(8,128)(2,1)S(1)} %get-tuple-element.63), channel_id=1, source_target_pairs={{0,3},{1,2},{2,1},{3,0},{4,7},{5,6},{6,5},{7,4},{8,11},{9,10},{10,... | collective-permute-start | bytes 393224 | tf_op jit(solution)/shard_map/ppermute | solution.py:15
  104.2 2.9 %collective-permute-done.26.refs_6_ = bf16[2,256,128]{2,1,0:T(8,128)(2,1)S(1)} collective-permute-done((bf16[2,256,128]{2,1,0:T(8,128)(2,1)S(1)}, bf16[2,256,128]{2,1,0:T(8,128)(2,1)S(1)}, u32[]{:S(2)}, u32[]{:S(2)}) %collective-permute-start.26) | collective-permute-done | bytes 131104 | tf_op jit(solution)/shard_map/ppermute | solution.py:15
  107.1 3.2 %collective-permute-done.27.refs_7_ = bf16[2,256,128]{2,1,0:T(8,128)(2,1)S(1)} collective-permute-done((bf16[2,256,128]{2,1,0:T(8,128)(2,1)S(1)}, bf16[2,256,128]{2,1,0:T(8,128)(2,1)S(1)}, u32[]{:S(2)}, u32[]{:S(2)}) %collective-permute-start.27) | collective-permute-done | bytes 131104 | tf_op jit(solution)/shard_map/ppermute | solution.py:15
  110.3 1.8 %shard_map.80 = (bf16[3,256,512]{2,1,0:T(8,128)(2,1)}, f32[256,512]{1,0:T(8,128)}) custom-call(s32[2]{0:T(128)S(1)} %pad_add_fusion.index_ref, bf16[2,256,128]{2,1,0:T(8,128)(2,1)S(1)} %get-tuple-element.54.refs_0_, bf16[2,256,128]{2,1,0:T(8,128)(2,1)S(1)} %collective-permute-done.22.refs_1_, bf16[2,256,128]{2,1,0:T(8,128)(2,1)S(1)} %collective-permute-done.23.refs_2_, ...), custom_call_target="tpu_custom_call" | custom-call | bytes 3600000 | tf_op jit(solution)/shard_map/pallas_call | solution.py:412
  (16 shorter events, 0.1 us)
Async XLA Ops:
  2.6 1.5 %copy-start.2 = (bf16[1,256,512]{2,1,0:T(8,128)(2,1)S(1)}, bf16[1,256,512]{2,1,0:T(8,128)(2,1)}, u32[]{:S(2)}) copy-start(bf16[1,256,512]{2,1,0:T(8,128)(2,1)} %param.7) | copy-start | bytes 786436
  2.8 38.4 %collective-permute-start.8 = (bf16[3,256,1024]{2,1,0:T(8,128)(2,1)S(1)}, bf16[3,256,1024]{2,1,0:T(8,128)(2,1)S(1)}, u32[]{:S(2)}, u32[]{:S(2)}) collective-permute-start(bf16[3,256,1024]{2,1,0:T(8,128)(2,1)S(1)} %pad_maximum_fusion.refs_0_), channel_id=1, source_target_pairs={{0,2},{1,3},{2,0},{3,1},{4,6},{5,7},{6,4},{7,5},{8,10},{9,11},{10,... | collective-permute-start | bytes 4718600 | tf_op jit(solution)/shard_map/ppermute | solution.py:15
  4.1 7.0 %collective-permute-start = (bf16[256,512]{1,0:T(8,128)(2,1)S(1)}, bf16[256,512]{1,0:T(8,128)(2,1)}, u32[]{:S(2)}, u32[]{:S(2)}) collective-permute-start(bf16[256,512]{1,0:T(8,128)(2,1)S(1)} %bitcast.27), channel_id=1, source_target_pairs={{0,4},{4,0},{8,12},{12,8},{16,20},{20,16},{24,28},{28,24},{1,5},{5... | collective-permute-start | bytes 786440 | tf_op jit(solution)/shard_map/ppermute | solution.py:15
  5.4 11.6 %collective-permute-start.1 = (bf16[256,512]{1,0:T(8,128)(2,1)S(1)}, bf16[256,512]{1,0:T(8,128)(2,1)}, u32[]{:S(2)}, u32[]{:S(2)}) collective-permute-start(bf16[256,512]{1,0:T(8,128)(2,1)S(1)} %bitcast.28), channel_id=1, source_target_pairs={{0,8},{4,12},{8,0},{12,4},{16,24},{20,28},{24,16},{28,20},{1,9},{5... | collective-permute-start | bytes 786440 | tf_op jit(solution)/shard_map/ppermute | solution.py:15
  5.5 11.9 %collective-permute-start.3 = (bf16[256,512]{1,0:T(8,128)(2,1)S(1)}, bf16[256,512]{1,0:T(8,128)(2,1)}, u32[]{:S(2)}, u32[]{:S(2)}) collective-permute-start(bf16[256,512]{1,0:T(8,128)(2,1)S(1)} %bitcast.29), channel_id=1, source_target_pairs={{0,16},{4,20},{8,24},{12,28},{16,0},{20,4},{24,8},{28,12},{1,17},{... | collective-permute-start | bytes 786440 | tf_op jit(solution)/shard_map/ppermute | solution.py:15
  5.7 2.2 %copy-start = (bf16[1024,8,256]{2,1,0:T(8,128)(2,1)S(1)}, bf16[1024,8,256]{2,1,0:T(8,128)(2,1)}, u32[]{:S(2)}) copy-start(bf16[1024,8,256]{2,1,0:T(8,128)(2,1)} %panel_ref.1) | copy-start | bytes 12582916
  7.8 20.3 %copy-start.1 = (f32[256,512]{1,0:T(8,128)S(1)}, f32[256,512]{1,0:T(8,128)}, u32[]{:S(2)}) copy-start(f32[256,512]{1,0:T(8,128)} %side_ref.1) | copy-start | bytes 1572868
  16.9 8.1 %collective-permute-start.5 = (bf16[256,512]{1,0:T(8,128)(2,1)S(1)}, bf16[256,512]{1,0:T(8,128)(2,1)S(1)}, u32[]{:S(2)}, u32[]{:S(2)}) collective-permute-start(bf16[256,512]{1,0:T(8,128)(2,1)S(1)} %bitcast.30), channel_id=1, source_target_pairs={{0,24},{4,28},{8,16},{12,20},{16,8},{20,12},{24,0},{28,4},{1,25},{... | collective-permute-start | bytes 786440 | tf_op jit(solution)/shard_map/ppermute | solution.py:15
  17.2 8.0 %collective-permute-start.2 = (bf16[256,512]{1,0:T(8,128)(2,1)}, bf16[256,512]{1,0:T(8,128)(2,1)S(1)}, u32[]{:S(2)}, u32[]{:S(2)}) collective-permute-start(bf16[256,512]{1,0:T(8,128)(2,1)} %collective-permute-done.1.refs_2_), channel_id=1, source_target_pairs={{0,4},{4,0},{8,12},{12,8},{16,20},{20,16},{24,28},{28,24},{1,5},{5... | collective-permute-start | bytes 786440 | tf_op jit(solution)/shard_map/ppermute | solution.py:15
  17.4 10.7 %collective-permute-start.4 = (bf16[256,512]{1,0:T(8,128)(2,1)}, bf16[256,512]{1,0:T(8,128)(2,1)S(1)}, u32[]{:S(2)}, u32[]{:S(2)}) collective-permute-start(bf16[256,512]{1,0:T(8,128)(2,1)} %collective-permute-done.3.refs_4_), channel_id=1, source_target_pairs={{0,4},{4,0},{8,12},{12,8},{16,20},{20,16},{24,28},{28,24},{1,5},{5... | collective-permute-start | bytes 786440 | tf_op jit(solution)/shard_map/ppermute | solution.py:15
  25.0 6.6 %collective-permute-start.6 = (bf16[256,512]{1,0:T(8,128)(2,1)S(1)}, bf16[256,512]{1,0:T(8,128)(2,1)S(1)}, u32[]{:S(2)}, u32[]{:S(2)}) collective-permute-start(bf16[256,512]{1,0:T(8,128)(2,1)S(1)} %collective-permute-done.5.refs_6_), channel_id=1, source_target_pairs={{0,4},{4,0},{8,12},{12,8},{16,20},{20,16},{24,28},{28,24},{1,5},{5... | collective-permute-start | bytes 786440 | tf_op jit(solution)/shard_map/ppermute | solution.py:15
  33.3 7.9 %collective-permute-start.7 = (bf16[2,1024,128]{2,1,0:T(8,128)(2,1)S(1)}, bf16[2,1024,128]{2,1,0:T(8,128)(2,1)S(1)}, u32[]{:S(2)}, u32[]{:S(2)}) collective-permute-start(bf16[2,1024,128]{2,1,0:T(8,128)(2,1)S(1)} %get-tuple-element.38), channel_id=1, source_target_pairs={{0,1},{1,0},{2,3},{3,2},{4,5},{5,4},{6,7},{7,6},{8,9},{9,8},{10,11... | collective-permute-start | bytes 1572872 | tf_op jit(solution)/shard_map/ppermute | solution.py:15
  39.7 5.3 %collective-permute-start.9 = (bf16[3,256,1024]{2,1,0:T(8,128)(2,1)S(1)}, bf16[3,256,1024]{2,1,0:T(8,128)(2,1)S(1)}, u32[]{:S(2)}, u32[]{:S(2)}) collective-permute-start(bf16[3,256,1024]{2,1,0:T(8,128)(2,1)S(1)} %pad_maximum_fusion.refs_0_), channel_id=1, source_target_pairs={{0,1},{1,0},{2,3},{3,2},{4,5},{5,4},{6,7},{7,6},{8,9},{9,8},{10,11... | collective-permute-start | bytes 4718600 | tf_op jit(solution)/shard_map/ppermute | solution.py:15
  41.2 4.5 %collective-permute-start.10 = (bf16[3,256,1024]{2,1,0:T(8,128)(2,1)S(1)}, bf16[3,256,1024]{2,1,0:T(8,128)(2,1)S(1)}, u32[]{:S(2)}, u32[]{:S(2)}) collective-permute-start(bf16[3,256,1024]{2,1,0:T(8,128)(2,1)S(1)} %collective-permute-done.8.refs_2_), channel_id=1, source_target_pairs={{0,1},{1,0},{2,3},{3,2},{4,5},{5,4},{6,7},{7,6},{8,9},{9,8},{10,11... | collective-permute-start | bytes 4718600 | tf_op jit(solution)/shard_map/ppermute | solution.py:15
  42.3 7.8 %collective-permute-start.11 = (bf16[1024,128]{1,0:T(8,128)(2,1)S(1)}, bf16[1024,128]{1,0:T(8,128)(2,1)S(1)}, u32[]{:S(2)}, u32[]{:S(2)}) collective-permute-start(bf16[1024,128]{1,0:T(8,128)(2,1)S(1)} %get-tuple-element.43), channel_id=1, source_target_pairs={{0,2},{1,3},{2,0},{3,1},{4,6},{5,7},{6,4},{7,5},{8,10},{9,11},{10,... | collective-permute-start | bytes 786440 | tf_op jit(solution)/shard_map/ppermute | solution.py:15
  43.6 8.0 %collective-permute-start.12 = (bf16[1024,128]{1,0:T(8,128)(2,1)S(1)}, bf16[1024,128]{1,0:T(8,128)(2,1)S(1)}, u32[]{:S(2)}, u32[]{:S(2)}) collective-permute-start(bf16[1024,128]{1,0:T(8,128)(2,1)S(1)} %get-tuple-element.47), channel_id=1, source_target_pairs={{0,4},{1,5},{2,6},{3,7}} | collective-permute-start | bytes 786440 | tf_op jit(solution)/shard_map/ppermute | solution.py:424
  44.2 7.4 %collective-permute-start.13 = (bf16[1024,128]{1,0:T(8,128)(2,1)S(1)}, bf16[1024,128]{1,0:T(8,128)(2,1)S(1)}, u32[]{:S(2)}, u32[]{:S(2)}) collective-permute-start(bf16[1024,128]{1,0:T(8,128)(2,1)S(1)} %get-tuple-element.43), channel_id=1, source_target_pairs={{0,6},{1,7},{2,4},{3,5}} | collective-permute-start | bytes 786440 | tf_op jit(solution)/shard_map/ppermute | solution.py:468
  50.9 3.3 %collective-permute-start.14 = (bf16[1024,128]{1,0:T(8,128)(2,1)S(1)}, bf16[1024,128]{1,0:T(8,128)(2,1)S(1)}, u32[]{:S(2)}, u32[]{:S(2)}) collective-permute-start(bf16[1024,128]{1,0:T(8,128)(2,1)S(1)} %get-tuple-element.44.own_ref.own0_ref), channel_id=1, source_target_pairs={{0,8},{1,9},{2,10},{3,11}} | collective-permute-start | bytes 786440 | tf_op jit(solution)/shard_map/ppermute | solution.py:424
  52.2 15.3 %collective-permute-start.15 = (bf16[1024,128]{1,0:T(8,128)(2,1)S(1)}, bf16[1024,128]{1,0:T(8,128)(2,1)S(1)}, u32[]{:S(2)}, u32[]{:S(2)}) collective-permute-start(bf16[1024,128]{1,0:T(8,128)(2,1)S(1)} %shard_map.74.own1_ref), channel_id=1, source_target_pairs={{4,8},{0,24},{5,9},{1,25},{6,10},{2,26},{7,11},{3,27}} | collective-permute-start | bytes 786440 | tf_op jit(solution)/shard_map/ppermute | solution.py:424
  53.5 14.0 %collective-permute-start.16 = (bf16[1024,128]{1,0:T(8,128)(2,1)S(1)}, bf16[1024,128]{1,0:T(8,128)(2,1)S(1)}, u32[]{:S(2)}, u32[]{:S(2)}) collective-permute-start(bf16[1024,128]{1,0:T(8,128)(2,1)S(1)} %shard_map.74.own1_ref), channel_id=1, source_target_pairs={{4,12},{0,16},{5,13},{1,17},{6,14},{2,18},{7,15},{3,19}} | collective-permute-start | bytes 786440 | tf_op jit(solution)/shard_map/ppermute | solution.py:424
  68.1 9.0 %collective-permute-start.17 = (bf16[1024,128]{1,0:T(8,128)(2,1)S(1)}, bf16[1024,128]{1,0:T(8,128)(2,1)S(1)}, u32[]{:S(2)}, u32[]{:S(2)}) collective-permute-start(bf16[1024,128]{1,0:T(8,128)(2,1)S(1)} %get-tuple-element.50.own2_ref), channel_id=1, source_target_pairs={{8,24},{12,20},{9,25},{13,21},{10,26},{14,22},{11,27},{15,23}} | collective-permute-start | bytes 786440 | tf_op jit(solution)/shard_map/ppermute | solution.py:424
  69.4 7.7 %collective-permute-start.18 = (bf16[1024,128]{1,0:T(8,128)(2,1)S(1)}, bf16[1024,128]{1,0:T(8,128)(2,1)S(1)}, u32[]{:S(2)}, u32[]{:S(2)}) collective-permute-start(bf16[1024,128]{1,0:T(8,128)(2,1)S(1)} %get-tuple-element.50.own2_ref), channel_id=1, source_target_pairs={{8,16},{12,28},{9,17},{13,29},{10,18},{14,30},{11,19},{15,31}} | collective-permute-start | bytes 786440 | tf_op jit(solution)/shard_map/ppermute | solution.py:424
  70.1 7.0 %collective-permute-start.19 = (bf16[1024,128]{1,0:T(8,128)(2,1)S(1)}, bf16[1024,128]{1,0:T(8,128)(2,1)S(1)}, u32[]{:S(2)}, u32[]{:S(2)}) collective-permute-start(bf16[1024,128]{1,0:T(8,128)(2,1)S(1)} %get-tuple-element.50.own2_ref), channel_id=1, source_target_pairs={{8,0},{0,12},{9,1},{1,13},{10,2},{2,14},{11,3},{3,15}} | collective-permute-start | bytes 786440 | tf_op jit(solution)/shard_map/ppermute | solution.py:424
  70.8 16.7 %collective-permute-start.21 = (bf16[1024,128]{1,0:T(8,128)(2,1)S(1)}, bf16[1024,128]{1,0:T(8,128)(2,1)S(1)}, u32[]{:S(2)}, u32[]{:S(2)}) collective-permute-start(bf16[1024,128]{1,0:T(8,128)(2,1)S(1)} %get-tuple-element.52.line0_ref), channel_id=1, source_target_pairs={{0,4},{16,20},{24,28},{1,5},{17,21},{25,29},{2,6},{18,22},{26,30},... | collective-permute-start | bytes 786440 | tf_op jit(solution)/shard_map/ppermute | solution.py:424
  77.7 22.9 %collective-permute-start.20 = (bf16[1024,128]{1,0:T(8,128)(2,1)S(1)}, bf16[1024,128]{1,0:T(8,128)(2,1)S(1)}, u32[]{:S(2)}, u32[]{:S(2)}) collective-permute-start(bf16[1024,128]{1,0:T(8,128)(2,1)S(1)} %shard_map.77.line_ref), channel_id=1, source_target_pairs={{0,4},{4,0},{8,12},{12,8},{16,20},{20,16},{24,28},{28,24},{1,5},{5... | collective-permute-start | bytes 786440 | tf_op jit(solution)/shard_map/ppermute | solution.py:15
  89.6 4.6 %collective-permute-start.22 = (bf16[2,256,128]{2,1,0:T(8,128)(2,1)S(1)}, bf16[2,256,128]{2,1,0:T(8,128)(2,1)S(1)}, u32[]{:S(2)}, u32[]{:S(2)}) collective-permute-start(bf16[2,256,128]{2,1,0:T(8,128)(2,1)S(1)} %get-tuple-element.69), channel_id=1, source_target_pairs={{0,1},{1,0},{2,3},{3,2},{4,5},{5,4},{6,7},{7,6},{8,9},{9,8},{10,11... | collective-permute-start | bytes 393224 | tf_op jit(solution)/shard_map/ppermute | solution.py:15
  92.5 5.1 %collective-permute-start.23 = (bf16[2,256,128]{2,1,0:T(8,128)(2,1)S(1)}, bf16[2,256,128]{2,1,0:T(8,128)(2,1)S(1)}, u32[]{:S(2)}, u32[]{:S(2)}) collective-permute-start(bf16[2,256,128]{2,1,0:T(8,128)(2,1)S(1)} %get-tuple-element.68), channel_id=1, source_target_pairs={{0,2},{1,3},{2,0},{3,1},{4,6},{5,7},{6,4},{7,5},{8,10},{9,11},{10,... | collective-permute-start | bytes 393224 | tf_op jit(solution)/shard_map/ppermute | solution.py:15
  93.3 7.3 %collective-permute-start.24 = (bf16[2,256,128]{2,1,0:T(8,128)(2,1)S(1)}, bf16[2,256,128]{2,1,0:T(8,128)(2,1)S(1)}, u32[]{:S(2)}, u32[]{:S(2)}) collective-permute-start(bf16[2,256,128]{2,1,0:T(8,128)(2,1)S(1)} %get-tuple-element.67), channel_id=1, source_target_pairs={{0,3},{1,2},{2,1},{3,0},{4,7},{5,6},{6,5},{7,4},{8,11},{9,10},{10,... | collective-permute-start | bytes 393224 | tf_op jit(solution)/shard_map/ppermute | solution.py:15
  102.0 2.2 %collective-permute-start.25 = (bf16[2,256,128]{2,1,0:T(8,128)(2,1)S(1)}, bf16[2,256,128]{2,1,0:T(8,128)(2,1)S(1)}, u32[]{:S(2)}, u32[]{:S(2)}) collective-permute-start(bf16[2,256,128]{2,1,0:T(8,128)(2,1)S(1)} %get-tuple-element.65), channel_id=1, source_target_pairs={{0,1},{1,0},{2,3},{3,2},{4,5},{5,4},{6,7},{7,6},{8,9},{9,8},{10,11... | collective-permute-start | bytes 393224 | tf_op jit(solution)/shard_map/ppermute | solution.py:15
  102.3 4.8 %collective-permute-start.26 = (bf16[2,256,128]{2,1,0:T(8,128)(2,1)S(1)}, bf16[2,256,128]{2,1,0:T(8,128)(2,1)S(1)}, u32[]{:S(2)}, u32[]{:S(2)}) collective-permute-start(bf16[2,256,128]{2,1,0:T(8,128)(2,1)S(1)} %get-tuple-element.64), channel_id=1, source_target_pairs={{0,2},{1,3},{2,0},{3,1},{4,6},{5,7},{6,4},{7,5},{8,10},{9,11},{10,... | collective-permute-start | bytes 393224 | tf_op jit(solution)/shard_map/ppermute | solution.py:15
  103.0 7.3 %collective-permute-start.27 = (bf16[2,256,128]{2,1,0:T(8,128)(2,1)S(1)}, bf16[2,256,128]{2,1,0:T(8,128)(2,1)S(1)}, u32[]{:S(2)}, u32[]{:S(2)}) collective-permute-start(bf16[2,256,128]{2,1,0:T(8,128)(2,1)S(1)} %get-tuple-element.63), channel_id=1, source_target_pairs={{0,3},{1,2},{2,1},{3,0},{4,7},{5,6},{6,5},{7,4},{8,11},{9,10},{10,... | collective-permute-start | bytes 393224 | tf_op jit(solution)/shard_map/ppermute | solution.py:15

commit v6 on v5

--- a/solution.py
+++ b/solution.py
@@ -320,7 +320,7 @@
         apply_strips(index_ref[1], (strips, 2), out_ref[...].astype(BF16), store)
 
 
-def second_step_kernel(index_ref, own_ref, ahead_ref, product_ref, first_ref, second_ref, solved_ref, line_ref):
+def second_step_kernel(index_ref, own_ref, ahead_ref, product_ref, first_ref, second_ref, solved_ref):
     row = index_ref[0]
 
     @pl.when(row == 2)
@@ -334,18 +334,15 @@
     def _():
         solved_ref[...] = jnp.zeros_like(solved_ref)
 
-    copy_where(row == 0, own_ref, line_ref)
-    copy_where(row == 4, second_ref, line_ref)
-    copy_where((row != 0) & (row != 4), first_ref, line_ref)
-
-
-def line_kernel(index_ref, own1_ref, own2_ref, z6_ref, z4_ref, z0_ref, out_ref):
-    row = index_ref[0]
-    copy_where(row == 0, z0_ref, out_ref)
-    copy_where(row == 1, own1_ref, out_ref)
-    copy_where((row == 2) | (row == 3), own2_ref, out_ref)
-    copy_where((row == 4) | (row == 7), z4_ref, out_ref)
-    copy_where((row == 5) | (row == 6), z6_ref, out_ref)
+
+def pick_kernel(holders, index_ref, *refs):
+    parts, (out_ref,) = refs[:-1], refs[-1:]
+    for row, part in enumerate(holders):
+        copy_where(index_ref[0] == row, parts[part], out_ref)
+
+
+def pick(index, holders, *parts):
+    return local(functools.partial(pick_kernel, holders), shape_of(parts[0].shape, BF16), [index] + list(parts))
 
 
 def update_either(index_ref, first, strips, value, source_ref, target_ref):
@@ -364,10 +361,10 @@
         target_ref[...] = source_ref[...]
 
 
-def middle_kernel(n_col, index_ref, current_ref, own0_ref, at2_ref, z0_ref, line0_ref, across0_ref, first_ref, line_ref, *refs):
+def middle_kernel(n_col, index_ref, current_ref, own0_ref, at2_ref, fourth_ref, line0_ref, across0_ref, first_ref, line_ref, *refs):
     strips, (out_ref, pieces_ref, known, between) = refs[:n_col], refs[n_col:]
     row = index_ref[0]
-    for holder, part in enumerate((own0_ref, across0_ref, at2_ref, z0_ref, line0_ref, across0_ref, line0_ref, across0_ref)):
+    for holder, part in enumerate((own0_ref, across0_ref, at2_ref, fourth_ref, line0_ref, across0_ref, line0_ref, across0_ref)):
         copy_where(row == holder, part, known)
     subtract(index_ref, (strips, 0), known[...], (row == 1) | (row > 2), current_ref, between)
     update_either(index_ref, lax.rem(row, 2) == 1, strips, line_ref[...], between, out_ref)
@@ -395,16 +392,35 @@
 
 
 def assemble_kernel(n_col, index_ref, *refs):
-    groups, (solved_ref, remaining_ref) = refs[: 2 * n_col], refs[2 * n_col :]
+    groups, (solved_ref, remaining_ref, remaining, sems, last_sem) = refs[: 2 * n_col], refs[2 * n_col :]
     middle, late = groups[:n_col], groups[n_col:]
     chunk = middle[0].shape[2]
     odd = lax.rem(index_ref[0], 2)
-    for f in range(n_col):
-        span = pl.ds(pl.multiple_of((index_ref[1] ^ f) * chunk, chunk), chunk)
-        solved_ref[0, :, span] = middle[f][0]
-        solved_ref[2 - odd, :, span] = middle[f][1]
-        solved_ref[1 + odd, :, span] = late[f][0]
-        remaining_ref[:, span] = late[f][1].astype(F32)
+    spans = [pl.ds(pl.multiple_of((index_ref[1] ^ f) * chunk, chunk), chunk) for f in range(n_col)]
+    copies = []
+    for f, span in enumerate(spans):
+        for part, k in ((middle[f].at[0], 0), (middle[f].at[1], 2 - odd), (late[f].at[0], 1 + odd)):
+            copies.append(pltpu.make_async_copy(part, solved_ref.at[k, :, span], sems.at[len(copies)]))
+            copies[-1].start()
+    for f, span in enumerate(spans):
+        remaining[:, span] = late[f][1].astype(F32)
+    copies.append(pltpu.make_async_copy(remaining, remaining_ref, last_sem))
+    copies[-1].start()
+    for copy in copies:
+        copy.wait()
+
+
+def assemble(index, middle, late, outs):
+    n_col = len(middle)
+    return pl.pallas_call(
+        functools.partial(assemble_kernel, n_col),
+        out_shape=outs,
+        in_specs=[SMEM] + [VMEM] * (2 * n_col),
+        out_specs=(HBM, HBM),
+        scratch_shapes=[pltpu.VMEM(outs[1].shape, F32), pltpu.SemaphoreType.DMA((3 * n_col,)), pltpu.SemaphoreType.DMA],
+        compiler_params=PARAMS,
+        cost_estimate=cost(1),
+    )(index, *middle, *late)
 
 
 def local(kernel, out_shape, operands, scratch=(), us=1):
@@ -449,7 +465,8 @@
     b2 = flip(block, "row", n_row, 2)
     b1 = flip(block, "row", n_row, 1)
     panel = order_panel(index, earlier_panel)
-    b1, b2, again, panel = gate(b1, b2, block, panel)
+    b2, again, panel = gate(b2, block, panel)
+    b4, b1 = gate(b4, b1)
     b6 = flip(again, "row", n_row, 6)
     b3 = flip(b2, "row", n_row, 1)
     b5 = flip(b4, "row", n_row, 1)
@@ -475,19 +492,21 @@
     current, own0, ahead = local(start, (wide, narrow, wide), [index, kept, moved] + slots)
     at2 = hop(own0, (0, 2))
     own1 = local(first_step_kernel, narrow, [index, own0, ahead, product, at1a, at1b])
-    first, second = hop(own1, (1, 2), (0, 6)), hop(own1, (1, 3), (0, 4))
+    first, second = hop(own1, (1, 2), (0, 6)), hop(own1, (1, 3))
+    third, fourth = hop(own1, (0, 4)), hop(own1, (1, 5), (0, 3))
     between = functools.partial(between_kernel, n_col)
     current, ahead = local(between, (wide, wide), [index, current, at2] + slots, us=8)
-    own2, line0 = local(second_step_kernel, (narrow, narrow), [index, own0, ahead, product, first, second])
-    z6 = hop(own2, (2, 6), (3, 5))
+    own2 = local(second_step_kernel, narrow, [index, own0, ahead, product, first, second])
+    z6 = hop(own2, (2, 6))
     z4 = hop(own2, (2, 4), (3, 7))
-    z0 = hop(own2, (2, 0), (0, 3))
+    z0 = hop(own2, (2, 0))
+    line0 = pick(index, (0, 0, 0, 0, 1, 0, 2, 0), own0, third, first)
     across0 = hop(line0, (0, 1), (4, 5), (6, 7))
-    line = local(line_kernel, narrow, [index, own1, own2, z6, z4, z0])
+    line = pick(index, (5, 0, 1, 1, 3, 4, 2, 3), own1, own2, z6, z4, fourth, z0)
     across = flip(line, "row", n_row, 1)
     pieces = shape_of((n_col, 2, strip, chunk), BF16)
     middle = functools.partial(middle_kernel, n_col)
-    parts = [own0, at2, z0, line0, across0, first, line]
+    parts = [own0, at2, fourth, line0, across0, first, line]
     scratch = [pltpu.VMEM((rows, chunk), BF16), pltpu.VMEM((rows, chunk), F32)]
     current, middle = local(middle, (wide, pieces), [index, current] + parts + slots, scratch, us=8)
     middle = swap_pieces(middle, n_col)
@@ -496,7 +515,7 @@
     late = local(finish, pieces, [index, current, across] + slots, [pltpu.VMEM((rows, chunk), F32)])
     late = swap_pieces(late, n_col)
     outs = (shape_of((step_count, strip, nrhs), BF16), shape_of((strip, nrhs), F32))
-    return local(functools.partial(assemble_kernel, n_col), outs, [index] + middle + late)
+    return assemble(index, middle, late, outs)
 
 
 def solution(mesh):

time: 112 us -> 110 us (0.982)
  waiting for transfers between devices: 51.4 us -> 45.3 us
  starting transfers between devices: 37.4 us -> 40.8 us
    ppermute x8 -> x10, waiting for transfers between devices: 17.7 us -> 14.1 us  [hop(): return lax.ppermute(value, 'row', pairs)]
    ppermute x19, waiting for transfers between devices: 33.8 us -> 31.1 us  [flip(): return lax.ppermute(value, axis, [(i, i ^ bit) for i in range(size)])]
    ppermute x19, starting transfers between devices: 29.4 us -> 31.5 us  [flip(): return lax.ppermute(value, axis, [(i, i ^ bit) for i in range(size)])]
    pallas_call x0 -> x1, Pallas kernels: none -> 1.71 us  [assemble(): pl.pallas_call(functools.partial(assemble_kernel, n_col), out_shape=outs,...]
    ppermute x8 -> x10, starting transfers between devices: 7.26 us -> 8.63 us  [hop(): return lax.ppermute(value, 'row', pairs)]
    pallas_call x12, Pallas kernels: 14.8 us -> 13.6 us  [local(): pl.pallas_call(kernel, out_shape=out_shape, in_specs=[SMEM] + [VMEM] * (l...]
  transfers between devices with their start and end apart: 28 -> 30, of which waited for: 14 -> 13; matrix products, arithmetic and copies ran while one was open for 0% -> 0% of each run, Pallas kernels for 13% -> 14%
where the time goes in v6:
time: 110 us
  waiting for transfers between devices  45.3 us (41%)
  starting transfers between devices  40.8 us (37%)
  Pallas kernels  18.4 us (17%)
  local copies, waits for them, and re-layouts  2.27 us (2%)
  other arithmetic  2.25 us (2%)
  between operations  1.11 us (1%)
    ppermute x19, starting transfers between devices, flip(): return lax.ppermute(value, axis, [(i, i ^ bit) for i in range(size)])  31.5 us
    ppermute x19, waiting for transfers between devices, flip(): return lax.ppermute(value, axis, [(i, i ^ bit) for i in range(size)])  31.1 us
    ppermute x10, waiting for transfers between devices, hop(): return lax.ppermute(value, 'row', pairs)  14.1 us
    pallas_call x12, Pallas kernels, local(): pl.pallas_call(kernel, out_shape=out_shape, in_specs=[SMEM] + [VMEM] * (l...  13.6 us
    ppermute x10, starting transfers between devices, hop(): return lax.ppermute(value, 'row', pairs)  8.63 us
    pallas_call x1, Pallas kernels, order_panel(): pl.pallas_call(order_kernel, out_shape=shape_of((rows, sources * width),...  3.08 us
  transfers between devices with their start and end apart: 30, of which 13 were waited for; matrix products, arithmetic and copies ran while one was open for 0% of the time, Pallas kernels for 14%

profile of v6, /device:TPU:25, one launch (start us, length us, event | category | flops | bytes accessed | tf_op | source)
XLA Modules:
  0.0 110.1 jit_solution(3037234055366878240)
XLA Ops:
  0.6 2.0 %bitcast_select_fusion.2 = (bf16[1,256,1024]{2,1,0:T(8,128)(2,1)S(1)}, bf16[1,256,1024]{2,1,0:T(8,128)(2,1)S(1)}, bf16[1,256,1024]{2,1,0:T(8,128)(2,1)S(1)}) fusion(bf16[256,3,1024]{2,0,1:T(8,128)(2,1)} %param.8, pred[]{:T(512)S(6)} %eq.10, bf16[3,256,1024]{2,1,0:T(8,128)(2,1)} %param.9, pred[]{:T(512)S(6)} %eq.12, pred[]{:T(512)S(6)} %eq.11), kind=kLoop, calls=%fused_computation.4 | loop fusion | flops 1048576 | bytes 4718595 | tf_op jit(solution)/shard_map/jit(_where)/select_n | solution.py:461
  2.6 0.0 copy-start.2
  2.7 0.2 pad_maximum_fusion.refs_0_
  2.8 1.3 %collective-permute-start.8 = (bf16[3,256,1024]{2,1,0:T(8,128)(2,1)S(1)}, bf16[3,256,1024]{2,1,0:T(8,128)(2,1)S(1)}, u32[]{:S(2)}, u32[]{:S(2)}) collective-permute-start(bf16[3,256,1024]{2,1,0:T(8,128)(2,1)S(1)} %pad_maximum_fusion.refs_0_), channel_id=1, source_target_pairs={{0,2},{1,3},{2,0},{3,1},{4,6},{5,7},{6,4},{7,5},{8,10},{9,11},{10,... | collective-permute-start | bytes 4718600 | tf_op jit(solution)/shard_map/ppermute | solution.py:15
  4.1 0.2 collective-permute-start
  4.3 0.1 collective-permute-start.1
  4.3 1.2 %collective-permute-start.2 = (bf16[256,512]{1,0:T(8,128)(2,1)S(1)}, bf16[256,512]{1,0:T(8,128)(2,1)}, u32[]{:S(2)}, u32[]{:S(2)}) collective-permute-start(bf16[256,512]{1,0:T(8,128)(2,1)S(1)} %bitcast.29), channel_id=1, source_target_pairs={{0,4},{4,0},{8,12},{12,8},{16,20},{20,16},{24,28},{28,24},{1,5},{5... | collective-permute-start | bytes 786440 | tf_op jit(solution)/shard_map/ppermute | solution.py:15
  5.6 0.1 pad_add_fusion.index_ref
  5.7 2.2 %copy-done = bf16[1024,8,256]{2,1,0:T(8,128)(2,1)S(1)} copy-done((bf16[1024,8,256]{2,1,0:T(8,128)(2,1)S(1)}, bf16[1024,8,256]{2,1,0:T(8,128)(2,1)}, u32[]{:S(2)}) %copy-start) | copy-done | bytes 4194328
  7.8 3.1 %shard_map.68.panel_ref = bf16[1024,2048]{1,0:T(8,128)(2,1)S(1)} custom-call(s32[2]{0:T(128)S(1)} %pad_add_fusion.index_ref, bf16[1024,8,256]{2,1,0:T(8,128)(2,1)S(1)} %copy-done), custom_call_target="tpu_custom_call" | custom-call | bytes 28800000 | tf_op jit(solution)/shard_map/pallas_call | solution.py:154
  10.9 4.8 %collective-permute-done.refs_2_ = bf16[256,512]{1,0:T(8,128)(2,1)} collective-permute-done((bf16[256,512]{1,0:T(8,128)(2,1)S(1)}, bf16[256,512]{1,0:T(8,128)(2,1)}, u32[]{:S(2)}, u32[]{:S(2)}) %collective-permute-start) | collective-permute-done | bytes 262176 | tf_op jit(solution)/shard_map/ppermute | solution.py:15
  15.7 0.8 collective-permute-start.5
  16.5 1.2 %collective-permute-start.3 = (bf16[256,512]{1,0:T(8,128)(2,1)}, bf16[256,512]{1,0:T(8,128)(2,1)S(1)}, u32[]{:S(2)}, u32[]{:S(2)}) collective-permute-start(bf16[256,512]{1,0:T(8,128)(2,1)} %collective-permute-done.refs_2_), channel_id=1, source_target_pairs={{0,4},{4,0},{8,12},{12,8},{16,20},{20,16},{24,28},{28,24},{1,5},{5... | collective-permute-start | bytes 786440 | tf_op jit(solution)/shard_map/ppermute | solution.py:15
  17.8 0.2 collective-permute-start.4
  18.0 5.8 %collective-permute-done.5.refs_6_ = bf16[256,512]{1,0:T(8,128)(2,1)S(1)} collective-permute-done((bf16[256,512]{1,0:T(8,128)(2,1)S(1)}, bf16[256,512]{1,0:T(8,128)(2,1)S(1)}, u32[]{:S(2)}, u32[]{:S(2)}) %collective-permute-start.5) | collective-permute-done | bytes 262176 | tf_op jit(solution)/shard_map/ppermute | solution.py:15
  23.8 1.2 %collective-permute-start.6 = (bf16[256,512]{1,0:T(8,128)(2,1)S(1)}, bf16[256,512]{1,0:T(8,128)(2,1)S(1)}, u32[]{:S(2)}, u32[]{:S(2)}) collective-permute-start(bf16[256,512]{1,0:T(8,128)(2,1)S(1)} %collective-permute-done.5.refs_6_), channel_id=1, source_target_pairs={{0,4},{4,0},{8,12},{12,8},{16,20},{20,16},{24,28},{28,24},{1,5},{5... | collective-permute-start | bytes 786440 | tf_op jit(solution)/shard_map/ppermute | solution.py:15
  25.0 0.0 collective-permute-done.3.refs_3_
  25.0 0.2 collective-permute-done.4.refs_5_
  25.2 3.3 %shard_map.69.total_ref = f32[1024,512]{1,0:T(8,128)S(1)} custom-call(s32[2]{0:T(128)S(1)} %pad_add_fusion.index_ref, bf16[1024,2048]{1,0:T(8,128)(2,1)S(1)} %shard_map.68.panel_ref, f32[256,512]{1,0:T(8,128)S(1)} %copy-done.1, bf16[256,512]{1,0:T(8,128)(2,1)S(1)} %bitcast.31, bf16[256,512]{1,0:T(8,128)(2,1)} %collective-permute-done.2.refs_1_, ...), custom_call_target="tpu_custom_call" | custom-call | bytes 28800000 | tf_op jit(solution)/shard_map/pallas_call | solution.py:428
  28.4 0.8 collective-permute-done.6.block_ref
  29.3 1.7 %shard_map.70 = (f32[2,1024,128]{2,1,0:T(8,128)S(1)}, bf16[2,1024,128]{2,1,0:T(8,128)(2,1)S(1)}) custom-call(s32[2]{0:T(128)S(1)} %pad_add_fusion.index_ref, bf16[1024,2048]{1,0:T(8,128)(2,1)S(1)} %shard_map.68.panel_ref, bf16[256,512]{1,0:T(8,128)(2,1)S(1)} %collective-permute-done.6.block_ref, f32[1024,512]{1,0:T(8,128)S(1)} %shard_map.69.total_ref), custom_call_target="tpu_custom_call" | custom-call | bytes 3600000 | tf_op jit(solution)/shard_map/pallas_call | solution.py:428
  31.0 9.9 %collective-permute-start.7 = (bf16[2,1024,128]{2,1,0:T(8,128)(2,1)S(1)}, bf16[2,1024,128]{2,1,0:T(8,128)(2,1)S(1)}, u32[]{:S(2)}, u32[]{:S(2)}) collective-permute-start(bf16[2,1024,128]{2,1,0:T(8,128)(2,1)S(1)} %get-tuple-element.38), channel_id=1, source_target_pairs={{0,1},{1,0},{2,3},{3,2},{4,5},{5,4},{6,7},{7,6},{8,9},{9,8},{10,11... | collective-permute-start | bytes 1572872 | tf_op jit(solution)/shard_map/ppermute | solution.py:15
  41.0 0.1 collective-permute-start.9
  41.0 1.5 %collective-permute-done.7.moved_ref = bf16[2,1024,128]{2,1,0:T(8,128)(2,1)S(1)} collective-permute-done((bf16[2,1024,128]{2,1,0:T(8,128)(2,1)S(1)}, bf16[2,1024,128]{2,1,0:T(8,128)(2,1)S(1)}, u32[]{:S(2)}, u32[]{:S(2)}) %collective-permute-start.7) | collective-permute-done | bytes 524320 | tf_op jit(solution)/shard_map/ppermute | solution.py:15
  42.5 0.0 collective-permute-done.8.refs_2_
  42.5 0.4 collective-permute-start.10
  42.9 0.7 shard_map.71
  43.6 0.1 collective-permute-start.11
  43.6 0.7 collective-permute-start.12
  44.3 0.7 collective-permute-start.13
  45.0 2.0 %collective-permute-done.10.refs_3_ = bf16[3,256,1024]{2,1,0:T(8,128)(2,1)S(1)} collective-permute-done((bf16[3,256,1024]{2,1,0:T(8,128)(2,1)S(1)}, bf16[3,256,1024]{2,1,0:T(8,128)(2,1)S(1)}, u32[]{:S(2)}, u32[]{:S(2)}) %collective-permute-start.10) | collective-permute-done | bytes 1572896 | tf_op jit(solution)/shard_map/ppermute | solution.py:15
  47.0 0.7 shard_map.72.product_ref
  47.7 3.7 %collective-permute-done.11.moved_ref = bf16[1024,128]{1,0:T(8,128)(2,1)S(1)} collective-permute-done((bf16[1024,128]{1,0:T(8,128)(2,1)S(1)}, bf16[1024,128]{1,0:T(8,128)(2,1)S(1)}, u32[]{:S(2)}, u32[]{:S(2)}) %collective-permute-start.11) | collective-permute-done | bytes 262176 | tf_op jit(solution)/shard_map/ppermute | solution.py:15
  51.4 0.8 shard_map.73
  52.2 0.7 collective-permute-start.14
  52.9 0.6 shard_map.74.refs_0_
  53.5 1.3 %collective-permute-start.15 = (bf16[1024,128]{1,0:T(8,128)(2,1)S(1)}, bf16[1024,128]{1,0:T(8,128)(2,1)S(1)}, u32[]{:S(2)}, u32[]{:S(2)}) collective-permute-start(bf16[1024,128]{1,0:T(8,128)(2,1)S(1)} %shard_map.74.refs_0_), channel_id=1, source_target_pairs={{4,8},{0,24},{5,9},{1,25},{6,10},{2,26},{7,11},{3,27}} | collective-permute-start | bytes 786440 | tf_op jit(solution)/shard_map/ppermute | solution.py:440
  54.8 0.7 collective-permute-start.16
  55.5 0.7 collective-permute-start.22
  56.2 0.7 collective-permute-start.19
  56.9 0.6 shard_map.75
  57.5 9.3 %collective-permute-done.15.first_ref.refs_2_ = bf16[1024,128]{1,0:T(8,128)(2,1)S(1)} collective-permute-done((bf16[1024,128]{1,0:T(8,128)(2,1)S(1)}, bf16[1024,128]{1,0:T(8,128)(2,1)S(1)}, u32[]{:S(2)}, u32[]{:S(2)}) %collective-permute-start.15) | collective-permute-done | bytes 262176 | tf_op jit(solution)/shard_map/ppermute | solution.py:440
  66.9 0.6 shard_map.76.refs_1_
  67.5 1.3 %collective-permute-start.17 = (bf16[1024,128]{1,0:T(8,128)(2,1)S(1)}, bf16[1024,128]{1,0:T(8,128)(2,1)S(1)}, u32[]{:S(2)}, u32[]{:S(2)}) collective-permute-start(bf16[1024,128]{1,0:T(8,128)(2,1)S(1)} %shard_map.76.refs_1_), channel_id=1, source_target_pairs={{8,24},{9,25},{10,26},{11,27}} | collective-permute-start | bytes 786440 | tf_op jit(solution)/shard_map/ppermute | solution.py:440
  68.8 0.7 collective-permute-start.18
  69.4 0.7 collective-permute-start.20
  70.1 0.6 shard_map.78.line0_ref
  70.8 1.3 %collective-permute-start.23 = (bf16[1024,128]{1,0:T(8,128)(2,1)S(1)}, bf16[1024,128]{1,0:T(8,128)(2,1)S(1)}, u32[]{:S(2)}, u32[]{:S(2)}) collective-permute-start(bf16[1024,128]{1,0:T(8,128)(2,1)S(1)} %shard_map.78.line0_ref), channel_id=1, source_target_pairs={{0,4},{16,20},{24,28},{1,5},{17,21},{25,29},{2,6},{18,22},{26,30},... | collective-permute-start | bytes 786440 | tf_op jit(solution)/shard_map/ppermute | solution.py:440
  72.1 4.8 %collective-permute-done.17.refs_2_ = bf16[1024,128]{1,0:T(8,128)(2,1)S(1)} collective-permute-done((bf16[1024,128]{1,0:T(8,128)(2,1)S(1)}, bf16[1024,128]{1,0:T(8,128)(2,1)S(1)}, u32[]{:S(2)}, u32[]{:S(2)}) %collective-permute-start.17) | collective-permute-done | bytes 262176 | tf_op jit(solution)/shard_map/ppermute | solution.py:440
  76.9 0.6 shard_map.77.line_ref
  77.5 9.4 %collective-permute-start.21 = (bf16[1024,128]{1,0:T(8,128)(2,1)S(1)}, bf16[1024,128]{1,0:T(8,128)(2,1)S(1)}, u32[]{:S(2)}, u32[]{:S(2)}) collective-permute-start(bf16[1024,128]{1,0:T(8,128)(2,1)S(1)} %shard_map.77.line_ref), channel_id=1, source_target_pairs={{0,4},{4,0},{8,12},{12,8},{16,20},{20,16},{24,28},{28,24},{1,5},{5... | collective-permute-start | bytes 786440 | tf_op jit(solution)/shard_map/ppermute | solution.py:15
  86.9 2.1 %shard_map.79 = (f32[1024,128]{1,0:T(8,128)S(1)}, bf16[4,2,256,128]{3,2,1,0:T(8,128)(2,1)S(1)}) custom-call(s32[2]{0:T(128)S(1)} %pad_add_fusion.index_ref, f32[1024,128]{1,0:T(8,128)S(1)} %get-tuple-element.50.current_ref, bf16[1024,128]{1,0:T(8,128)(2,1)S(1)} %get-tuple-element.44.own_ref.refs_0_.own0_ref, ...), custom_call_target="tpu_custom_call" | custom-call | bytes 28800000 | tf_op jit(solution)/shard_map/pallas_call | solution.py:428
  89.1 1.4 %collective-permute-start.24 = (bf16[2,256,128]{2,1,0:T(8,128)(2,1)S(1)}, bf16[2,256,128]{2,1,0:T(8,128)(2,1)S(1)}, u32[]{:S(2)}, u32[]{:S(2)}) collective-permute-start(bf16[2,256,128]{2,1,0:T(8,128)(2,1)S(1)} %get-tuple-element.67), channel_id=1, source_target_pairs={{0,1},{1,0},{2,3},{3,2},{4,5},{5,4},{6,7},{7,6},{8,9},{9,8},{10,11... | collective-permute-start | bytes 393224 | tf_op jit(solution)/shard_map/ppermute | solution.py:15
  90.4 0.8 collective-permute-start.25
  91.2 0.9 collective-permute-start.26
  92.2 3.4 %collective-permute-done.25.refs_2_ = bf16[2,256,128]{2,1,0:T(8,128)(2,1)S(1)} collective-permute-done((bf16[2,256,128]{2,1,0:T(8,128)(2,1)S(1)}, bf16[2,256,128]{2,1,0:T(8,128)(2,1)S(1)}, u32[]{:S(2)}, u32[]{:S(2)}) %collective-permute-start.25) | collective-permute-done | bytes 131104 | tf_op jit(solution)/shard_map/ppermute | solution.py:15
  95.5 3.0 %collective-permute-done.26.refs_3_ = bf16[2,256,128]{2,1,0:T(8,128)(2,1)S(1)} collective-permute-done((bf16[2,256,128]{2,1,0:T(8,128)(2,1)S(1)}, bf16[2,256,128]{2,1,0:T(8,128)(2,1)S(1)}, u32[]{:S(2)}, u32[]{:S(2)}) %collective-permute-start.26) | collective-permute-done | bytes 131104 | tf_op jit(solution)/shard_map/ppermute | solution.py:15
  98.5 1.3 %shard_map.80 = bf16[4,2,256,128]{3,2,1,0:T(8,128)(2,1)S(1)} custom-call(s32[2]{0:T(128)S(1)} %pad_add_fusion.index_ref, f32[1024,128]{1,0:T(8,128)S(1)} %get-tuple-element.56.current_ref, bf16[1024,128]{1,0:T(8,128)(2,1)S(1)} %collective-permute-done.21.value_ref, bf16[3,256,1024]{2,1,0:T(8,128)(2,1)S(1)} %pad_maximum_fusion.refs_0_, ...), custom_call_target="tpu_custom_call" | custom-call | bytes 3600000 | tf_op jit(solution)/shard_map/pallas_call | solution.py:428
  99.9 0.3 collective-permute-start.27
  100.2 0.8 collective-permute-start.28
  101.0 1.1 %collective-permute-start.29 = (bf16[2,256,128]{2,1,0:T(8,128)(2,1)S(1)}, bf16[2,256,128]{2,1,0:T(8,128)(2,1)S(1)}, u32[]{:S(2)}, u32[]{:S(2)}) collective-permute-start(bf16[2,256,128]{2,1,0:T(8,128)(2,1)S(1)} %get-tuple-element.61), channel_id=1, source_target_pairs={{0,3},{1,2},{2,1},{3,0},{4,7},{5,6},{6,5},{7,4},{8,11},{9,10},{10,... | collective-permute-start | bytes 393224 | tf_op jit(solution)/shard_map/ppermute | solution.py:15
  102.1 2.9 %collective-permute-done.28.refs_6_ = bf16[2,256,128]{2,1,0:T(8,128)(2,1)S(1)} collective-permute-done((bf16[2,256,128]{2,1,0:T(8,128)(2,1)S(1)}, bf16[2,256,128]{2,1,0:T(8,128)(2,1)S(1)}, u32[]{:S(2)}, u32[]{:S(2)}) %collective-permute-start.28) | collective-permute-done | bytes 131104 | tf_op jit(solution)/shard_map/ppermute | solution.py:15
  105.0 3.2 %collective-permute-done.29.refs_7_ = bf16[2,256,128]{2,1,0:T(8,128)(2,1)S(1)} collective-permute-done((bf16[2,256,128]{2,1,0:T(8,128)(2,1)S(1)}, bf16[2,256,128]{2,1,0:T(8,128)(2,1)S(1)}, u32[]{:S(2)}, u32[]{:S(2)}) %collective-permute-start.29) | collective-permute-done | bytes 131104 | tf_op jit(solution)/shard_map/ppermute | solution.py:15
  108.2 1.7 %shard_map.81 = (bf16[3,256,512]{2,1,0:T(8,128)(2,1)}, f32[256,512]{1,0:T(8,128)}) custom-call(s32[2]{0:T(128)S(1)} %pad_add_fusion.index_ref, bf16[2,256,128]{2,1,0:T(8,128)(2,1)S(1)} %get-tuple-element.52.refs_0_, bf16[2,256,128]{2,1,0:T(8,128)(2,1)S(1)} %collective-permute-done.24.refs_1_, bf16[2,256,128]{2,1,0:T(8,128)(2,1)S(1)} %collective-permute-done.25.refs_2_, ...), custom_call_target="tpu_custom_call" | custom-call | bytes 3600000 | tf_op jit(solution)/shard_map/pallas_call | solution.py:415
  (21 shorter events, 0.1 us)
Async XLA Ops:
  2.6 1.5 %copy-start.2 = (bf16[1,256,512]{2,1,0:T(8,128)(2,1)S(1)}, bf16[1,256,512]{2,1,0:T(8,128)(2,1)}, u32[]{:S(2)}) copy-start(bf16[1,256,512]{2,1,0:T(8,128)(2,1)} %param.7) | copy-start | bytes 786436
  2.8 39.7 %collective-permute-start.8 = (bf16[3,256,1024]{2,1,0:T(8,128)(2,1)S(1)}, bf16[3,256,1024]{2,1,0:T(8,128)(2,1)S(1)}, u32[]{:S(2)}, u32[]{:S(2)}) collective-permute-start(bf16[3,256,1024]{2,1,0:T(8,128)(2,1)S(1)} %pad_maximum_fusion.refs_0_), channel_id=1, source_target_pairs={{0,2},{1,3},{2,0},{3,1},{4,6},{5,7},{6,4},{7,5},{8,10},{9,11},{10,... | collective-permute-start | bytes 4718600 | tf_op jit(solution)/shard_map/ppermute | solution.py:15
  4.1 11.6 %collective-permute-start = (bf16[256,512]{1,0:T(8,128)(2,1)S(1)}, bf16[256,512]{1,0:T(8,128)(2,1)}, u32[]{:S(2)}, u32[]{:S(2)}) collective-permute-start(bf16[256,512]{1,0:T(8,128)(2,1)S(1)} %bitcast.27), channel_id=1, source_target_pairs={{0,8},{4,12},{8,0},{12,4},{16,24},{20,28},{24,16},{28,20},{1,9},{5... | collective-permute-start | bytes 786440 | tf_op jit(solution)/shard_map/ppermute | solution.py:15
  4.3 12.2 %collective-permute-start.1 = (bf16[256,512]{1,0:T(8,128)(2,1)S(1)}, bf16[256,512]{1,0:T(8,128)(2,1)}, u32[]{:S(2)}, u32[]{:S(2)}) collective-permute-start(bf16[256,512]{1,0:T(8,128)(2,1)S(1)} %bitcast.28), channel_id=1, source_target_pairs={{0,16},{4,20},{8,24},{12,28},{16,0},{20,4},{24,8},{28,12},{1,17},{... | collective-permute-start | bytes 786440 | tf_op jit(solution)/shard_map/ppermute | solution.py:15
  4.3 12.2 %collective-permute-start.2 = (bf16[256,512]{1,0:T(8,128)(2,1)S(1)}, bf16[256,512]{1,0:T(8,128)(2,1)}, u32[]{:S(2)}, u32[]{:S(2)}) collective-permute-start(bf16[256,512]{1,0:T(8,128)(2,1)S(1)} %bitcast.29), channel_id=1, source_target_pairs={{0,4},{4,0},{8,12},{12,8},{16,20},{20,16},{24,28},{28,24},{1,5},{5... | collective-permute-start | bytes 786440 | tf_op jit(solution)/shard_map/ppermute | solution.py:15
  5.7 2.2 %copy-start = (bf16[1024,8,256]{2,1,0:T(8,128)(2,1)S(1)}, bf16[1024,8,256]{2,1,0:T(8,128)(2,1)}, u32[]{:S(2)}) copy-start(bf16[1024,8,256]{2,1,0:T(8,128)(2,1)} %panel_ref.1) | copy-start | bytes 12582916
  7.8 17.3 %copy-start.1 = (f32[256,512]{1,0:T(8,128)S(1)}, f32[256,512]{1,0:T(8,128)}, u32[]{:S(2)}) copy-start(f32[256,512]{1,0:T(8,128)} %side_ref.1) | copy-start | bytes 1572868
  15.7 8.1 %collective-permute-start.5 = (bf16[256,512]{1,0:T(8,128)(2,1)S(1)}, bf16[256,512]{1,0:T(8,128)(2,1)S(1)}, u32[]{:S(2)}, u32[]{:S(2)}) collective-permute-start(bf16[256,512]{1,0:T(8,128)(2,1)S(1)} %bitcast.30), channel_id=1, source_target_pairs={{0,24},{4,28},{8,16},{12,20},{16,8},{20,12},{24,0},{28,4},{1,25},{... | collective-permute-start | bytes 786440 | tf_op jit(solution)/shard_map/ppermute | solution.py:15
  16.5 8.5 %collective-permute-start.3 = (bf16[256,512]{1,0:T(8,128)(2,1)}, bf16[256,512]{1,0:T(8,128)(2,1)S(1)}, u32[]{:S(2)}, u32[]{:S(2)}) collective-permute-start(bf16[256,512]{1,0:T(8,128)(2,1)} %collective-permute-done.refs_2_), channel_id=1, source_target_pairs={{0,4},{4,0},{8,12},{12,8},{16,20},{20,16},{24,28},{28,24},{1,5},{5... | collective-permute-start | bytes 786440 | tf_op jit(solution)/shard_map/ppermute | solution.py:15
  17.8 7.4 %collective-permute-start.4 = (bf16[256,512]{1,0:T(8,128)(2,1)}, bf16[256,512]{1,0:T(8,128)(2,1)S(1)}, u32[]{:S(2)}, u32[]{:S(2)}) collective-permute-start(bf16[256,512]{1,0:T(8,128)(2,1)} %collective-permute-done.1.refs_4_), channel_id=1, source_target_pairs={{0,4},{4,0},{8,12},{12,8},{16,20},{20,16},{24,28},{28,24},{1,5},{5... | collective-permute-start | bytes 786440 | tf_op jit(solution)/shard_map/ppermute | solution.py:15
  23.8 5.5 %collective-permute-start.6 = (bf16[256,512]{1,0:T(8,128)(2,1)S(1)}, bf16[256,512]{1,0:T(8,128)(2,1)S(1)}, u32[]{:S(2)}, u32[]{:S(2)}) collective-permute-start(bf16[256,512]{1,0:T(8,128)(2,1)S(1)} %collective-permute-done.5.refs_6_), channel_id=1, source_target_pairs={{0,4},{4,0},{8,12},{12,8},{16,20},{20,16},{24,28},{28,24},{1,5},{5... | collective-permute-start | bytes 786440 | tf_op jit(solution)/shard_map/ppermute | solution.py:15
  31.0 11.5 %collective-permute-start.7 = (bf16[2,1024,128]{2,1,0:T(8,128)(2,1)S(1)}, bf16[2,1024,128]{2,1,0:T(8,128)(2,1)S(1)}, u32[]{:S(2)}, u32[]{:S(2)}) collective-permute-start(bf16[2,1024,128]{2,1,0:T(8,128)(2,1)S(1)} %get-tuple-element.38), channel_id=1, source_target_pairs={{0,1},{1,0},{2,3},{3,2},{4,5},{5,4},{6,7},{7,6},{8,9},{9,8},{10,11... | collective-permute-start | bytes 1572872 | tf_op jit(solution)/shard_map/ppermute | solution.py:15
  41.0 4.0 %collective-permute-start.9 = (bf16[3,256,1024]{2,1,0:T(8,128)(2,1)S(1)}, bf16[3,256,1024]{2,1,0:T(8,128)(2,1)S(1)}, u32[]{:S(2)}, u32[]{:S(2)}) collective-permute-start(bf16[3,256,1024]{2,1,0:T(8,128)(2,1)S(1)} %pad_maximum_fusion.refs_0_), channel_id=1, source_target_pairs={{0,1},{1,0},{2,3},{3,2},{4,5},{5,4},{6,7},{7,6},{8,9},{9,8},{10,11... | collective-permute-start | bytes 4718600 | tf_op jit(solution)/shard_map/ppermute | solution.py:15
  42.5 4.5 %collective-permute-start.10 = (bf16[3,256,1024]{2,1,0:T(8,128)(2,1)S(1)}, bf16[3,256,1024]{2,1,0:T(8,128)(2,1)S(1)}, u32[]{:S(2)}, u32[]{:S(2)}) collective-permute-start(bf16[3,256,1024]{2,1,0:T(8,128)(2,1)S(1)} %collective-permute-done.8.refs_2_), channel_id=1, source_target_pairs={{0,1},{1,0},{2,3},{3,2},{4,5},{5,4},{6,7},{7,6},{8,9},{9,8},{10,11... | collective-permute-start | bytes 4718600 | tf_op jit(solution)/shard_map/ppermute | solution.py:15
  43.6 7.8 %collective-permute-start.11 = (bf16[1024,128]{1,0:T(8,128)(2,1)S(1)}, bf16[1024,128]{1,0:T(8,128)(2,1)S(1)}, u32[]{:S(2)}, u32[]{:S(2)}) collective-permute-start(bf16[1024,128]{1,0:T(8,128)(2,1)S(1)} %get-tuple-element.43), channel_id=1, source_target_pairs={{0,2},{1,3},{2,0},{3,1},{4,6},{5,7},{6,4},{7,5},{8,10},{9,11},{10,... | collective-permute-start | bytes 786440 | tf_op jit(solution)/shard_map/ppermute | solution.py:15
  43.6 9.3 %collective-permute-start.12 = (bf16[1024,128]{1,0:T(8,128)(2,1)S(1)}, bf16[1024,128]{1,0:T(8,128)(2,1)S(1)}, u32[]{:S(2)}, u32[]{:S(2)}) collective-permute-start(bf16[1024,128]{1,0:T(8,128)(2,1)S(1)} %get-tuple-element.47), channel_id=1, source_target_pairs={{0,4},{1,5},{2,6},{3,7}} | collective-permute-start | bytes 786440 | tf_op jit(solution)/shard_map/ppermute | solution.py:440
  44.3 8.6 %collective-permute-start.13 = (bf16[1024,128]{1,0:T(8,128)(2,1)S(1)}, bf16[1024,128]{1,0:T(8,128)(2,1)S(1)}, u32[]{:S(2)}, u32[]{:S(2)}) collective-permute-start(bf16[1024,128]{1,0:T(8,128)(2,1)S(1)} %get-tuple-element.43), channel_id=1, source_target_pairs={{0,6},{1,7},{2,4},{3,5}} | collective-permute-start | bytes 786440 | tf_op jit(solution)/shard_map/ppermute | solution.py:485
  52.2 4.7 %collective-permute-start.14 = (bf16[1024,128]{1,0:T(8,128)(2,1)S(1)}, bf16[1024,128]{1,0:T(8,128)(2,1)S(1)}, u32[]{:S(2)}, u32[]{:S(2)}) collective-permute-start(bf16[1024,128]{1,0:T(8,128)(2,1)S(1)} %get-tuple-element.44.own_ref.refs_0_.own0_ref), channel_id=1, source_target_pairs={{0,8},{1,9},{2,10},{3,11}} | collective-permute-start | bytes 786440 | tf_op jit(solution)/shard_map/ppermute | solution.py:440
  53.5 13.3 %collective-permute-start.15 = (bf16[1024,128]{1,0:T(8,128)(2,1)S(1)}, bf16[1024,128]{1,0:T(8,128)(2,1)S(1)}, u32[]{:S(2)}, u32[]{:S(2)}) collective-permute-start(bf16[1024,128]{1,0:T(8,128)(2,1)S(1)} %shard_map.74.refs_0_), channel_id=1, source_target_pairs={{4,8},{0,24},{5,9},{1,25},{6,10},{2,26},{7,11},{3,27}} | collective-permute-start | bytes 786440 | tf_op jit(solution)/shard_map/ppermute | solution.py:440
  54.8 12.0 %collective-permute-start.16 = (bf16[1024,128]{1,0:T(8,128)(2,1)S(1)}, bf16[1024,128]{1,0:T(8,128)(2,1)S(1)}, u32[]{:S(2)}, u32[]{:S(2)}) collective-permute-start(bf16[1024,128]{1,0:T(8,128)(2,1)S(1)} %shard_map.74.refs_0_), channel_id=1, source_target_pairs={{4,12},{5,13},{6,14},{7,15}} | collective-permute-start | bytes 786440 | tf_op jit(solution)/shard_map/ppermute | solution.py:440
  55.5 14.6 %collective-permute-start.22 = (bf16[1024,128]{1,0:T(8,128)(2,1)S(1)}, bf16[1024,128]{1,0:T(8,128)(2,1)S(1)}, u32[]{:S(2)}, u32[]{:S(2)}) collective-permute-start(bf16[1024,128]{1,0:T(8,128)(2,1)S(1)} %shard_map.74.refs_0_), channel_id=1, source_target_pairs={{0,16},{1,17},{2,18},{3,19}} | collective-permute-start | bytes 786440 | tf_op jit(solution)/shard_map/ppermute | solution.py:440
  56.2 15.9 %collective-permute-start.19 = (bf16[1024,128]{1,0:T(8,128)(2,1)S(1)}, bf16[1024,128]{1,0:T(8,128)(2,1)S(1)}, u32[]{:S(2)}, u32[]{:S(2)}) collective-permute-start(bf16[1024,128]{1,0:T(8,128)(2,1)S(1)} %shard_map.74.refs_0_), channel_id=1, source_target_pairs={{4,20},{0,12},{5,21},{1,13},{6,22},{2,14},{7,23},{3,15}} | collective-permute-start | bytes 786440 | tf_op jit(solution)/shard_map/ppermute | solution.py:440
  67.5 9.4 %collective-permute-start.17 = (bf16[1024,128]{1,0:T(8,128)(2,1)S(1)}, bf16[1024,128]{1,0:T(8,128)(2,1)S(1)}, u32[]{:S(2)}, u32[]{:S(2)}) collective-permute-start(bf16[1024,128]{1,0:T(8,128)(2,1)S(1)} %shard_map.76.refs_1_), channel_id=1, source_target_pairs={{8,24},{9,25},{10,26},{11,27}} | collective-permute-start | bytes 786440 | tf_op jit(solution)/shard_map/ppermute | solution.py:440
  68.8 8.1 %collective-permute-start.18 = (bf16[1024,128]{1,0:T(8,128)(2,1)S(1)}, bf16[1024,128]{1,0:T(8,128)(2,1)S(1)}, u32[]{:S(2)}, u32[]{:S(2)}) collective-permute-start(bf16[1024,128]{1,0:T(8,128)(2,1)S(1)} %shard_map.76.refs_1_), channel_id=1, source_target_pairs={{8,16},{12,28},{9,17},{13,29},{10,18},{14,30},{11,19},{15,31}} | collective-permute-start | bytes 786440 | tf_op jit(solution)/shard_map/ppermute | solution.py:440
  69.4 7.4 %collective-permute-start.20 = (bf16[1024,128]{1,0:T(8,128)(2,1)S(1)}, bf16[1024,128]{1,0:T(8,128)(2,1)S(1)}, u32[]{:S(2)}, u32[]{:S(2)}) collective-permute-start(bf16[1024,128]{1,0:T(8,128)(2,1)S(1)} %shard_map.76.refs_1_), channel_id=1, source_target_pairs={{8,0},{9,1},{10,2},{11,3}} | collective-permute-start | bytes 786440 | tf_op jit(solution)/shard_map/ppermute | solution.py:440
  70.8 16.2 %collective-permute-start.23 = (bf16[1024,128]{1,0:T(8,128)(2,1)S(1)}, bf16[1024,128]{1,0:T(8,128)(2,1)S(1)}, u32[]{:S(2)}, u32[]{:S(2)}) collective-permute-start(bf16[1024,128]{1,0:T(8,128)(2,1)S(1)} %shard_map.78.line0_ref), channel_id=1, source_target_pairs={{0,4},{16,20},{24,28},{1,5},{17,21},{25,29},{2,6},{18,22},{26,30},... | collective-permute-start | bytes 786440 | tf_op jit(solution)/shard_map/ppermute | solution.py:440
  77.5 21.0 %collective-permute-start.21 = (bf16[1024,128]{1,0:T(8,128)(2,1)S(1)}, bf16[1024,128]{1,0:T(8,128)(2,1)S(1)}, u32[]{:S(2)}, u32[]{:S(2)}) collective-permute-start(bf16[1024,128]{1,0:T(8,128)(2,1)S(1)} %shard_map.77.line_ref), channel_id=1, source_target_pairs={{0,4},{4,0},{8,12},{12,8},{16,20},{20,16},{24,28},{28,24},{1,5},{5... | collective-permute-start | bytes 786440 | tf_op jit(solution)/shard_map/ppermute | solution.py:15
  89.1 3.1 %collective-permute-start.24 = (bf16[2,256,128]{2,1,0:T(8,128)(2,1)S(1)}, bf16[2,256,128]{2,1,0:T(8,128)(2,1)S(1)}, u32[]{:S(2)}, u32[]{:S(2)}) collective-permute-start(bf16[2,256,128]{2,1,0:T(8,128)(2,1)S(1)} %get-tuple-element.67), channel_id=1, source_target_pairs={{0,1},{1,0},{2,3},{3,2},{4,5},{5,4},{6,7},{7,6},{8,9},{9,8},{10,11... | collective-permute-start | bytes 393224 | tf_op jit(solution)/shard_map/ppermute | solution.py:15
  90.4 5.1 %collective-permute-start.25 = (bf16[2,256,128]{2,1,0:T(8,128)(2,1)S(1)}, bf16[2,256,128]{2,1,0:T(8,128)(2,1)S(1)}, u32[]{:S(2)}, u32[]{:S(2)}) collective-permute-start(bf16[2,256,128]{2,1,0:T(8,128)(2,1)S(1)} %get-tuple-element.66), channel_id=1, source_target_pairs={{0,2},{1,3},{2,0},{3,1},{4,6},{5,7},{6,4},{7,5},{8,10},{9,11},{10,... | collective-permute-start | bytes 393224 | tf_op jit(solution)/shard_map/ppermute | solution.py:15
  91.2 7.3 %collective-permute-start.26 = (bf16[2,256,128]{2,1,0:T(8,128)(2,1)S(1)}, bf16[2,256,128]{2,1,0:T(8,128)(2,1)S(1)}, u32[]{:S(2)}, u32[]{:S(2)}) collective-permute-start(bf16[2,256,128]{2,1,0:T(8,128)(2,1)S(1)} %get-tuple-element.65), channel_id=1, source_target_pairs={{0,3},{1,2},{2,1},{3,0},{4,7},{5,6},{6,5},{7,4},{8,11},{9,10},{10,... | collective-permute-start | bytes 393224 | tf_op jit(solution)/shard_map/ppermute | solution.py:15
  99.9 2.2 %collective-permute-start.27 = (bf16[2,256,128]{2,1,0:T(8,128)(2,1)S(1)}, bf16[2,256,128]{2,1,0:T(8,128)(2,1)S(1)}, u32[]{:S(2)}, u32[]{:S(2)}) collective-permute-start(bf16[2,256,128]{2,1,0:T(8,128)(2,1)S(1)} %get-tuple-element.63), channel_id=1, source_target_pairs={{0,1},{1,0},{2,3},{3,2},{4,5},{5,4},{6,7},{7,6},{8,9},{9,8},{10,11... | collective-permute-start | bytes 393224 | tf_op jit(solution)/shard_map/ppermute | solution.py:15
  100.2 4.8 %collective-permute-start.28 = (bf16[2,256,128]{2,1,0:T(8,128)(2,1)S(1)}, bf16[2,256,128]{2,1,0:T(8,128)(2,1)S(1)}, u32[]{:S(2)}, u32[]{:S(2)}) collective-permute-start(bf16[2,256,128]{2,1,0:T(8,128)(2,1)S(1)} %get-tuple-element.62), channel_id=1, source_target_pairs={{0,2},{1,3},{2,0},{3,1},{4,6},{5,7},{6,4},{7,5},{8,10},{9,11},{10,... | collective-permute-start | bytes 393224 | tf_op jit(solution)/shard_map/ppermute | solution.py:15
  101.0 7.3 %collective-permute-start.29 = (bf16[2,256,128]{2,1,0:T(8,128)(2,1)S(1)}, bf16[2,256,128]{2,1,0:T(8,128)(2,1)S(1)}, u32[]{:S(2)}, u32[]{:S(2)}) collective-permute-start(bf16[2,256,128]{2,1,0:T(8,128)(2,1)S(1)} %get-tuple-element.61), channel_id=1, source_target_pairs={{0,3},{1,2},{2,1},{3,0},{4,7},{5,6},{6,5},{7,4},{8,11},{9,10},{10,... | collective-permute-start | bytes 393224 | tf_op jit(solution)/shard_map/ppermute | solution.py:15

commit v7 on v6

--- a/solution.py
+++ b/solution.py
@@ -510,7 +510,6 @@
     scratch = [pltpu.VMEM((rows, chunk), BF16), pltpu.VMEM((rows, chunk), F32)]
     current, middle = local(middle, (wide, pieces), [index, current] + parts + slots, scratch, us=8)
     middle = swap_pieces(middle, n_col)
-    across, *middle = gate(across, *middle)
     finish = functools.partial(finish_kernel, n_col)
     late = local(finish, pieces, [index, current, across] + slots, [pltpu.VMEM((rows, chunk), F32)])
     late = swap_pieces(late, n_col)

time: 110 us -> 106 us (0.964)
  starting transfers between devices: 40.8 us -> 38.3 us
  waiting for transfers between devices: 45.3 us -> 43.6 us
    ppermute x19, waiting for transfers between devices: 31.1 us -> 27.5 us  [flip(): return lax.ppermute(value, axis, [(i, i ^ bit) for i in range(size)])]
    ppermute x19, starting transfers between devices: 31.5 us -> 29 us  [flip(): return lax.ppermute(value, axis, [(i, i ^ bit) for i in range(size)])]
    ppermute x10, waiting for transfers between devices: 14.1 us -> 16.1 us  [hop(): return lax.ppermute(value, 'row', pairs)]
  transfers between devices with their start and end apart: 30 -> 30, of which waited for: 13 -> 13; matrix products, arithmetic and copies ran while one was open for 0% -> 0% of each run, Pallas kernels for 14% -> 16%
where the time goes in v7:
time: 106 us
  waiting for transfers between devices  43.6 us (41%)
  starting transfers between devices  38.3 us (36%)
  Pallas kernels  18.4 us (17%)
  local copies, waits for them, and re-layouts  2.27 us (2%)
  other arithmetic  2.25 us (2%)
  between operations  1.1 us (1%)
    ppermute x19, starting transfers between devices, flip(): return lax.ppermute(value, axis, [(i, i ^ bit) for i in range(size)])  29 us
    ppermute x19, waiting for transfers between devices, flip(): return lax.ppermute(value, axis, [(i, i ^ bit) for i in range(size)])  27.5 us
    ppermute x10, waiting for transfers between devices, hop(): return lax.ppermute(value, 'row', pairs)  16.1 us
    pallas_call x12, Pallas kernels, local(): pl.pallas_call(kernel, out_shape=out_shape, in_specs=[SMEM] + [VMEM] * (l...  13.6 us
    ppermute x10, starting transfers between devices, hop(): return lax.ppermute(value, 'row', pairs)  8.62 us
    pallas_call x1, Pallas kernels, order_panel(): pl.pallas_call(order_kernel, out_shape=shape_of((rows, sources * width),...  3.08 us
    unnamed x6, local copies, waits for them, and re-layouts  2.2 us
  transfers between devices with their start and end apart: 30, of which 13 were waited for; matrix products, arithmetic and copies ran while one was open for 0% of the time, Pallas kernels for 16%

profile of v7, /device:TPU:25, one launch (start us, length us, event | category | flops | bytes accessed | tf_op | source)
XLA Modules:
  0.0 106.0 jit_solution(6213890178270290180)
XLA Ops:
  0.6 2.0 %bitcast_select_fusion.2 = (bf16[1,256,1024]{2,1,0:T(8,128)(2,1)S(1)}, bf16[1,256,1024]{2,1,0:T(8,128)(2,1)S(1)}, bf16[1,256,1024]{2,1,0:T(8,128)(2,1)S(1)}) fusion(bf16[256,3,1024]{2,0,1:T(8,128)(2,1)} %param.8, pred[]{:T(512)S(6)} %eq.10, bf16[3,256,1024]{2,1,0:T(8,128)(2,1)} %param.9, pred[]{:T(512)S(6)} %eq.12, pred[]{:T(512)S(6)} %eq.11), kind=kLoop, calls=%fused_computation.4 | loop fusion | flops 1048576 | bytes 4718595 | tf_op jit(solution)/shard_map/jit(_where)/select_n | solution.py:461
  2.6 0.0 copy-start.2
  2.7 0.2 pad_maximum_fusion.refs_0_
  2.8 1.3 %collective-permute-start.8 = (bf16[3,256,1024]{2,1,0:T(8,128)(2,1)S(1)}, bf16[3,256,1024]{2,1,0:T(8,128)(2,1)S(1)}, u32[]{:S(2)}, u32[]{:S(2)}) collective-permute-start(bf16[3,256,1024]{2,1,0:T(8,128)(2,1)S(1)} %pad_maximum_fusion.refs_0_), channel_id=1, source_target_pairs={{0,2},{1,3},{2,0},{3,1},{4,6},{5,7},{6,4},{7,5},{8,10},{9,11},{10,... | collective-permute-start | bytes 4718600 | tf_op jit(solution)/shard_map/ppermute | solution.py:15
  4.1 0.2 collective-permute-start
  4.3 0.1 collective-permute-start.1
  4.3 1.2 %collective-permute-start.2 = (bf16[256,512]{1,0:T(8,128)(2,1)S(1)}, bf16[256,512]{1,0:T(8,128)(2,1)}, u32[]{:S(2)}, u32[]{:S(2)}) collective-permute-start(bf16[256,512]{1,0:T(8,128)(2,1)S(1)} %bitcast.29), channel_id=1, source_target_pairs={{0,4},{4,0},{8,12},{12,8},{16,20},{20,16},{24,28},{28,24},{1,5},{5... | collective-permute-start | bytes 786440 | tf_op jit(solution)/shard_map/ppermute | solution.py:15
  5.6 0.1 pad_add_fusion.index_ref
  5.7 2.2 %copy-done = bf16[1024,8,256]{2,1,0:T(8,128)(2,1)S(1)} copy-done((bf16[1024,8,256]{2,1,0:T(8,128)(2,1)S(1)}, bf16[1024,8,256]{2,1,0:T(8,128)(2,1)}, u32[]{:S(2)}) %copy-start) | copy-done | bytes 4194328
  7.8 3.1 %shard_map.68.panel_ref = bf16[1024,2048]{1,0:T(8,128)(2,1)S(1)} custom-call(s32[2]{0:T(128)S(1)} %pad_add_fusion.index_ref, bf16[1024,8,256]{2,1,0:T(8,128)(2,1)S(1)} %copy-done), custom_call_target="tpu_custom_call" | custom-call | bytes 28800000 | tf_op jit(solution)/shard_map/pallas_call | solution.py:154
  10.9 4.8 %collective-permute-done.refs_2_ = bf16[256,512]{1,0:T(8,128)(2,1)} collective-permute-done((bf16[256,512]{1,0:T(8,128)(2,1)S(1)}, bf16[256,512]{1,0:T(8,128)(2,1)}, u32[]{:S(2)}, u32[]{:S(2)}) %collective-permute-start) | collective-permute-done | bytes 262176 | tf_op jit(solution)/shard_map/ppermute | solution.py:15
  15.7 0.8 collective-permute-start.5
  16.5 1.2 %collective-permute-start.3 = (bf16[256,512]{1,0:T(8,128)(2,1)}, bf16[256,512]{1,0:T(8,128)(2,1)S(1)}, u32[]{:S(2)}, u32[]{:S(2)}) collective-permute-start(bf16[256,512]{1,0:T(8,128)(2,1)} %collective-permute-done.refs_2_), channel_id=1, source_target_pairs={{0,4},{4,0},{8,12},{12,8},{16,20},{20,16},{24,28},{28,24},{1,5},{5... | collective-permute-start | bytes 786440 | tf_op jit(solution)/shard_map/ppermute | solution.py:15
  17.8 0.2 collective-permute-start.4
  18.0 5.8 %collective-permute-done.5.refs_6_ = bf16[256,512]{1,0:T(8,128)(2,1)S(1)} collective-permute-done((bf16[256,512]{1,0:T(8,128)(2,1)S(1)}, bf16[256,512]{1,0:T(8,128)(2,1)S(1)}, u32[]{:S(2)}, u32[]{:S(2)}) %collective-permute-start.5) | collective-permute-done | bytes 262176 | tf_op jit(solution)/shard_map/ppermute | solution.py:15
  23.8 1.2 %collective-permute-start.6 = (bf16[256,512]{1,0:T(8,128)(2,1)S(1)}, bf16[256,512]{1,0:T(8,128)(2,1)S(1)}, u32[]{:S(2)}, u32[]{:S(2)}) collective-permute-start(bf16[256,512]{1,0:T(8,128)(2,1)S(1)} %collective-permute-done.5.refs_6_), channel_id=1, source_target_pairs={{0,4},{4,0},{8,12},{12,8},{16,20},{20,16},{24,28},{28,24},{1,5},{5... | collective-permute-start | bytes 786440 | tf_op jit(solution)/shard_map/ppermute | solution.py:15
  25.0 0.0 collective-permute-done.3.refs_3_
  25.0 2.9 %collective-permute-done.4.refs_5_ = bf16[256,512]{1,0:T(8,128)(2,1)S(1)} collective-permute-done((bf16[256,512]{1,0:T(8,128)(2,1)}, bf16[256,512]{1,0:T(8,128)(2,1)S(1)}, u32[]{:S(2)}, u32[]{:S(2)}) %collective-permute-start.4) | collective-permute-done | bytes 262176 | tf_op jit(solution)/shard_map/ppermute | solution.py:15
  27.9 3.3 %shard_map.69.total_ref = f32[1024,512]{1,0:T(8,128)S(1)} custom-call(s32[2]{0:T(128)S(1)} %pad_add_fusion.index_ref, bf16[1024,2048]{1,0:T(8,128)(2,1)S(1)} %shard_map.68.panel_ref, f32[256,512]{1,0:T(8,128)S(1)} %copy-done.1, bf16[256,512]{1,0:T(8,128)(2,1)S(1)} %bitcast.31, bf16[256,512]{1,0:T(8,128)(2,1)} %collective-permute-done.2.refs_1_, ...), custom_call_target="tpu_custom_call" | custom-call | bytes 28800000 | tf_op jit(solution)/shard_map/pallas_call | solution.py:428
  31.1 0.3 collective-permute-done.6.block_ref
  31.4 1.7 %shard_map.70 = (f32[2,1024,128]{2,1,0:T(8,128)S(1)}, bf16[2,1024,128]{2,1,0:T(8,128)(2,1)S(1)}) custom-call(s32[2]{0:T(128)S(1)} %pad_add_fusion.index_ref, bf16[1024,2048]{1,0:T(8,128)(2,1)S(1)} %shard_map.68.panel_ref, bf16[256,512]{1,0:T(8,128)(2,1)S(1)} %collective-permute-done.6.block_ref, f32[1024,512]{1,0:T(8,128)S(1)} %shard_map.69.total_ref), custom_call_target="tpu_custom_call" | custom-call | bytes 3600000 | tf_op jit(solution)/shard_map/pallas_call | solution.py:428
  33.2 5.8 %collective-permute-start.7 = (bf16[2,1024,128]{2,1,0:T(8,128)(2,1)S(1)}, bf16[2,1024,128]{2,1,0:T(8,128)(2,1)S(1)}, u32[]{:S(2)}, u32[]{:S(2)}) collective-permute-start(bf16[2,1024,128]{2,1,0:T(8,128)(2,1)S(1)} %get-tuple-element.33), channel_id=1, source_target_pairs={{0,1},{1,0},{2,3},{3,2},{4,5},{5,4},{6,7},{7,6},{8,9},{9,8},{10,11... | collective-permute-start | bytes 1572872 | tf_op jit(solution)/shard_map/ppermute | solution.py:15
  39.0 0.1 collective-permute-start.9
  39.1 1.5 %collective-permute-done.7.moved_ref = bf16[2,1024,128]{2,1,0:T(8,128)(2,1)S(1)} collective-permute-done((bf16[2,1024,128]{2,1,0:T(8,128)(2,1)S(1)}, bf16[2,1024,128]{2,1,0:T(8,128)(2,1)S(1)}, u32[]{:S(2)}, u32[]{:S(2)}) %collective-permute-start.7) | collective-permute-done | bytes 524320 | tf_op jit(solution)/shard_map/ppermute | solution.py:15
  40.5 0.0 collective-permute-done.8.refs_2_
  40.5 0.4 collective-permute-start.10
  40.9 0.7 shard_map.71
  41.6 0.6 collective-permute-start.11
  42.2 0.7 collective-permute-start.13
  42.9 0.7 collective-permute-start.14
  43.6 1.5 %collective-permute-done.10.refs_3_ = bf16[3,256,1024]{2,1,0:T(8,128)(2,1)S(1)} collective-permute-done((bf16[3,256,1024]{2,1,0:T(8,128)(2,1)S(1)}, bf16[3,256,1024]{2,1,0:T(8,128)(2,1)S(1)}, u32[]{:S(2)}, u32[]{:S(2)}) %collective-permute-start.10) | collective-permute-done | bytes 1572896 | tf_op jit(solution)/shard_map/ppermute | solution.py:15
  45.0 0.7 shard_map.72.product_ref
  45.7 3.7 %collective-permute-done.11.moved_ref = bf16[1024,128]{1,0:T(8,128)(2,1)S(1)} collective-permute-done((bf16[1024,128]{1,0:T(8,128)(2,1)S(1)}, bf16[1024,128]{1,0:T(8,128)(2,1)S(1)}, u32[]{:S(2)}, u32[]{:S(2)}) %collective-permute-start.11) | collective-permute-done | bytes 262176 | tf_op jit(solution)/shard_map/ppermute | solution.py:15
  49.4 0.8 shard_map.73
  50.2 0.7 collective-permute-start.12
  50.9 0.6 shard_map.75.refs_0_
  51.5 1.3 %collective-permute-start.17 = (bf16[1024,128]{1,0:T(8,128)(2,1)S(1)}, bf16[1024,128]{1,0:T(8,128)(2,1)S(1)}, u32[]{:S(2)}, u32[]{:S(2)}) collective-permute-start(bf16[1024,128]{1,0:T(8,128)(2,1)S(1)} %shard_map.75.refs_0_), channel_id=1, source_target_pairs={{4,8},{0,24},{5,9},{1,25},{6,10},{2,26},{7,11},{3,27}} | collective-permute-start | bytes 786440 | tf_op jit(solution)/shard_map/ppermute | solution.py:440
  52.8 0.7 collective-permute-start.19
  53.5 0.7 collective-permute-start.16
  54.2 0.7 collective-permute-start.15
  54.9 0.6 shard_map.74
  55.5 11.3 %collective-permute-done.17.refs_2_.first_ref = bf16[1024,128]{1,0:T(8,128)(2,1)S(1)} collective-permute-done((bf16[1024,128]{1,0:T(8,128)(2,1)S(1)}, bf16[1024,128]{1,0:T(8,128)(2,1)S(1)}, u32[]{:S(2)}, u32[]{:S(2)}) %collective-permute-start.17) | collective-permute-done | bytes 262176 | tf_op jit(solution)/shard_map/ppermute | solution.py:440
  66.9 0.6 shard_map.77.refs_1_
  67.5 1.3 %collective-permute-start.20 = (bf16[1024,128]{1,0:T(8,128)(2,1)S(1)}, bf16[1024,128]{1,0:T(8,128)(2,1)S(1)}, u32[]{:S(2)}, u32[]{:S(2)}) collective-permute-start(bf16[1024,128]{1,0:T(8,128)(2,1)S(1)} %shard_map.77.refs_1_), channel_id=1, source_target_pairs={{8,24},{9,25},{10,26},{11,27}} | collective-permute-start | bytes 786440 | tf_op jit(solution)/shard_map/ppermute | solution.py:440
  68.8 0.7 collective-permute-start.21
  69.4 0.7 collective-permute-start.22
  70.1 0.6 shard_map.76.line0_ref
  70.8 1.3 %collective-permute-start.18 = (bf16[1024,128]{1,0:T(8,128)(2,1)S(1)}, bf16[1024,128]{1,0:T(8,128)(2,1)S(1)}, u32[]{:S(2)}, u32[]{:S(2)}) collective-permute-start(bf16[1024,128]{1,0:T(8,128)(2,1)S(1)} %shard_map.76.line0_ref), channel_id=1, source_target_pairs={{0,4},{16,20},{24,28},{1,5},{17,21},{25,29},{2,6},{18,22},{26,30},... | collective-permute-start | bytes 786440 | tf_op jit(solution)/shard_map/ppermute | solution.py:440
  72.1 4.8 %collective-permute-done.20.refs_2_ = bf16[1024,128]{1,0:T(8,128)(2,1)S(1)} collective-permute-done((bf16[1024,128]{1,0:T(8,128)(2,1)S(1)}, bf16[1024,128]{1,0:T(8,128)(2,1)S(1)}, u32[]{:S(2)}, u32[]{:S(2)}) %collective-permute-start.20) | collective-permute-done | bytes 262176 | tf_op jit(solution)/shard_map/ppermute | solution.py:440
  76.9 0.6 shard_map.78.line_ref
  77.5 9.4 %collective-permute-start.26 = (bf16[1024,128]{1,0:T(8,128)(2,1)S(1)}, bf16[1024,128]{1,0:T(8,128)(2,1)S(1)}, u32[]{:S(2)}, u32[]{:S(2)}) collective-permute-start(bf16[1024,128]{1,0:T(8,128)(2,1)S(1)} %shard_map.78.line_ref), channel_id=1, source_target_pairs={{0,4},{4,0},{8,12},{12,8},{16,20},{20,16},{24,28},{28,24},{1,5},{5... | collective-permute-start | bytes 786440 | tf_op jit(solution)/shard_map/ppermute | solution.py:15
  86.9 2.1 %shard_map.79 = (f32[1024,128]{1,0:T(8,128)S(1)}, bf16[4,2,256,128]{3,2,1,0:T(8,128)(2,1)S(1)}) custom-call(s32[2]{0:T(128)S(1)} %pad_add_fusion.index_ref, f32[1024,128]{1,0:T(8,128)S(1)} %get-tuple-element.41.current_ref, bf16[1024,128]{1,0:T(8,128)(2,1)S(1)} %get-tuple-element.40.own_ref.refs_0_.own0_ref, ...), custom_call_target="tpu_custom_call" | custom-call | bytes 28800000 | tf_op jit(solution)/shard_map/pallas_call | solution.py:428
  89.1 1.4 %collective-permute-start.23 = (bf16[2,256,128]{2,1,0:T(8,128)(2,1)S(1)}, bf16[2,256,128]{2,1,0:T(8,128)(2,1)S(1)}, u32[]{:S(2)}, u32[]{:S(2)}) collective-permute-start(bf16[2,256,128]{2,1,0:T(8,128)(2,1)S(1)} %get-tuple-element.57), channel_id=1, source_target_pairs={{0,1},{1,0},{2,3},{3,2},{4,5},{5,4},{6,7},{7,6},{8,9},{9,8},{10,11... | collective-permute-start | bytes 393224 | tf_op jit(solution)/shard_map/ppermute | solution.py:15
  90.4 0.8 collective-permute-start.24
  91.2 0.9 collective-permute-start.25
  92.1 0.4 collective-permute-done.26.value_ref
  92.6 1.3 %shard_map.80 = bf16[4,2,256,128]{3,2,1,0:T(8,128)(2,1)S(1)} custom-call(s32[2]{0:T(128)S(1)} %pad_add_fusion.index_ref, f32[1024,128]{1,0:T(8,128)S(1)} %get-tuple-element.47.current_ref, bf16[1024,128]{1,0:T(8,128)(2,1)S(1)} %collective-permute-done.26.value_ref, bf16[3,256,1024]{2,1,0:T(8,128)(2,1)S(1)} %pad_maximum_fusion.refs_0_, ...), custom_call_target="tpu_custom_call" | custom-call | bytes 3600000 | tf_op jit(solution)/shard_map/pallas_call | solution.py:428
  94.0 1.7 %collective-permute-start.27 = (bf16[2,256,128]{2,1,0:T(8,128)(2,1)S(1)}, bf16[2,256,128]{2,1,0:T(8,128)(2,1)S(1)}, u32[]{:S(2)}, u32[]{:S(2)}) collective-permute-start(bf16[2,256,128]{2,1,0:T(8,128)(2,1)S(1)} %get-tuple-element.53), channel_id=1, source_target_pairs={{0,1},{1,0},{2,3},{3,2},{4,5},{5,4},{6,7},{7,6},{8,9},{9,8},{10,11... | collective-permute-start | bytes 393224 | tf_op jit(solution)/shard_map/ppermute | solution.py:15
  95.6 0.8 collective-permute-start.28
  96.4 0.9 collective-permute-start.29
  97.4 1.5 %collective-permute-done.25.refs_3_ = bf16[2,256,128]{2,1,0:T(8,128)(2,1)S(1)} collective-permute-done((bf16[2,256,128]{2,1,0:T(8,128)(2,1)S(1)}, bf16[2,256,128]{2,1,0:T(8,128)(2,1)S(1)}, u32[]{:S(2)}, u32[]{:S(2)}) %collective-permute-start.25) | collective-permute-done | bytes 131104 | tf_op jit(solution)/shard_map/ppermute | solution.py:15
  98.8 2.4 %collective-permute-done.28.refs_6_ = bf16[2,256,128]{2,1,0:T(8,128)(2,1)S(1)} collective-permute-done((bf16[2,256,128]{2,1,0:T(8,128)(2,1)S(1)}, bf16[2,256,128]{2,1,0:T(8,128)(2,1)S(1)}, u32[]{:S(2)}, u32[]{:S(2)}) %collective-permute-start.28) | collective-permute-done | bytes 131104 | tf_op jit(solution)/shard_map/ppermute | solution.py:15
  101.2 2.9 %collective-permute-done.29.refs_7_ = bf16[2,256,128]{2,1,0:T(8,128)(2,1)S(1)} collective-permute-done((bf16[2,256,128]{2,1,0:T(8,128)(2,1)S(1)}, bf16[2,256,128]{2,1,0:T(8,128)(2,1)S(1)}, u32[]{:S(2)}, u32[]{:S(2)}) %collective-permute-start.29) | collective-permute-done | bytes 131104 | tf_op jit(solution)/shard_map/ppermute | solution.py:15
  104.1 1.7 %shard_map.81 = (bf16[3,256,512]{2,1,0:T(8,128)(2,1)}, f32[256,512]{1,0:T(8,128)}) custom-call(s32[2]{0:T(128)S(1)} %pad_add_fusion.index_ref, bf16[2,256,128]{2,1,0:T(8,128)(2,1)S(1)} %get-tuple-element.58.refs_0_, bf16[2,256,128]{2,1,0:T(8,128)(2,1)S(1)} %collective-permute-done.23.refs_1_, bf16[2,256,128]{2,1,0:T(8,128)(2,1)S(1)} %collective-permute-done.24.refs_2_, ...), custom_call_target="tpu_custom_call" | custom-call | bytes 3600000 | tf_op jit(solution)/shard_map/pallas_call | solution.py:415
  (21 shorter events, 0.1 us)
Async XLA Ops:
  2.6 1.5 %copy-start.2 = (bf16[1,256,512]{2,1,0:T(8,128)(2,1)S(1)}, bf16[1,256,512]{2,1,0:T(8,128)(2,1)}, u32[]{:S(2)}) copy-start(bf16[1,256,512]{2,1,0:T(8,128)(2,1)} %param.7) | copy-start | bytes 786436
  2.8 37.7 %collective-permute-start.8 = (bf16[3,256,1024]{2,1,0:T(8,128)(2,1)S(1)}, bf16[3,256,1024]{2,1,0:T(8,128)(2,1)S(1)}, u32[]{:S(2)}, u32[]{:S(2)}) collective-permute-start(bf16[3,256,1024]{2,1,0:T(8,128)(2,1)S(1)} %pad_maximum_fusion.refs_0_), channel_id=1, source_target_pairs={{0,2},{1,3},{2,0},{3,1},{4,6},{5,7},{6,4},{7,5},{8,10},{9,11},{10,... | collective-permute-start | bytes 4718600 | tf_op jit(solution)/shard_map/ppermute | solution.py:15
  4.1 11.6 %collective-permute-start = (bf16[256,512]{1,0:T(8,128)(2,1)S(1)}, bf16[256,512]{1,0:T(8,128)(2,1)}, u32[]{:S(2)}, u32[]{:S(2)}) collective-permute-start(bf16[256,512]{1,0:T(8,128)(2,1)S(1)} %bitcast.27), channel_id=1, source_target_pairs={{0,8},{4,12},{8,0},{12,4},{16,24},{20,28},{24,16},{28,20},{1,9},{5... | collective-permute-start | bytes 786440 | tf_op jit(solution)/shard_map/ppermute | solution.py:15
  4.3 13.5 %collective-permute-start.1 = (bf16[256,512]{1,0:T(8,128)(2,1)S(1)}, bf16[256,512]{1,0:T(8,128)(2,1)}, u32[]{:S(2)}, u32[]{:S(2)}) collective-permute-start(bf16[256,512]{1,0:T(8,128)(2,1)S(1)} %bitcast.28), channel_id=1, source_target_pairs={{0,16},{4,20},{8,24},{12,28},{16,0},{20,4},{24,8},{28,12},{1,17},{... | collective-permute-start | bytes 786440 | tf_op jit(solution)/shard_map/ppermute | solution.py:15
  4.3 13.4 %collective-permute-start.2 = (bf16[256,512]{1,0:T(8,128)(2,1)S(1)}, bf16[256,512]{1,0:T(8,128)(2,1)}, u32[]{:S(2)}, u32[]{:S(2)}) collective-permute-start(bf16[256,512]{1,0:T(8,128)(2,1)S(1)} %bitcast.29), channel_id=1, source_target_pairs={{0,4},{4,0},{8,12},{12,8},{16,20},{20,16},{24,28},{28,24},{1,5},{5... | collective-permute-start | bytes 786440 | tf_op jit(solution)/shard_map/ppermute | solution.py:15
  5.7 2.2 %copy-start = (bf16[1024,8,256]{2,1,0:T(8,128)(2,1)S(1)}, bf16[1024,8,256]{2,1,0:T(8,128)(2,1)}, u32[]{:S(2)}) copy-start(bf16[1024,8,256]{2,1,0:T(8,128)(2,1)} %panel_ref.1) | copy-start | bytes 12582916
  7.8 20.0 %copy-start.1 = (f32[256,512]{1,0:T(8,128)S(1)}, f32[256,512]{1,0:T(8,128)}, u32[]{:S(2)}) copy-start(f32[256,512]{1,0:T(8,128)} %side_ref.1) | copy-start | bytes 1572868
  15.7 8.1 %collective-permute-start.5 = (bf16[256,512]{1,0:T(8,128)(2,1)S(1)}, bf16[256,512]{1,0:T(8,128)(2,1)S(1)}, u32[]{:S(2)}, u32[]{:S(2)}) collective-permute-start(bf16[256,512]{1,0:T(8,128)(2,1)S(1)} %bitcast.30), channel_id=1, source_target_pairs={{0,24},{4,28},{8,16},{12,20},{16,8},{20,12},{24,0},{28,4},{1,25},{... | collective-permute-start | bytes 786440 | tf_op jit(solution)/shard_map/ppermute | solution.py:15
  16.5 8.5 %collective-permute-start.3 = (bf16[256,512]{1,0:T(8,128)(2,1)}, bf16[256,512]{1,0:T(8,128)(2,1)S(1)}, u32[]{:S(2)}, u32[]{:S(2)}) collective-permute-start(bf16[256,512]{1,0:T(8,128)(2,1)} %collective-permute-done.refs_2_), channel_id=1, source_target_pairs={{0,4},{4,0},{8,12},{12,8},{16,20},{20,16},{24,28},{28,24},{1,5},{5... | collective-permute-start | bytes 786440 | tf_op jit(solution)/shard_map/ppermute | solution.py:15
  17.8 10.1 %collective-permute-start.4 = (bf16[256,512]{1,0:T(8,128)(2,1)}, bf16[256,512]{1,0:T(8,128)(2,1)S(1)}, u32[]{:S(2)}, u32[]{:S(2)}) collective-permute-start(bf16[256,512]{1,0:T(8,128)(2,1)} %collective-permute-done.1.refs_4_), channel_id=1, source_target_pairs={{0,4},{4,0},{8,12},{12,8},{16,20},{20,16},{24,28},{28,24},{1,5},{5... | collective-permute-start | bytes 786440 | tf_op jit(solution)/shard_map/ppermute | solution.py:15
  23.8 7.7 %collective-permute-start.6 = (bf16[256,512]{1,0:T(8,128)(2,1)S(1)}, bf16[256,512]{1,0:T(8,128)(2,1)S(1)}, u32[]{:S(2)}, u32[]{:S(2)}) collective-permute-start(bf16[256,512]{1,0:T(8,128)(2,1)S(1)} %collective-permute-done.5.refs_6_), channel_id=1, source_target_pairs={{0,4},{4,0},{8,12},{12,8},{16,20},{20,16},{24,28},{28,24},{1,5},{5... | collective-permute-start | bytes 786440 | tf_op jit(solution)/shard_map/ppermute | solution.py:15
  33.2 7.4 %collective-permute-start.7 = (bf16[2,1024,128]{2,1,0:T(8,128)(2,1)S(1)}, bf16[2,1024,128]{2,1,0:T(8,128)(2,1)S(1)}, u32[]{:S(2)}, u32[]{:S(2)}) collective-permute-start(bf16[2,1024,128]{2,1,0:T(8,128)(2,1)S(1)} %get-tuple-element.33), channel_id=1, source_target_pairs={{0,1},{1,0},{2,3},{3,2},{4,5},{5,4},{6,7},{7,6},{8,9},{9,8},{10,11... | collective-permute-start | bytes 1572872 | tf_op jit(solution)/shard_map/ppermute | solution.py:15
  39.0 4.6 %collective-permute-start.9 = (bf16[3,256,1024]{2,1,0:T(8,128)(2,1)S(1)}, bf16[3,256,1024]{2,1,0:T(8,128)(2,1)S(1)}, u32[]{:S(2)}, u32[]{:S(2)}) collective-permute-start(bf16[3,256,1024]{2,1,0:T(8,128)(2,1)S(1)} %pad_maximum_fusion.refs_0_), channel_id=1, source_target_pairs={{0,1},{1,0},{2,3},{3,2},{4,5},{5,4},{6,7},{7,6},{8,9},{9,8},{10,11... | collective-permute-start | bytes 4718600 | tf_op jit(solution)/shard_map/ppermute | solution.py:15
  40.5 4.5 %collective-permute-start.10 = (bf16[3,256,1024]{2,1,0:T(8,128)(2,1)S(1)}, bf16[3,256,1024]{2,1,0:T(8,128)(2,1)S(1)}, u32[]{:S(2)}, u32[]{:S(2)}) collective-permute-start(bf16[3,256,1024]{2,1,0:T(8,128)(2,1)S(1)} %collective-permute-done.8.refs_2_), channel_id=1, source_target_pairs={{0,1},{1,0},{2,3},{3,2},{4,5},{5,4},{6,7},{7,6},{8,9},{9,8},{10,11... | collective-permute-start | bytes 4718600 | tf_op jit(solution)/shard_map/ppermute | solution.py:15
  41.6 7.8 %collective-permute-start.11 = (bf16[1024,128]{1,0:T(8,128)(2,1)S(1)}, bf16[1024,128]{1,0:T(8,128)(2,1)S(1)}, u32[]{:S(2)}, u32[]{:S(2)}) collective-permute-start(bf16[1024,128]{1,0:T(8,128)(2,1)S(1)} %get-tuple-element.38), channel_id=1, source_target_pairs={{0,2},{1,3},{2,0},{3,1},{4,6},{5,7},{6,4},{7,5},{8,10},{9,11},{10,... | collective-permute-start | bytes 786440 | tf_op jit(solution)/shard_map/ppermute | solution.py:15
  42.2 8.7 %collective-permute-start.13 = (bf16[1024,128]{1,0:T(8,128)(2,1)S(1)}, bf16[1024,128]{1,0:T(8,128)(2,1)S(1)}, u32[]{:S(2)}, u32[]{:S(2)}) collective-permute-start(bf16[1024,128]{1,0:T(8,128)(2,1)S(1)} %get-tuple-element.44), channel_id=1, source_target_pairs={{0,4},{1,5},{2,6},{3,7}} | collective-permute-start | bytes 786440 | tf_op jit(solution)/shard_map/ppermute | solution.py:440
  42.9 8.1 %collective-permute-start.14 = (bf16[1024,128]{1,0:T(8,128)(2,1)S(1)}, bf16[1024,128]{1,0:T(8,128)(2,1)S(1)}, u32[]{:S(2)}, u32[]{:S(2)}) collective-permute-start(bf16[1024,128]{1,0:T(8,128)(2,1)S(1)} %get-tuple-element.38), channel_id=1, source_target_pairs={{0,6},{1,7},{2,4},{3,5}} | collective-permute-start | bytes 786440 | tf_op jit(solution)/shard_map/ppermute | solution.py:485
  50.2 4.7 %collective-permute-start.12 = (bf16[1024,128]{1,0:T(8,128)(2,1)S(1)}, bf16[1024,128]{1,0:T(8,128)(2,1)S(1)}, u32[]{:S(2)}, u32[]{:S(2)}) collective-permute-start(bf16[1024,128]{1,0:T(8,128)(2,1)S(1)} %get-tuple-element.40.own_ref.refs_0_.own0_ref), channel_id=1, source_target_pairs={{0,8},{1,9},{2,10},{3,11}} | collective-permute-start | bytes 786440 | tf_op jit(solution)/shard_map/ppermute | solution.py:440
  51.5 15.3 %collective-permute-start.17 = (bf16[1024,128]{1,0:T(8,128)(2,1)S(1)}, bf16[1024,128]{1,0:T(8,128)(2,1)S(1)}, u32[]{:S(2)}, u32[]{:S(2)}) collective-permute-start(bf16[1024,128]{1,0:T(8,128)(2,1)S(1)} %shard_map.75.refs_0_), channel_id=1, source_target_pairs={{4,8},{0,24},{5,9},{1,25},{6,10},{2,26},{7,11},{3,27}} | collective-permute-start | bytes 786440 | tf_op jit(solution)/shard_map/ppermute | solution.py:440
  52.8 14.0 %collective-permute-start.19 = (bf16[1024,128]{1,0:T(8,128)(2,1)S(1)}, bf16[1024,128]{1,0:T(8,128)(2,1)S(1)}, u32[]{:S(2)}, u32[]{:S(2)}) collective-permute-start(bf16[1024,128]{1,0:T(8,128)(2,1)S(1)} %shard_map.75.refs_0_), channel_id=1, source_target_pairs={{4,12},{5,13},{6,14},{7,15}} | collective-permute-start | bytes 786440 | tf_op jit(solution)/shard_map/ppermute | solution.py:440
  53.5 16.6 %collective-permute-start.16 = (bf16[1024,128]{1,0:T(8,128)(2,1)S(1)}, bf16[1024,128]{1,0:T(8,128)(2,1)S(1)}, u32[]{:S(2)}, u32[]{:S(2)}) collective-permute-start(bf16[1024,128]{1,0:T(8,128)(2,1)S(1)} %shard_map.75.refs_0_), channel_id=1, source_target_pairs={{0,16},{1,17},{2,18},{3,19}} | collective-permute-start | bytes 786440 | tf_op jit(solution)/shard_map/ppermute | solution.py:440
  54.2 17.9 %collective-permute-start.15 = (bf16[1024,128]{1,0:T(8,128)(2,1)S(1)}, bf16[1024,128]{1,0:T(8,128)(2,1)S(1)}, u32[]{:S(2)}, u32[]{:S(2)}) collective-permute-start(bf16[1024,128]{1,0:T(8,128)(2,1)S(1)} %shard_map.75.refs_0_), channel_id=1, source_target_pairs={{4,20},{0,12},{5,21},{1,13},{6,22},{2,14},{7,23},{3,15}} | collective-permute-start | bytes 786440 | tf_op jit(solution)/shard_map/ppermute | solution.py:440
  67.5 9.4 %collective-permute-start.20 = (bf16[1024,128]{1,0:T(8,128)(2,1)S(1)}, bf16[1024,128]{1,0:T(8,128)(2,1)S(1)}, u32[]{:S(2)}, u32[]{:S(2)}) collective-permute-start(bf16[1024,128]{1,0:T(8,128)(2,1)S(1)} %shard_map.77.refs_1_), channel_id=1, source_target_pairs={{8,24},{9,25},{10,26},{11,27}} | collective-permute-start | bytes 786440 | tf_op jit(solution)/shard_map/ppermute | solution.py:440
  68.8 8.1 %collective-permute-start.21 = (bf16[1024,128]{1,0:T(8,128)(2,1)S(1)}, bf16[1024,128]{1,0:T(8,128)(2,1)S(1)}, u32[]{:S(2)}, u32[]{:S(2)}) collective-permute-start(bf16[1024,128]{1,0:T(8,128)(2,1)S(1)} %shard_map.77.refs_1_), channel_id=1, source_target_pairs={{8,16},{12,28},{9,17},{13,29},{10,18},{14,30},{11,19},{15,31}} | collective-permute-start | bytes 786440 | tf_op jit(solution)/shard_map/ppermute | solution.py:440
  69.4 7.4 %collective-permute-start.22 = (bf16[1024,128]{1,0:T(8,128)(2,1)S(1)}, bf16[1024,128]{1,0:T(8,128)(2,1)S(1)}, u32[]{:S(2)}, u32[]{:S(2)}) collective-permute-start(bf16[1024,128]{1,0:T(8,128)(2,1)S(1)} %shard_map.77.refs_1_), channel_id=1, source_target_pairs={{8,0},{9,1},{10,2},{11,3}} | collective-permute-start | bytes 786440 | tf_op jit(solution)/shard_map/ppermute | solution.py:440
  70.8 16.2 %collective-permute-start.18 = (bf16[1024,128]{1,0:T(8,128)(2,1)S(1)}, bf16[1024,128]{1,0:T(8,128)(2,1)S(1)}, u32[]{:S(2)}, u32[]{:S(2)}) collective-permute-start(bf16[1024,128]{1,0:T(8,128)(2,1)S(1)} %shard_map.76.line0_ref), channel_id=1, source_target_pairs={{0,4},{16,20},{24,28},{1,5},{17,21},{25,29},{2,6},{18,22},{26,30},... | collective-permute-start | bytes 786440 | tf_op jit(solution)/shard_map/ppermute | solution.py:440
  77.5 15.1 %collective-permute-start.26 = (bf16[1024,128]{1,0:T(8,128)(2,1)S(1)}, bf16[1024,128]{1,0:T(8,128)(2,1)S(1)}, u32[]{:S(2)}, u32[]{:S(2)}) collective-permute-start(bf16[1024,128]{1,0:T(8,128)(2,1)S(1)} %shard_map.78.line_ref), channel_id=1, source_target_pairs={{0,4},{4,0},{8,12},{12,8},{16,20},{20,16},{24,28},{28,24},{1,5},{5... | collective-permute-start | bytes 786440 | tf_op jit(solution)/shard_map/ppermute | solution.py:15
  89.1 7.4 %collective-permute-start.23 = (bf16[2,256,128]{2,1,0:T(8,128)(2,1)S(1)}, bf16[2,256,128]{2,1,0:T(8,128)(2,1)S(1)}, u32[]{:S(2)}, u32[]{:S(2)}) collective-permute-start(bf16[2,256,128]{2,1,0:T(8,128)(2,1)S(1)} %get-tuple-element.57), channel_id=1, source_target_pairs={{0,1},{1,0},{2,3},{3,2},{4,5},{5,4},{6,7},{7,6},{8,9},{9,8},{10,11... | collective-permute-start | bytes 393224 | tf_op jit(solution)/shard_map/ppermute | solution.py:15
  90.4 6.9 %collective-permute-start.24 = (bf16[2,256,128]{2,1,0:T(8,128)(2,1)S(1)}, bf16[2,256,128]{2,1,0:T(8,128)(2,1)S(1)}, u32[]{:S(2)}, u32[]{:S(2)}) collective-permute-start(bf16[2,256,128]{2,1,0:T(8,128)(2,1)S(1)} %get-tuple-element.56), channel_id=1, source_target_pairs={{0,2},{1,3},{2,0},{3,1},{4,6},{5,7},{6,4},{7,5},{8,10},{9,11},{10,... | collective-permute-start | bytes 393224 | tf_op jit(solution)/shard_map/ppermute | solution.py:15
  91.2 7.6 %collective-permute-start.25 = (bf16[2,256,128]{2,1,0:T(8,128)(2,1)S(1)}, bf16[2,256,128]{2,1,0:T(8,128)(2,1)S(1)}, u32[]{:S(2)}, u32[]{:S(2)}) collective-permute-start(bf16[2,256,128]{2,1,0:T(8,128)(2,1)S(1)} %get-tuple-element.55), channel_id=1, source_target_pairs={{0,3},{1,2},{2,1},{3,0},{4,7},{5,6},{6,5},{7,4},{8,11},{9,10},{10,... | collective-permute-start | bytes 393224 | tf_op jit(solution)/shard_map/ppermute | solution.py:15
  94.0 4.8 %collective-permute-start.27 = (bf16[2,256,128]{2,1,0:T(8,128)(2,1)S(1)}, bf16[2,256,128]{2,1,0:T(8,128)(2,1)S(1)}, u32[]{:S(2)}, u32[]{:S(2)}) collective-permute-start(bf16[2,256,128]{2,1,0:T(8,128)(2,1)S(1)} %get-tuple-element.53), channel_id=1, source_target_pairs={{0,1},{1,0},{2,3},{3,2},{4,5},{5,4},{6,7},{7,6},{8,9},{9,8},{10,11... | collective-permute-start | bytes 393224 | tf_op jit(solution)/shard_map/ppermute | solution.py:15
  95.6 5.6 %collective-permute-start.28 = (bf16[2,256,128]{2,1,0:T(8,128)(2,1)S(1)}, bf16[2,256,128]{2,1,0:T(8,128)(2,1)S(1)}, u32[]{:S(2)}, u32[]{:S(2)}) collective-permute-start(bf16[2,256,128]{2,1,0:T(8,128)(2,1)S(1)} %get-tuple-element.52), channel_id=1, source_target_pairs={{0,2},{1,3},{2,0},{3,1},{4,6},{5,7},{6,4},{7,5},{8,10},{9,11},{10,... | collective-permute-start | bytes 393224 | tf_op jit(solution)/shard_map/ppermute | solution.py:15
  96.4 7.7 %collective-permute-start.29 = (bf16[2,256,128]{2,1,0:T(8,128)(2,1)S(1)}, bf16[2,256,128]{2,1,0:T(8,128)(2,1)S(1)}, u32[]{:S(2)}, u32[]{:S(2)}) collective-permute-start(bf16[2,256,128]{2,1,0:T(8,128)(2,1)S(1)} %get-tuple-element.51), channel_id=1, source_target_pairs={{0,3},{1,2},{2,1},{3,0},{4,7},{5,6},{6,5},{7,4},{8,11},{9,10},{10,... | collective-permute-start | bytes 393224 | tf_op jit(solution)/shard_map/ppermute | solution.py:15

commit v8 on v7

--- a/solution.py
+++ b/solution.py
@@ -184,20 +184,31 @@
     return local(kernel, shape_of((panel.shape[0], nrhs), F32), [index, panel, side] + blocks, scratch, us=8)
 
 
-def split_kernel(n_col, index_ref, panel_ref, block_ref, total_ref, kept_ref, sent_ref, scratch):
+def split_kernel(n_col, index_ref, panel_ref, *refs):
+    blocks, (total_ref, kept_ref, sent_ref) = refs[:-3], refs[-3:]
     chunk = kept_ref.shape[2]
-    strip = scratch.shape[0]
+    width = blocks[0].shape[0]
+    strip = total_ref.shape[0] // n_col
     core = lax.rem(index_ref[1], 2)
+    first = panel_ref.shape[1] - len(blocks) * width
 
     def tile(t, carry):
         span = pl.ds(pl.multiple_of(t * strip, strip), strip)
-        scratch[...] = total_ref[span, :] + matmul(panel_ref[span, panel_ref.shape[1] - block_ref.shape[0] :], block_ref[...])
-        for h in range(n_col // 2):
-            kept_ref[h, span, :] = scratch[:, pl.ds(pl.multiple_of((2 * h + core) * chunk, chunk), chunk)]
-            sent_ref[h, span, :] = scratch[:, pl.ds(pl.multiple_of((2 * h + 1 - core) * chunk, chunk), chunk)].astype(BF16)
+        total = total_ref[span, :]
+        for b, block in enumerate(blocks):
+            total = total + matmul(panel_ref[span, first + b * width : first + (b + 1) * width], block[...])
+        for parity in range(2):
+
+            @pl.when(core == parity)
+            def _():
+                for h in range(n_col // 2):
+                    mine, other = 2 * h + parity, 2 * h + 1 - parity
+                    kept_ref[h, span, :] = total[:, mine * chunk : (mine + 1) * chunk]
+                    sent_ref[h, span, :] = total[:, other * chunk : (other + 1) * chunk].astype(BF16)
+
         return carry
 
-    lax.fori_loop(0, total_ref.shape[0] // strip, tile, 0)
+    lax.fori_loop(0, n_col, tile, 0)
 
 
 def reduce_kernel(bit, index_ref, kept_ref, moved_ref, keep_ref, also_ref, send_ref):
@@ -345,43 +356,50 @@
     return local(functools.partial(pick_kernel, holders), shape_of(parts[0].shape, BF16), [index] + list(parts))
 
 
-def update_either(index_ref, first, strips, value, source_ref, target_ref):
-    row = index_ref[0]
-
-    @pl.when((row > 2) & first)
-    def _():
-        subtract(index_ref, (strips, 1), value, row > 2, source_ref, target_ref)
-
-    @pl.when((row > 2) & jnp.logical_not(first))
-    def _():
-        subtract(index_ref, (strips, 2), value, row > 2, source_ref, target_ref)
-
-    @pl.when(row <= 2)
-    def _():
-        target_ref[...] = source_ref[...]
-
-
-def middle_kernel(n_col, index_ref, current_ref, own0_ref, at2_ref, fourth_ref, line0_ref, across0_ref, first_ref, line_ref, *refs):
-    strips, (out_ref, pieces_ref, known, between) = refs[:n_col], refs[n_col:]
+def known_kernel(index_ref, own0_ref, at2_ref, fourth_ref, line0_ref, across0_ref, line_ref, known_ref, pieces_ref):
     row = index_ref[0]
     for holder, part in enumerate((own0_ref, across0_ref, at2_ref, fourth_ref, line0_ref, across0_ref, line0_ref, across0_ref)):
-        copy_where(row == holder, part, known)
-    subtract(index_ref, (strips, 0), known[...], (row == 1) | (row > 2), current_ref, between)
-    update_either(index_ref, lax.rem(row, 2) == 1, strips, line_ref[...], between, out_ref)
+        copy_where(row == holder, part, known_ref)
+    cut(index_ref, known_ref, pieces_ref, 0)
+    cut(index_ref, line_ref, pieces_ref, 1)
+
+
+def middle_kernel(n_col, index_ref, current_ref, known_ref, first_ref, line_ref, *refs):
+    strips, (out_ref, between) = refs[:n_col], refs[n_col:]
+    row = index_ref[0]
+    odd = lax.rem(row, 2) == 1
+    subtract(index_ref, (strips, 0), known_ref[...], (row == 1) | (row > 2), current_ref, between)
+    copy_where(row < 2, between, out_ref)
 
     @pl.when(row == 2)
     def _():
         subtract(index_ref, (strips, 1), first_ref[...], row == 2, between, out_ref)
 
-    cut(index_ref, known, pieces_ref, 0)
-    cut(index_ref, line_ref, pieces_ref, 1)
-
-
-def finish_kernel(n_col, index_ref, current_ref, value_ref, *refs):
-    strips, (pieces_ref, scratch) = refs[:n_col], refs[n_col:]
-    update_either(index_ref, lax.rem(index_ref[0], 2) == 0, strips, value_ref[...], current_ref, scratch)
-    cut(index_ref, value_ref, pieces_ref, 0)
-    cut(index_ref, scratch, pieces_ref, 1)
+    for slot, mine in ((1, odd), (2, jnp.logical_not(odd))):
+
+        @pl.when((row > 2) & mine)
+        def _():
+            subtract(index_ref, (strips, slot), line_ref[...], row > 2, between, out_ref)
+
+
+def finish_kernel(distances, index_ref, current_ref, value_ref, *refs):
+    strips, (pieces_ref,) = refs[:-1], refs[-1:]
+    row, col = index_ref[0], index_ref[1]
+    odd = lax.rem(row, 2) == 1
+    width = pieces_ref.shape[2]
+    for i, (f, strip) in enumerate(zip(distances, strips)):
+        span = pl.ds(pl.multiple_of((col ^ f) * width, width), width)
+        pieces_ref[i, 0] = value_ref[span, :]
+
+        @pl.when(row <= 2)
+        def _():
+            pieces_ref[i, 1] = current_ref[span, :].astype(BF16)
+
+        for slot, mine in ((2, odd), (1, jnp.logical_not(odd))):
+
+            @pl.when((row > 2) & mine)
+            def _():
+                pieces_ref[i, 1] = (current_ref[span, :] - matmul(strip[slot], value_ref[...])).astype(BF16)
 
 
 def cut(index_ref, value_ref, pieces_ref, k):
@@ -475,7 +493,7 @@
     total, b7 = gate(total, b7)
     part = (n_col // 2, rows, chunk)
     split = functools.partial(split_kernel, n_col)
-    kept, sent = local(split, (shape_of(part, F32), shape_of(part, BF16)), [index, panel, b7, total], [pltpu.VMEM((strip, nrhs), F32)])
+    kept, sent = local(split, (shape_of(part, F32), shape_of(part, BF16)), [index, panel, b7, total])
     moved = flip(sent, "col", n_col, 1)
     moved, over = gate(moved, over)
     slots = [own, flip(own, "col", n_col, 1), over, flip(over, "col", n_col, 1)]
@@ -505,14 +523,17 @@
     line = pick(index, (5, 0, 1, 1, 3, 4, 2, 3), own1, own2, z6, z4, fourth, z0)
     across = flip(line, "row", n_row, 1)
     pieces = shape_of((n_col, 2, strip, chunk), BF16)
-    middle = functools.partial(middle_kernel, n_col)
-    parts = [own0, at2, fourth, line0, across0, first, line]
-    scratch = [pltpu.VMEM((rows, chunk), BF16), pltpu.VMEM((rows, chunk), F32)]
-    current, middle = local(middle, (wide, pieces), [index, current] + parts + slots, scratch, us=8)
+    known, middle = local(known_kernel, (narrow, pieces), [index, own0, at2, fourth, line0, across0, line])
     middle = swap_pieces(middle, n_col)
-    finish = functools.partial(finish_kernel, n_col)
-    late = local(finish, pieces, [index, current, across] + slots, [pltpu.VMEM((rows, chunk), F32)])
-    late = swap_pieces(late, n_col)
+    scratch = [pltpu.VMEM((rows, chunk), F32)]
+    current = local(functools.partial(middle_kernel, n_col), wide, [index, current, known, first, line] + slots, scratch, us=8)
+    late = {}
+    for distances, us in (((2, 3), 1), ((0, 1), 8)):
+        part = shape_of((2, 2, strip, chunk), BF16)
+        finish = functools.partial(finish_kernel, distances)
+        part = local(finish, part, [index, current, across] + [slots[f] for f in distances], us=us)
+        late.update(zip(distances, (part[0], part[1])))
+    late = swap_pieces([late[f] for f in range(n_col)], n_col)
     outs = (shape_of((step_count, strip, nrhs), BF16), shape_of((strip, nrhs), F32))
     return assemble(index, middle, late, outs)
 

time: 106 us -> 105 us (level)
  waiting for transfers between devices: 43.6 us -> 40.7 us
  Pallas kernels: 18.4 us -> 19.8 us
    ppermute x19, waiting for transfers between devices: 27.5 us -> 24.6 us  [flip(): return lax.ppermute(value, axis, [(i, i ^ bit) for i in range(size)])]
    pallas_call x12 -> x14, Pallas kernels: 13.6 us -> 15 us  [local(): pl.pallas_call(kernel, out_shape=out_shape, in_specs=[SMEM] + [VMEM] * (l...]
  transfers between devices with their start and end apart: 30 -> 30, of which waited for: 13 -> 11; matrix products, arithmetic and copies ran while one was open for 0% -> 0% of each run, Pallas kernels for 16% -> 17%
where the time goes in v8:
time: 105 us; the launch traced here: 104 us
  waiting for transfers between devices  40.7 us (39%)
  starting transfers between devices  38.1 us (36%)
  Pallas kernels  19.8 us (19%)
  local copies, waits for them, and re-layouts  2.27 us (2%)
  other arithmetic  2.25 us (2%)
  between operations  1.16 us (1%)
    ppermute x19, starting transfers between devices, flip(): return lax.ppermute(value, axis, [(i, i ^ bit) for i in range(size)])  28.8 us
    ppermute x19, waiting for transfers between devices, flip(): return lax.ppermute(value, axis, [(i, i ^ bit) for i in range(size)])  24.6 us
    ppermute x10, waiting for transfers between devices, hop(): return lax.ppermute(value, 'row', pairs)  16.1 us
    pallas_call x14, Pallas kernels, local(): pl.pallas_call(kernel, out_shape=out_shape, in_specs=[SMEM] + [VMEM] * (l...  15 us
    ppermute x10, starting transfers between devices, hop(): return lax.ppermute(value, 'row', pairs)  8.62 us
    pallas_call x1, Pallas kernels, order_panel(): pl.pallas_call(order_kernel, out_shape=shape_of((rows, sources * width),...  3.08 us
    unnamed x6, local copies, waits for them, and re-layouts  2.2 us
  transfers between devices with their start and end apart: 30, of which 11 were waited for; matrix products, arithmetic and copies ran while one was open for 0% of the time, Pallas kernels for 17%

profile of v8, /device:TPU:25, one launch (start us, length us, event | category | flops | bytes accessed | tf_op | source)
XLA Modules:
  0.0 104.3 jit_solution(14048554961108240397)
XLA Ops:
  0.6 2.0 %bitcast_select_fusion.2 = (bf16[1,256,1024]{2,1,0:T(8,128)(2,1)S(1)}, bf16[1,256,1024]{2,1,0:T(8,128)(2,1)S(1)}, bf16[1,256,1024]{2,1,0:T(8,128)(2,1)S(1)}) fusion(bf16[256,3,1024]{2,0,1:T(8,128)(2,1)} %param.8, pred[]{:T(512)S(6)} %eq.10, bf16[3,256,1024]{2,1,0:T(8,128)(2,1)} %param.9, pred[]{:T(512)S(6)} %eq.12, pred[]{:T(512)S(6)} %eq.11), kind=kLoop, calls=%fused_computation.4 | loop fusion | flops 1048576 | bytes 4718595 | tf_op jit(solution)/shard_map/jit(_where)/select_n | solution.py:479
  2.6 0.0 copy-start.2
  2.7 0.2 pad_maximum_fusion.refs_0_
  2.8 1.3 %collective-permute-start.8 = (bf16[3,256,1024]{2,1,0:T(8,128)(2,1)S(1)}, bf16[3,256,1024]{2,1,0:T(8,128)(2,1)S(1)}, u32[]{:S(2)}, u32[]{:S(2)}) collective-permute-start(bf16[3,256,1024]{2,1,0:T(8,128)(2,1)S(1)} %pad_maximum_fusion.refs_0_), channel_id=1, source_target_pairs={{0,2},{1,3},{2,0},{3,1},{4,6},{5,7},{6,4},{7,5},{8,10},{9,11},{10,... | collective-permute-start | bytes 4718600 | tf_op jit(solution)/shard_map/ppermute | solution.py:15
  4.1 0.2 collective-permute-start
  4.3 0.1 collective-permute-start.1
  4.3 1.2 %collective-permute-start.2 = (bf16[256,512]{1,0:T(8,128)(2,1)S(1)}, bf16[256,512]{1,0:T(8,128)(2,1)}, u32[]{:S(2)}, u32[]{:S(2)}) collective-permute-start(bf16[256,512]{1,0:T(8,128)(2,1)S(1)} %bitcast.29), channel_id=1, source_target_pairs={{0,4},{4,0},{8,12},{12,8},{16,20},{20,16},{24,28},{28,24},{1,5},{5... | collective-permute-start | bytes 786440 | tf_op jit(solution)/shard_map/ppermute | solution.py:15
  5.6 0.1 pad_add_fusion.index_ref
  5.7 2.2 %copy-done = bf16[1024,8,256]{2,1,0:T(8,128)(2,1)S(1)} copy-done((bf16[1024,8,256]{2,1,0:T(8,128)(2,1)S(1)}, bf16[1024,8,256]{2,1,0:T(8,128)(2,1)}, u32[]{:S(2)}) %copy-start) | copy-done | bytes 4194328
  7.8 3.1 %shard_map.68.panel_ref = bf16[1024,2048]{1,0:T(8,128)(2,1)S(1)} custom-call(s32[2]{0:T(128)S(1)} %pad_add_fusion.index_ref, bf16[1024,8,256]{2,1,0:T(8,128)(2,1)S(1)} %copy-done), custom_call_target="tpu_custom_call" | custom-call | bytes 28800000 | tf_op jit(solution)/shard_map/pallas_call | solution.py:154
  10.9 4.8 %collective-permute-done.refs_2_ = bf16[256,512]{1,0:T(8,128)(2,1)} collective-permute-done((bf16[256,512]{1,0:T(8,128)(2,1)S(1)}, bf16[256,512]{1,0:T(8,128)(2,1)}, u32[]{:S(2)}, u32[]{:S(2)}) %collective-permute-start) | collective-permute-done | bytes 262176 | tf_op jit(solution)/shard_map/ppermute | solution.py:15
  15.7 0.8 collective-permute-start.5
  16.5 1.2 %collective-permute-start.3 = (bf16[256,512]{1,0:T(8,128)(2,1)}, bf16[256,512]{1,0:T(8,128)(2,1)S(1)}, u32[]{:S(2)}, u32[]{:S(2)}) collective-permute-start(bf16[256,512]{1,0:T(8,128)(2,1)} %collective-permute-done.refs_2_), channel_id=1, source_target_pairs={{0,4},{4,0},{8,12},{12,8},{16,20},{20,16},{24,28},{28,24},{1,5},{5... | collective-permute-start | bytes 786440 | tf_op jit(solution)/shard_map/ppermute | solution.py:15
  17.8 0.0 collective-permute-done.1.refs_4_
  17.8 0.0 collective-permute-done.2.refs_1_
  17.8 0.2 collective-permute-start.4
  18.0 5.8 %collective-permute-done.5.refs_6_ = bf16[256,512]{1,0:T(8,128)(2,1)S(1)} collective-permute-done((bf16[256,512]{1,0:T(8,128)(2,1)S(1)}, bf16[256,512]{1,0:T(8,128)(2,1)S(1)}, u32[]{:S(2)}, u32[]{:S(2)}) %collective-permute-start.5) | collective-permute-done | bytes 262176 | tf_op jit(solution)/shard_map/ppermute | solution.py:15
  23.8 1.2 %collective-permute-start.6 = (bf16[256,512]{1,0:T(8,128)(2,1)S(1)}, bf16[256,512]{1,0:T(8,128)(2,1)S(1)}, u32[]{:S(2)}, u32[]{:S(2)}) collective-permute-start(bf16[256,512]{1,0:T(8,128)(2,1)S(1)} %collective-permute-done.5.refs_6_), channel_id=1, source_target_pairs={{0,4},{4,0},{8,12},{12,8},{16,20},{20,16},{24,28},{28,24},{1,5},{5... | collective-permute-start | bytes 786440 | tf_op jit(solution)/shard_map/ppermute | solution.py:15
  25.0 2.9 %collective-permute-done.4.refs_5_ = bf16[256,512]{1,0:T(8,128)(2,1)S(1)} collective-permute-done((bf16[256,512]{1,0:T(8,128)(2,1)}, bf16[256,512]{1,0:T(8,128)(2,1)S(1)}, u32[]{:S(2)}, u32[]{:S(2)}) %collective-permute-start.4) | collective-permute-done | bytes 262176 | tf_op jit(solution)/shard_map/ppermute | solution.py:15
  27.9 3.3 %shard_map.69.refs_1_ = f32[1024,512]{1,0:T(8,128)S(1)} custom-call(s32[2]{0:T(128)S(1)} %pad_add_fusion.index_ref, bf16[1024,2048]{1,0:T(8,128)(2,1)S(1)} %shard_map.68.panel_ref, f32[256,512]{1,0:T(8,128)S(1)} %copy-done.1, bf16[256,512]{1,0:T(8,128)(2,1)S(1)} %bitcast.31, bf16[256,512]{1,0:T(8,128)(2,1)} %collective-permute-done.2.refs_1_, ...), custom_call_target="tpu_custom_call" | custom-call | bytes 28800000 | tf_op jit(solution)/shard_map/pallas_call | solution.py:446
  31.1 0.3 collective-permute-done.6.refs_0_
  31.4 1.6 %shard_map.70 = (f32[2,1024,128]{2,1,0:T(8,128)S(1)}, bf16[2,1024,128]{2,1,0:T(8,128)(2,1)S(1)}) custom-call(s32[2]{0:T(128)S(1)} %pad_add_fusion.index_ref, bf16[1024,2048]{1,0:T(8,128)(2,1)S(1)} %shard_map.68.panel_ref, bf16[256,512]{1,0:T(8,128)(2,1)S(1)} %collective-permute-done.6.refs_0_, f32[1024,512]{1,0:T(8,128)S(1)} %shard_map.69.refs_1_), custom_call_target="tpu_custom_call" | custom-call | bytes 3600000 | tf_op jit(solution)/shard_map/pallas_call | solution.py:446
  33.0 5.8 %collective-permute-start.7 = (bf16[2,1024,128]{2,1,0:T(8,128)(2,1)S(1)}, bf16[2,1024,128]{2,1,0:T(8,128)(2,1)S(1)}, u32[]{:S(2)}, u32[]{:S(2)}) collective-permute-start(bf16[2,1024,128]{2,1,0:T(8,128)(2,1)S(1)} %get-tuple-element.33), channel_id=1, source_target_pairs={{0,1},{1,0},{2,3},{3,2},{4,5},{5,4},{6,7},{7,6},{8,9},{9,8},{10,11... | collective-permute-start | bytes 1572872 | tf_op jit(solution)/shard_map/ppermute | solution.py:15
  38.8 0.1 collective-permute-start.9
  38.9 1.5 %collective-permute-done.7.moved_ref = bf16[2,1024,128]{2,1,0:T(8,128)(2,1)S(1)} collective-permute-done((bf16[2,1024,128]{2,1,0:T(8,128)(2,1)S(1)}, bf16[2,1024,128]{2,1,0:T(8,128)(2,1)S(1)}, u32[]{:S(2)}, u32[]{:S(2)}) %collective-permute-start.7) | collective-permute-done | bytes 524320 | tf_op jit(solution)/shard_map/ppermute | solution.py:15
  40.3 0.4 collective-permute-start.10
  40.7 0.7 shard_map.71
  41.4 0.6 collective-permute-start.11
  42.0 0.7 collective-permute-start.13
  42.7 0.7 collective-permute-start.14
  43.4 1.5 %collective-permute-done.10.refs_3_.refs_1_ = bf16[3,256,1024]{2,1,0:T(8,128)(2,1)S(1)} collective-permute-done((bf16[3,256,1024]{2,1,0:T(8,128)(2,1)S(1)}, bf16[3,256,1024]{2,1,0:T(8,128)(2,1)S(1)}, u32[]{:S(2)}, u32[]{:S(2)}) %collective-permute-start.10) | collective-permute-done | bytes 1572896 | tf_op jit(solution)/shard_map/ppermute | solution.py:15
  44.8 0.7 shard_map.72.product_ref
  45.5 3.7 %collective-permute-done.11.moved_ref = bf16[1024,128]{1,0:T(8,128)(2,1)S(1)} collective-permute-done((bf16[1024,128]{1,0:T(8,128)(2,1)S(1)}, bf16[1024,128]{1,0:T(8,128)(2,1)S(1)}, u32[]{:S(2)}, u32[]{:S(2)}) %collective-permute-start.11) | collective-permute-done | bytes 262176 | tf_op jit(solution)/shard_map/ppermute | solution.py:15
  49.2 0.8 shard_map.73
  50.1 0.7 collective-permute-start.12
  50.8 0.6 shard_map.74.refs_0_
  51.4 1.3 %collective-permute-start.17 = (bf16[1024,128]{1,0:T(8,128)(2,1)S(1)}, bf16[1024,128]{1,0:T(8,128)(2,1)S(1)}, u32[]{:S(2)}, u32[]{:S(2)}) collective-permute-start(bf16[1024,128]{1,0:T(8,128)(2,1)S(1)} %shard_map.74.refs_0_), channel_id=1, source_target_pairs={{4,8},{0,24},{5,9},{1,25},{6,10},{2,26},{7,11},{3,27}} | collective-permute-start | bytes 786440 | tf_op jit(solution)/shard_map/ppermute | solution.py:458
  52.7 0.7 collective-permute-start.19
  53.3 0.7 collective-permute-start.16
  54.0 0.7 collective-permute-start.15
  54.7 0.6 shard_map.76
  55.4 11.3 %collective-permute-done.17.refs_2_.first_ref = bf16[1024,128]{1,0:T(8,128)(2,1)S(1)} collective-permute-done((bf16[1024,128]{1,0:T(8,128)(2,1)S(1)}, bf16[1024,128]{1,0:T(8,128)(2,1)S(1)}, u32[]{:S(2)}, u32[]{:S(2)}) %collective-permute-start.17) | collective-permute-done | bytes 262176 | tf_op jit(solution)/shard_map/ppermute | solution.py:458
  66.7 0.6 shard_map.77.refs_1_
  67.3 1.3 %collective-permute-start.20 = (bf16[1024,128]{1,0:T(8,128)(2,1)S(1)}, bf16[1024,128]{1,0:T(8,128)(2,1)S(1)}, u32[]{:S(2)}, u32[]{:S(2)}) collective-permute-start(bf16[1024,128]{1,0:T(8,128)(2,1)S(1)} %shard_map.77.refs_1_), channel_id=1, source_target_pairs={{8,24},{9,25},{10,26},{11,27}} | collective-permute-start | bytes 786440 | tf_op jit(solution)/shard_map/ppermute | solution.py:458
  68.6 0.7 collective-permute-start.21
  69.3 0.7 collective-permute-start.22
  70.0 0.6 shard_map.75.line0_ref
  70.6 1.3 %collective-permute-start.18 = (bf16[1024,128]{1,0:T(8,128)(2,1)S(1)}, bf16[1024,128]{1,0:T(8,128)(2,1)S(1)}, u32[]{:S(2)}, u32[]{:S(2)}) collective-permute-start(bf16[1024,128]{1,0:T(8,128)(2,1)S(1)} %shard_map.75.line0_ref), channel_id=1, source_target_pairs={{0,4},{16,20},{24,28},{1,5},{17,21},{25,29},{2,6},{18,22},{26,30},... | collective-permute-start | bytes 786440 | tf_op jit(solution)/shard_map/ppermute | solution.py:458
  71.9 4.8 %collective-permute-done.20.refs_2_ = bf16[1024,128]{1,0:T(8,128)(2,1)S(1)} collective-permute-done((bf16[1024,128]{1,0:T(8,128)(2,1)S(1)}, bf16[1024,128]{1,0:T(8,128)(2,1)S(1)}, u32[]{:S(2)}, u32[]{:S(2)}) %collective-permute-start.20) | collective-permute-done | bytes 262176 | tf_op jit(solution)/shard_map/ppermute | solution.py:458
  76.7 0.6 shard_map.78.line_ref
  77.3 9.4 %collective-permute-start.26 = (bf16[1024,128]{1,0:T(8,128)(2,1)S(1)}, bf16[1024,128]{1,0:T(8,128)(2,1)S(1)}, u32[]{:S(2)}, u32[]{:S(2)}) collective-permute-start(bf16[1024,128]{1,0:T(8,128)(2,1)S(1)} %shard_map.78.line_ref), channel_id=1, source_target_pairs={{0,4},{4,0},{8,12},{12,8},{16,20},{20,16},{24,28},{28,24},{1,5},{5... | collective-permute-start | bytes 786440 | tf_op jit(solution)/shard_map/ppermute | solution.py:15
  86.8 0.6 shard_map.79
  87.5 1.3 %collective-permute-start.23 = (bf16[2,256,128]{2,1,0:T(8,128)(2,1)S(1)}, bf16[2,256,128]{2,1,0:T(8,128)(2,1)S(1)}, u32[]{:S(2)}, u32[]{:S(2)}) collective-permute-start(bf16[2,256,128]{2,1,0:T(8,128)(2,1)S(1)} %get-tuple-element.53), channel_id=1, source_target_pairs={{0,1},{1,0},{2,3},{3,2},{4,5},{5,4},{6,7},{7,6},{8,9},{9,8},{10,11... | collective-permute-start | bytes 393224 | tf_op jit(solution)/shard_map/ppermute | solution.py:15
  88.8 0.8 collective-permute-start.24
  89.6 0.9 collective-permute-start.25
  90.5 2.0 %shard_map.80.current_ref = f32[1024,128]{1,0:T(8,128)S(1)} custom-call(s32[2]{0:T(128)S(1)} %pad_add_fusion.index_ref, f32[1024,128]{1,0:T(8,128)S(1)} %get-tuple-element.46.current_ref, bf16[1024,128]{1,0:T(8,128)(2,1)S(1)} %get-tuple-element.47.known_ref, bf16[1024,128]{1,0:T(8,128)(2,1)S(1)} %collective-permute-done.17.refs_2_.first_ref, ...), custom_call_target="tpu_custom_call" | custom-call | bytes 28800000 | tf_op jit(solution)/shard_map/pallas_call | solution.py:446
  92.5 1.1 %shard_map.82 = bf16[2,2,256,128]{3,2,1,0:T(8,128)(2,1)S(1)} custom-call(s32[2]{0:T(128)S(1)} %pad_add_fusion.index_ref, f32[1024,128]{1,0:T(8,128)S(1)} %shard_map.80.current_ref, bf16[1024,128]{1,0:T(8,128)(2,1)S(1)} %collective-permute-done.26.value_ref, bf16[3,256,1024]{2,1,0:T(8,128)(2,1)S(1)} %collective-permute-done.8.refs_2_.refs_0_, ...), custom_call_target="tpu_custom_call" | custom-call | bytes 3600000 | tf_op jit(solution)/shard_map/pallas_call | solution.py:446
  93.7 0.8 collective-permute-start.28
  94.6 2.3 %collective-permute-start.29 = (bf16[2,256,128]{2,1,0:T(8,128)(2,1)S(1)}, bf16[2,256,128]{2,1,0:T(8,128)(2,1)S(1)}, u32[]{:S(2)}, u32[]{:S(2)}) collective-permute-start(bf16[2,256,128]{2,1,0:T(8,128)(2,1)S(1)} %get-tuple-element.55), channel_id=1, source_target_pairs={{0,3},{1,2},{2,1},{3,0},{4,7},{5,6},{6,5},{7,4},{8,11},{9,10},{10,... | collective-permute-start | bytes 393224 | tf_op jit(solution)/shard_map/ppermute | solution.py:15
  96.9 1.1 %shard_map.81 = bf16[2,2,256,128]{3,2,1,0:T(8,128)(2,1)S(1)} custom-call(s32[2]{0:T(128)S(1)} %pad_add_fusion.index_ref, f32[1024,128]{1,0:T(8,128)S(1)} %shard_map.80.current_ref, bf16[1024,128]{1,0:T(8,128)(2,1)S(1)} %collective-permute-done.26.value_ref, bf16[3,256,1024]{2,1,0:T(8,128)(2,1)S(1)} %pad_maximum_fusion.refs_0_, ...), custom_call_target="tpu_custom_call" | custom-call | bytes 28800000 | tf_op jit(solution)/shard_map/pallas_call | solution.py:446
  98.1 0.1 collective-permute-start.27
  98.2 0.4 collective-permute-done.28.refs_6_
  98.6 3.9 %collective-permute-done.29.refs_7_ = bf16[2,256,128]{2,1,0:T(8,128)(2,1)S(1)} collective-permute-done((bf16[2,256,128]{2,1,0:T(8,128)(2,1)S(1)}, bf16[2,256,128]{2,1,0:T(8,128)(2,1)S(1)}, u32[]{:S(2)}, u32[]{:S(2)}) %collective-permute-start.29) | collective-permute-done | bytes 131104 | tf_op jit(solution)/shard_map/ppermute | solution.py:15
  102.5 1.7 %shard_map.83 = (bf16[3,256,512]{2,1,0:T(8,128)(2,1)}, f32[256,512]{1,0:T(8,128)}) custom-call(s32[2]{0:T(128)S(1)} %pad_add_fusion.index_ref, bf16[2,256,128]{2,1,0:T(8,128)(2,1)S(1)} %get-tuple-element.54.refs_0_, bf16[2,256,128]{2,1,0:T(8,128)(2,1)S(1)} %collective-permute-done.23.refs_1_, bf16[2,256,128]{2,1,0:T(8,128)(2,1)S(1)} %collective-permute-done.24.refs_2_, ...), custom_call_target="tpu_custom_call" | custom-call | bytes 3600000 | tf_op jit(solution)/shard_map/pallas_call | solution.py:433
  (24 shorter events, 0.1 us)
Async XLA Ops:
  2.6 1.5 %copy-start.2 = (bf16[1,256,512]{2,1,0:T(8,128)(2,1)S(1)}, bf16[1,256,512]{2,1,0:T(8,128)(2,1)}, u32[]{:S(2)}) copy-start(bf16[1,256,512]{2,1,0:T(8,128)(2,1)} %param.7) | copy-start | bytes 786436
  2.8 37.5 %collective-permute-start.8 = (bf16[3,256,1024]{2,1,0:T(8,128)(2,1)S(1)}, bf16[3,256,1024]{2,1,0:T(8,128)(2,1)S(1)}, u32[]{:S(2)}, u32[]{:S(2)}) collective-permute-start(bf16[3,256,1024]{2,1,0:T(8,128)(2,1)S(1)} %pad_maximum_fusion.refs_0_), channel_id=1, source_target_pairs={{0,2},{1,3},{2,0},{3,1},{4,6},{5,7},{6,4},{7,5},{8,10},{9,11},{10,... | collective-permute-start | bytes 4718600 | tf_op jit(solution)/shard_map/ppermute | solution.py:15
  4.1 11.6 %collective-permute-start = (bf16[256,512]{1,0:T(8,128)(2,1)S(1)}, bf16[256,512]{1,0:T(8,128)(2,1)}, u32[]{:S(2)}, u32[]{:S(2)}) collective-permute-start(bf16[256,512]{1,0:T(8,128)(2,1)S(1)} %bitcast.27), channel_id=1, source_target_pairs={{0,8},{4,12},{8,0},{12,4},{16,24},{20,28},{24,16},{28,20},{1,9},{5... | collective-permute-start | bytes 786440 | tf_op jit(solution)/shard_map/ppermute | solution.py:15
  4.3 13.5 %collective-permute-start.1 = (bf16[256,512]{1,0:T(8,128)(2,1)S(1)}, bf16[256,512]{1,0:T(8,128)(2,1)}, u32[]{:S(2)}, u32[]{:S(2)}) collective-permute-start(bf16[256,512]{1,0:T(8,128)(2,1)S(1)} %bitcast.28), channel_id=1, source_target_pairs={{0,16},{4,20},{8,24},{12,28},{16,0},{20,4},{24,8},{28,12},{1,17},{... | collective-permute-start | bytes 786440 | tf_op jit(solution)/shard_map/ppermute | solution.py:15
  4.3 13.4 %collective-permute-start.2 = (bf16[256,512]{1,0:T(8,128)(2,1)S(1)}, bf16[256,512]{1,0:T(8,128)(2,1)}, u32[]{:S(2)}, u32[]{:S(2)}) collective-permute-start(bf16[256,512]{1,0:T(8,128)(2,1)S(1)} %bitcast.29), channel_id=1, source_target_pairs={{0,4},{4,0},{8,12},{12,8},{16,20},{20,16},{24,28},{28,24},{1,5},{5... | collective-permute-start | bytes 786440 | tf_op jit(solution)/shard_map/ppermute | solution.py:15
  5.7 2.2 %copy-start = (bf16[1024,8,256]{2,1,0:T(8,128)(2,1)S(1)}, bf16[1024,8,256]{2,1,0:T(8,128)(2,1)}, u32[]{:S(2)}) copy-start(bf16[1024,8,256]{2,1,0:T(8,128)(2,1)} %panel_ref.1) | copy-start | bytes 12582916
  7.8 20.0 %copy-start.1 = (f32[256,512]{1,0:T(8,128)S(1)}, f32[256,512]{1,0:T(8,128)}, u32[]{:S(2)}) copy-start(f32[256,512]{1,0:T(8,128)} %side_ref.1) | copy-start | bytes 1572868
  15.7 8.1 %collective-permute-start.5 = (bf16[256,512]{1,0:T(8,128)(2,1)S(1)}, bf16[256,512]{1,0:T(8,128)(2,1)S(1)}, u32[]{:S(2)}, u32[]{:S(2)}) collective-permute-start(bf16[256,512]{1,0:T(8,128)(2,1)S(1)} %bitcast.30), channel_id=1, source_target_pairs={{0,24},{4,28},{8,16},{12,20},{16,8},{20,12},{24,0},{28,4},{1,25},{... | collective-permute-start | bytes 786440 | tf_op jit(solution)/shard_map/ppermute | solution.py:15
  16.5 8.5 %collective-permute-start.3 = (bf16[256,512]{1,0:T(8,128)(2,1)}, bf16[256,512]{1,0:T(8,128)(2,1)S(1)}, u32[]{:S(2)}, u32[]{:S(2)}) collective-permute-start(bf16[256,512]{1,0:T(8,128)(2,1)} %collective-permute-done.refs_2_), channel_id=1, source_target_pairs={{0,4},{4,0},{8,12},{12,8},{16,20},{20,16},{24,28},{28,24},{1,5},{5... | collective-permute-start | bytes 786440 | tf_op jit(solution)/shard_map/ppermute | solution.py:15
  17.8 10.1 %collective-permute-start.4 = (bf16[256,512]{1,0:T(8,128)(2,1)}, bf16[256,512]{1,0:T(8,128)(2,1)S(1)}, u32[]{:S(2)}, u32[]{:S(2)}) collective-permute-start(bf16[256,512]{1,0:T(8,128)(2,1)} %collective-permute-done.1.refs_4_), channel_id=1, source_target_pairs={{0,4},{4,0},{8,12},{12,8},{16,20},{20,16},{24,28},{28,24},{1,5},{5... | collective-permute-start | bytes 786440 | tf_op jit(solution)/shard_map/ppermute | solution.py:15
  23.8 7.7 %collective-permute-start.6 = (bf16[256,512]{1,0:T(8,128)(2,1)S(1)}, bf16[256,512]{1,0:T(8,128)(2,1)S(1)}, u32[]{:S(2)}, u32[]{:S(2)}) collective-permute-start(bf16[256,512]{1,0:T(8,128)(2,1)S(1)} %collective-permute-done.5.refs_6_), channel_id=1, source_target_pairs={{0,4},{4,0},{8,12},{12,8},{16,20},{20,16},{24,28},{28,24},{1,5},{5... | collective-permute-start | bytes 786440 | tf_op jit(solution)/shard_map/ppermute | solution.py:15
  33.0 7.3 %collective-permute-start.7 = (bf16[2,1024,128]{2,1,0:T(8,128)(2,1)S(1)}, bf16[2,1024,128]{2,1,0:T(8,128)(2,1)S(1)}, u32[]{:S(2)}, u32[]{:S(2)}) collective-permute-start(bf16[2,1024,128]{2,1,0:T(8,128)(2,1)S(1)} %get-tuple-element.33), channel_id=1, source_target_pairs={{0,1},{1,0},{2,3},{3,2},{4,5},{5,4},{6,7},{7,6},{8,9},{9,8},{10,11... | collective-permute-start | bytes 1572872 | tf_op jit(solution)/shard_map/ppermute | solution.py:15
  38.8 4.6 %collective-permute-start.9 = (bf16[3,256,1024]{2,1,0:T(8,128)(2,1)S(1)}, bf16[3,256,1024]{2,1,0:T(8,128)(2,1)S(1)}, u32[]{:S(2)}, u32[]{:S(2)}) collective-permute-start(bf16[3,256,1024]{2,1,0:T(8,128)(2,1)S(1)} %pad_maximum_fusion.refs_0_), channel_id=1, source_target_pairs={{0,1},{1,0},{2,3},{3,2},{4,5},{5,4},{6,7},{7,6},{8,9},{9,8},{10,11... | collective-permute-start | bytes 4718600 | tf_op jit(solution)/shard_map/ppermute | solution.py:15
  40.3 4.5 %collective-permute-start.10 = (bf16[3,256,1024]{2,1,0:T(8,128)(2,1)S(1)}, bf16[3,256,1024]{2,1,0:T(8,128)(2,1)S(1)}, u32[]{:S(2)}, u32[]{:S(2)}) collective-permute-start(bf16[3,256,1024]{2,1,0:T(8,128)(2,1)S(1)} %collective-permute-done.8.refs_2_.refs_0_), channel_id=1, source_target_pairs={{0,1},{1,0},{2,3},{3,2},{4,5},{5,4},{6,7},{7,6},{8,9},{9,8},{10,11... | collective-permute-start | bytes 4718600 | tf_op jit(solution)/shard_map/ppermute | solution.py:15
  41.4 7.8 %collective-permute-start.11 = (bf16[1024,128]{1,0:T(8,128)(2,1)S(1)}, bf16[1024,128]{1,0:T(8,128)(2,1)S(1)}, u32[]{:S(2)}, u32[]{:S(2)}) collective-permute-start(bf16[1024,128]{1,0:T(8,128)(2,1)S(1)} %get-tuple-element.38), channel_id=1, source_target_pairs={{0,2},{1,3},{2,0},{3,1},{4,6},{5,7},{6,4},{7,5},{8,10},{9,11},{10,... | collective-permute-start | bytes 786440 | tf_op jit(solution)/shard_map/ppermute | solution.py:15
  42.0 8.7 %collective-permute-start.13 = (bf16[1024,128]{1,0:T(8,128)(2,1)S(1)}, bf16[1024,128]{1,0:T(8,128)(2,1)S(1)}, u32[]{:S(2)}, u32[]{:S(2)}) collective-permute-start(bf16[1024,128]{1,0:T(8,128)(2,1)S(1)} %get-tuple-element.42), channel_id=1, source_target_pairs={{0,4},{1,5},{2,6},{3,7}} | collective-permute-start | bytes 786440 | tf_op jit(solution)/shard_map/ppermute | solution.py:458
  42.7 8.1 %collective-permute-start.14 = (bf16[1024,128]{1,0:T(8,128)(2,1)S(1)}, bf16[1024,128]{1,0:T(8,128)(2,1)S(1)}, u32[]{:S(2)}, u32[]{:S(2)}) collective-permute-start(bf16[1024,128]{1,0:T(8,128)(2,1)S(1)} %get-tuple-element.38), channel_id=1, source_target_pairs={{0,6},{1,7},{2,4},{3,5}} | collective-permute-start | bytes 786440 | tf_op jit(solution)/shard_map/ppermute | solution.py:503
  50.1 4.7 %collective-permute-start.12 = (bf16[1024,128]{1,0:T(8,128)(2,1)S(1)}, bf16[1024,128]{1,0:T(8,128)(2,1)S(1)}, u32[]{:S(2)}, u32[]{:S(2)}) collective-permute-start(bf16[1024,128]{1,0:T(8,128)(2,1)S(1)} %get-tuple-element.39.own_ref.refs_0_.own0_ref), channel_id=1, source_target_pairs={{0,8},{1,9},{2,10},{3,11}} | collective-permute-start | bytes 786440 | tf_op jit(solution)/shard_map/ppermute | solution.py:458
  51.4 15.3 %collective-permute-start.17 = (bf16[1024,128]{1,0:T(8,128)(2,1)S(1)}, bf16[1024,128]{1,0:T(8,128)(2,1)S(1)}, u32[]{:S(2)}, u32[]{:S(2)}) collective-permute-start(bf16[1024,128]{1,0:T(8,128)(2,1)S(1)} %shard_map.74.refs_0_), channel_id=1, source_target_pairs={{4,8},{0,24},{5,9},{1,25},{6,10},{2,26},{7,11},{3,27}} | collective-permute-start | bytes 786440 | tf_op jit(solution)/shard_map/ppermute | solution.py:458
  52.7 14.0 %collective-permute-start.19 = (bf16[1024,128]{1,0:T(8,128)(2,1)S(1)}, bf16[1024,128]{1,0:T(8,128)(2,1)S(1)}, u32[]{:S(2)}, u32[]{:S(2)}) collective-permute-start(bf16[1024,128]{1,0:T(8,128)(2,1)S(1)} %shard_map.74.refs_0_), channel_id=1, source_target_pairs={{4,12},{5,13},{6,14},{7,15}} | collective-permute-start | bytes 786440 | tf_op jit(solution)/shard_map/ppermute | solution.py:458
  53.3 16.6 %collective-permute-start.16 = (bf16[1024,128]{1,0:T(8,128)(2,1)S(1)}, bf16[1024,128]{1,0:T(8,128)(2,1)S(1)}, u32[]{:S(2)}, u32[]{:S(2)}) collective-permute-start(bf16[1024,128]{1,0:T(8,128)(2,1)S(1)} %shard_map.74.refs_0_), channel_id=1, source_target_pairs={{0,16},{1,17},{2,18},{3,19}} | collective-permute-start | bytes 786440 | tf_op jit(solution)/shard_map/ppermute | solution.py:458
  54.0 17.9 %collective-permute-start.15 = (bf16[1024,128]{1,0:T(8,128)(2,1)S(1)}, bf16[1024,128]{1,0:T(8,128)(2,1)S(1)}, u32[]{:S(2)}, u32[]{:S(2)}) collective-permute-start(bf16[1024,128]{1,0:T(8,128)(2,1)S(1)} %shard_map.74.refs_0_), channel_id=1, source_target_pairs={{4,20},{0,12},{5,21},{1,13},{6,22},{2,14},{7,23},{3,15}} | collective-permute-start | bytes 786440 | tf_op jit(solution)/shard_map/ppermute | solution.py:458
  67.3 9.4 %collective-permute-start.20 = (bf16[1024,128]{1,0:T(8,128)(2,1)S(1)}, bf16[1024,128]{1,0:T(8,128)(2,1)S(1)}, u32[]{:S(2)}, u32[]{:S(2)}) collective-permute-start(bf16[1024,128]{1,0:T(8,128)(2,1)S(1)} %shard_map.77.refs_1_), channel_id=1, source_target_pairs={{8,24},{9,25},{10,26},{11,27}} | collective-permute-start | bytes 786440 | tf_op jit(solution)/shard_map/ppermute | solution.py:458
  68.6 8.1 %collective-permute-start.21 = (bf16[1024,128]{1,0:T(8,128)(2,1)S(1)}, bf16[1024,128]{1,0:T(8,128)(2,1)S(1)}, u32[]{:S(2)}, u32[]{:S(2)}) collective-permute-start(bf16[1024,128]{1,0:T(8,128)(2,1)S(1)} %shard_map.77.refs_1_), channel_id=1, source_target_pairs={{8,16},{12,28},{9,17},{13,29},{10,18},{14,30},{11,19},{15,31}} | collective-permute-start | bytes 786440 | tf_op jit(solution)/shard_map/ppermute | solution.py:458
  69.3 7.4 %collective-permute-start.22 = (bf16[1024,128]{1,0:T(8,128)(2,1)S(1)}, bf16[1024,128]{1,0:T(8,128)(2,1)S(1)}, u32[]{:S(2)}, u32[]{:S(2)}) collective-permute-start(bf16[1024,128]{1,0:T(8,128)(2,1)S(1)} %shard_map.77.refs_1_), channel_id=1, source_target_pairs={{8,0},{9,1},{10,2},{11,3}} | collective-permute-start | bytes 786440 | tf_op jit(solution)/shard_map/ppermute | solution.py:458
  70.6 16.2 %collective-permute-start.18 = (bf16[1024,128]{1,0:T(8,128)(2,1)S(1)}, bf16[1024,128]{1,0:T(8,128)(2,1)S(1)}, u32[]{:S(2)}, u32[]{:S(2)}) collective-permute-start(bf16[1024,128]{1,0:T(8,128)(2,1)S(1)} %shard_map.75.line0_ref), channel_id=1, source_target_pairs={{0,4},{16,20},{24,28},{1,5},{17,21},{25,29},{2,6},{18,22},{26,30},... | collective-permute-start | bytes 786440 | tf_op jit(solution)/shard_map/ppermute | solution.py:458
  77.3 15.2 %collective-permute-start.26 = (bf16[1024,128]{1,0:T(8,128)(2,1)S(1)}, bf16[1024,128]{1,0:T(8,128)(2,1)S(1)}, u32[]{:S(2)}, u32[]{:S(2)}) collective-permute-start(bf16[1024,128]{1,0:T(8,128)(2,1)S(1)} %shard_map.78.line_ref), channel_id=1, source_target_pairs={{0,4},{4,0},{8,12},{12,8},{16,20},{20,16},{24,28},{28,24},{1,5},{5... | collective-permute-start | bytes 786440 | tf_op jit(solution)/shard_map/ppermute | solution.py:15
  87.5 10.6 %collective-permute-start.23 = (bf16[2,256,128]{2,1,0:T(8,128)(2,1)S(1)}, bf16[2,256,128]{2,1,0:T(8,128)(2,1)S(1)}, u32[]{:S(2)}, u32[]{:S(2)}) collective-permute-start(bf16[2,256,128]{2,1,0:T(8,128)(2,1)S(1)} %get-tuple-element.53), channel_id=1, source_target_pairs={{0,1},{1,0},{2,3},{3,2},{4,5},{5,4},{6,7},{7,6},{8,9},{9,8},{10,11... | collective-permute-start | bytes 393224 | tf_op jit(solution)/shard_map/ppermute | solution.py:15
  88.8 9.4 %collective-permute-start.24 = (bf16[2,256,128]{2,1,0:T(8,128)(2,1)S(1)}, bf16[2,256,128]{2,1,0:T(8,128)(2,1)S(1)}, u32[]{:S(2)}, u32[]{:S(2)}) collective-permute-start(bf16[2,256,128]{2,1,0:T(8,128)(2,1)S(1)} %get-tuple-element.52), channel_id=1, source_target_pairs={{0,2},{1,3},{2,0},{3,1},{4,6},{5,7},{6,4},{7,5},{8,10},{9,11},{10,... | collective-permute-start | bytes 393224 | tf_op jit(solution)/shard_map/ppermute | solution.py:15
  89.6 8.6 %collective-permute-start.25 = (bf16[2,256,128]{2,1,0:T(8,128)(2,1)S(1)}, bf16[2,256,128]{2,1,0:T(8,128)(2,1)S(1)}, u32[]{:S(2)}, u32[]{:S(2)}) collective-permute-start(bf16[2,256,128]{2,1,0:T(8,128)(2,1)S(1)} %get-tuple-element.51), channel_id=1, source_target_pairs={{0,3},{1,2},{2,1},{3,0},{4,7},{5,6},{6,5},{7,4},{8,11},{9,10},{10,... | collective-permute-start | bytes 393224 | tf_op jit(solution)/shard_map/ppermute | solution.py:15
  93.7 4.9 %collective-permute-start.28 = (bf16[2,256,128]{2,1,0:T(8,128)(2,1)S(1)}, bf16[2,256,128]{2,1,0:T(8,128)(2,1)S(1)}, u32[]{:S(2)}, u32[]{:S(2)}) collective-permute-start(bf16[2,256,128]{2,1,0:T(8,128)(2,1)S(1)} %get-tuple-element.56), channel_id=1, source_target_pairs={{0,2},{1,3},{2,0},{3,1},{4,6},{5,7},{6,4},{7,5},{8,10},{9,11},{10,... | collective-permute-start | bytes 393224 | tf_op jit(solution)/shard_map/ppermute | solution.py:15
  94.6 7.9 %collective-permute-start.29 = (bf16[2,256,128]{2,1,0:T(8,128)(2,1)S(1)}, bf16[2,256,128]{2,1,0:T(8,128)(2,1)S(1)}, u32[]{:S(2)}, u32[]{:S(2)}) collective-permute-start(bf16[2,256,128]{2,1,0:T(8,128)(2,1)S(1)} %get-tuple-element.55), channel_id=1, source_target_pairs={{0,3},{1,2},{2,1},{3,0},{4,7},{5,6},{6,5},{7,4},{8,11},{9,10},{10,... | collective-permute-start | bytes 393224 | tf_op jit(solution)/shard_map/ppermute | solution.py:15
  98.1 4.4 %collective-permute-start.27 = (bf16[2,256,128]{2,1,0:T(8,128)(2,1)S(1)}, bf16[2,256,128]{2,1,0:T(8,128)(2,1)S(1)}, u32[]{:S(2)}, u32[]{:S(2)}) collective-permute-start(bf16[2,256,128]{2,1,0:T(8,128)(2,1)S(1)} %get-tuple-element.57), channel_id=1, source_target_pairs={{0,1},{1,0},{2,3},{3,2},{4,5},{5,4},{6,7},{7,6},{8,9},{9,8},{10,11... | collective-permute-start | bytes 393224 | tf_op jit(solution)/shard_map/ppermute | solution.py:15

commit v9 on v8

--- a/solution.py
+++ b/solution.py
@@ -356,9 +356,9 @@
     return local(functools.partial(pick_kernel, holders), shape_of(parts[0].shape, BF16), [index] + list(parts))
 
 
-def known_kernel(index_ref, own0_ref, at2_ref, fourth_ref, line0_ref, across0_ref, line_ref, known_ref, pieces_ref):
+def known_kernel(index_ref, own0_ref, z0_ref, at2_ref, fourth_ref, line0_ref, across0_ref, line_ref, known_ref, pieces_ref):
     row = index_ref[0]
-    for holder, part in enumerate((own0_ref, across0_ref, at2_ref, fourth_ref, line0_ref, across0_ref, line0_ref, across0_ref)):
+    for holder, part in enumerate((own0_ref, z0_ref, at2_ref, fourth_ref, line0_ref, across0_ref, line0_ref, across0_ref)):
         copy_where(row == holder, part, known_ref)
     cut(index_ref, known_ref, pieces_ref, 0)
     cut(index_ref, line_ref, pieces_ref, 1)
@@ -517,13 +517,13 @@
     own2 = local(second_step_kernel, narrow, [index, own0, ahead, product, first, second])
     z6 = hop(own2, (2, 6))
     z4 = hop(own2, (2, 4), (3, 7))
-    z0 = hop(own2, (2, 0))
+    z0 = hop(own2, (2, 0), (0, 1))
     line0 = pick(index, (0, 0, 0, 0, 1, 0, 2, 0), own0, third, first)
-    across0 = hop(line0, (0, 1), (4, 5), (6, 7))
+    across0 = hop(line0, (4, 5), (6, 7))
     line = pick(index, (5, 0, 1, 1, 3, 4, 2, 3), own1, own2, z6, z4, fourth, z0)
     across = flip(line, "row", n_row, 1)
     pieces = shape_of((n_col, 2, strip, chunk), BF16)
-    known, middle = local(known_kernel, (narrow, pieces), [index, own0, at2, fourth, line0, across0, line])
+    known, middle = local(known_kernel, (narrow, pieces), [index, own0, z0, at2, fourth, line0, across0, line])
     middle = swap_pieces(middle, n_col)
     scratch = [pltpu.VMEM((rows, chunk), F32)]
     current = local(functools.partial(middle_kernel, n_col), wide, [index, current, known, first, line] + slots, scratch, us=8)

time: 105 us -> 105 us (level)
  no operation moved by 1% of the time
where the time goes in v9:
time: 105 us; the launch traced here: 104 us
  waiting for transfers between devices  41 us (39%)
  starting transfers between devices  37.9 us (36%)
  Pallas kernels  19.8 us (19%)
  local copies, waits for them, and re-layouts  2.27 us (2%)
  other arithmetic  2.25 us (2%)
  between operations  1.16 us (1%)
    ppermute x19, starting transfers between devices, flip(): return lax.ppermute(value, axis, [(i, i ^ bit) for i in range(size)])  28.6 us
    ppermute x19, waiting for transfers between devices, flip(): return lax.ppermute(value, axis, [(i, i ^ bit) for i in range(size)])  25.3 us
    ppermute x10, waiting for transfers between devices, hop(): return lax.ppermute(value, 'row', pairs)  15.7 us
    pallas_call x14, Pallas kernels, local(): pl.pallas_call(kernel, out_shape=out_shape, in_specs=[SMEM] + [VMEM] * (l...  15 us
    ppermute x10, starting transfers between devices, hop(): return lax.ppermute(value, 'row', pairs)  8.62 us
    pallas_call x1, Pallas kernels, order_panel(): pl.pallas_call(order_kernel, out_shape=shape_of((rows, sources * width),...  3.08 us
    unnamed x6, local copies, waits for them, and re-layouts  2.2 us
  transfers between devices with their start and end apart: 30, of which 11 were waited for; matrix products, arithmetic and copies ran while one was open for 0% of the time, Pallas kernels for 17%

profile of v9, /device:TPU:25, one launch (start us, length us, event | category | flops | bytes accessed | tf_op | source)
XLA Modules:
  0.0 104.3 jit_solution(8908992086804071377)
XLA Ops:
  0.6 2.0 %bitcast_select_fusion.2 = (bf16[1,256,1024]{2,1,0:T(8,128)(2,1)S(1)}, bf16[1,256,1024]{2,1,0:T(8,128)(2,1)S(1)}, bf16[1,256,1024]{2,1,0:T(8,128)(2,1)S(1)}) fusion(bf16[256,3,1024]{2,0,1:T(8,128)(2,1)} %param.8, pred[]{:T(512)S(6)} %eq.10, bf16[3,256,1024]{2,1,0:T(8,128)(2,1)} %param.9, pred[]{:T(512)S(6)} %eq.12, pred[]{:T(512)S(6)} %eq.11), kind=kLoop, calls=%fused_computation.4 | loop fusion | flops 1048576 | bytes 4718595 | tf_op jit(solution)/shard_map/jit(_where)/select_n | solution.py:479
  2.6 0.0 copy-start.2
  2.7 0.2 pad_maximum_fusion.refs_0_
  2.8 1.3 %collective-permute-start.8 = (bf16[3,256,1024]{2,1,0:T(8,128)(2,1)S(1)}, bf16[3,256,1024]{2,1,0:T(8,128)(2,1)S(1)}, u32[]{:S(2)}, u32[]{:S(2)}) collective-permute-start(bf16[3,256,1024]{2,1,0:T(8,128)(2,1)S(1)} %pad_maximum_fusion.refs_0_), channel_id=1, source_target_pairs={{0,2},{1,3},{2,0},{3,1},{4,6},{5,7},{6,4},{7,5},{8,10},{9,11},{10,... | collective-permute-start | bytes 4718600 | tf_op jit(solution)/shard_map/ppermute | solution.py:15
  4.1 0.2 collective-permute-start
  4.3 0.1 collective-permute-start.1
  4.3 1.2 %collective-permute-start.2 = (bf16[256,512]{1,0:T(8,128)(2,1)S(1)}, bf16[256,512]{1,0:T(8,128)(2,1)}, u32[]{:S(2)}, u32[]{:S(2)}) collective-permute-start(bf16[256,512]{1,0:T(8,128)(2,1)S(1)} %bitcast.29), channel_id=1, source_target_pairs={{0,4},{4,0},{8,12},{12,8},{16,20},{20,16},{24,28},{28,24},{1,5},{5... | collective-permute-start | bytes 786440 | tf_op jit(solution)/shard_map/ppermute | solution.py:15
  5.6 0.1 pad_add_fusion.index_ref
  5.7 2.2 %copy-done = bf16[1024,8,256]{2,1,0:T(8,128)(2,1)S(1)} copy-done((bf16[1024,8,256]{2,1,0:T(8,128)(2,1)S(1)}, bf16[1024,8,256]{2,1,0:T(8,128)(2,1)}, u32[]{:S(2)}) %copy-start) | copy-done | bytes 4194328
  7.8 3.1 %shard_map.68.panel_ref = bf16[1024,2048]{1,0:T(8,128)(2,1)S(1)} custom-call(s32[2]{0:T(128)S(1)} %pad_add_fusion.index_ref, bf16[1024,8,256]{2,1,0:T(8,128)(2,1)S(1)} %copy-done), custom_call_target="tpu_custom_call" | custom-call | bytes 28800000 | tf_op jit(solution)/shard_map/pallas_call | solution.py:154
  10.9 4.8 %collective-permute-done.refs_2_ = bf16[256,512]{1,0:T(8,128)(2,1)} collective-permute-done((bf16[256,512]{1,0:T(8,128)(2,1)S(1)}, bf16[256,512]{1,0:T(8,128)(2,1)}, u32[]{:S(2)}, u32[]{:S(2)}) %collective-permute-start) | collective-permute-done | bytes 262176 | tf_op jit(solution)/shard_map/ppermute | solution.py:15
  15.7 0.8 collective-permute-start.5
  16.5 1.2 %collective-permute-start.3 = (bf16[256,512]{1,0:T(8,128)(2,1)}, bf16[256,512]{1,0:T(8,128)(2,1)S(1)}, u32[]{:S(2)}, u32[]{:S(2)}) collective-permute-start(bf16[256,512]{1,0:T(8,128)(2,1)} %collective-permute-done.refs_2_), channel_id=1, source_target_pairs={{0,4},{4,0},{8,12},{12,8},{16,20},{20,16},{24,28},{28,24},{1,5},{5... | collective-permute-start | bytes 786440 | tf_op jit(solution)/shard_map/ppermute | solution.py:15
  17.8 0.2 collective-permute-start.4
  18.0 5.8 %collective-permute-done.5.refs_6_ = bf16[256,512]{1,0:T(8,128)(2,1)S(1)} collective-permute-done((bf16[256,512]{1,0:T(8,128)(2,1)S(1)}, bf16[256,512]{1,0:T(8,128)(2,1)S(1)}, u32[]{:S(2)}, u32[]{:S(2)}) %collective-permute-start.5) | collective-permute-done | bytes 262176 | tf_op jit(solution)/shard_map/ppermute | solution.py:15
  23.8 1.2 %collective-permute-start.6 = (bf16[256,512]{1,0:T(8,128)(2,1)S(1)}, bf16[256,512]{1,0:T(8,128)(2,1)S(1)}, u32[]{:S(2)}, u32[]{:S(2)}) collective-permute-start(bf16[256,512]{1,0:T(8,128)(2,1)S(1)} %collective-permute-done.5.refs_6_), channel_id=1, source_target_pairs={{0,4},{4,0},{8,12},{12,8},{16,20},{20,16},{24,28},{28,24},{1,5},{5... | collective-permute-start | bytes 786440 | tf_op jit(solution)/shard_map/ppermute | solution.py:15
  25.0 0.0 collective-permute-done.3.refs_3_
  25.0 2.9 %collective-permute-done.4.refs_5_ = bf16[256,512]{1,0:T(8,128)(2,1)S(1)} collective-permute-done((bf16[256,512]{1,0:T(8,128)(2,1)}, bf16[256,512]{1,0:T(8,128)(2,1)S(1)}, u32[]{:S(2)}, u32[]{:S(2)}) %collective-permute-start.4) | collective-permute-done | bytes 262176 | tf_op jit(solution)/shard_map/ppermute | solution.py:15
  27.9 3.3 %shard_map.69.refs_1_ = f32[1024,512]{1,0:T(8,128)S(1)} custom-call(s32[2]{0:T(128)S(1)} %pad_add_fusion.index_ref, bf16[1024,2048]{1,0:T(8,128)(2,1)S(1)} %shard_map.68.panel_ref, f32[256,512]{1,0:T(8,128)S(1)} %copy-done.1, bf16[256,512]{1,0:T(8,128)(2,1)S(1)} %bitcast.31, bf16[256,512]{1,0:T(8,128)(2,1)} %collective-permute-done.2.refs_1_, ...), custom_call_target="tpu_custom_call" | custom-call | bytes 28800000 | tf_op jit(solution)/shard_map/pallas_call | solution.py:446
  31.1 0.3 collective-permute-done.6.refs_0_
  31.4 1.6 %shard_map.70 = (f32[2,1024,128]{2,1,0:T(8,128)S(1)}, bf16[2,1024,128]{2,1,0:T(8,128)(2,1)S(1)}) custom-call(s32[2]{0:T(128)S(1)} %pad_add_fusion.index_ref, bf16[1024,2048]{1,0:T(8,128)(2,1)S(1)} %shard_map.68.panel_ref, bf16[256,512]{1,0:T(8,128)(2,1)S(1)} %collective-permute-done.6.refs_0_, f32[1024,512]{1,0:T(8,128)S(1)} %shard_map.69.refs_1_), custom_call_target="tpu_custom_call" | custom-call | bytes 3600000 | tf_op jit(solution)/shard_map/pallas_call | solution.py:446
  33.0 5.8 %collective-permute-start.7 = (bf16[2,1024,128]{2,1,0:T(8,128)(2,1)S(1)}, bf16[2,1024,128]{2,1,0:T(8,128)(2,1)S(1)}, u32[]{:S(2)}, u32[]{:S(2)}) collective-permute-start(bf16[2,1024,128]{2,1,0:T(8,128)(2,1)S(1)} %get-tuple-element.33), channel_id=1, source_target_pairs={{0,1},{1,0},{2,3},{3,2},{4,5},{5,4},{6,7},{7,6},{8,9},{9,8},{10,11... | collective-permute-start | bytes 1572872 | tf_op jit(solution)/shard_map/ppermute | solution.py:15
  38.8 0.1 collective-permute-start.9
  38.9 1.5 %collective-permute-done.7.moved_ref = bf16[2,1024,128]{2,1,0:T(8,128)(2,1)S(1)} collective-permute-done((bf16[2,1024,128]{2,1,0:T(8,128)(2,1)S(1)}, bf16[2,1024,128]{2,1,0:T(8,128)(2,1)S(1)}, u32[]{:S(2)}, u32[]{:S(2)}) %collective-permute-start.7) | collective-permute-done | bytes 524320 | tf_op jit(solution)/shard_map/ppermute | solution.py:15
  40.3 0.0 collective-permute-done.8.refs_2_.refs_0_
  40.3 0.4 collective-permute-start.10
  40.7 0.7 shard_map.71
  41.4 0.6 collective-permute-start.11
  42.0 0.7 collective-permute-start.13
  42.7 0.7 collective-permute-start.14
  43.4 1.5 %collective-permute-done.10.refs_3_.refs_1_ = bf16[3,256,1024]{2,1,0:T(8,128)(2,1)S(1)} collective-permute-done((bf16[3,256,1024]{2,1,0:T(8,128)(2,1)S(1)}, bf16[3,256,1024]{2,1,0:T(8,128)(2,1)S(1)}, u32[]{:S(2)}, u32[]{:S(2)}) %collective-permute-start.10) | collective-permute-done | bytes 1572896 | tf_op jit(solution)/shard_map/ppermute | solution.py:15
  44.8 0.7 shard_map.72.product_ref
  45.5 3.7 %collective-permute-done.11.moved_ref = bf16[1024,128]{1,0:T(8,128)(2,1)S(1)} collective-permute-done((bf16[1024,128]{1,0:T(8,128)(2,1)S(1)}, bf16[1024,128]{1,0:T(8,128)(2,1)S(1)}, u32[]{:S(2)}, u32[]{:S(2)}) %collective-permute-start.11) | collective-permute-done | bytes 262176 | tf_op jit(solution)/shard_map/ppermute | solution.py:15
  49.2 0.8 shard_map.73
  50.1 0.7 collective-permute-start.12
  50.8 0.6 shard_map.75.refs_0_
  51.4 1.3 %collective-permute-start.15 = (bf16[1024,128]{1,0:T(8,128)(2,1)S(1)}, bf16[1024,128]{1,0:T(8,128)(2,1)S(1)}, u32[]{:S(2)}, u32[]{:S(2)}) collective-permute-start(bf16[1024,128]{1,0:T(8,128)(2,1)S(1)} %shard_map.75.refs_0_), channel_id=1, source_target_pairs={{4,8},{0,24},{5,9},{1,25},{6,10},{2,26},{7,11},{3,27}} | collective-permute-start | bytes 786440 | tf_op jit(solution)/shard_map/ppermute | solution.py:458
  52.7 0.7 collective-permute-start.16
  53.3 0.7 collective-permute-start.19
  54.0 0.7 collective-permute-start.18
  54.7 0.6 shard_map.74
  55.4 11.3 %collective-permute-done.15.first_ref.refs_2_ = bf16[1024,128]{1,0:T(8,128)(2,1)S(1)} collective-permute-done((bf16[1024,128]{1,0:T(8,128)(2,1)S(1)}, bf16[1024,128]{1,0:T(8,128)(2,1)S(1)}, u32[]{:S(2)}, u32[]{:S(2)}) %collective-permute-start.15) | collective-permute-done | bytes 262176 | tf_op jit(solution)/shard_map/ppermute | solution.py:458
  66.7 0.6 shard_map.76.refs_1_
  67.3 0.7 collective-permute-start.17
  68.0 1.3 %collective-permute-start.21 = (bf16[1024,128]{1,0:T(8,128)(2,1)S(1)}, bf16[1024,128]{1,0:T(8,128)(2,1)S(1)}, u32[]{:S(2)}, u32[]{:S(2)}) collective-permute-start(bf16[1024,128]{1,0:T(8,128)(2,1)S(1)} %shard_map.76.refs_1_), channel_id=1, source_target_pairs={{8,24},{9,25},{10,26},{11,27}} | collective-permute-start | bytes 786440 | tf_op jit(solution)/shard_map/ppermute | solution.py:458
  69.3 0.7 collective-permute-start.22
  70.0 0.6 shard_map.77.line0_ref
  70.6 1.3 %collective-permute-start.20 = (bf16[1024,128]{1,0:T(8,128)(2,1)S(1)}, bf16[1024,128]{1,0:T(8,128)(2,1)S(1)}, u32[]{:S(2)}, u32[]{:S(2)}) collective-permute-start(bf16[1024,128]{1,0:T(8,128)(2,1)S(1)} %shard_map.77.line0_ref), channel_id=1, source_target_pairs={{16,20},{24,28},{17,21},{25,29},{18,22},{26,30},{19,23},{27,31}} | collective-permute-start | bytes 786440 | tf_op jit(solution)/shard_map/ppermute | solution.py:458
  71.9 4.3 %collective-permute-done.21.refs_2_ = bf16[1024,128]{1,0:T(8,128)(2,1)S(1)} collective-permute-done((bf16[1024,128]{1,0:T(8,128)(2,1)S(1)}, bf16[1024,128]{1,0:T(8,128)(2,1)S(1)}, u32[]{:S(2)}, u32[]{:S(2)}) %collective-permute-start.21) | collective-permute-done | bytes 262176 | tf_op jit(solution)/shard_map/ppermute | solution.py:458
  76.3 0.6 shard_map.78.line_ref
  76.9 9.2 %collective-permute-start.26 = (bf16[1024,128]{1,0:T(8,128)(2,1)S(1)}, bf16[1024,128]{1,0:T(8,128)(2,1)S(1)}, u32[]{:S(2)}, u32[]{:S(2)}) collective-permute-start(bf16[1024,128]{1,0:T(8,128)(2,1)S(1)} %shard_map.78.line_ref), channel_id=1, source_target_pairs={{0,4},{4,0},{8,12},{12,8},{16,20},{20,16},{24,28},{28,24},{1,5},{5... | collective-permute-start | bytes 786440 | tf_op jit(solution)/shard_map/ppermute | solution.py:15
  86.1 0.6 shard_map.79
  86.8 2.0 %collective-permute-start.23 = (bf16[2,256,128]{2,1,0:T(8,128)(2,1)S(1)}, bf16[2,256,128]{2,1,0:T(8,128)(2,1)S(1)}, u32[]{:S(2)}, u32[]{:S(2)}) collective-permute-start(bf16[2,256,128]{2,1,0:T(8,128)(2,1)S(1)} %get-tuple-element.53), channel_id=1, source_target_pairs={{0,1},{1,0},{2,3},{3,2},{4,5},{5,4},{6,7},{7,6},{8,9},{9,8},{10,11... | collective-permute-start | bytes 393224 | tf_op jit(solution)/shard_map/ppermute | solution.py:15
  88.8 0.8 collective-permute-start.24
  89.6 0.9 collective-permute-start.25
  90.5 2.0 %shard_map.80.current_ref = f32[1024,128]{1,0:T(8,128)S(1)} custom-call(s32[2]{0:T(128)S(1)} %pad_add_fusion.index_ref, f32[1024,128]{1,0:T(8,128)S(1)} %get-tuple-element.46.current_ref, bf16[1024,128]{1,0:T(8,128)(2,1)S(1)} %get-tuple-element.47.known_ref, bf16[1024,128]{1,0:T(8,128)(2,1)S(1)} %collective-permute-done.15.first_ref.refs_2_, ...), custom_call_target="tpu_custom_call" | custom-call | bytes 28800000 | tf_op jit(solution)/shard_map/pallas_call | solution.py:446
  92.5 1.1 %shard_map.82 = bf16[2,2,256,128]{3,2,1,0:T(8,128)(2,1)S(1)} custom-call(s32[2]{0:T(128)S(1)} %pad_add_fusion.index_ref, f32[1024,128]{1,0:T(8,128)S(1)} %shard_map.80.current_ref, bf16[1024,128]{1,0:T(8,128)(2,1)S(1)} %collective-permute-done.26.value_ref, bf16[3,256,1024]{2,1,0:T(8,128)(2,1)S(1)} %collective-permute-done.8.refs_2_.refs_0_, ...), custom_call_target="tpu_custom_call" | custom-call | bytes 3600000 | tf_op jit(solution)/shard_map/pallas_call | solution.py:446
  93.7 0.8 collective-permute-start.28
  94.5 1.7 %collective-permute-start.29 = (bf16[2,256,128]{2,1,0:T(8,128)(2,1)S(1)}, bf16[2,256,128]{2,1,0:T(8,128)(2,1)S(1)}, u32[]{:S(2)}, u32[]{:S(2)}) collective-permute-start(bf16[2,256,128]{2,1,0:T(8,128)(2,1)S(1)} %get-tuple-element.55), channel_id=1, source_target_pairs={{0,3},{1,2},{2,1},{3,0},{4,7},{5,6},{6,5},{7,4},{8,11},{9,10},{10,... | collective-permute-start | bytes 393224 | tf_op jit(solution)/shard_map/ppermute | solution.py:15
  96.2 1.1 %shard_map.81 = bf16[2,2,256,128]{3,2,1,0:T(8,128)(2,1)S(1)} custom-call(s32[2]{0:T(128)S(1)} %pad_add_fusion.index_ref, f32[1024,128]{1,0:T(8,128)S(1)} %shard_map.80.current_ref, bf16[1024,128]{1,0:T(8,128)(2,1)S(1)} %collective-permute-done.26.value_ref, bf16[3,256,1024]{2,1,0:T(8,128)(2,1)S(1)} %pad_maximum_fusion.refs_0_, ...), custom_call_target="tpu_custom_call" | custom-call | bytes 28800000 | tf_op jit(solution)/shard_map/pallas_call | solution.py:446
  97.4 0.1 collective-permute-start.27
  97.5 1.8 %collective-permute-done.28.refs_6_ = bf16[2,256,128]{2,1,0:T(8,128)(2,1)S(1)} collective-permute-done((bf16[2,256,128]{2,1,0:T(8,128)(2,1)S(1)}, bf16[2,256,128]{2,1,0:T(8,128)(2,1)S(1)}, u32[]{:S(2)}, u32[]{:S(2)}) %collective-permute-start.28) | collective-permute-done | bytes 131104 | tf_op jit(solution)/shard_map/ppermute | solution.py:15
  99.3 3.2 %collective-permute-done.29.refs_7_ = bf16[2,256,128]{2,1,0:T(8,128)(2,1)S(1)} collective-permute-done((bf16[2,256,128]{2,1,0:T(8,128)(2,1)S(1)}, bf16[2,256,128]{2,1,0:T(8,128)(2,1)S(1)}, u32[]{:S(2)}, u32[]{:S(2)}) %collective-permute-start.29) | collective-permute-done | bytes 131104 | tf_op jit(solution)/shard_map/ppermute | solution.py:15
  102.5 1.7 %shard_map.83 = (bf16[3,256,512]{2,1,0:T(8,128)(2,1)}, f32[256,512]{1,0:T(8,128)}) custom-call(s32[2]{0:T(128)S(1)} %pad_add_fusion.index_ref, bf16[2,256,128]{2,1,0:T(8,128)(2,1)S(1)} %get-tuple-element.54.refs_0_, bf16[2,256,128]{2,1,0:T(8,128)(2,1)S(1)} %collective-permute-done.23.refs_1_, bf16[2,256,128]{2,1,0:T(8,128)(2,1)S(1)} %collective-permute-done.24.refs_2_, ...), custom_call_target="tpu_custom_call" | custom-call | bytes 3600000 | tf_op jit(solution)/shard_map/pallas_call | solution.py:433
  (24 shorter events, 0.1 us)
Async XLA Ops:
  2.6 1.5 %copy-start.2 = (bf16[1,256,512]{2,1,0:T(8,128)(2,1)S(1)}, bf16[1,256,512]{2,1,0:T(8,128)(2,1)}, u32[]{:S(2)}) copy-start(bf16[1,256,512]{2,1,0:T(8,128)(2,1)} %param.7) | copy-start | bytes 786436
  2.8 37.5 %collective-permute-start.8 = (bf16[3,256,1024]{2,1,0:T(8,128)(2,1)S(1)}, bf16[3,256,1024]{2,1,0:T(8,128)(2,1)S(1)}, u32[]{:S(2)}, u32[]{:S(2)}) collective-permute-start(bf16[3,256,1024]{2,1,0:T(8,128)(2,1)S(1)} %pad_maximum_fusion.refs_0_), channel_id=1, source_target_pairs={{0,2},{1,3},{2,0},{3,1},{4,6},{5,7},{6,4},{7,5},{8,10},{9,11},{10,... | collective-permute-start | bytes 4718600 | tf_op jit(solution)/shard_map/ppermute | solution.py:15
  4.1 11.6 %collective-permute-start = (bf16[256,512]{1,0:T(8,128)(2,1)S(1)}, bf16[256,512]{1,0:T(8,128)(2,1)}, u32[]{:S(2)}, u32[]{:S(2)}) collective-permute-start(bf16[256,512]{1,0:T(8,128)(2,1)S(1)} %bitcast.27), channel_id=1, source_target_pairs={{0,8},{4,12},{8,0},{12,4},{16,24},{20,28},{24,16},{28,20},{1,9},{5... | collective-permute-start | bytes 786440 | tf_op jit(solution)/shard_map/ppermute | solution.py:15
  4.3 13.5 %collective-permute-start.1 = (bf16[256,512]{1,0:T(8,128)(2,1)S(1)}, bf16[256,512]{1,0:T(8,128)(2,1)}, u32[]{:S(2)}, u32[]{:S(2)}) collective-permute-start(bf16[256,512]{1,0:T(8,128)(2,1)S(1)} %bitcast.28), channel_id=1, source_target_pairs={{0,16},{4,20},{8,24},{12,28},{16,0},{20,4},{24,8},{28,12},{1,17},{... | collective-permute-start | bytes 786440 | tf_op jit(solution)/shard_map/ppermute | solution.py:15
  4.3 13.4 %collective-permute-start.2 = (bf16[256,512]{1,0:T(8,128)(2,1)S(1)}, bf16[256,512]{1,0:T(8,128)(2,1)}, u32[]{:S(2)}, u32[]{:S(2)}) collective-permute-start(bf16[256,512]{1,0:T(8,128)(2,1)S(1)} %bitcast.29), channel_id=1, source_target_pairs={{0,4},{4,0},{8,12},{12,8},{16,20},{20,16},{24,28},{28,24},{1,5},{5... | collective-permute-start | bytes 786440 | tf_op jit(solution)/shard_map/ppermute | solution.py:15
  5.7 2.2 %copy-start = (bf16[1024,8,256]{2,1,0:T(8,128)(2,1)S(1)}, bf16[1024,8,256]{2,1,0:T(8,128)(2,1)}, u32[]{:S(2)}) copy-start(bf16[1024,8,256]{2,1,0:T(8,128)(2,1)} %panel_ref.1) | copy-start | bytes 12582916
  7.8 20.0 %copy-start.1 = (f32[256,512]{1,0:T(8,128)S(1)}, f32[256,512]{1,0:T(8,128)}, u32[]{:S(2)}) copy-start(f32[256,512]{1,0:T(8,128)} %side_ref.1) | copy-start | bytes 1572868
  15.7 8.1 %collective-permute-start.5 = (bf16[256,512]{1,0:T(8,128)(2,1)S(1)}, bf16[256,512]{1,0:T(8,128)(2,1)S(1)}, u32[]{:S(2)}, u32[]{:S(2)}) collective-permute-start(bf16[256,512]{1,0:T(8,128)(2,1)S(1)} %bitcast.30), channel_id=1, source_target_pairs={{0,24},{4,28},{8,16},{12,20},{16,8},{20,12},{24,0},{28,4},{1,25},{... | collective-permute-start | bytes 786440 | tf_op jit(solution)/shard_map/ppermute | solution.py:15
  16.5 8.5 %collective-permute-start.3 = (bf16[256,512]{1,0:T(8,128)(2,1)}, bf16[256,512]{1,0:T(8,128)(2,1)S(1)}, u32[]{:S(2)}, u32[]{:S(2)}) collective-permute-start(bf16[256,512]{1,0:T(8,128)(2,1)} %collective-permute-done.refs_2_), channel_id=1, source_target_pairs={{0,4},{4,0},{8,12},{12,8},{16,20},{20,16},{24,28},{28,24},{1,5},{5... | collective-permute-start | bytes 786440 | tf_op jit(solution)/shard_map/ppermute | solution.py:15
  17.8 10.1 %collective-permute-start.4 = (bf16[256,512]{1,0:T(8,128)(2,1)}, bf16[256,512]{1,0:T(8,128)(2,1)S(1)}, u32[]{:S(2)}, u32[]{:S(2)}) collective-permute-start(bf16[256,512]{1,0:T(8,128)(2,1)} %collective-permute-done.1.refs_4_), channel_id=1, source_target_pairs={{0,4},{4,0},{8,12},{12,8},{16,20},{20,16},{24,28},{28,24},{1,5},{5... | collective-permute-start | bytes 786440 | tf_op jit(solution)/shard_map/ppermute | solution.py:15
  23.8 7.7 %collective-permute-start.6 = (bf16[256,512]{1,0:T(8,128)(2,1)S(1)}, bf16[256,512]{1,0:T(8,128)(2,1)S(1)}, u32[]{:S(2)}, u32[]{:S(2)}) collective-permute-start(bf16[256,512]{1,0:T(8,128)(2,1)S(1)} %collective-permute-done.5.refs_6_), channel_id=1, source_target_pairs={{0,4},{4,0},{8,12},{12,8},{16,20},{20,16},{24,28},{28,24},{1,5},{5... | collective-permute-start | bytes 786440 | tf_op jit(solution)/shard_map/ppermute | solution.py:15
  33.0 7.3 %collective-permute-start.7 = (bf16[2,1024,128]{2,1,0:T(8,128)(2,1)S(1)}, bf16[2,1024,128]{2,1,0:T(8,128)(2,1)S(1)}, u32[]{:S(2)}, u32[]{:S(2)}) collective-permute-start(bf16[2,1024,128]{2,1,0:T(8,128)(2,1)S(1)} %get-tuple-element.33), channel_id=1, source_target_pairs={{0,1},{1,0},{2,3},{3,2},{4,5},{5,4},{6,7},{7,6},{8,9},{9,8},{10,11... | collective-permute-start | bytes 1572872 | tf_op jit(solution)/shard_map/ppermute | solution.py:15
  38.8 4.6 %collective-permute-start.9 = (bf16[3,256,1024]{2,1,0:T(8,128)(2,1)S(1)}, bf16[3,256,1024]{2,1,0:T(8,128)(2,1)S(1)}, u32[]{:S(2)}, u32[]{:S(2)}) collective-permute-start(bf16[3,256,1024]{2,1,0:T(8,128)(2,1)S(1)} %pad_maximum_fusion.refs_0_), channel_id=1, source_target_pairs={{0,1},{1,0},{2,3},{3,2},{4,5},{5,4},{6,7},{7,6},{8,9},{9,8},{10,11... | collective-permute-start | bytes 4718600 | tf_op jit(solution)/shard_map/ppermute | solution.py:15
  40.3 4.5 %collective-permute-start.10 = (bf16[3,256,1024]{2,1,0:T(8,128)(2,1)S(1)}, bf16[3,256,1024]{2,1,0:T(8,128)(2,1)S(1)}, u32[]{:S(2)}, u32[]{:S(2)}) collective-permute-start(bf16[3,256,1024]{2,1,0:T(8,128)(2,1)S(1)} %collective-permute-done.8.refs_2_.refs_0_), channel_id=1, source_target_pairs={{0,1},{1,0},{2,3},{3,2},{4,5},{5,4},{6,7},{7,6},{8,9},{9,8},{10,11... | collective-permute-start | bytes 4718600 | tf_op jit(solution)/shard_map/ppermute | solution.py:15
  41.4 7.8 %collective-permute-start.11 = (bf16[1024,128]{1,0:T(8,128)(2,1)S(1)}, bf16[1024,128]{1,0:T(8,128)(2,1)S(1)}, u32[]{:S(2)}, u32[]{:S(2)}) collective-permute-start(bf16[1024,128]{1,0:T(8,128)(2,1)S(1)} %get-tuple-element.38), channel_id=1, source_target_pairs={{0,2},{1,3},{2,0},{3,1},{4,6},{5,7},{6,4},{7,5},{8,10},{9,11},{10,... | collective-permute-start | bytes 786440 | tf_op jit(solution)/shard_map/ppermute | solution.py:15
  42.0 8.7 %collective-permute-start.13 = (bf16[1024,128]{1,0:T(8,128)(2,1)S(1)}, bf16[1024,128]{1,0:T(8,128)(2,1)S(1)}, u32[]{:S(2)}, u32[]{:S(2)}) collective-permute-start(bf16[1024,128]{1,0:T(8,128)(2,1)S(1)} %get-tuple-element.44), channel_id=1, source_target_pairs={{0,4},{1,5},{2,6},{3,7}} | collective-permute-start | bytes 786440 | tf_op jit(solution)/shard_map/ppermute | solution.py:458
  42.7 8.1 %collective-permute-start.14 = (bf16[1024,128]{1,0:T(8,128)(2,1)S(1)}, bf16[1024,128]{1,0:T(8,128)(2,1)S(1)}, u32[]{:S(2)}, u32[]{:S(2)}) collective-permute-start(bf16[1024,128]{1,0:T(8,128)(2,1)S(1)} %get-tuple-element.38), channel_id=1, source_target_pairs={{0,6},{1,7},{2,4},{3,5}} | collective-permute-start | bytes 786440 | tf_op jit(solution)/shard_map/ppermute | solution.py:503
  50.1 4.7 %collective-permute-start.12 = (bf16[1024,128]{1,0:T(8,128)(2,1)S(1)}, bf16[1024,128]{1,0:T(8,128)(2,1)S(1)}, u32[]{:S(2)}, u32[]{:S(2)}) collective-permute-start(bf16[1024,128]{1,0:T(8,128)(2,1)S(1)} %get-tuple-element.39.own_ref.refs_0_.own0_ref), channel_id=1, source_target_pairs={{0,8},{1,9},{2,10},{3,11}} | collective-permute-start | bytes 786440 | tf_op jit(solution)/shard_map/ppermute | solution.py:458
  51.4 15.3 %collective-permute-start.15 = (bf16[1024,128]{1,0:T(8,128)(2,1)S(1)}, bf16[1024,128]{1,0:T(8,128)(2,1)S(1)}, u32[]{:S(2)}, u32[]{:S(2)}) collective-permute-start(bf16[1024,128]{1,0:T(8,128)(2,1)S(1)} %shard_map.75.refs_0_), channel_id=1, source_target_pairs={{4,8},{0,24},{5,9},{1,25},{6,10},{2,26},{7,11},{3,27}} | collective-permute-start | bytes 786440 | tf_op jit(solution)/shard_map/ppermute | solution.py:458
  52.7 14.0 %collective-permute-start.16 = (bf16[1024,128]{1,0:T(8,128)(2,1)S(1)}, bf16[1024,128]{1,0:T(8,128)(2,1)S(1)}, u32[]{:S(2)}, u32[]{:S(2)}) collective-permute-start(bf16[1024,128]{1,0:T(8,128)(2,1)S(1)} %shard_map.75.refs_0_), channel_id=1, source_target_pairs={{4,12},{5,13},{6,14},{7,15}} | collective-permute-start | bytes 786440 | tf_op jit(solution)/shard_map/ppermute | solution.py:458
  53.3 16.6 %collective-permute-start.19 = (bf16[1024,128]{1,0:T(8,128)(2,1)S(1)}, bf16[1024,128]{1,0:T(8,128)(2,1)S(1)}, u32[]{:S(2)}, u32[]{:S(2)}) collective-permute-start(bf16[1024,128]{1,0:T(8,128)(2,1)S(1)} %shard_map.75.refs_0_), channel_id=1, source_target_pairs={{0,16},{1,17},{2,18},{3,19}} | collective-permute-start | bytes 786440 | tf_op jit(solution)/shard_map/ppermute | solution.py:458
  54.0 17.9 %collective-permute-start.18 = (bf16[1024,128]{1,0:T(8,128)(2,1)S(1)}, bf16[1024,128]{1,0:T(8,128)(2,1)S(1)}, u32[]{:S(2)}, u32[]{:S(2)}) collective-permute-start(bf16[1024,128]{1,0:T(8,128)(2,1)S(1)} %shard_map.75.refs_0_), channel_id=1, source_target_pairs={{4,20},{0,12},{5,21},{1,13},{6,22},{2,14},{7,23},{3,15}} | collective-permute-start | bytes 786440 | tf_op jit(solution)/shard_map/ppermute | solution.py:458
  67.3 4.6 %collective-permute-start.17 = (bf16[1024,128]{1,0:T(8,128)(2,1)S(1)}, bf16[1024,128]{1,0:T(8,128)(2,1)S(1)}, u32[]{:S(2)}, u32[]{:S(2)}) collective-permute-start(bf16[1024,128]{1,0:T(8,128)(2,1)S(1)} %shard_map.76.refs_1_), channel_id=1, source_target_pairs={{8,0},{0,4},{9,1},{1,5},{10,2},{2,6},{11,3},{3,7}} | collective-permute-start | bytes 786440 | tf_op jit(solution)/shard_map/ppermute | solution.py:458
  68.0 8.3 %collective-permute-start.21 = (bf16[1024,128]{1,0:T(8,128)(2,1)S(1)}, bf16[1024,128]{1,0:T(8,128)(2,1)S(1)}, u32[]{:S(2)}, u32[]{:S(2)}) collective-permute-start(bf16[1024,128]{1,0:T(8,128)(2,1)S(1)} %shard_map.76.refs_1_), channel_id=1, source_target_pairs={{8,24},{9,25},{10,26},{11,27}} | collective-permute-start | bytes 786440 | tf_op jit(solution)/shard_map/ppermute | solution.py:458
  69.3 7.0 %collective-permute-start.22 = (bf16[1024,128]{1,0:T(8,128)(2,1)S(1)}, bf16[1024,128]{1,0:T(8,128)(2,1)S(1)}, u32[]{:S(2)}, u32[]{:S(2)}) collective-permute-start(bf16[1024,128]{1,0:T(8,128)(2,1)S(1)} %shard_map.76.refs_1_), channel_id=1, source_target_pairs={{8,16},{12,28},{9,17},{13,29},{10,18},{14,30},{11,19},{15,31}} | collective-permute-start | bytes 786440 | tf_op jit(solution)/shard_map/ppermute | solution.py:458
  70.6 15.5 %collective-permute-start.20 = (bf16[1024,128]{1,0:T(8,128)(2,1)S(1)}, bf16[1024,128]{1,0:T(8,128)(2,1)S(1)}, u32[]{:S(2)}, u32[]{:S(2)}) collective-permute-start(bf16[1024,128]{1,0:T(8,128)(2,1)S(1)} %shard_map.77.line0_ref), channel_id=1, source_target_pairs={{16,20},{24,28},{17,21},{25,29},{18,22},{26,30},{19,23},{27,31}} | collective-permute-start | bytes 786440 | tf_op jit(solution)/shard_map/ppermute | solution.py:458
  76.9 15.6 %collective-permute-start.26 = (bf16[1024,128]{1,0:T(8,128)(2,1)S(1)}, bf16[1024,128]{1,0:T(8,128)(2,1)S(1)}, u32[]{:S(2)}, u32[]{:S(2)}) collective-permute-start(bf16[1024,128]{1,0:T(8,128)(2,1)S(1)} %shard_map.78.line_ref), channel_id=1, source_target_pairs={{0,4},{4,0},{8,12},{12,8},{16,20},{20,16},{24,28},{28,24},{1,5},{5... | collective-permute-start | bytes 786440 | tf_op jit(solution)/shard_map/ppermute | solution.py:15
  86.8 10.6 %collective-permute-start.23 = (bf16[2,256,128]{2,1,0:T(8,128)(2,1)S(1)}, bf16[2,256,128]{2,1,0:T(8,128)(2,1)S(1)}, u32[]{:S(2)}, u32[]{:S(2)}) collective-permute-start(bf16[2,256,128]{2,1,0:T(8,128)(2,1)S(1)} %get-tuple-element.53), channel_id=1, source_target_pairs={{0,1},{1,0},{2,3},{3,2},{4,5},{5,4},{6,7},{7,6},{8,9},{9,8},{10,11... | collective-permute-start | bytes 393224 | tf_op jit(solution)/shard_map/ppermute | solution.py:15
  88.8 8.7 %collective-permute-start.24 = (bf16[2,256,128]{2,1,0:T(8,128)(2,1)S(1)}, bf16[2,256,128]{2,1,0:T(8,128)(2,1)S(1)}, u32[]{:S(2)}, u32[]{:S(2)}) collective-permute-start(bf16[2,256,128]{2,1,0:T(8,128)(2,1)S(1)} %get-tuple-element.52), channel_id=1, source_target_pairs={{0,2},{1,3},{2,0},{3,1},{4,6},{5,7},{6,4},{7,5},{8,10},{9,11},{10,... | collective-permute-start | bytes 393224 | tf_op jit(solution)/shard_map/ppermute | solution.py:15
  89.6 7.9 %collective-permute-start.25 = (bf16[2,256,128]{2,1,0:T(8,128)(2,1)S(1)}, bf16[2,256,128]{2,1,0:T(8,128)(2,1)S(1)}, u32[]{:S(2)}, u32[]{:S(2)}) collective-permute-start(bf16[2,256,128]{2,1,0:T(8,128)(2,1)S(1)} %get-tuple-element.51), channel_id=1, source_target_pairs={{0,3},{1,2},{2,1},{3,0},{4,7},{5,6},{6,5},{7,4},{8,11},{9,10},{10,... | collective-permute-start | bytes 393224 | tf_op jit(solution)/shard_map/ppermute | solution.py:15
  93.7 5.6 %collective-permute-start.28 = (bf16[2,256,128]{2,1,0:T(8,128)(2,1)S(1)}, bf16[2,256,128]{2,1,0:T(8,128)(2,1)S(1)}, u32[]{:S(2)}, u32[]{:S(2)}) collective-permute-start(bf16[2,256,128]{2,1,0:T(8,128)(2,1)S(1)} %get-tuple-element.56), channel_id=1, source_target_pairs={{0,2},{1,3},{2,0},{3,1},{4,6},{5,7},{6,4},{7,5},{8,10},{9,11},{10,... | collective-permute-start | bytes 393224 | tf_op jit(solution)/shard_map/ppermute | solution.py:15
  94.5 7.9 %collective-permute-start.29 = (bf16[2,256,128]{2,1,0:T(8,128)(2,1)S(1)}, bf16[2,256,128]{2,1,0:T(8,128)(2,1)S(1)}, u32[]{:S(2)}, u32[]{:S(2)}) collective-permute-start(bf16[2,256,128]{2,1,0:T(8,128)(2,1)S(1)} %get-tuple-element.55), channel_id=1, source_target_pairs={{0,3},{1,2},{2,1},{3,0},{4,7},{5,6},{6,5},{7,4},{8,11},{9,10},{10,... | collective-permute-start | bytes 393224 | tf_op jit(solution)/shard_map/ppermute | solution.py:15
  97.4 5.1 %collective-permute-start.27 = (bf16[2,256,128]{2,1,0:T(8,128)(2,1)S(1)}, bf16[2,256,128]{2,1,0:T(8,128)(2,1)S(1)}, u32[]{:S(2)}, u32[]{:S(2)}) collective-permute-start(bf16[2,256,128]{2,1,0:T(8,128)(2,1)S(1)} %get-tuple-element.57), channel_id=1, source_target_pairs={{0,1},{1,0},{2,3},{3,2},{4,5},{5,4},{6,7},{7,6},{8,9},{9,8},{10,11... | collective-permute-start | bytes 393224 | tf_op jit(solution)/shard_map/ppermute | solution.py:15

commit v10 on v9

--- a/solution.py
+++ b/solution.py
@@ -356,9 +356,9 @@
     return local(functools.partial(pick_kernel, holders), shape_of(parts[0].shape, BF16), [index] + list(parts))
 
 
-def known_kernel(index_ref, own0_ref, z0_ref, at2_ref, fourth_ref, line0_ref, across0_ref, line_ref, known_ref, pieces_ref):
+def known_kernel(index_ref, own0_ref, to1_ref, at2_ref, fourth_ref, line0_ref, across0_ref, line_ref, known_ref, pieces_ref):
     row = index_ref[0]
-    for holder, part in enumerate((own0_ref, z0_ref, at2_ref, fourth_ref, line0_ref, across0_ref, line0_ref, across0_ref)):
+    for holder, part in enumerate((own0_ref, to1_ref, at2_ref, fourth_ref, line0_ref, across0_ref, line0_ref, across0_ref)):
         copy_where(row == holder, part, known_ref)
     cut(index_ref, known_ref, pieces_ref, 0)
     cut(index_ref, line_ref, pieces_ref, 1)
@@ -509,21 +509,23 @@
     start = functools.partial(start_kernel, n_col)
     current, own0, ahead = local(start, (wide, narrow, wide), [index, kept, moved] + slots)
     at2 = hop(own0, (0, 2))
+    to1 = hop(own0, (0, 1))
+    at2, to1 = gate(at2, to1)
     own1 = local(first_step_kernel, narrow, [index, own0, ahead, product, at1a, at1b])
     first, second = hop(own1, (1, 2), (0, 6)), hop(own1, (1, 3))
-    third, fourth = hop(own1, (0, 4)), hop(own1, (1, 5), (0, 3))
+    third, fourth = hop(own1, (0, 4)), hop(own1, (1, 7), (0, 3))
     between = functools.partial(between_kernel, n_col)
     current, ahead = local(between, (wide, wide), [index, current, at2] + slots, us=8)
     own2 = local(second_step_kernel, narrow, [index, own0, ahead, product, first, second])
+    z4 = hop(own2, (2, 4), (3, 5))
     z6 = hop(own2, (2, 6))
-    z4 = hop(own2, (2, 4), (3, 7))
-    z0 = hop(own2, (2, 0), (0, 1))
+    z0 = hop(own2, (2, 0))
     line0 = pick(index, (0, 0, 0, 0, 1, 0, 2, 0), own0, third, first)
     across0 = hop(line0, (4, 5), (6, 7))
-    line = pick(index, (5, 0, 1, 1, 3, 4, 2, 3), own1, own2, z6, z4, fourth, z0)
+    line = pick(index, (5, 0, 1, 1, 2, 2, 3, 4), own1, own2, z4, z6, fourth, z0)
     across = flip(line, "row", n_row, 1)
     pieces = shape_of((n_col, 2, strip, chunk), BF16)
-    known, middle = local(known_kernel, (narrow, pieces), [index, own0, z0, at2, fourth, line0, across0, line])
+    known, middle = local(known_kernel, (narrow, pieces), [index, own0, to1, at2, fourth, line0, across0, line])
     middle = swap_pieces(middle, n_col)
     scratch = [pltpu.VMEM((rows, chunk), F32)]
     current = local(functools.partial(middle_kernel, n_col), wide, [index, current, known, first, line] + slots, scratch, us=8)

time: 105 us -> 104 us (level); the launches traced: 104 us -> 102 us
  starting transfers between devices: 37.9 us -> 32.7 us
  waiting for transfers between devices: 41 us -> 43.9 us
    ppermute x19, starting transfers between devices: 28.6 us -> 22.7 us  [flip(): return lax.ppermute(value, axis, [(i, i ^ bit) for i in range(size)])]
    ppermute x10 -> x11, waiting for transfers between devices: 15.7 us -> 19.4 us  [hop(): return lax.ppermute(value, 'row', pairs)]
    ppermute x10 -> x11, starting transfers between devices: 8.62 us -> 9.3 us  [hop(): return lax.ppermute(value, 'row', pairs)]
  transfers between devices with their start and end apart: 30 -> 31, of which waited for: 11 -> 10; matrix products, arithmetic and copies ran while one was open for 0% -> 0% of each run, Pallas kernels for 17% -> 18%
where the time goes in v10:
time: 104 us; the launch traced here: 102 us
  waiting for transfers between devices  43.9 us (42%)
  starting transfers between devices  32.7 us (31%)
  Pallas kernels  19.8 us (19%)
  local copies, waits for them, and re-layouts  2.27 us (2%)
  other arithmetic  2.25 us (2%)
  between operations  1.2 us (1%)
    ppermute x19, waiting for transfers between devices, flip(): return lax.ppermute(value, axis, [(i, i ^ bit) for i in range(size)])  24.5 us
    ppermute x19, starting transfers between devices, flip(): return lax.ppermute(value, axis, [(i, i ^ bit) for i in range(size)])  22.7 us
    ppermute x11, waiting for transfers between devices, hop(): return lax.ppermute(value, 'row', pairs)  19.4 us
    pallas_call x14, Pallas kernels, local(): pl.pallas_call(kernel, out_shape=out_shape, in_specs=[SMEM] + [VMEM] * (l...  15 us
    ppermute x11, starting transfers between devices, hop(): return lax.ppermute(value, 'row', pairs)  9.3 us
    pallas_call x1, Pallas kernels, order_panel(): pl.pallas_call(order_kernel, out_shape=shape_of((rows, sources * width),...  3.08 us
    unnamed x6, local copies, waits for them, and re-layouts  2.2 us
  transfers between devices with their start and end apart: 31, of which 10 were waited for; matrix products, arithmetic and copies ran while one was open for 0% of the time, Pallas kernels for 18%

profile of v10, /device:TPU:25, one launch (start us, length us, event | category | flops | bytes accessed | tf_op | source)
XLA Modules:
  0.0 102.1 jit_solution(176048400543003913)
XLA Ops:
  0.6 2.0 %bitcast_select_fusion.2 = (bf16[1,256,1024]{2,1,0:T(8,128)(2,1)S(1)}, bf16[1,256,1024]{2,1,0:T(8,128)(2,1)S(1)}, bf16[1,256,1024]{2,1,0:T(8,128)(2,1)S(1)}) fusion(bf16[256,3,1024]{2,0,1:T(8,128)(2,1)} %param.8, pred[]{:T(512)S(6)} %eq.10, bf16[3,256,1024]{2,1,0:T(8,128)(2,1)} %param.9, pred[]{:T(512)S(6)} %eq.12, pred[]{:T(512)S(6)} %eq.11), kind=kLoop, calls=%fused_computation.4 | loop fusion | flops 1048576 | bytes 4718595 | tf_op jit(solution)/shard_map/jit(_where)/select_n | solution.py:479
  2.6 0.0 copy-start.2
  2.7 0.2 pad_maximum_fusion.refs_0_
  2.8 1.3 %collective-permute-start.8 = (bf16[3,256,1024]{2,1,0:T(8,128)(2,1)S(1)}, bf16[3,256,1024]{2,1,0:T(8,128)(2,1)S(1)}, u32[]{:S(2)}, u32[]{:S(2)}) collective-permute-start(bf16[3,256,1024]{2,1,0:T(8,128)(2,1)S(1)} %pad_maximum_fusion.refs_0_), channel_id=1, source_target_pairs={{0,2},{1,3},{2,0},{3,1},{4,6},{5,7},{6,4},{7,5},{8,10},{9,11},{10,... | collective-permute-start | bytes 4718600 | tf_op jit(solution)/shard_map/ppermute | solution.py:15
  4.1 0.2 collective-permute-start
  4.3 0.1 collective-permute-start.1
  4.3 1.2 %collective-permute-start.2 = (bf16[256,512]{1,0:T(8,128)(2,1)S(1)}, bf16[256,512]{1,0:T(8,128)(2,1)}, u32[]{:S(2)}, u32[]{:S(2)}) collective-permute-start(bf16[256,512]{1,0:T(8,128)(2,1)S(1)} %bitcast.29), channel_id=1, source_target_pairs={{0,4},{4,0},{8,12},{12,8},{16,20},{20,16},{24,28},{28,24},{1,5},{5... | collective-permute-start | bytes 786440 | tf_op jit(solution)/shard_map/ppermute | solution.py:15
  5.6 0.1 pad_add_fusion.index_ref
  5.7 2.2 %copy-done = bf16[1024,8,256]{2,1,0:T(8,128)(2,1)S(1)} copy-done((bf16[1024,8,256]{2,1,0:T(8,128)(2,1)S(1)}, bf16[1024,8,256]{2,1,0:T(8,128)(2,1)}, u32[]{:S(2)}) %copy-start) | copy-done | bytes 4194328
  7.8 3.1 %shard_map.68.panel_ref = bf16[1024,2048]{1,0:T(8,128)(2,1)S(1)} custom-call(s32[2]{0:T(128)S(1)} %pad_add_fusion.index_ref, bf16[1024,8,256]{2,1,0:T(8,128)(2,1)S(1)} %copy-done), custom_call_target="tpu_custom_call" | custom-call | bytes 28800000 | tf_op jit(solution)/shard_map/pallas_call | solution.py:154
  10.9 4.8 %collective-permute-done.refs_2_ = bf16[256,512]{1,0:T(8,128)(2,1)} collective-permute-done((bf16[256,512]{1,0:T(8,128)(2,1)S(1)}, bf16[256,512]{1,0:T(8,128)(2,1)}, u32[]{:S(2)}, u32[]{:S(2)}) %collective-permute-start) | collective-permute-done | bytes 262176 | tf_op jit(solution)/shard_map/ppermute | solution.py:15
  15.7 0.8 collective-permute-start.5
  16.5 1.2 %collective-permute-start.3 = (bf16[256,512]{1,0:T(8,128)(2,1)}, bf16[256,512]{1,0:T(8,128)(2,1)S(1)}, u32[]{:S(2)}, u32[]{:S(2)}) collective-permute-start(bf16[256,512]{1,0:T(8,128)(2,1)} %collective-permute-done.refs_2_), channel_id=1, source_target_pairs={{0,4},{4,0},{8,12},{12,8},{16,20},{20,16},{24,28},{28,24},{1,5},{5... | collective-permute-start | bytes 786440 | tf_op jit(solution)/shard_map/ppermute | solution.py:15
  17.8 0.2 collective-permute-start.4
  18.0 5.8 %collective-permute-done.5.refs_6_ = bf16[256,512]{1,0:T(8,128)(2,1)S(1)} collective-permute-done((bf16[256,512]{1,0:T(8,128)(2,1)S(1)}, bf16[256,512]{1,0:T(8,128)(2,1)S(1)}, u32[]{:S(2)}, u32[]{:S(2)}) %collective-permute-start.5) | collective-permute-done | bytes 262176 | tf_op jit(solution)/shard_map/ppermute | solution.py:15
  23.8 1.2 %collective-permute-start.6 = (bf16[256,512]{1,0:T(8,128)(2,1)S(1)}, bf16[256,512]{1,0:T(8,128)(2,1)S(1)}, u32[]{:S(2)}, u32[]{:S(2)}) collective-permute-start(bf16[256,512]{1,0:T(8,128)(2,1)S(1)} %collective-permute-done.5.refs_6_), channel_id=1, source_target_pairs={{0,4},{4,0},{8,12},{12,8},{16,20},{20,16},{24,28},{28,24},{1,5},{5... | collective-permute-start | bytes 786440 | tf_op jit(solution)/shard_map/ppermute | solution.py:15
  25.0 0.0 collective-permute-done.3.refs_3_
  25.0 2.9 %collective-permute-done.4.refs_5_ = bf16[256,512]{1,0:T(8,128)(2,1)S(1)} collective-permute-done((bf16[256,512]{1,0:T(8,128)(2,1)}, bf16[256,512]{1,0:T(8,128)(2,1)S(1)}, u32[]{:S(2)}, u32[]{:S(2)}) %collective-permute-start.4) | collective-permute-done | bytes 262176 | tf_op jit(solution)/shard_map/ppermute | solution.py:15
  27.9 3.3 %shard_map.69.refs_1_ = f32[1024,512]{1,0:T(8,128)S(1)} custom-call(s32[2]{0:T(128)S(1)} %pad_add_fusion.index_ref, bf16[1024,2048]{1,0:T(8,128)(2,1)S(1)} %shard_map.68.panel_ref, f32[256,512]{1,0:T(8,128)S(1)} %copy-done.1, bf16[256,512]{1,0:T(8,128)(2,1)S(1)} %bitcast.31, bf16[256,512]{1,0:T(8,128)(2,1)} %collective-permute-done.2.refs_1_, ...), custom_call_target="tpu_custom_call" | custom-call | bytes 28800000 | tf_op jit(solution)/shard_map/pallas_call | solution.py:446
  31.1 0.3 collective-permute-done.6.refs_0_
  31.4 1.6 %shard_map.70 = (f32[2,1024,128]{2,1,0:T(8,128)S(1)}, bf16[2,1024,128]{2,1,0:T(8,128)(2,1)S(1)}) custom-call(s32[2]{0:T(128)S(1)} %pad_add_fusion.index_ref, bf16[1024,2048]{1,0:T(8,128)(2,1)S(1)} %shard_map.68.panel_ref, bf16[256,512]{1,0:T(8,128)(2,1)S(1)} %collective-permute-done.6.refs_0_, f32[1024,512]{1,0:T(8,128)S(1)} %shard_map.69.refs_1_), custom_call_target="tpu_custom_call" | custom-call | bytes 3600000 | tf_op jit(solution)/shard_map/pallas_call | solution.py:446
  33.0 5.8 %collective-permute-start.7 = (bf16[2,1024,128]{2,1,0:T(8,128)(2,1)S(1)}, bf16[2,1024,128]{2,1,0:T(8,128)(2,1)S(1)}, u32[]{:S(2)}, u32[]{:S(2)}) collective-permute-start(bf16[2,1024,128]{2,1,0:T(8,128)(2,1)S(1)} %get-tuple-element.35), channel_id=1, source_target_pairs={{0,1},{1,0},{2,3},{3,2},{4,5},{5,4},{6,7},{7,6},{8,9},{9,8},{10,11... | collective-permute-start | bytes 1572872 | tf_op jit(solution)/shard_map/ppermute | solution.py:15
  38.8 0.1 collective-permute-start.9
  38.9 1.5 %collective-permute-done.7.moved_ref = bf16[2,1024,128]{2,1,0:T(8,128)(2,1)S(1)} collective-permute-done((bf16[2,1024,128]{2,1,0:T(8,128)(2,1)S(1)}, bf16[2,1024,128]{2,1,0:T(8,128)(2,1)S(1)}, u32[]{:S(2)}, u32[]{:S(2)}) %collective-permute-start.7) | collective-permute-done | bytes 524320 | tf_op jit(solution)/shard_map/ppermute | solution.py:15
  40.3 0.0 collective-permute-done.8.refs_2_.refs_0_
  40.3 0.4 collective-permute-start.10
  40.7 0.7 shard_map.71
  41.4 0.6 collective-permute-start.11
  42.0 0.7 collective-permute-start.14
  42.7 0.7 collective-permute-start.15
  43.4 1.5 %collective-permute-done.10.refs_3_.refs_1_ = bf16[3,256,1024]{2,1,0:T(8,128)(2,1)S(1)} collective-permute-done((bf16[3,256,1024]{2,1,0:T(8,128)(2,1)S(1)}, bf16[3,256,1024]{2,1,0:T(8,128)(2,1)S(1)}, u32[]{:S(2)}, u32[]{:S(2)}) %collective-permute-start.10) | collective-permute-done | bytes 1572896 | tf_op jit(solution)/shard_map/ppermute | solution.py:15
  44.8 0.7 shard_map.72.product_ref
  45.5 3.7 %collective-permute-done.11.moved_ref = bf16[1024,128]{1,0:T(8,128)(2,1)S(1)} collective-permute-done((bf16[1024,128]{1,0:T(8,128)(2,1)S(1)}, bf16[1024,128]{1,0:T(8,128)(2,1)S(1)}, u32[]{:S(2)}, u32[]{:S(2)}) %collective-permute-start.11) | collective-permute-done | bytes 262176 | tf_op jit(solution)/shard_map/ppermute | solution.py:15
  49.2 0.8 shard_map.73
  50.1 0.7 collective-permute-start.12
  50.7 0.7 collective-permute-start.13
  51.5 0.6 shard_map.74.refs_0_
  52.0 1.3 %collective-permute-start.18 = (bf16[1024,128]{1,0:T(8,128)(2,1)S(1)}, bf16[1024,128]{1,0:T(8,128)(2,1)S(1)}, u32[]{:S(2)}, u32[]{:S(2)}) collective-permute-start(bf16[1024,128]{1,0:T(8,128)(2,1)S(1)} %shard_map.74.refs_0_), channel_id=1, source_target_pairs={{4,8},{0,24},{5,9},{1,25},{6,10},{2,26},{7,11},{3,27}} | collective-permute-start | bytes 786440 | tf_op jit(solution)/shard_map/ppermute | solution.py:458
  53.3 0.7 collective-permute-start.20
  54.0 0.7 collective-permute-start.17
  54.7 0.7 collective-permute-start.16
  55.4 0.6 shard_map.76
  56.0 9.8 %collective-permute-done.18.refs_2_.first_ref = bf16[1024,128]{1,0:T(8,128)(2,1)S(1)} collective-permute-done((bf16[1024,128]{1,0:T(8,128)(2,1)S(1)}, bf16[1024,128]{1,0:T(8,128)(2,1)S(1)}, u32[]{:S(2)}, u32[]{:S(2)}) %collective-permute-start.18) | collective-permute-done | bytes 262176 | tf_op jit(solution)/shard_map/ppermute | solution.py:458
  65.8 0.6 shard_map.77.refs_1_
  66.4 0.7 collective-permute-start.21
  67.1 1.3 %collective-permute-start.22 = (bf16[1024,128]{1,0:T(8,128)(2,1)S(1)}, bf16[1024,128]{1,0:T(8,128)(2,1)S(1)}, u32[]{:S(2)}, u32[]{:S(2)}) collective-permute-start(bf16[1024,128]{1,0:T(8,128)(2,1)S(1)} %shard_map.77.refs_1_), channel_id=1, source_target_pairs={{8,24},{9,25},{10,26},{11,27}} | collective-permute-start | bytes 786440 | tf_op jit(solution)/shard_map/ppermute | solution.py:458
  68.4 0.7 collective-permute-start.23
  69.1 0.6 shard_map.75.line0_ref
  69.7 1.3 %collective-permute-start.19 = (bf16[1024,128]{1,0:T(8,128)(2,1)S(1)}, bf16[1024,128]{1,0:T(8,128)(2,1)S(1)}, u32[]{:S(2)}, u32[]{:S(2)}) collective-permute-start(bf16[1024,128]{1,0:T(8,128)(2,1)S(1)} %shard_map.75.line0_ref), channel_id=1, source_target_pairs={{16,20},{24,28},{17,21},{25,29},{18,22},{26,30},{19,23},{27,31}} | collective-permute-start | bytes 786440 | tf_op jit(solution)/shard_map/ppermute | solution.py:458
  71.1 9.6 %collective-permute-done.22.refs_3_ = bf16[1024,128]{1,0:T(8,128)(2,1)S(1)} collective-permute-done((bf16[1024,128]{1,0:T(8,128)(2,1)S(1)}, bf16[1024,128]{1,0:T(8,128)(2,1)S(1)}, u32[]{:S(2)}, u32[]{:S(2)}) %collective-permute-start.22) | collective-permute-done | bytes 262176 | tf_op jit(solution)/shard_map/ppermute | solution.py:458
  80.7 0.6 shard_map.78.line_ref
  81.3 0.1 collective-permute-start.27
  81.4 0.6 shard_map.79
  82.1 4.2 %collective-permute-start.24 = (bf16[2,256,128]{2,1,0:T(8,128)(2,1)S(1)}, bf16[2,256,128]{2,1,0:T(8,128)(2,1)S(1)}, u32[]{:S(2)}, u32[]{:S(2)}) collective-permute-start(bf16[2,256,128]{2,1,0:T(8,128)(2,1)S(1)} %get-tuple-element.57), channel_id=1, source_target_pairs={{0,1},{1,0},{2,3},{3,2},{4,5},{5,4},{6,7},{7,6},{8,9},{9,8},{10,11... | collective-permute-start | bytes 393224 | tf_op jit(solution)/shard_map/ppermute | solution.py:15
  86.3 0.7 collective-permute-start.25
  87.0 1.0 collective-permute-start.26
  88.0 2.0 %shard_map.80.current_ref = f32[1024,128]{1,0:T(8,128)S(1)} custom-call(s32[2]{0:T(128)S(1)} %pad_add_fusion.index_ref, f32[1024,128]{1,0:T(8,128)S(1)} %get-tuple-element.50.current_ref, bf16[1024,128]{1,0:T(8,128)(2,1)S(1)} %get-tuple-element.51.known_ref, bf16[1024,128]{1,0:T(8,128)(2,1)S(1)} %collective-permute-done.18.refs_2_.first_ref, ...), custom_call_target="tpu_custom_call" | custom-call | bytes 28800000 | tf_op jit(solution)/shard_map/pallas_call | solution.py:446
  90.0 1.1 %shard_map.82 = bf16[2,2,256,128]{3,2,1,0:T(8,128)(2,1)S(1)} custom-call(s32[2]{0:T(128)S(1)} %pad_add_fusion.index_ref, f32[1024,128]{1,0:T(8,128)S(1)} %shard_map.80.current_ref, bf16[1024,128]{1,0:T(8,128)(2,1)S(1)} %collective-permute-done.27.value_ref, bf16[3,256,1024]{2,1,0:T(8,128)(2,1)S(1)} %collective-permute-done.8.refs_2_.refs_0_, ...), custom_call_target="tpu_custom_call" | custom-call | bytes 3600000 | tf_op jit(solution)/shard_map/pallas_call | solution.py:446
  91.2 0.7 collective-permute-start.29
  92.0 2.8 %collective-permute-start.30 = (bf16[2,256,128]{2,1,0:T(8,128)(2,1)S(1)}, bf16[2,256,128]{2,1,0:T(8,128)(2,1)S(1)}, u32[]{:S(2)}, u32[]{:S(2)}) collective-permute-start(bf16[2,256,128]{2,1,0:T(8,128)(2,1)S(1)} %get-tuple-element.59), channel_id=1, source_target_pairs={{0,3},{1,2},{2,1},{3,0},{4,7},{5,6},{6,5},{7,4},{8,11},{9,10},{10,... | collective-permute-start | bytes 393224 | tf_op jit(solution)/shard_map/ppermute | solution.py:15
  94.8 1.1 %shard_map.81 = bf16[2,2,256,128]{3,2,1,0:T(8,128)(2,1)S(1)} custom-call(s32[2]{0:T(128)S(1)} %pad_add_fusion.index_ref, f32[1024,128]{1,0:T(8,128)S(1)} %shard_map.80.current_ref, bf16[1024,128]{1,0:T(8,128)(2,1)S(1)} %collective-permute-done.27.value_ref, bf16[3,256,1024]{2,1,0:T(8,128)(2,1)S(1)} %pad_maximum_fusion.refs_0_, ...), custom_call_target="tpu_custom_call" | custom-call | bytes 28800000 | tf_op jit(solution)/shard_map/pallas_call | solution.py:446
  95.9 0.1 collective-permute-start.28
  96.0 4.2 %collective-permute-done.30.refs_7_ = bf16[2,256,128]{2,1,0:T(8,128)(2,1)S(1)} collective-permute-done((bf16[2,256,128]{2,1,0:T(8,128)(2,1)S(1)}, bf16[2,256,128]{2,1,0:T(8,128)(2,1)S(1)}, u32[]{:S(2)}, u32[]{:S(2)}) %collective-permute-start.30) | collective-permute-done | bytes 131104 | tf_op jit(solution)/shard_map/ppermute | solution.py:15
  100.2 1.7 %shard_map.83 = (bf16[3,256,512]{2,1,0:T(8,128)(2,1)}, f32[256,512]{1,0:T(8,128)}) custom-call(s32[2]{0:T(128)S(1)} %pad_add_fusion.index_ref, bf16[2,256,128]{2,1,0:T(8,128)(2,1)S(1)} %get-tuple-element.58.refs_0_, bf16[2,256,128]{2,1,0:T(8,128)(2,1)S(1)} %collective-permute-done.24.refs_1_, bf16[2,256,128]{2,1,0:T(8,128)(2,1)S(1)} %collective-permute-done.25.refs_2_, ...), custom_call_target="tpu_custom_call" | custom-call | bytes 3600000 | tf_op jit(solution)/shard_map/pallas_call | solution.py:433
  (26 shorter events, 0.1 us)
Async XLA Ops:
  2.6 1.5 %copy-start.2 = (bf16[1,256,512]{2,1,0:T(8,128)(2,1)S(1)}, bf16[1,256,512]{2,1,0:T(8,128)(2,1)}, u32[]{:S(2)}) copy-start(bf16[1,256,512]{2,1,0:T(8,128)(2,1)} %param.7) | copy-start | bytes 786436
  2.8 37.5 %collective-permute-start.8 = (bf16[3,256,1024]{2,1,0:T(8,128)(2,1)S(1)}, bf16[3,256,1024]{2,1,0:T(8,128)(2,1)S(1)}, u32[]{:S(2)}, u32[]{:S(2)}) collective-permute-start(bf16[3,256,1024]{2,1,0:T(8,128)(2,1)S(1)} %pad_maximum_fusion.refs_0_), channel_id=1, source_target_pairs={{0,2},{1,3},{2,0},{3,1},{4,6},{5,7},{6,4},{7,5},{8,10},{9,11},{10,... | collective-permute-start | bytes 4718600 | tf_op jit(solution)/shard_map/ppermute | solution.py:15
  4.1 11.6 %collective-permute-start = (bf16[256,512]{1,0:T(8,128)(2,1)S(1)}, bf16[256,512]{1,0:T(8,128)(2,1)}, u32[]{:S(2)}, u32[]{:S(2)}) collective-permute-start(bf16[256,512]{1,0:T(8,128)(2,1)S(1)} %bitcast.27), channel_id=1, source_target_pairs={{0,8},{4,12},{8,0},{12,4},{16,24},{20,28},{24,16},{28,20},{1,9},{5... | collective-permute-start | bytes 786440 | tf_op jit(solution)/shard_map/ppermute | solution.py:15
  4.3 13.5 %collective-permute-start.1 = (bf16[256,512]{1,0:T(8,128)(2,1)S(1)}, bf16[256,512]{1,0:T(8,128)(2,1)}, u32[]{:S(2)}, u32[]{:S(2)}) collective-permute-start(bf16[256,512]{1,0:T(8,128)(2,1)S(1)} %bitcast.28), channel_id=1, source_target_pairs={{0,16},{4,20},{8,24},{12,28},{16,0},{20,4},{24,8},{28,12},{1,17},{... | collective-permute-start | bytes 786440 | tf_op jit(solution)/shard_map/ppermute | solution.py:15
  4.3 13.4 %collective-permute-start.2 = (bf16[256,512]{1,0:T(8,128)(2,1)S(1)}, bf16[256,512]{1,0:T(8,128)(2,1)}, u32[]{:S(2)}, u32[]{:S(2)}) collective-permute-start(bf16[256,512]{1,0:T(8,128)(2,1)S(1)} %bitcast.29), channel_id=1, source_target_pairs={{0,4},{4,0},{8,12},{12,8},{16,20},{20,16},{24,28},{28,24},{1,5},{5... | collective-permute-start | bytes 786440 | tf_op jit(solution)/shard_map/ppermute | solution.py:15
  5.7 2.2 %copy-start = (bf16[1024,8,256]{2,1,0:T(8,128)(2,1)S(1)}, bf16[1024,8,256]{2,1,0:T(8,128)(2,1)}, u32[]{:S(2)}) copy-start(bf16[1024,8,256]{2,1,0:T(8,128)(2,1)} %panel_ref.1) | copy-start | bytes 12582916
  7.8 20.0 %copy-start.1 = (f32[256,512]{1,0:T(8,128)S(1)}, f32[256,512]{1,0:T(8,128)}, u32[]{:S(2)}) copy-start(f32[256,512]{1,0:T(8,128)} %side_ref.1) | copy-start | bytes 1572868
  15.7 8.1 %collective-permute-start.5 = (bf16[256,512]{1,0:T(8,128)(2,1)S(1)}, bf16[256,512]{1,0:T(8,128)(2,1)S(1)}, u32[]{:S(2)}, u32[]{:S(2)}) collective-permute-start(bf16[256,512]{1,0:T(8,128)(2,1)S(1)} %bitcast.30), channel_id=1, source_target_pairs={{0,24},{4,28},{8,16},{12,20},{16,8},{20,12},{24,0},{28,4},{1,25},{... | collective-permute-start | bytes 786440 | tf_op jit(solution)/shard_map/ppermute | solution.py:15
  16.5 8.5 %collective-permute-start.3 = (bf16[256,512]{1,0:T(8,128)(2,1)}, bf16[256,512]{1,0:T(8,128)(2,1)S(1)}, u32[]{:S(2)}, u32[]{:S(2)}) collective-permute-start(bf16[256,512]{1,0:T(8,128)(2,1)} %collective-permute-done.refs_2_), channel_id=1, source_target_pairs={{0,4},{4,0},{8,12},{12,8},{16,20},{20,16},{24,28},{28,24},{1,5},{5... | collective-permute-start | bytes 786440 | tf_op jit(solution)/shard_map/ppermute | solution.py:15
  17.8 10.1 %collective-permute-start.4 = (bf16[256,512]{1,0:T(8,128)(2,1)}, bf16[256,512]{1,0:T(8,128)(2,1)S(1)}, u32[]{:S(2)}, u32[]{:S(2)}) collective-permute-start(bf16[256,512]{1,0:T(8,128)(2,1)} %collective-permute-done.1.refs_4_), channel_id=1, source_target_pairs={{0,4},{4,0},{8,12},{12,8},{16,20},{20,16},{24,28},{28,24},{1,5},{5... | collective-permute-start | bytes 786440 | tf_op jit(solution)/shard_map/ppermute | solution.py:15
  23.8 7.7 %collective-permute-start.6 = (bf16[256,512]{1,0:T(8,128)(2,1)S(1)}, bf16[256,512]{1,0:T(8,128)(2,1)S(1)}, u32[]{:S(2)}, u32[]{:S(2)}) collective-permute-start(bf16[256,512]{1,0:T(8,128)(2,1)S(1)} %collective-permute-done.5.refs_6_), channel_id=1, source_target_pairs={{0,4},{4,0},{8,12},{12,8},{16,20},{20,16},{24,28},{28,24},{1,5},{5... | collective-permute-start | bytes 786440 | tf_op jit(solution)/shard_map/ppermute | solution.py:15
  33.0 7.3 %collective-permute-start.7 = (bf16[2,1024,128]{2,1,0:T(8,128)(2,1)S(1)}, bf16[2,1024,128]{2,1,0:T(8,128)(2,1)S(1)}, u32[]{:S(2)}, u32[]{:S(2)}) collective-permute-start(bf16[2,1024,128]{2,1,0:T(8,128)(2,1)S(1)} %get-tuple-element.35), channel_id=1, source_target_pairs={{0,1},{1,0},{2,3},{3,2},{4,5},{5,4},{6,7},{7,6},{8,9},{9,8},{10,11... | collective-permute-start | bytes 1572872 | tf_op jit(solution)/shard_map/ppermute | solution.py:15
  38.8 4.6 %collective-permute-start.9 = (bf16[3,256,1024]{2,1,0:T(8,128)(2,1)S(1)}, bf16[3,256,1024]{2,1,0:T(8,128)(2,1)S(1)}, u32[]{:S(2)}, u32[]{:S(2)}) collective-permute-start(bf16[3,256,1024]{2,1,0:T(8,128)(2,1)S(1)} %pad_maximum_fusion.refs_0_), channel_id=1, source_target_pairs={{0,1},{1,0},{2,3},{3,2},{4,5},{5,4},{6,7},{7,6},{8,9},{9,8},{10,11... | collective-permute-start | bytes 4718600 | tf_op jit(solution)/shard_map/ppermute | solution.py:15
  40.3 4.5 %collective-permute-start.10 = (bf16[3,256,1024]{2,1,0:T(8,128)(2,1)S(1)}, bf16[3,256,1024]{2,1,0:T(8,128)(2,1)S(1)}, u32[]{:S(2)}, u32[]{:S(2)}) collective-permute-start(bf16[3,256,1024]{2,1,0:T(8,128)(2,1)S(1)} %collective-permute-done.8.refs_2_.refs_0_), channel_id=1, source_target_pairs={{0,1},{1,0},{2,3},{3,2},{4,5},{5,4},{6,7},{7,6},{8,9},{9,8},{10,11... | collective-permute-start | bytes 4718600 | tf_op jit(solution)/shard_map/ppermute | solution.py:15
  41.4 7.8 %collective-permute-start.11 = (bf16[1024,128]{1,0:T(8,128)(2,1)S(1)}, bf16[1024,128]{1,0:T(8,128)(2,1)S(1)}, u32[]{:S(2)}, u32[]{:S(2)}) collective-permute-start(bf16[1024,128]{1,0:T(8,128)(2,1)S(1)} %get-tuple-element.40), channel_id=1, source_target_pairs={{0,2},{1,3},{2,0},{3,1},{4,6},{5,7},{6,4},{7,5},{8,10},{9,11},{10,... | collective-permute-start | bytes 786440 | tf_op jit(solution)/shard_map/ppermute | solution.py:15
  42.0 9.4 %collective-permute-start.14 = (bf16[1024,128]{1,0:T(8,128)(2,1)S(1)}, bf16[1024,128]{1,0:T(8,128)(2,1)S(1)}, u32[]{:S(2)}, u32[]{:S(2)}) collective-permute-start(bf16[1024,128]{1,0:T(8,128)(2,1)S(1)} %get-tuple-element.46), channel_id=1, source_target_pairs={{0,4},{1,5},{2,6},{3,7}} | collective-permute-start | bytes 786440 | tf_op jit(solution)/shard_map/ppermute | solution.py:458
  42.7 8.8 %collective-permute-start.15 = (bf16[1024,128]{1,0:T(8,128)(2,1)S(1)}, bf16[1024,128]{1,0:T(8,128)(2,1)S(1)}, u32[]{:S(2)}, u32[]{:S(2)}) collective-permute-start(bf16[1024,128]{1,0:T(8,128)(2,1)S(1)} %get-tuple-element.40), channel_id=1, source_target_pairs={{0,6},{1,7},{2,4},{3,5}} | collective-permute-start | bytes 786440 | tf_op jit(solution)/shard_map/ppermute | solution.py:503
  50.1 4.7 %collective-permute-start.12 = (bf16[1024,128]{1,0:T(8,128)(2,1)S(1)}, bf16[1024,128]{1,0:T(8,128)(2,1)S(1)}, u32[]{:S(2)}, u32[]{:S(2)}) collective-permute-start(bf16[1024,128]{1,0:T(8,128)(2,1)S(1)} %get-tuple-element.41.own_ref.refs_0_.own0_ref), channel_id=1, source_target_pairs={{0,8},{1,9},{2,10},{3,11}} | collective-permute-start | bytes 786440 | tf_op jit(solution)/shard_map/ppermute | solution.py:458
  50.7 4.7 %collective-permute-start.13 = (bf16[1024,128]{1,0:T(8,128)(2,1)S(1)}, bf16[1024,128]{1,0:T(8,128)(2,1)S(1)}, u32[]{:S(2)}, u32[]{:S(2)}) collective-permute-start(bf16[1024,128]{1,0:T(8,128)(2,1)S(1)} %get-tuple-element.41.own_ref.refs_0_.own0_ref), channel_id=1, source_target_pairs={{0,4},{1,5},{2,6},{3,7}} | collective-permute-start | bytes 786440 | tf_op jit(solution)/shard_map/ppermute | solution.py:458
  52.0 13.8 %collective-permute-start.18 = (bf16[1024,128]{1,0:T(8,128)(2,1)S(1)}, bf16[1024,128]{1,0:T(8,128)(2,1)S(1)}, u32[]{:S(2)}, u32[]{:S(2)}) collective-permute-start(bf16[1024,128]{1,0:T(8,128)(2,1)S(1)} %shard_map.74.refs_0_), channel_id=1, source_target_pairs={{4,8},{0,24},{5,9},{1,25},{6,10},{2,26},{7,11},{3,27}} | collective-permute-start | bytes 786440 | tf_op jit(solution)/shard_map/ppermute | solution.py:458
  53.3 12.5 %collective-permute-start.20 = (bf16[1024,128]{1,0:T(8,128)(2,1)S(1)}, bf16[1024,128]{1,0:T(8,128)(2,1)S(1)}, u32[]{:S(2)}, u32[]{:S(2)}) collective-permute-start(bf16[1024,128]{1,0:T(8,128)(2,1)S(1)} %shard_map.74.refs_0_), channel_id=1, source_target_pairs={{4,12},{5,13},{6,14},{7,15}} | collective-permute-start | bytes 786440 | tf_op jit(solution)/shard_map/ppermute | solution.py:458
  54.0 15.1 %collective-permute-start.17 = (bf16[1024,128]{1,0:T(8,128)(2,1)S(1)}, bf16[1024,128]{1,0:T(8,128)(2,1)S(1)}, u32[]{:S(2)}, u32[]{:S(2)}) collective-permute-start(bf16[1024,128]{1,0:T(8,128)(2,1)S(1)} %shard_map.74.refs_0_), channel_id=1, source_target_pairs={{0,16},{1,17},{2,18},{3,19}} | collective-permute-start | bytes 786440 | tf_op jit(solution)/shard_map/ppermute | solution.py:458
  54.7 16.3 %collective-permute-start.16 = (bf16[1024,128]{1,0:T(8,128)(2,1)S(1)}, bf16[1024,128]{1,0:T(8,128)(2,1)S(1)}, u32[]{:S(2)}, u32[]{:S(2)}) collective-permute-start(bf16[1024,128]{1,0:T(8,128)(2,1)S(1)} %shard_map.74.refs_0_), channel_id=1, source_target_pairs={{4,28},{0,12},{5,29},{1,13},{6,30},{2,14},{7,31},{3,15}} | collective-permute-start | bytes 786440 | tf_op jit(solution)/shard_map/ppermute | solution.py:458
  66.4 4.6 %collective-permute-start.21 = (bf16[1024,128]{1,0:T(8,128)(2,1)S(1)}, bf16[1024,128]{1,0:T(8,128)(2,1)S(1)}, u32[]{:S(2)}, u32[]{:S(2)}) collective-permute-start(bf16[1024,128]{1,0:T(8,128)(2,1)S(1)} %shard_map.77.refs_1_), channel_id=1, source_target_pairs={{8,16},{12,20},{9,17},{13,21},{10,18},{14,22},{11,19},{15,23}} | collective-permute-start | bytes 786440 | tf_op jit(solution)/shard_map/ppermute | solution.py:458
  67.1 13.6 %collective-permute-start.22 = (bf16[1024,128]{1,0:T(8,128)(2,1)S(1)}, bf16[1024,128]{1,0:T(8,128)(2,1)S(1)}, u32[]{:S(2)}, u32[]{:S(2)}) collective-permute-start(bf16[1024,128]{1,0:T(8,128)(2,1)S(1)} %shard_map.77.refs_1_), channel_id=1, source_target_pairs={{8,24},{9,25},{10,26},{11,27}} | collective-permute-start | bytes 786440 | tf_op jit(solution)/shard_map/ppermute | solution.py:458
  68.4 12.3 %collective-permute-start.23 = (bf16[1024,128]{1,0:T(8,128)(2,1)S(1)}, bf16[1024,128]{1,0:T(8,128)(2,1)S(1)}, u32[]{:S(2)}, u32[]{:S(2)}) collective-permute-start(bf16[1024,128]{1,0:T(8,128)(2,1)S(1)} %shard_map.77.refs_1_), channel_id=1, source_target_pairs={{8,0},{9,1},{10,2},{11,3}} | collective-permute-start | bytes 786440 | tf_op jit(solution)/shard_map/ppermute | solution.py:458
  69.7 11.6 %collective-permute-start.19 = (bf16[1024,128]{1,0:T(8,128)(2,1)S(1)}, bf16[1024,128]{1,0:T(8,128)(2,1)S(1)}, u32[]{:S(2)}, u32[]{:S(2)}) collective-permute-start(bf16[1024,128]{1,0:T(8,128)(2,1)S(1)} %shard_map.75.line0_ref), channel_id=1, source_target_pairs={{16,20},{24,28},{17,21},{25,29},{18,22},{26,30},{19,23},{27,31}} | collective-permute-start | bytes 786440 | tf_op jit(solution)/shard_map/ppermute | solution.py:458
  81.3 8.7 %collective-permute-start.27 = (bf16[1024,128]{1,0:T(8,128)(2,1)S(1)}, bf16[1024,128]{1,0:T(8,128)(2,1)S(1)}, u32[]{:S(2)}, u32[]{:S(2)}) collective-permute-start(bf16[1024,128]{1,0:T(8,128)(2,1)S(1)} %shard_map.78.line_ref), channel_id=1, source_target_pairs={{0,4},{4,0},{8,12},{12,8},{16,20},{20,16},{24,28},{28,24},{1,5},{5... | collective-permute-start | bytes 786440 | tf_op jit(solution)/shard_map/ppermute | solution.py:15
  82.1 13.9 %collective-permute-start.24 = (bf16[2,256,128]{2,1,0:T(8,128)(2,1)S(1)}, bf16[2,256,128]{2,1,0:T(8,128)(2,1)S(1)}, u32[]{:S(2)}, u32[]{:S(2)}) collective-permute-start(bf16[2,256,128]{2,1,0:T(8,128)(2,1)S(1)} %get-tuple-element.57), channel_id=1, source_target_pairs={{0,1},{1,0},{2,3},{3,2},{4,5},{5,4},{6,7},{7,6},{8,9},{9,8},{10,11... | collective-permute-start | bytes 393224 | tf_op jit(solution)/shard_map/ppermute | solution.py:15
  86.3 9.7 %collective-permute-start.25 = (bf16[2,256,128]{2,1,0:T(8,128)(2,1)S(1)}, bf16[2,256,128]{2,1,0:T(8,128)(2,1)S(1)}, u32[]{:S(2)}, u32[]{:S(2)}) collective-permute-start(bf16[2,256,128]{2,1,0:T(8,128)(2,1)S(1)} %get-tuple-element.56), channel_id=1, source_target_pairs={{0,2},{1,3},{2,0},{3,1},{4,6},{5,7},{6,4},{7,5},{8,10},{9,11},{10,... | collective-permute-start | bytes 393224 | tf_op jit(solution)/shard_map/ppermute | solution.py:15
  87.0 9.0 %collective-permute-start.26 = (bf16[2,256,128]{2,1,0:T(8,128)(2,1)S(1)}, bf16[2,256,128]{2,1,0:T(8,128)(2,1)S(1)}, u32[]{:S(2)}, u32[]{:S(2)}) collective-permute-start(bf16[2,256,128]{2,1,0:T(8,128)(2,1)S(1)} %get-tuple-element.55), channel_id=1, source_target_pairs={{0,3},{1,2},{2,1},{3,0},{4,7},{5,6},{6,5},{7,4},{8,11},{9,10},{10,... | collective-permute-start | bytes 393224 | tf_op jit(solution)/shard_map/ppermute | solution.py:15
  91.2 4.8 %collective-permute-start.29 = (bf16[2,256,128]{2,1,0:T(8,128)(2,1)S(1)}, bf16[2,256,128]{2,1,0:T(8,128)(2,1)S(1)}, u32[]{:S(2)}, u32[]{:S(2)}) collective-permute-start(bf16[2,256,128]{2,1,0:T(8,128)(2,1)S(1)} %get-tuple-element.60), channel_id=1, source_target_pairs={{0,2},{1,3},{2,0},{3,1},{4,6},{5,7},{6,4},{7,5},{8,10},{9,11},{10,... | collective-permute-start | bytes 393224 | tf_op jit(solution)/shard_map/ppermute | solution.py:15
  92.0 8.3 %collective-permute-start.30 = (bf16[2,256,128]{2,1,0:T(8,128)(2,1)S(1)}, bf16[2,256,128]{2,1,0:T(8,128)(2,1)S(1)}, u32[]{:S(2)}, u32[]{:S(2)}) collective-permute-start(bf16[2,256,128]{2,1,0:T(8,128)(2,1)S(1)} %get-tuple-element.59), channel_id=1, source_target_pairs={{0,3},{1,2},{2,1},{3,0},{4,7},{5,6},{6,5},{7,4},{8,11},{9,10},{10,... | collective-permute-start | bytes 393224 | tf_op jit(solution)/shard_map/ppermute | solution.py:15
  95.9 4.3 %collective-permute-start.28 = (bf16[2,256,128]{2,1,0:T(8,128)(2,1)S(1)}, bf16[2,256,128]{2,1,0:T(8,128)(2,1)S(1)}, u32[]{:S(2)}, u32[]{:S(2)}) collective-permute-start(bf16[2,256,128]{2,1,0:T(8,128)(2,1)S(1)} %get-tuple-element.61), channel_id=1, source_target_pairs={{0,1},{1,0},{2,3},{3,2},{4,5},{5,4},{6,7},{7,6},{8,9},{9,8},{10,11... | collective-permute-start | bytes 393224 | tf_op jit(solution)/shard_map/ppermute | solution.py:15
